TPU v7x, 32 devices: a whole 2x2x4 slice. The times are simulated.
32 devices in a mesh: seq: 8 (over z, x), ch: 4 (over y, core).
Axes of the slice: x: 2, y: 2, z: 4, core: 2. Of those that a mesh axis runs over, the one named last changes fastest.
Arguments:
- out_gate: bfloat16 [3072, 4096], P('seq', 'ch'), may hold values from -6 to 6
- in_gate: bfloat16 [3072, 4096], P('seq', 'ch'), may hold values from -6 to 6
- values: bfloat16 [3072, 4096], P('seq', 'ch'), may hold values from -6 to 6
- short_filter: float32 [3, 3, 4096], P(None, None, 'ch'), may hold values from -3 to 3
- long_filter: float32 [3072, 4096], P('seq', 'ch'), may hold values from -1.5 to 1.5
- skip_gain: float32 [4096], P('ch'), may hold values from -4 to 4
- out_weight: bfloat16 [4096, 4096], P(None, 'ch'), may hold values from -0.09375 to 0.09375
Outputs:
- projected: bfloat16 [3072, 4096], P('seq', 'ch')
All inputs are finite; a program needn't handle non-finite values.
Results may differ from a plain program's by a relative error of at most 0.0049.
Values may be sent and summed in bfloat16 or wider, within the bound.
No kernel may reach another device: no remote copies, remote signals or barrier semaphores. Data moves between devices by JAX's collectives and lax.ppermute only.
A program may use at most 128 MiB of HBM per device.

v0:
```python
import math

import jax
import jax.numpy as jnp
from jax import lax
from jax.sharding import PartitionSpec as P

highest = lax.Precision.HIGHEST


def shifted(block, axis, distance):
    devices = range(lax.axis_size(axis))
    route = [(i - distance, i) for i in devices if i - distance in devices]
    return lax.ppermute(block, axis, route)


def phase_table(row_ids, col_ids, modulus, direction):
    product = row_ids[:, None] * col_ids[None, :] % modulus
    angles = product.astype(jnp.float32) * (direction * 2.0 * math.pi / modulus)
    return (jnp.cos(angles), jnp.sin(angles))


def contract(pattern, first_op, second_op):
    return jnp.einsum(pattern, first_op, second_op, precision=highest)


def complex_apply(pattern, phases, operand):
    cosine, sine_part = phases
    real_part, imaginary = operand
    return (
        contract(pattern, cosine, real_part) - contract(pattern, sine_part, imaginary),
        contract(pattern, cosine, imaginary) + contract(pattern, sine_part, real_part),
    )


def complex_times(first_op, second_op):
    return (
        first_op[0] * second_op[0] - first_op[1] * second_op[1],
        first_op[0] * second_op[1] + first_op[1] * second_op[0],
    )


def sequence_conv(mixed_in, long_filter):
    seq_count = lax.axis_size("seq")
    seq_index = lax.axis_index("seq")
    row_count = mixed_in.shape[0]
    total_len = row_count * seq_count
    piece_rows = row_count // seq_count
    rows_b = jnp.arange(row_count, dtype=jnp.int32)
    device_ids = jnp.arange(seq_count, dtype=jnp.int32)
    positions = seq_index * row_count + rows_b
    angles = positions.astype(jnp.float32) * (math.pi / total_len)
    cosines = jnp.cos(angles)[:, None]
    sines = jnp.sin(angles)[:, None]
    planes = jnp.stack([mixed_in, long_filter])[:, None]
    spread = lax.all_to_all(planes, "seq", split_axis=2, concat_axis=1, tiled=True)
    local_b = seq_index * piece_rows + jnp.arange(piece_rows, dtype=jnp.int32)
    arrived_pos = device_ids[:, None] * row_count + local_b[None, :]
    arrived_angles = arrived_pos.astype(jnp.float32) * (math.pi / total_len)
    arrived_cos = jnp.cos(arrived_angles)[:, :, None]
    arrived_sin = jnp.sin(arrived_angles)[:, :, None]
    zeros_plane = jnp.zeros_like(spread[0])
    real_part = jnp.stack([spread[0], spread[0] * arrived_cos, spread[1], spread[1] * arrived_cos])
    imaginary = jnp.stack(
        [zeros_plane, -spread[0] * arrived_sin, zeros_plane, -spread[1] * arrived_sin]
    )
    sectioned = complex_apply(
        "kp,xpbc->xkbc",
        phase_table(device_ids, device_ids, seq_count, -1.0),
        (real_part, imaginary),
    )
    twist_table = phase_table(device_ids, local_b, total_len, -1.0)
    sectioned = complex_times(sectioned, (twist_table[0][:, :, None], twist_table[1][:, :, None]))
    arrived = (
        lax.all_to_all(sectioned[0], "seq", split_axis=1, concat_axis=2, tiled=True),
        lax.all_to_all(sectioned[1], "seq", split_axis=1, concat_axis=2, tiled=True),
    )
    spectra = complex_apply("mb,xkbc->xkmc", phase_table(rows_b, rows_b, row_count, -1.0), arrived)
    product = complex_times((spectra[0][:2], spectra[1][:2]), (spectra[0][2:], spectra[1][2:]))
    sectioned = complex_apply("mb,xkmc->xkbc", phase_table(rows_b, rows_b, row_count, 1.0), product)
    twist_table = phase_table(seq_index.reshape(1), rows_b, total_len, 1.0)
    sectioned = complex_times(sectioned, (twist_table[0][:, :, None], twist_table[1][:, :, None]))
    returned = (
        lax.all_to_all(sectioned[0], "seq", split_axis=2, concat_axis=1, tiled=True),
        lax.all_to_all(sectioned[1], "seq", split_axis=2, concat_axis=1, tiled=True),
    )
    sectioned = complex_apply(
        "kp,xkbc->xpbc", phase_table(device_ids, device_ids, seq_count, 1.0), returned
    )
    restored = (
        lax.all_to_all(sectioned[0], "seq", split_axis=1, concat_axis=2, tiled=True),
        lax.all_to_all(sectioned[1], "seq", split_axis=1, concat_axis=2, tiled=True),
    )
    real_out = restored[0][:, 0] / total_len
    imag_out = restored[1][:, 0] / total_len
    return 0.5 * (real_out[0] + cosines * real_out[1] - sines * imag_out[1])


def on_device(out_gate, in_gate, values, short_filter, long_filter, skip_gain, out_weight):
    tap_count = short_filter.shape[1]
    row_count = out_gate.shape[0]
    stacked = jnp.stack([out_gate, in_gate, values])
    rim_rows = shifted(stacked[:, row_count - (tap_count - 1) :], "seq", 1)
    widened = jnp.concatenate([rim_rows, stacked], axis=1).astype(jnp.float32)
    shorted = short_filter[:, 0, None, :] * widened[:, tap_count - 1 :]
    for offset in range(1, tap_count):
        start_row = tap_count - 1 - offset
        shorted = (
            shorted
            + short_filter[:, offset, None, :] * widened[:, start_row : start_row + row_count]
        )
    gate_late = shorted[0]
    mixed_in = shorted[1] * shorted[2]
    long_out = sequence_conv(mixed_in, long_filter)
    filtered = long_out + skip_gain * mixed_in
    mixed = (gate_late * filtered).astype(jnp.bfloat16)
    summed = jnp.dot(
        lax.all_gather(mixed, "ch", axis=1, tiled=True),
        out_weight,
        preferred_element_type=jnp.float32,
    )
    return summed.astype(jnp.bfloat16)


def solution(mesh):
    return jax.shard_map(
        on_device,
        mesh=mesh,
        in_specs=(
            P("seq", "ch"),
            P("seq", "ch"),
            P("seq", "ch"),
            P(None, None, "ch"),
            P("seq", "ch"),
            P("ch"),
            P(None, "ch"),
        ),
        out_specs=P("seq", "ch"),
        check_vma=False,
    )
```

profile of v0, /device:TPU:1, one launch (start us, length us, event | category | flops | bytes accessed | tf_op | source)
XLA Modules:
  0.0 929.9 jit_solution(14585842419580291444)
XLA Ops:
  6.5 0.8 pad_maximum_fusion.6
  7.3 3.9 collective-permute-start
  11.3 0.9 fusion.207
  12.3 2.3 maximum_convert_fusion
  14.6 1.4 fusion.4
  16.0 0.3 slice_multiply_fusion.3
  16.2 2.3 copy-done.9
  18.5 0.4 maximum_bitcast_fusion
  18.9 4.9 copy.74
  23.8 6.0 all-to-all-start
  30.3 68.0 %all-to-all-done = f32[2,1,384,1024]{3,1,0,2:T(1,128)S(1)} async-done(((f32[2,1,384,1024]{3,1,0,2:T(1,128)}), f32[2,1,384,1024]{3,1,0,2:T(1,128)S(1)}, u32[]{:S(2)}, u32[]{:S(2)}) %all-to-all-start) | async-done | bytes 3145760 | tf_op jit(solution)/shard_map/all_to_all | solution.py:56
  98.3 2.2 fusion.204
  100.5 0.3 copy.128
  100.8 0.3 copy.129
  101.2 1.0 fusion.205
  102.2 1.0 fusion.206
  103.3 8.9 fusion.7
  112.2 9.3 %fusion.6 = f32[4,48,1024,8]{2,3,1,0:T(8,128)S(1)} fusion(f32[1,8,48,1024]{3,1,2,0:T(8,128)S(1)} %get-tuple-element.19, f32[1,8,48,1024]{3,1,2,0:T(8,128)S(1)} %get-tuple-element.18, f32[1,8,48,1024]{3,1,2,0:T(8,128)S(1)} %get-tuple-element.16, f32[1,8,48,1024]{3,1,2,0:T(8,128)S(1)} %get-tuple-element.15), kind=kOutput, calls=%fused_computation.17 | convolution fusion | flops 155714432 | bytes 12582912 | tf_op jit(solution)/shard_map/kp,xpbc->xkbc/dot_general | solution.py:24
  121.8 8.2 fusion.3
  130.0 14.8 %fusion = (f32[4,8,48,1024]{3,1,2,0:T(8,128)}, f32[4,8,48,1024]{3,1,2,0:T(8,128)}) fusion(f32[8,48]{0,1:T(8,128)S(1)} %copy.90, f32[8,48]{0,1:T(8,128)S(1)} %copy.87, f32[4,48,1024,8]{2,3,1,0:T(8,128)S(1)} %fusion.6, f32[4,48,1024,8]{2,3,1,0:T(8,128)S(1)} %fusion.7, f32[4,48,1024,8]{2,3,1,0:T(8,128)} %fusion.3, f32[1,8,48,1024]{3,1,2,0:T(8,128)} %copy-done.4, ...), kind=kOutput, calls=%fused_computation.4 | convolution fusion | flops 168297344 | bytes 36178944 | tf_op jit(solution)/shard_map/kp,xpbc->xkbc/dot_general | solution.py:24
  144.8 9.1 copy.91
  153.9 5.8 all-to-all-start.1
  159.8 9.1 copy.94
  168.9 127.4 %all-to-all-done.1 = f32[4,8,48,1024]{3,2,0,1:T(8,128)} async-done(((f32[4,8,48,1024]{3,2,0,1:T(8,128)}), f32[4,8,48,1024]{3,2,0,1:T(8,128)}, u32[]{:S(2)}, u32[]{:S(2)}) %all-to-all-start.1) | async-done | bytes 6291488 | tf_op jit(solution)/shard_map/all_to_all | solution.py:75
  296.3 5.5 all-to-all-start.2
  301.8 3.4 copy.92
  305.2 2.6 copy-done
  307.8 27.6 %fusion.53 = f32[4,1024,384]{2,1,0:T(8,128)} fusion(f32[4,384,1024]{2,1,0:T(8,128)S(1)} %bitcast.169), kind=kOutput, calls=%fused_computation.79 | convolution fusion | flops 7249084416 | bytes 12582912 | tf_op jit(solution)/shard_map/mb,xkbc->xkmc/dot_general | solution.py:24
  335.4 102.8 %all-to-all-done.2 = f32[4,8,48,1024]{3,2,0,1:T(8,128)} async-done(((f32[4,8,48,1024]{3,2,0,1:T(8,128)}), f32[4,8,48,1024]{3,2,0,1:T(8,128)}, u32[]{:S(2)}, u32[]{:S(2)}) %all-to-all-start.2) | async-done | bytes 6291488 | tf_op jit(solution)/shard_map/all_to_all | solution.py:76
  438.3 3.5 copy.95
  441.8 25.6 %fusion.51 = f32[4,1024,384]{2,1,0:T(8,128)S(1)} fusion(f32[4,384,1024]{2,1,0:T(8,128)S(1)} %bitcast.173), kind=kOutput, calls=%fused_computation.77 | convolution fusion | flops 7249084416 | bytes 12582912 | tf_op jit(solution)/shard_map/mb,xkbc->xkmc/dot_general | solution.py:24
  467.4 25.2 %subtract_bitcast_fusion = f32[4,1,384,1024]{2,3,0,1:T(8,128)S(1)} fusion(f32[4,1024,384]{2,1,0:T(8,128)S(1)} %bitcast.178, f32[4,384,1024]{2,1,0:T(8,128)S(1)} %bitcast.174), kind=kOutput, calls=%fused_computation.9 | convolution fusion | flops 7250657280 | bytes 18874368 | tf_op jit(solution)/shard_map/mb,xkbc->xkmc/dot_general | solution.py:24
  492.7 27.8 %add_bitcast_fusion = f32[4,1,384,1024]{2,3,0,1:T(8,128)} fusion(f32[4,1024,384]{2,1,0:T(8,128)S(1)} %fusion.51, f32[4,384,1024]{2,1,0:T(8,128)S(1)} %bitcast.172), kind=kOutput, calls=%fused_computation.8 | convolution fusion | flops 7250657280 | bytes 18874368 | tf_op jit(solution)/shard_map/mb,xkbc->xkmc/dot_general | solution.py:24
  520.5 3.7 multiply_subtract_fusion
  524.1 8.8 fusion.14
  532.9 8.9 fusion.12
  541.8 9.3 %fusion.28 = f32[2,1024,384]{2,1,0:T(8,128)S(1)} fusion(f32[2,1024,384]{2,1,0:T(8,128)S(1)} %fusion.14, f32[2,1,384,1024]{2,3,0,1:T(8,128)S(1)} %get-tuple-element.7), kind=kOutput, calls=%fused_computation.50 | convolution fusion | flops 3625992192 | bytes 9437184 | tf_op jit(solution)/shard_map/mb,xkmc->xkbc/dot_general | solution.py:24
  551.1 10.5 %fusion.9 = (f32[2,1,384,1024]{2,3,0,1:T(8,128)}, f32[2,1,384,1024]{2,3,0,1:T(8,128)S(1)}) fusion(f32[2,1024,384]{2,1,0:T(8,128)S(1)} %fusion.28, f32[384]{0:T(512)S(1)} %get-tuple-element.30, f32[384]{0:T(512)S(1)} %get-tuple-element.31, f32[2,1024,384]{2,1,0:T(8,128)S(1)} %fusion.12, f32[2,1,384,1024]{2,3,0,1:T(8,128)S(1)} %get-tuple-element.7), kind=kOutput, calls=%fused_computation.23 | convolution fusion | flops 3630710784 | bytes 15731712 | tf_op jit(solution)/shard_map/mb,xkmc->xkbc/dot_general | solution.py:24
  561.6 3.5 copy.102
  565.1 5.6 all-to-all-start.4
  570.7 5.8 copy.99
  576.5 64.2 %all-to-all-done.4 = f32[2,1,384,1024]{3,0,1,2:T(2,128)S(1)} async-done(((f32[2,1,384,1024]{3,0,1,2:T(2,128)}), f32[2,1,384,1024]{3,0,1,2:T(2,128)S(1)}, u32[]{:S(2)}, u32[]{:S(2)}) %all-to-all-start.4) | async-done | bytes 3145760 | tf_op jit(solution)/shard_map/all_to_all | solution.py:85
  640.7 1.7 copy-done.5
  642.4 4.6 all-to-all-start.3
  647.1 2.9 copy.103
  650.0 7.2 fusion.22
  657.1 59.2 %all-to-all-done.3 = f32[2,1,384,1024]{3,0,1,2:T(2,128)} async-done(((f32[2,1,384,1024]{3,0,1,2:T(2,128)}), f32[2,1,384,1024]{3,0,1,2:T(2,128)}, u32[]{:S(2)}, u32[]{:S(2)}) %all-to-all-start.3) | async-done | bytes 3145760 | tf_op jit(solution)/shard_map/all_to_all | solution.py:84
  716.3 3.1 copy.100
  719.4 5.8 subtract_bitcast_fusion.1
  725.3 3.5 copy.105
  728.8 5.5 all-to-all-start.5
  734.3 5.5 fusion.20
  739.8 5.8 add_bitcast_fusion.1
  745.6 3.5 copy.109
  749.1 54.5 %all-to-all-done.5 = f32[2,8,48,1024]{3,2,0,1:T(8,128)} async-done(((f32[2,8,48,1024]{3,2,0,1:T(8,128)}), f32[2,8,48,1024]{3,2,0,1:T(8,128)}, u32[]{:S(2)}, u32[]{:S(2)}) %all-to-all-start.5) | async-done | bytes 3145760 | tf_op jit(solution)/shard_map/all_to_all | solution.py:91
  803.6 5.5 all-to-all-start.6
  809.2 2.2 copy_multiply_fusion
  811.4 1.9 fusion.203
  813.3 65.8 %all-to-all-done.6 = f32[2,8,48,1024]{3,2,0,1:T(8,128)S(1)} async-done(((f32[2,8,48,1024]{3,2,0,1:T(8,128)}), f32[2,8,48,1024]{3,2,0,1:T(8,128)S(1)}, u32[]{:S(2)}, u32[]{:S(2)}) %all-to-all-start.6) | async-done | bytes 3145760 | tf_op jit(solution)/shard_map/all_to_all | solution.py:92
  879.3 1.2 copy-done.7
  880.6 0.5 copy-done.8
  881.0 3.8 fusion.39
  884.9 29.1 %all-gather.2.cloned.1.call-done = bf16[384,4096]{1,0:T(8,128)(2,1)} async-done(((bf16[384,1024]{1,0:T(8,128)(2,1)}), bf16[384,4096]{1,0:T(8,128)(2,1)}) %all-gather.2.cloned.1.call-update) | async-done | bytes 3145744 | tf_op jit(solution)/shard_map/all_gather | solution.py:118
  914.0 8.6 convolution_convert_fusion
  (43 shorter events, 1.0 us)
Async XLA Ops:
  7.3 4.9 collective-permute-start
  15.9 3.0 copy-start.1
  15.9 2.6 copy-start.9
  23.8 74.5 %all-to-all-start = ((f32[2,1,384,1024]{3,1,0,2:T(1,128)}), f32[2,1,384,1024]{3,1,0,2:T(1,128)S(1)}, u32[]{:S(2)}, u32[]{:S(2)}) async-start(f32[2,1,384,1024]{3,1,0,2:T(1,128)} %copy.74), calls=%async_computation | async-start | bytes 6291456 | tf_op jit(solution)/shard_map/all_to_all | solution.py:56
  103.3 18.5 %copy-start.4 = (f32[1,8,48,1024]{3,1,2,0:T(8,128)}, f32[1,8,48,1024]{3,1,2,0:T(8,128)S(1)}, u32[]{:S(2)}) copy-start(f32[1,8,48,1024]{3,1,2,0:T(8,128)S(1)} %get-tuple-element.20) | copy-start | bytes 4718596
  153.9 142.4 %all-to-all-start.1 = ((f32[4,8,48,1024]{3,2,0,1:T(8,128)}), f32[4,8,48,1024]{3,2,0,1:T(8,128)}, u32[]{:S(2)}, u32[]{:S(2)}) async-start(f32[4,8,48,1024]{3,2,0,1:T(8,128)} %copy.91), calls=%async_computation.1 | async-start | bytes 12582912 | tf_op jit(solution)/shard_map/all_to_all | solution.py:75
  296.3 142.0 %all-to-all-start.2 = ((f32[4,8,48,1024]{3,2,0,1:T(8,128)}), f32[4,8,48,1024]{3,2,0,1:T(8,128)}, u32[]{:S(2)}, u32[]{:S(2)}) async-start(f32[4,8,48,1024]{3,2,0,1:T(8,128)} %copy.94), calls=%async_computation.2 | async-start | bytes 12582912 | tf_op jit(solution)/shard_map/all_to_all | solution.py:76
  305.2 2.6 copy-start
  438.3 29.1 %slice-start.2 = ((s8[6291456]{0:T(1024)(128)(4,1)}), s8[4194304]{0:T(1024)(128)(4,1)S(1)}, s32[]{:S(2)}) async-start(s8[6291456]{0:T(1024)(128)(4,1)} %bitcast.177), calls=%async_computation.10 | async-start | bytes 8388608
  441.8 25.6 %slice-start.3 = ((s8[6291456]{0:T(1024)(128)(4,1)}), s8[2097152]{0:T(1024)(128)(4,1)S(1)}, s32[]{:S(2)}) async-start(s8[6291456]{0:T(1024)(128)(4,1)} %bitcast.177), calls=%async_computation.11 | async-start | bytes 4194304
  441.8 50.8 %slice-start = ((s8[6291456]{0:T(1024)(128)(4,1)}), s8[4194304]{0:T(1024)(128)(4,1)S(1)}, s32[]{:S(2)}) async-start(s8[6291456]{0:T(1024)(128)(4,1)} %bitcast.170), calls=%async_computation.8 | async-start | bytes 8388608
  467.4 25.2 %slice-start.1 = ((s8[6291456]{0:T(1024)(128)(4,1)}), s8[2097152]{0:T(1024)(128)(4,1)S(1)}, s32[]{:S(2)}) async-start(s8[6291456]{0:T(1024)(128)(4,1)} %bitcast.170), calls=%async_computation.9 | async-start | bytes 4194304
  565.1 75.6 %all-to-all-start.4 = ((f32[2,1,384,1024]{3,0,1,2:T(2,128)}), f32[2,1,384,1024]{3,0,1,2:T(2,128)S(1)}, u32[]{:S(2)}, u32[]{:S(2)}) async-start(f32[2,1,384,1024]{3,0,1,2:T(2,128)} %copy.102), calls=%async_computation.4 | async-start | bytes 6291456 | tf_op jit(solution)/shard_map/all_to_all | solution.py:85
  640.7 1.7 copy-start.5
  642.4 73.9 %all-to-all-start.3 = ((f32[2,1,384,1024]{3,0,1,2:T(2,128)}), f32[2,1,384,1024]{3,0,1,2:T(2,128)}, u32[]{:S(2)}, u32[]{:S(2)}) async-start(f32[2,1,384,1024]{3,0,1,2:T(2,128)} %copy.99), calls=%async_computation.3 | async-start | bytes 6291456 | tf_op jit(solution)/shard_map/all_to_all | solution.py:84
  716.3 3.1 copy-start.6
  719.4 5.9 copy-start.2
  728.8 74.8 %all-to-all-start.5 = ((f32[2,8,48,1024]{3,2,0,1:T(8,128)}), f32[2,8,48,1024]{3,2,0,1:T(8,128)}, u32[]{:S(2)}, u32[]{:S(2)}) async-start(f32[2,8,48,1024]{3,2,0,1:T(8,128)} %copy.105), calls=%async_computation.5 | async-start | bytes 6291456 | tf_op jit(solution)/shard_map/all_to_all | solution.py:91
  734.3 5.5 copy-start.3
  803.6 75.5 %all-to-all-start.6 = ((f32[2,8,48,1024]{3,2,0,1:T(8,128)}), f32[2,8,48,1024]{3,2,0,1:T(8,128)S(1)}, u32[]{:S(2)}, u32[]{:S(2)}) async-start(f32[2,8,48,1024]{3,2,0,1:T(8,128)} %copy.109), calls=%async_computation.6 | async-start | bytes 6291456 | tf_op jit(solution)/shard_map/all_to_all | solution.py:92
  809.1 104.9 %all-gather.2.cloned.1.call-start = ((), (), s32[]{:S(2)}) async-start(), calls=%async_computation.7 | async-start | bytes 3932160 | tf_op jit(solution)/shard_map/all_gather | solution.py:118
  813.3 66.0 %copy-start.10 = (f32[1024]{0:T(1024)S(1)}, f32[1024]{0:T(1024)}, u32[]{:S(2)}) copy-start(f32[1024]{0:T(1024)} %param.12) | copy-start | bytes 12292
  879.1 1.4 copy-start.7
  879.1 1.9 copy-start.8
Sparse Core Ops, SparseCore 0:
  885.0 28.9 all-gather.1
where the time goes:
time: 936 us; the launch traced here: 930 us
  waiting for transfers between devices  571 us (61%)
  matrix products  218 us (23%)
  local copies, waits for them, and re-layouts  66.7 us (7%)
  starting transfers between devices  42.4 us (5%)
  other arithmetic  17.3 us (2%)
  between operations  14.3 us (2%)
    dot_general x16, matrix products, contract(): return jnp.einsum(pattern, first_op, second_op, precision=highest)  209 us
    all_to_all x2, waiting for transfers between devices, sequence_conv(): lax.all_to_all(sectioned[0], 'seq', split_axis=1, concat_axis=2, tiled=True)  182 us
    all_to_all x2, waiting for transfers between devices, sequence_conv(): lax.all_to_all(sectioned[1], 'seq', split_axis=1, concat_axis=2, tiled=True)  169 us
    all_to_all x1, waiting for transfers between devices, sequence_conv(): lax.all_to_all(planes, 'seq', split_axis=2, concat_axis=1, tiled=True)  68 us
    all_to_all x1, waiting for transfers between devices, sequence_conv(): lax.all_to_all(sectioned[1], 'seq', split_axis=2, concat_axis=1, tiled=True)  64.2 us
    all_to_all x1, waiting for transfers between devices, sequence_conv(): lax.all_to_all(sectioned[0], 'seq', split_axis=2, concat_axis=1, tiled=True)  59.2 us
    all_gather x1, waiting for transfers between devices, on_device(): lax.all_gather(mixed, 'ch', axis=1, tiled=True)  29.1 us
  transfers between devices with their start and end apart: 9, of which 8 were waited for; matrix products, arithmetic and copies ran while one was open for 8% of the time, Pallas kernels for 0%

commit v1 on v0

v1 whole, which is shorter than its diff:
```python
import functools
import math

import jax
import jax.numpy as jnp
import ml_dtypes
import numpy as np
from jax import lax
from jax.experimental import pallas as pl
from jax.experimental.pallas import tpu as pltpu
from jax.sharding import PartitionSpec as P

LANES = 128
ROW_PARTS = 2
BF16 = jnp.bfloat16
F32 = jnp.float32


def two_terms(table):
    high = table.astype(ml_dtypes.bfloat16)
    low = (table - high.astype(np.float64)).astype(ml_dtypes.bfloat16)
    return high, low


def transform_tables(rows):
    order = np.concatenate([np.arange(0, rows, 2), np.arange(1, rows, 2)])
    product = (2 * order[:, None] + 1) * np.arange(rows)[None, :] % (4 * rows)
    angles = product * (math.pi / (2 * rows))
    forward = np.concatenate([np.cos(angles), -np.sin(angles)])
    fwd_high, fwd_low = two_terms(forward)
    inv_high, inv_low = two_terms(forward.T / rows)
    return (
        np.concatenate([fwd_high, fwd_low], axis=1),
        np.concatenate([inv_high, inv_low, inv_high], axis=1),
    )


def short_conv(pad_ref, block, rim, taps):
    rows = block.shape[0]
    pad_ref[pl.ds(0, 8), :] = rim
    pad_ref[pl.ds(8, rows), :] = block
    total = taps[0:1] * block
    for offset in range(1, taps.shape[0]):
        total = total + taps[offset : offset + 1] * pad_ref[pl.ds(8 - offset, rows), :]
    return total


def mix_kernel(gate_ref, value_ref, rim_ref, taps_ref, out_ref, pad_a, pad_b):
    first = short_conv(pad_a, gate_ref[...].astype(F32), rim_ref[1], taps_ref[1])
    second = short_conv(pad_b, value_ref[...].astype(F32), rim_ref[2], taps_ref[2])
    out_ref[0] = (first * second).astype(out_ref.dtype)


def mix_inputs(in_gate, values, rims, taps):
    rows, width = in_gate.shape
    span = LANES
    parts = width // span
    return pl.pallas_call(
        mix_kernel,
        grid=(parts,),
        in_specs=[
            pl.BlockSpec((rows, span), lambda i: (0, i)),
            pl.BlockSpec((rows, span), lambda i: (0, i)),
            pl.BlockSpec((3, 8, span), lambda i: (0, 0, i)),
            pl.BlockSpec((3, taps.shape[1], span), lambda i: (0, 0, i)),
        ],
        out_specs=pl.BlockSpec((1, rows, span), lambda i: (i, 0, 0)),
        out_shape=jax.ShapeDtypeStruct((parts, rows, span), BF16),
        scratch_shapes=[pltpu.VMEM((rows + 8, span), F32)] * 2,
        cost_estimate=pl.CostEstimate(flops=12 * rows * width, bytes_accessed=6 * rows * width, transcendentals=0),
    )(in_gate, values, rims, taps)


def side_kernel(late_ref, gate_ref, value_ref, rim_ref, taps_ref, skip_ref, late_out, skip_out, pad_a, pad_b, pad_c):
    late_out[...] = short_conv(pad_a, late_ref[...].astype(F32), rim_ref[0], taps_ref[0])
    first = short_conv(pad_b, gate_ref[...].astype(F32), rim_ref[1], taps_ref[1])
    second = short_conv(pad_c, value_ref[...].astype(F32), rim_ref[2], taps_ref[2])
    skip_out[...] = skip_ref[...] * (first * second)


def side_terms(out_gate, in_gate, values, rims, taps, skip_gain):
    rows, width = in_gate.shape
    span = min(width, 128)
    column = pl.BlockSpec((rows, span), lambda i: (0, i))
    return pl.pallas_call(
        side_kernel,
        grid=(width // span,),
        in_specs=[
            column,
            column,
            column,
            pl.BlockSpec((3, 8, span), lambda i: (0, 0, i)),
            pl.BlockSpec((3, taps.shape[1], span), lambda i: (0, 0, i)),
            pl.BlockSpec((1, span), lambda i: (0, i)),
        ],
        out_specs=[column, column],
        out_shape=[jax.ShapeDtypeStruct((rows, width), F32)] * 2,
        scratch_shapes=[pltpu.VMEM((rows + 8, span), F32)] * 3,
        cost_estimate=pl.CostEstimate(flops=20 * rows * width, bytes_accessed=14 * rows * width, transcendentals=0),
    )(out_gate, in_gate, values, rims, taps, skip_gain.reshape(1, width))


def pair_of(ref, at):
    return jnp.concatenate([ref[at], ref[at + 1]], axis=1)


def forward_into(table_ref, signal_ref, out_ref):
    blocks, _, lanes = signal_ref.shape

    @pl.loop(0, blocks // 2)
    def _(step):
        pair = pair_of(signal_ref, 2 * step)
        spectra = jnp.dot(table_ref[...], jnp.concatenate([pair, pair], axis=0), preferred_element_type=F32)
        out_ref[2 * step] = spectra[:, :lanes]
        out_ref[2 * step + 1] = spectra[:, lanes:]


def forward_kernel(table_ref, signal_ref, out_ref):
    forward_into(table_ref, signal_ref, out_ref)


def forward(table, signal):
    blocks, rows, lanes = signal.shape
    return pl.pallas_call(
        forward_kernel,
        out_shape=jax.ShapeDtypeStruct((blocks, 2 * rows, lanes), F32),
        compiler_params=pltpu.CompilerParams(vmem_limit_bytes=60 << 20),
        cost_estimate=pl.CostEstimate(flops=8 * blocks * rows * rows * lanes, bytes_accessed=10 * blocks * rows * lanes, transcendentals=0),
    )(table, signal)


def conv_kernel(table_ref, inverse_ref, signal_ref, filter_ref, *rest):
    out_refs, (spectra_ref, high_ref, low_ref) = rest[:-3], rest[-3:]
    blocks, rows, lanes = signal_ref.shape
    forward_into(table_ref, signal_ref, spectra_ref)
    half = rows // 2
    tile = 16

    def multiply(base, turn):
        def body(step, carry):
            start = pl.multiple_of(base + step * tile, tile)
            real, imag = pl.ds(start, tile), pl.ds(rows + start, tile)
            before = None
            for at in range(blocks):
                sum_real = sum_imag = None
                for other in range(at + 1):
                    a_real, a_imag = filter_ref[other, real, :], filter_ref[other, imag, :]
                    b_real, b_imag = spectra_ref[at - other, real, :], spectra_ref[at - other, imag, :]
                    part_real = a_real * b_real - a_imag * b_imag
                    part_imag = a_real * b_imag + a_imag * b_real
                    sum_real = part_real if sum_real is None else sum_real + part_real
                    sum_imag = part_imag if sum_imag is None else sum_imag + part_imag
                out_real, out_imag = sum_real, sum_imag
                if before is not None:
                    out_real = sum_real - turn * before[1]
                    out_imag = sum_imag + turn * before[0]
                before = (sum_real, sum_imag)
                for place, value in ((real, out_real), (imag, out_imag)):
                    high = value.astype(BF16)
                    high_ref[at, place, :] = high
                    low_ref[at, place, :] = (value - high.astype(F32)).astype(BF16)
            return carry

        lax.fori_loop(0, half // tile, body, 0)

    multiply(0, 1.0)
    multiply(half, -1.0)

    part_rows = rows // len(out_refs)
    for part, out_ref in enumerate(out_refs):

        @pl.loop(0, blocks // 2)
        def _(step):
            high, low = pair_of(high_ref, 2 * step), pair_of(low_ref, 2 * step)
            result = jnp.dot(
                inverse_ref[pl.ds(part * part_rows, part_rows), :],
                jnp.concatenate([high, high, low], axis=0),
                preferred_element_type=F32,
            ).astype(out_ref.dtype)
            out_ref[2 * step] = result[:, :lanes]
            out_ref[2 * step + 1] = result[:, lanes:]


def block_conv(table, inverse, signal, filter_spectra, parts):
    blocks, rows, lanes = signal.shape
    return pl.pallas_call(
        conv_kernel,
        out_shape=[jax.ShapeDtypeStruct((blocks, rows // parts, lanes), BF16)] * parts,
        scratch_shapes=[
            pltpu.VMEM((blocks, 2 * rows, lanes), F32),
            pltpu.VMEM((blocks, 2 * rows, lanes), BF16),
            pltpu.VMEM((blocks, 2 * rows, lanes), BF16),
        ],
        compiler_params=pltpu.CompilerParams(vmem_limit_bytes=60 << 20),
        cost_estimate=pl.CostEstimate(flops=20 * blocks * rows * rows * lanes, bytes_accessed=10 * blocks * rows * lanes, transcendentals=0),
    )(table, inverse, signal, filter_spectra)


def gate_kernel(long_ref, late_ref, skip_ref, out_ref):
    out_ref[...] = (late_ref[...] * (long_ref[0].astype(F32) + skip_ref[...])).astype(out_ref.dtype)


def gate_rows(long_part, late, skip, part):
    blocks, rows, lanes = long_part.shape
    column = pl.BlockSpec((rows, lanes), lambda i: (part, i))
    return pl.pallas_call(
        gate_kernel,
        grid=(blocks,),
        in_specs=[pl.BlockSpec((1, rows, lanes), lambda i: (i, 0, 0)), column, column],
        out_specs=pl.BlockSpec((rows, lanes), lambda i: (0, i)),
        out_shape=jax.ShapeDtypeStruct((rows, blocks * lanes), BF16),
        cost_estimate=pl.CostEstimate(flops=3 * blocks * rows * lanes, bytes_accessed=12 * blocks * rows * lanes, transcendentals=0),
    )(long_part, late, skip)


def project_kernel(order_ref, *refs):
    del order_ref
    *mixed_refs, weight_ref, out_ref, total_ref = refs
    step = pl.program_id(0)
    for at, mixed_ref in enumerate(mixed_refs):

        @pl.when(step == at)
        def _():
            product = jnp.dot(mixed_ref[...], weight_ref[...], preferred_element_type=F32)
            total_ref[...] = product if at == 0 else total_ref[...] + product

    @pl.when(step == len(mixed_refs) - 1)
    def _():
        out_ref[...] = total_ref[...].astype(out_ref.dtype)


def project(pieces, weight, order):
    rows, depth = pieces[0].shape
    width = weight.shape[1]
    count = len(pieces)
    whole = pl.BlockSpec((rows, depth), lambda i, order: (0, 0))
    return pl.pallas_call(
        project_kernel,
        grid_spec=pltpu.PrefetchScalarGridSpec(
            num_scalar_prefetch=1,
            grid=(count,),
            in_specs=[whole] * count + [pl.BlockSpec((depth, width), lambda i, order: (order[i], 0))],
            out_specs=pl.BlockSpec((rows, width), lambda i, order: (0, 0)),
            scratch_shapes=[pltpu.VMEM((rows, width), F32)],
        ),
        out_shape=jax.ShapeDtypeStruct((rows, width), BF16),
        compiler_params=pltpu.CompilerParams(vmem_limit_bytes=40 << 20),
        cost_estimate=pl.CostEstimate(flops=2 * rows * depth * count * width, bytes_accessed=2 * depth * count * width, transcendentals=0),
    )(order, *pieces, weight)


def gather_channels(block):
    count = lax.axis_size("ch")
    held = {0: block}
    bit = count // 2
    while bit:
        route = [(i, i ^ bit) for i in range(count)]
        held.update({at ^ bit: lax.ppermute(part, "ch", route) for at, part in list(held.items())})
        bit //= 2
    return [held[at] for at in range(count)]


def exchange(blocks):
    return lax.all_to_all(blocks, "seq", split_axis=0, concat_axis=0, tiled=True)


def send_spans(slices):
    count, rows, lanes = slices.shape
    devices = lax.axis_size("seq")
    cut = devices // count
    if cut > 1:
        slices = slices.reshape(count, rows, cut, lanes // cut).transpose(0, 2, 1, 3).reshape(devices, rows, lanes // cut)
    blocks = exchange(slices)
    return jnp.pad(blocks, ((0, 0), (0, 0), (0, lanes - lanes // cut))) if cut > 1 else blocks


def return_spans(blocks, count):
    devices, rows, lanes = blocks.shape
    cut = devices // count
    if cut == 1:
        return exchange(blocks)
    arrived = exchange(blocks[:, :, : lanes // cut])
    return arrived.reshape(count, cut, rows, lanes // cut).transpose(0, 2, 1, 3).reshape(count, rows, lanes)


def on_device(out_gate, in_gate, values, short_filter, long_filter, skip_gain, out_weight):
    rows, width = out_gate.shape
    devices = lax.axis_size("seq")
    slices = width // LANES
    taps = short_filter.shape[1]
    table, inverse = transform_tables(rows)

    rim = jnp.stack([a[rows - (taps - 1) :] for a in (out_gate, in_gate, values)])
    rim = lax.ppermute(rim, "seq", [(i, i + 1) for i in range(devices - 1)])
    rims = jnp.pad(rim.astype(F32), ((0, 0), (8 - (taps - 1), 0), (0, 0)))

    filter_slices = long_filter.astype(BF16).reshape(rows, slices, LANES).transpose(1, 0, 2)
    filter_whole = send_spans(filter_slices)
    mixed_whole = send_spans(mix_inputs(in_gate, values, rims, short_filter))

    filter_spectra = forward(table, filter_whole)
    late, skip = side_terms(out_gate, in_gate, values, rims, short_filter, skip_gain)
    long_parts = block_conv(table, inverse, mixed_whole, filter_spectra, ROW_PARTS)
    channel = lax.axis_index("ch")
    order = jnp.bitwise_xor(channel, jnp.arange(lax.axis_size("ch"), dtype=jnp.int32))
    outs = []
    for part, long_part in enumerate(long_parts):
        returned = return_spans(long_part, slices)
        mixed = gate_rows(returned, late, skip, part)
        outs.append(project(gather_channels(mixed), out_weight, order))
    return jnp.concatenate(outs, axis=0)


def solution(mesh):
    return jax.shard_map(
        on_device,
        mesh=mesh,
        in_specs=(
            P("seq", "ch"),
            P("seq", "ch"),
            P("seq", "ch"),
            P(None, None, "ch"),
            P("seq", "ch"),
            P("ch"),
            P(None, "ch"),
        ),
        out_specs=P("seq", "ch"),
        check_vma=False,
    )
```

time: 936 us -> 138 us (0.15)
  waiting for transfers between devices: 571 us -> 27.4 us
  matrix products: 218 us -> 0 us
  local copies, waits for them, and re-layouts: 66.7 us -> 12.8 us
  Pallas kernels: 0 us -> 45.9 us
  other arithmetic: 17.3 us -> 1.62 us
  blocking collectives: 0 us -> 14.8 us
  between operations: 14.3 us -> 0.11 us
    all_to_all x7 -> x3, waiting for transfers between devices: 542 us -> 21.1 us  [exchange(): lax.all_to_all(blocks, 'seq', split_axis=0, concat_axis=0, tiled=True)]
    dot_general x17 -> x0, matrix products: 218 us -> none  [the longest x16 209 us: contract(): return jnp.einsum(pattern, first_op, second_op, precision=highest)]
    pallas_call x0 -> x8, Pallas kernels: none -> 45.9 us  [the longest x1 11.4 us: block_conv(): pl.pallas_call(conv_kernel, out_shape=[jax.ShapeDtypeStruct((blocks, rows...]
    all_gather x1 -> x0, waiting for transfers between devices: 29.1 us -> none  [on_device(): lax.all_gather(mixed, 'ch', axis=1, tiled=True)]
    sub x3 -> x0, local copies, waits for them, and re-layouts: 18.4 us -> none  [the longest x2 14.9 us: complex_times(): first_op[0] * second_op[0] - first_op[1] * second_op[1]]
    all_to_all x7 -> x3, starting transfers between devices: 38.5 us -> 21.9 us  [exchange(): lax.all_to_all(blocks, 'seq', split_axis=0, concat_axis=0, tiled=True)]
    add x3 -> x0, local copies, waits for them, and re-layouts: 16 us -> none  [the longest x2 12.6 us: complex_times(): first_op[0] * second_op[1] + first_op[1] * second_op[0]]
    all_to_all x0 -> x1, blocking collectives: none -> 14.8 us  [exchange(): lax.all_to_all(blocks, 'seq', split_axis=0, concat_axis=0, tiled=True)]
  transfers between devices with their start and end apart: 9 -> 10, of which waited for: 8 -> 4; matrix products, arithmetic and copies ran while one was open for 8% -> 2% of each run, Pallas kernels for 0% -> 23%
where the time goes in v1:
time: 138 us; the launch traced here: 136 us
  Pallas kernels  45.9 us (33%)
  starting transfers between devices  33.8 us (24%)
  waiting for transfers between devices  27.4 us (20%)
  blocking collectives  14.8 us (11%)
  local copies, waits for them, and re-layouts  12.8 us (9%)
  other arithmetic  1.62 us (1%)
    all_to_all x3, starting transfers between devices, exchange(): lax.all_to_all(blocks, 'seq', split_axis=0, concat_axis=0, tiled=True)  21.9 us
    all_to_all x3, waiting for transfers between devices, exchange(): lax.all_to_all(blocks, 'seq', split_axis=0, concat_axis=0, tiled=True)  21.1 us
    all_to_all x1, blocking collectives, exchange(): lax.all_to_all(blocks, 'seq', split_axis=0, concat_axis=0, tiled=True)  14.8 us
    pallas_call x1, Pallas kernels, block_conv(): pl.pallas_call(conv_kernel, out_shape=[jax.ShapeDtypeStruct((blocks, rows...  11.4 us
    pallas_call x2, Pallas kernels, gate_rows(): pl.pallas_call(gate_kernel, grid=(blocks,), in_specs=[pl.BlockSpec((1, ro...  10.7 us
    unnamed x15, local copies, waits for them, and re-layouts  10.1 us
    ppermute x6, starting transfers between devices, gather_channels(): lax.ppermute(part, 'ch', route)  8.6 us
    pallas_call x1, Pallas kernels, side_terms(): pl.pallas_call(side_kernel, grid=(width // span,), in_specs=[column, colu...  6.73 us
  transfers between devices with their start and end apart: 10, of which 4 were waited for; matrix products, arithmetic and copies ran while one was open for 2% of the time, Pallas kernels for 23%

profile of v1, /device:TPU:1, one launch (start us, length us, event | category | flops | bytes accessed | tf_op | source)
XLA Modules:
  0.0 136.5 jit_solution(7480526592662937115)
XLA Ops:
  0.0 1.8 %copy.10 = bf16[384,1024]{0,1:T(8,128)(2,1)S(1)} copy(f32[384,1024]{1,0:T(8,128)} %param.13) | data formatting | bytes 2359296 | tf_op args[4]
  1.8 1.2 copy.11
  2.9 6.4 %all-to-all-start.1 = ((bf16[8,384,128]{2,1,0:T(8,128)(2,1)}), bf16[8,384,128]{2,1,0:T(8,128)(2,1)S(1)}, u32[]{:S(2)}, u32[]{:S(2)}) async-start(bf16[8,384,128]{2,1,0:T(8,128)(2,1)} %bitcast.4), calls=%async_computation.1 | async-start | bytes 1572864 | tf_op jit(solution)/shard_map/all_to_all | solution.py:264
  9.3 0.7 slice_bitcast_fusion.2
  10.0 0.7 slice_bitcast_fusion
  10.8 3.4 %collective-permute-start = (bf16[3,2,1024]{2,1,0:T(2,128)(2,1)S(1)}, bf16[3,2,1024]{2,1,0:T(2,128)(2,1)S(1)}, u32[]{:S(2)}, u32[]{:S(2)}) collective-permute-start(bf16[3,2,1024]{2,1,0:T(2,128)(2,1)S(1)} %pad_maximum_fusion.1), channel_id=1, source_target_pairs={{0,4},{4,8},{8,12},{12,16},{16,20},{20,24},{24,28},{1,5},{5,9},{9,... | collective-permute-start | bytes 36872 | tf_op jit(solution)/shard_map/ppermute | solution.py:294
  14.2 0.8 collective-permute-done
  15.0 0.7 pad_convert_fusion.rim_ref
  15.6 5.8 %shard_map.91 = bf16[8,384,128]{2,1,0:T(8,128)(2,1)} custom-call(bf16[384,1024]{1,0:T(8,128)(2,1)} %gate_ref.3, bf16[384,1024]{1,0:T(8,128)(2,1)} %value_ref.3, f32[3,8,1024]{2,1,0:T(8,128)} %pad_convert_fusion.rim_ref, f32[3,3,1024]{2,1,0:T(4,128)} %taps_ref.3), custom_call_target="tpu_custom_call" | custom-call | flops 4718592 | bytes 2359296 | tf_op jit(solution)/shard_map/pallas_call | solution.py:58
  21.4 6.9 %all-to-all-done.1.signal_ref = bf16[8,384,128]{2,1,0:T(8,128)(2,1)S(1)} async-done(((bf16[8,384,128]{2,1,0:T(8,128)(2,1)}), bf16[8,384,128]{2,1,0:T(8,128)(2,1)S(1)}, u32[]{:S(2)}, u32[]{:S(2)}) %all-to-all-start.1) | async-done | bytes 786464 | tf_op jit(solution)/shard_map/all_to_all | solution.py:264
  28.3 0.0 copy-start.4
  28.3 10.7 %all-to-all-start = ((bf16[8,384,128]{2,1,0:T(8,128)(2,1)}), bf16[8,384,128]{2,1,0:T(8,128)(2,1)S(1)}, u32[]{:S(2)}, u32[]{:S(2)}) async-start(bf16[8,384,128]{2,1,0:T(8,128)(2,1)} %shard_map.91), calls=%async_computation | async-start | bytes 1572864 | tf_op jit(solution)/shard_map/all_to_all | solution.py:264
  39.1 0.0 copy-done.4
  39.1 5.0 %shard_map.92.filter_ref = f32[8,768,128]{2,1,0:T(8,128)} custom-call(bf16[768,768]{1,0:T(8,128)(2,1)} %constant.12.clone.table_ref, bf16[8,384,128]{2,1,0:T(8,128)(2,1)} %copy-done.4), custom_call_target="tpu_custom_call" | custom-call | flops 1207959552 | bytes 3932160 | tf_op jit(solution)/shard_map/pallas_call | solution.py:124
  44.1 14.2 %all-to-all-done.signal_ref = bf16[8,384,128]{2,1,0:T(8,128)(2,1)S(1)} async-done(((bf16[8,384,128]{2,1,0:T(8,128)(2,1)}), bf16[8,384,128]{2,1,0:T(8,128)(2,1)S(1)}, u32[]{:S(2)}, u32[]{:S(2)}) %all-to-all-start) | async-done | bytes 786464 | tf_op jit(solution)/shard_map/all_to_all | solution.py:264
  58.4 0.0 copy-start.6
  58.4 0.9 copy-done.6
  59.2 11.4 %shard_map.93 = (bf16[8,192,128]{2,1,0:T(8,128)(2,1)}, bf16[8,192,128]{2,1,0:T(8,128)(2,1)}) custom-call(bf16[768,768]{1,0:T(8,128)(2,1)} %constant.12.clone.table_ref, bf16[384,2304]{1,0:T(8,128)(2,1)} %constant.13.clone.inverse_ref, bf16[8,384,128]{2,1,0:T(8,128)(2,1)} %copy-done.6, f32[8,768,128]{2,1,0:T(8,128)} %shard_map.92.filter_ref), custom_call_target="tpu_custom_call" | custom-call | flops 3019898880 | bytes 3932160 | tf_op jit(solution)/shard_map/pallas_call | solution.py:186
  70.6 14.8 %all_to_all.20.long_ref = bf16[8,192,128]{2,1,0:T(8,128)(2,1)} all-to-all(bf16[8,192,128]{2,1,0:T(8,128)(2,1)} %get-tuple-element.9), channel_id=1, replica_groups=mesh['seq'=8,'ch'=4] {'seq'}, dimensions={0} | all-to-all | bytes 786432 | tf_op jit(solution)/shard_map/all_to_all | solution.py:264
  85.5 4.8 %all-to-all-start.3 = ((bf16[8,192,128]{2,1,0:T(8,128)(2,1)}), bf16[8,192,128]{2,1,0:T(8,128)(2,1)S(1)}, u32[]{:S(2)}, u32[]{:S(2)}) async-start(bf16[8,192,128]{2,1,0:T(8,128)(2,1)} %get-tuple-element.12), calls=%async_computation.3 | async-start | bytes 786432 | tf_op jit(solution)/shard_map/all_to_all | solution.py:264
  90.3 6.7 %shard_map.94 = (f32[384,1024]{1,0:T(8,128)}, f32[384,1024]{1,0:T(8,128)}) custom-call(bf16[384,1024]{1,0:T(8,128)(2,1)} %late_ref.1, bf16[384,1024]{1,0:T(8,128)(2,1)} %gate_ref.3, bf16[384,1024]{1,0:T(8,128)(2,1)} %value_ref.3, f32[3,8,1024]{2,1,0:T(8,128)} %pad_convert_fusion.rim_ref, f32[3,3,1024]{2,1,0:T(4,128)} %taps_ref.3, f32[1,1024]{1,0:T(1,128)} %bitcast.10), custom_call_target="tpu_custom_call" | custom-call | flops 7864320 | bytes 5505024 | tf_op jit(solution)/shard_map/pallas_call | solution.py:85
  97.0 5.3 %shard_map.95.refs_0_ = bf16[192,1024]{1,0:T(8,128)(2,1)} custom-call(bf16[8,192,128]{2,1,0:T(8,128)(2,1)} %all_to_all.20.long_ref, f32[384,1024]{1,0:T(8,128)} %get-tuple-element.10.late_ref, f32[384,1024]{1,0:T(8,128)} %get-tuple-element.11.skip_ref), custom_call_target="tpu_custom_call" | custom-call | flops 589824 | bytes 2359296 | tf_op jit(solution)/shard_map/pallas_call | solution.py:206
  102.3 0.0 copy-start.2
  102.3 1.2 collective-permute-start.2
  103.6 0.0 all-to-all-done.3.long_ref
  103.6 0.0 copy-start.5
  103.6 0.7 copy-done.5
  104.3 5.3 %shard_map.97.refs_0_ = bf16[192,1024]{1,0:T(8,128)(2,1)} custom-call(bf16[8,192,128]{2,1,0:T(8,128)(2,1)} %copy-done.5, f32[384,1024]{1,0:T(8,128)} %get-tuple-element.10.late_ref, f32[384,1024]{1,0:T(8,128)} %get-tuple-element.11.skip_ref), custom_call_target="tpu_custom_call" | custom-call | flops 589824 | bytes 2359296 | tf_op jit(solution)/shard_map/pallas_call | solution.py:206
  109.7 0.2 collective-permute-start.5
  109.9 0.0 copy-done.2
  109.9 2.2 %collective-permute-start.1 = (bf16[192,1024]{1,0:T(8,128)(2,1)S(1)}, bf16[192,1024]{1,0:T(8,128)(2,1)S(1)}, u32[]{:S(2)}, u32[]{:S(2)}) collective-permute-start(bf16[192,1024]{1,0:T(8,128)(2,1)S(1)} %copy-done.2), channel_id=1, source_target_pairs={{0,1},{1,0},{2,3},{3,2},{4,5},{5,4},{6,7},{7,6},{8,9},{9,8},{10,11... | collective-permute-start | bytes 1179656 | tf_op jit(solution)/shard_map/ppermute | solution.py:258
  112.1 0.0 collective-permute-done.2.refs_2_
  112.1 3.2 %collective-permute-start.3 = (bf16[192,1024]{1,0:T(8,128)(2,1)S(1)}, bf16[192,1024]{1,0:T(8,128)(2,1)S(1)}, u32[]{:S(2)}, u32[]{:S(2)}) collective-permute-start(bf16[192,1024]{1,0:T(8,128)(2,1)S(1)} %collective-permute-done.2.refs_2_), channel_id=1, source_target_pairs={{0,1},{1,0},{2,3},{3,2},{4,5},{5,4},{6,7},{7,6},{8,9},{9,8},{10,11... | collective-permute-start | bytes 1179656 | tf_op jit(solution)/shard_map/ppermute | solution.py:258
  115.3 0.0 collective-permute-start.4
  115.3 5.5 %collective-permute-done.5.refs_2_ = bf16[192,1024]{1,0:T(8,128)(2,1)S(1)} collective-permute-done((bf16[192,1024]{1,0:T(8,128)(2,1)}, bf16[192,1024]{1,0:T(8,128)(2,1)S(1)}, u32[]{:S(2)}, u32[]{:S(2)}) %collective-permute-start.5) | collective-permute-done | bytes 393248 | tf_op jit(solution)/shard_map/ppermute | solution.py:258
  120.8 1.7 %collective-permute-start.6 = (bf16[192,1024]{1,0:T(8,128)(2,1)S(1)}, bf16[192,1024]{1,0:T(8,128)(2,1)S(1)}, u32[]{:S(2)}, u32[]{:S(2)}) collective-permute-start(bf16[192,1024]{1,0:T(8,128)(2,1)S(1)} %collective-permute-done.5.refs_2_), channel_id=1, source_target_pairs={{0,1},{1,0},{2,3},{3,2},{4,5},{5,4},{6,7},{7,6},{8,9},{9,8},{10,11... | collective-permute-start | bytes 1179656 | tf_op jit(solution)/shard_map/ppermute | solution.py:258
  122.5 0.0 collective-permute-done.1.refs_1_
  122.5 0.0 collective-permute-done.3.refs_3_
  122.5 0.0 copy-start
  122.5 3.4 %copy-done = bf16[4096,1024]{1,0:T(8,128)(2,1)S(1)} copy-done((bf16[4096,1024]{1,0:T(8,128)(2,1)S(1)}, bf16[4096,1024]{1,0:T(8,128)(2,1)}, u32[]{:S(2)}) %copy-start) | copy-done | bytes 8388632
  125.9 0.0 copy-start.3
  125.9 3.1 %shard_map.96 = bf16[192,1024]{1,0:T(8,128)(2,1)S(1)} custom-call(s32[4]{0:T(128)S(1)} %iota_xor_fusion.order_ref, bf16[192,1024]{1,0:T(8,128)(2,1)S(1)} %copy-done.2, bf16[192,1024]{1,0:T(8,128)(2,1)S(1)} %collective-permute-done.1.refs_1_, bf16[192,1024]{1,0:T(8,128)(2,1)S(1)} %collective-permute-done.2.refs_2_, ...), custom_call_target="tpu_custom_call" | custom-call | flops 1610612736 | bytes 8388608 | tf_op jit(solution)/shard_map/pallas_call | solution.py:237
  129.0 0.0 collective-permute-done.4.refs_1_
  129.0 0.0 collective-permute-done.6.refs_3_
  129.1 0.0 copy-done.3
  129.1 0.0 copy-start.1
  129.1 3.4 %copy-done.1 = bf16[4096,1024]{1,0:T(8,128)(2,1)S(1)} copy-done((bf16[4096,1024]{1,0:T(8,128)(2,1)S(1)}, bf16[4096,1024]{1,0:T(8,128)(2,1)}, u32[]{:S(2)}) %copy-start.1) | copy-done | bytes 8388632
  132.5 3.1 %shard_map.98 = bf16[192,1024]{1,0:T(8,128)(2,1)S(1)} custom-call(s32[4]{0:T(128)S(1)} %iota_xor_fusion.order_ref, bf16[192,1024]{1,0:T(8,128)(2,1)S(1)} %copy-done.3, bf16[192,1024]{1,0:T(8,128)(2,1)S(1)} %collective-permute-done.4.refs_1_, bf16[192,1024]{1,0:T(8,128)(2,1)S(1)} %collective-permute-done.5.refs_2_, ...), custom_call_target="tpu_custom_call" | custom-call | flops 1610612736 | bytes 8388608 | tf_op jit(solution)/shard_map/pallas_call | solution.py:237
  135.6 0.9 pad_maximum_fusion
  (2 shorter events, 0.0 us)
Async XLA Ops:
  2.9 25.4 %all-to-all-start.1 = ((bf16[8,384,128]{2,1,0:T(8,128)(2,1)}), bf16[8,384,128]{2,1,0:T(8,128)(2,1)S(1)}, u32[]{:S(2)}, u32[]{:S(2)}) async-start(bf16[8,384,128]{2,1,0:T(8,128)(2,1)} %bitcast.4), calls=%async_computation.1 | async-start | bytes 1572864 | tf_op jit(solution)/shard_map/all_to_all | solution.py:264
  10.8 4.2 %collective-permute-start = (bf16[3,2,1024]{2,1,0:T(2,128)(2,1)S(1)}, bf16[3,2,1024]{2,1,0:T(2,128)(2,1)S(1)}, u32[]{:S(2)}, u32[]{:S(2)}) collective-permute-start(bf16[3,2,1024]{2,1,0:T(2,128)(2,1)S(1)} %pad_maximum_fusion.1), channel_id=1, source_target_pairs={{0,4},{4,8},{8,12},{12,16},{16,20},{20,24},{24,28},{1,5},{5,9},{9,... | collective-permute-start | bytes 36872 | tf_op jit(solution)/shard_map/ppermute | solution.py:294
  28.3 10.7 %copy-start.4 = (bf16[8,384,128]{2,1,0:T(8,128)(2,1)}, bf16[8,384,128]{2,1,0:T(8,128)(2,1)S(1)}, u32[]{:S(2)}) copy-start(bf16[8,384,128]{2,1,0:T(8,128)(2,1)S(1)} %all-to-all-done.1.signal_ref) | copy-start | bytes 2359300
  28.3 30.0 %all-to-all-start = ((bf16[8,384,128]{2,1,0:T(8,128)(2,1)}), bf16[8,384,128]{2,1,0:T(8,128)(2,1)S(1)}, u32[]{:S(2)}, u32[]{:S(2)}) async-start(bf16[8,384,128]{2,1,0:T(8,128)(2,1)} %shard_map.91), calls=%async_computation | async-start | bytes 1572864 | tf_op jit(solution)/shard_map/all_to_all | solution.py:264
  58.4 0.9 copy-start.6
  85.5 18.1 %all-to-all-start.3 = ((bf16[8,192,128]{2,1,0:T(8,128)(2,1)}), bf16[8,192,128]{2,1,0:T(8,128)(2,1)S(1)}, u32[]{:S(2)}, u32[]{:S(2)}) async-start(bf16[8,192,128]{2,1,0:T(8,128)(2,1)} %get-tuple-element.12), calls=%async_computation.3 | async-start | bytes 786432 | tf_op jit(solution)/shard_map/all_to_all | solution.py:264
  102.3 7.5 %copy-start.2 = (bf16[192,1024]{1,0:T(8,128)(2,1)S(1)}, bf16[192,1024]{1,0:T(8,128)(2,1)}, u32[]{:S(2)}) copy-start(bf16[192,1024]{1,0:T(8,128)(2,1)} %shard_map.95.refs_0_) | copy-start | bytes 1179652
  102.3 9.7 %collective-permute-start.2 = (bf16[192,1024]{1,0:T(8,128)(2,1)}, bf16[192,1024]{1,0:T(8,128)(2,1)S(1)}, u32[]{:S(2)}, u32[]{:S(2)}) collective-permute-start(bf16[192,1024]{1,0:T(8,128)(2,1)} %shard_map.95.refs_0_), channel_id=1, source_target_pairs={{0,2},{1,3},{2,0},{3,1},{4,6},{5,7},{6,4},{7,5},{8,10},{9,11},{10,... | collective-permute-start | bytes 1179656 | tf_op jit(solution)/shard_map/ppermute | solution.py:258
  103.6 0.7 copy-start.5
  109.7 11.1 %collective-permute-start.5 = (bf16[192,1024]{1,0:T(8,128)(2,1)}, bf16[192,1024]{1,0:T(8,128)(2,1)S(1)}, u32[]{:S(2)}, u32[]{:S(2)}) collective-permute-start(bf16[192,1024]{1,0:T(8,128)(2,1)} %shard_map.97.refs_0_), channel_id=1, source_target_pairs={{0,2},{1,3},{2,0},{3,1},{4,6},{5,7},{6,4},{7,5},{8,10},{9,11},{10,... | collective-permute-start | bytes 1179656 | tf_op jit(solution)/shard_map/ppermute | solution.py:258
  109.9 12.6 %collective-permute-start.1 = (bf16[192,1024]{1,0:T(8,128)(2,1)S(1)}, bf16[192,1024]{1,0:T(8,128)(2,1)S(1)}, u32[]{:S(2)}, u32[]{:S(2)}) collective-permute-start(bf16[192,1024]{1,0:T(8,128)(2,1)S(1)} %copy-done.2), channel_id=1, source_target_pairs={{0,1},{1,0},{2,3},{3,2},{4,5},{5,4},{6,7},{7,6},{8,9},{9,8},{10,11... | collective-permute-start | bytes 1179656 | tf_op jit(solution)/shard_map/ppermute | solution.py:258
  112.1 10.4 %collective-permute-start.3 = (bf16[192,1024]{1,0:T(8,128)(2,1)S(1)}, bf16[192,1024]{1,0:T(8,128)(2,1)S(1)}, u32[]{:S(2)}, u32[]{:S(2)}) collective-permute-start(bf16[192,1024]{1,0:T(8,128)(2,1)S(1)} %collective-permute-done.2.refs_2_), channel_id=1, source_target_pairs={{0,1},{1,0},{2,3},{3,2},{4,5},{5,4},{6,7},{7,6},{8,9},{9,8},{10,11... | collective-permute-start | bytes 1179656 | tf_op jit(solution)/shard_map/ppermute | solution.py:258
  115.3 13.7 %collective-permute-start.4 = (bf16[192,1024]{1,0:T(8,128)(2,1)}, bf16[192,1024]{1,0:T(8,128)(2,1)S(1)}, u32[]{:S(2)}, u32[]{:S(2)}) collective-permute-start(bf16[192,1024]{1,0:T(8,128)(2,1)} %shard_map.97.refs_0_), channel_id=1, source_target_pairs={{0,1},{1,0},{2,3},{3,2},{4,5},{5,4},{6,7},{7,6},{8,9},{9,8},{10,11... | collective-permute-start | bytes 1179656 | tf_op jit(solution)/shard_map/ppermute | solution.py:258
  120.8 8.3 %collective-permute-start.6 = (bf16[192,1024]{1,0:T(8,128)(2,1)S(1)}, bf16[192,1024]{1,0:T(8,128)(2,1)S(1)}, u32[]{:S(2)}, u32[]{:S(2)}) collective-permute-start(bf16[192,1024]{1,0:T(8,128)(2,1)S(1)} %collective-permute-done.5.refs_2_), channel_id=1, source_target_pairs={{0,1},{1,0},{2,3},{3,2},{4,5},{5,4},{6,7},{7,6},{8,9},{9,8},{10,11... | collective-permute-start | bytes 1179656 | tf_op jit(solution)/shard_map/ppermute | solution.py:258
  122.5 3.4 %copy-start = (bf16[4096,1024]{1,0:T(8,128)(2,1)S(1)}, bf16[4096,1024]{1,0:T(8,128)(2,1)}, u32[]{:S(2)}) copy-start(bf16[4096,1024]{1,0:T(8,128)(2,1)} %refs_4_.3) | copy-start | bytes 25165828
  125.9 3.2 %copy-start.3 = (bf16[192,1024]{1,0:T(8,128)(2,1)S(1)}, bf16[192,1024]{1,0:T(8,128)(2,1)}, u32[]{:S(2)}) copy-start(bf16[192,1024]{1,0:T(8,128)(2,1)} %shard_map.97.refs_0_) | copy-start | bytes 1179652
  129.1 3.4 %copy-start.1 = (bf16[4096,1024]{1,0:T(8,128)(2,1)S(1)}, bf16[4096,1024]{1,0:T(8,128)(2,1)}, u32[]{:S(2)}) copy-start(bf16[4096,1024]{1,0:T(8,128)(2,1)} %refs_4_.3) | copy-start | bytes 25165828

commit v2 on v1

--- a/solution.py
+++ b/solution.py
@@ -37,7 +37,7 @@
 
 def short_conv(pad_ref, block, rim, taps):
     rows = block.shape[0]
-    pad_ref[pl.ds(0, 8), :] = rim
+    pad_ref[pl.ds(8 - rim.shape[0], rim.shape[0]), :] = rim
     pad_ref[pl.ds(8, rows), :] = block
     total = taps[0:1] * block
     for offset in range(1, taps.shape[0]):
@@ -61,7 +61,7 @@
         in_specs=[
             pl.BlockSpec((rows, span), lambda i: (0, i)),
             pl.BlockSpec((rows, span), lambda i: (0, i)),
-            pl.BlockSpec((3, 8, span), lambda i: (0, 0, i)),
+            pl.BlockSpec((3, taps.shape[1] - 1, span), lambda i: (0, 0, i)),
             pl.BlockSpec((3, taps.shape[1], span), lambda i: (0, 0, i)),
         ],
         out_specs=pl.BlockSpec((1, rows, span), lambda i: (i, 0, 0)),
@@ -89,7 +89,7 @@
             column,
             column,
             column,
-            pl.BlockSpec((3, 8, span), lambda i: (0, 0, i)),
+            pl.BlockSpec((3, taps.shape[1] - 1, span), lambda i: (0, 0, i)),
             pl.BlockSpec((3, taps.shape[1], span), lambda i: (0, 0, i)),
             pl.BlockSpec((1, span), lambda i: (0, i)),
         ],
@@ -283,7 +283,355 @@
     return arrived.reshape(count, cut, rows, lanes // cut).transpose(0, 2, 1, 3).reshape(count, rows, lanes)
 
 
-def on_device(out_gate, in_gate, values, short_filter, long_filter, skip_gain, out_weight):
+OFFSETS = (0, 4, 1, 2, 3, 5, 6, 7)
+FILTER_ORDER = (4, 1, 5, 2, 6, 3, 7)
+SIGNAL_ORDER = (4, 1, 5, 2, 6, 3, 7)
+EARLY = (0, 4, 1, 5)
+LATE = (2, 6, 3, 7)
+GROUP = 4
+PER = 2
+PIECE_ORDER = (0, 2, 1, 3)
+
+
+def cost(flops, scale=0):
+    return pl.CostEstimate(flops=scale * flops, bytes_accessed=scale * flops // 128, transcendentals=0)
+
+
+def lanes_at(order_ref, place):
+    return pl.ds(pl.multiple_of(order_ref[place] * LANES, LANES), LANES)
+
+
+def whole_specs(count):
+    return [pl.BlockSpec(memory_space=pltpu.VMEM)] * count
+
+
+def cut_kernel(order_ref, filter_ref, *out_refs):
+    for place, out_ref in enumerate(out_refs):
+        out_ref[...] = filter_ref[:, lanes_at(order_ref, place)].astype(BF16)
+
+
+def cut_filter(order, long_filter):
+    rows, width = long_filter.shape
+    count = width // LANES
+    return pl.pallas_call(
+        cut_kernel,
+        in_specs=[pl.BlockSpec(memory_space=pltpu.SMEM)] + whole_specs(1),
+        out_specs=whole_specs(count),
+        out_shape=[jax.ShapeDtypeStruct((rows, LANES), BF16)] * count,
+        compiler_params=pltpu.CompilerParams(vmem_limit_bytes=8 << 20),
+        cost_estimate=cost(rows * width),
+    )(order, long_filter)
+
+
+def rim_kernel(count, order_ref, *refs):
+    del order_ref
+    ends = [ref[...].astype(F32)[-count:] for ref in refs[:3]]
+    refs[-1][...] = jnp.concatenate(ends, axis=0).astype(BF16)
+
+
+def rim_rows(order, arrays, count):
+    rows, width = arrays[0].shape
+    last = pl.BlockSpec((16, width), lambda i: (rows // 16 - 1, 0))
+    return pl.pallas_call(
+        functools.partial(rim_kernel, count),
+        grid=(1,),
+        in_specs=[pl.BlockSpec(memory_space=pl.ANY)] + [last] * 3,
+        out_specs=pl.BlockSpec((3 * count, width), lambda i: (0, 0)),
+        out_shape=jax.ShapeDtypeStruct((3 * count, width), BF16),
+        compiler_params=pltpu.CompilerParams(vmem_limit_bytes=56 << 20),
+        cost_estimate=pl.CostEstimate(flops=0, bytes_accessed=100 * width, transcendentals=0),
+    )(order, *arrays)
+
+
+def rim_of(rim_ref, which, at):
+    count = rim_ref.shape[0] // 3
+    return rim_ref[:, at].astype(F32)[which * count : (which + 1) * count]
+
+
+def mix_slices_kernel(order_ref, gate_ref, value_ref, rim_ref, taps_ref, gain_ref, *rest):
+    out_refs, skip_ref, (pad_a, pad_b) = rest[:-3], rest[-3], rest[-2:]
+    for place, out_ref in enumerate(out_refs):
+        at = lanes_at(order_ref, place)
+        first = short_conv(pad_a.at[place % 2], gate_ref[:, at].astype(F32), rim_of(rim_ref, 1, at), taps_ref[1, :, at])
+        second = short_conv(pad_b.at[place % 2], value_ref[:, at].astype(F32), rim_of(rim_ref, 2, at), taps_ref[2, :, at])
+        mixed = first * second
+        out_ref[...] = mixed.astype(BF16)
+        skip_ref[place] = gain_ref[:, at] * mixed
+
+
+def mix_slices(order, in_gate, values, rims, taps, skip_gain):
+    rows, width = in_gate.shape
+    count = width // LANES
+    return pl.pallas_call(
+        mix_slices_kernel,
+        in_specs=[pl.BlockSpec(memory_space=pltpu.SMEM)] + whole_specs(5),
+        out_specs=whole_specs(count + 1),
+        out_shape=[jax.ShapeDtypeStruct((rows, LANES), BF16)] * count + [jax.ShapeDtypeStruct((count, rows, LANES), F32)],
+        scratch_shapes=[pltpu.VMEM((2, rows + 8, LANES), F32)] * 2,
+        compiler_params=pltpu.CompilerParams(vmem_limit_bytes=12 << 20),
+        cost_estimate=pl.CostEstimate(flops=14 * rows * width, bytes_accessed=10 * rows * width, transcendentals=0),
+    )(order, in_gate, values, rims, taps, skip_gain.reshape(1, width))
+
+
+def late_kernel(order_ref, late_ref, rim_ref, taps_ref, out_ref, pad):
+    for place in range(out_ref.shape[0]):
+        at = lanes_at(order_ref, place)
+        out_ref[place] = short_conv(pad.at[place % 2], late_ref[:, at].astype(F32), rim_of(rim_ref, 0, at), taps_ref[0, :, at])
+
+
+def late_slices(order, out_gate, rims, taps):
+    rows, width = out_gate.shape
+    count = width // LANES
+    return pl.pallas_call(
+        late_kernel,
+        in_specs=[pl.BlockSpec(memory_space=pltpu.SMEM)] + whole_specs(3),
+        out_specs=pl.BlockSpec(memory_space=pltpu.VMEM),
+        out_shape=jax.ShapeDtypeStruct((count, rows, LANES), F32),
+        scratch_shapes=[pltpu.VMEM((2, rows + 8, LANES), F32)],
+        compiler_params=pltpu.CompilerParams(vmem_limit_bytes=8 << 20),
+        cost_estimate=pl.CostEstimate(flops=6 * rows * width, bytes_accessed=6 * rows * width, transcendentals=0),
+    )(order, out_gate, rims, taps)
+
+
+def spectra_into(order_ref, places, table, signal_refs, out_ref):
+    columns = jnp.concatenate([ref[...] for ref in signal_refs], axis=1)
+    spectra = jnp.dot(table, jnp.concatenate([columns, columns], axis=0), preferred_element_type=F32)
+    for at, place in enumerate(places):
+        out_ref[order_ref[place]] = spectra[:, at * LANES : (at + 1) * LANES]
+
+
+def spectra_kernel(places, order_ref, table_ref, weight_ref, *refs):
+    del weight_ref
+    signal_refs, out_ref = refs[:-1], refs[-1]
+    for base in range(0, len(signal_refs), GROUP):
+        end = base + GROUP
+        spectra_into(order_ref, places[base:end], table_ref[...], signal_refs[base:end], out_ref)
+
+
+def spectra_of(order, table, weight, blocks, places, count):
+    rows, lanes = blocks[0].shape
+    given = len(places)
+    return pl.pallas_call(
+        functools.partial(spectra_kernel, places),
+        in_specs=[pl.BlockSpec(memory_space=pltpu.SMEM)] + whole_specs(1) + [pl.BlockSpec(memory_space=pl.ANY)] + whole_specs(given),
+        out_specs=pl.BlockSpec(memory_space=pltpu.VMEM),
+        out_shape=jax.ShapeDtypeStruct((count, 2 * rows, lanes), F32),
+        compiler_params=pltpu.CompilerParams(vmem_limit_bytes=12 << 20),
+        cost_estimate=pl.CostEstimate(flops=8 * given * rows * rows * lanes, bytes_accessed=10 * given * rows * lanes, transcendentals=0),
+    )(order, table, weight, *[blocks[place] for place in places])
+
+
+def multiply_spectra(filter_ref, spectra_ref, high_ref, low_ref):
+    blocks, depth, _ = spectra_ref.shape
+    rows = depth // 2
+    half, tile = rows // 2, 16
+
+    def multiply(base, turn):
+        def body(step, carry):
+            start = pl.multiple_of(base + step * tile, tile)
+            real, imag = pl.ds(start, tile), pl.ds(rows + start, tile)
+            before = None
+            for at in range(blocks):
+                sum_real = sum_imag = None
+                for other in range(at + 1):
+                    a_real, a_imag = filter_ref[other, real, :], filter_ref[other, imag, :]
+                    b_real, b_imag = spectra_ref[at - other, real, :], spectra_ref[at - other, imag, :]
+                    part_real = a_real * b_real - a_imag * b_imag
+                    part_imag = a_real * b_imag + a_imag * b_real
+                    sum_real = part_real if sum_real is None else sum_real + part_real
+                    sum_imag = part_imag if sum_imag is None else sum_imag + part_imag
+                out_real, out_imag = sum_real, sum_imag
+                if before is not None:
+                    out_real = sum_real - turn * before[1]
+                    out_imag = sum_imag + turn * before[0]
+                before = (sum_real, sum_imag)
+                for place, value in ((real, out_real), (imag, out_imag)):
+                    high = value.astype(BF16)
+                    high_ref[at, place, :] = high
+                    low_ref[at, place, :] = (value - high.astype(F32)).astype(BF16)
+            return carry
+
+        lax.fori_loop(0, half // tile, body, 0)
+
+    multiply(0, 1.0)
+    multiply(half, -1.0)
+
+
+def inverse_into(order_ref, base, inverse, high_ref, low_ref, out_refs):
+    places = [order_ref[base + at] for at in range(len(out_refs))]
+    high = jnp.concatenate([high_ref[place] for place in places], axis=1)
+    low = jnp.concatenate([low_ref[place] for place in places], axis=1)
+    result = jnp.dot(inverse, jnp.concatenate([high, high, low], axis=0), preferred_element_type=F32).astype(BF16)
+    for at, out_ref in enumerate(out_refs):
+        out_ref[...] = result[:, at * LANES : (at + 1) * LANES]
+
+
+def conv_slices_kernel(places, order_ref, table_ref, inverse_ref, filter_ref, early_ref, *refs):
+    del early_ref
+    count = filter_ref.shape[0]
+    signal_refs = refs[: len(places)]
+    spectra_ref, *out_refs, high_ref, low_ref = refs[-count - 3 :]
+    spectra_into(order_ref, places, table_ref[...], signal_refs, spectra_ref)
+    multiply_spectra(filter_ref, spectra_ref, high_ref, low_ref)
+    for base in range(0, count, GROUP):
+        inverse_into(order_ref, base, inverse_ref[...], high_ref, low_ref, out_refs[base : base + GROUP])
+
+
+def conv_slices(order, table, inverse, filter_spectra, early_spectra, blocks, places, after):
+    rows, lanes = blocks[0].shape
+    count = filter_spectra.shape[0]
+    _, *outs = pl.pallas_call(
+        functools.partial(conv_slices_kernel, places),
+        in_specs=[pl.BlockSpec(memory_space=pltpu.SMEM)] + whole_specs(4 + len(places)) + [pl.BlockSpec(memory_space=pl.ANY)] * len(after),
+        out_specs=whole_specs(1 + count),
+        out_shape=[jax.ShapeDtypeStruct((count, 2 * rows, lanes), F32)]
+        + [jax.ShapeDtypeStruct((rows, lanes), BF16)] * count,
+        input_output_aliases={4: 0},
+        scratch_shapes=[pltpu.VMEM((count, 2 * rows, lanes), BF16)] * 2,
+        compiler_params=pltpu.CompilerParams(vmem_limit_bytes=20 << 20),
+        cost_estimate=cost(14 * count * rows * rows * lanes, 1),
+    )(order, table, inverse, filter_spectra, early_spectra, *[blocks[place] for place in places], *after)
+    return outs
+
+
+def gate_chunk_kernel(first, late_ref, skip_ref, *refs):
+    out_ref = refs[-1]
+    for at, long_ref in enumerate(refs[:-1]):
+        mixed = late_ref[first + at] * (long_ref[...].astype(F32) + skip_ref[first + at])
+        out_ref[:, at * LANES : (at + 1) * LANES] = mixed.astype(BF16)
+
+
+def gate_chunk(late, skip, long_blocks, first):
+    rows, lanes = long_blocks[0].shape
+    count = len(long_blocks)
+    return pl.pallas_call(
+        functools.partial(gate_chunk_kernel, first),
+        in_specs=whole_specs(2 + count),
+        out_specs=pl.BlockSpec(memory_space=pltpu.VMEM),
+        out_shape=jax.ShapeDtypeStruct((rows, count * lanes), BF16),
+        compiler_params=pltpu.CompilerParams(vmem_limit_bytes=8 << 20),
+        cost_estimate=cost(3 * count * rows * lanes),
+    )(late, skip, *long_blocks)
+
+
+def weight_kernel(order_ref, channel_ref, weight_ref, out_ref, arrived):
+    count, owners = out_ref.shape[:2]
+    depth = weight_ref.shape[0] // owners
+    copies = []
+    for place in range(count):
+        for offset in range(owners):
+            start = pl.multiple_of((channel_ref[0] ^ offset) * depth + order_ref[place] * LANES, LANES)
+            rows = weight_ref.at[pl.ds(start, LANES), :]
+            copies.append(pltpu.make_async_copy(rows, out_ref.at[place, offset], arrived.at[place, offset]))
+    for copy in copies:
+        copy.start()
+    for copy in copies:
+        copy.wait()
+
+
+def weight_rows_of(order, channel, weight):
+    depth, width = weight.shape
+    count, owners = order.shape[0], len(PIECE_ORDER)
+    return pl.pallas_call(
+        weight_kernel,
+        in_specs=[pl.BlockSpec(memory_space=pltpu.SMEM)] * 2 + [pl.BlockSpec(memory_space=pl.ANY)],
+        out_specs=pl.BlockSpec(memory_space=pltpu.VMEM),
+        out_shape=jax.ShapeDtypeStruct((count, owners, LANES, width), BF16),
+        scratch_shapes=[pltpu.SemaphoreType.DMA((count, owners))],
+        compiler_params=pltpu.CompilerParams(vmem_limit_bytes=10 << 20),
+        cost_estimate=pl.CostEstimate(flops=0, bytes_accessed=4 * depth * width, transcendentals=0),
+    )(order, channel, weight)
+
+
+def add_chunk(chunk, rows_ref, piece_refs, total):
+    pieces = jnp.concatenate([ref[...] for ref in piece_refs], axis=1)
+    rows = [rows_ref[chunk * PER + at, offset] for offset in PIECE_ORDER for at in range(PER)]
+    product = jnp.dot(pieces, jnp.concatenate(rows, axis=0), preferred_element_type=F32)
+    return product if total is None else total + product
+
+
+def join_kernel(*refs):
+    refs[-1][...] = jnp.concatenate([ref[...] for ref in refs[:-1]], axis=1)
+
+
+def join(blocks):
+    rows, lanes = blocks[0].shape
+    count = len(blocks)
+    return pl.pallas_call(
+        join_kernel,
+        in_specs=whole_specs(count),
+        out_specs=pl.BlockSpec(memory_space=pltpu.VMEM),
+        out_shape=jax.ShapeDtypeStruct((rows, count * lanes), blocks[0].dtype),
+        compiler_params=pltpu.CompilerParams(vmem_limit_bytes=8 << 20),
+        cost_estimate=cost(4 * rows * lanes),
+    )(*blocks)
+
+
+def project_kernel_slices(chunks, rows_ref, *refs):
+    refs, more, out_ref = refs[: 2 * len(chunks)], refs[2 * len(chunks) : -1], refs[-1]
+    total = more[0][...] if more else None
+    for at, chunk in enumerate(chunks):
+        total = add_chunk(chunk, rows_ref, refs[2 * at : 2 * at + 2], total)
+    out_ref[...] = total.astype(out_ref.dtype)
+
+
+def project_slices(weight_rows, chunks, pieces, total, out_type):
+    rows, depth = pieces[0].shape
+    width = weight_rows.shape[3]
+    more = () if total is None else (total,)
+    return pl.pallas_call(
+        functools.partial(project_kernel_slices, chunks),
+        in_specs=whole_specs(1 + len(pieces) + len(more)),
+        out_specs=pl.BlockSpec(memory_space=pltpu.VMEM),
+        out_shape=jax.ShapeDtypeStruct((rows, width), out_type),
+        compiler_params=pltpu.CompilerParams(vmem_limit_bytes=14 << 20),
+        cost_estimate=cost(0),
+    )(weight_rows, *pieces, *more)
+
+
+def swap_blocks(blocks, sequence):
+    count = lax.axis_size("seq")
+    arrived = list(blocks)
+    for offset in sequence:
+        place = OFFSETS.index(offset)
+        arrived[place] = lax.ppermute(blocks[place], "seq", [(i, i ^ offset) for i in range(count)])
+    return arrived
+
+
+def on_device_slices(out_gate, in_gate, values, short_filter, long_filter, skip_gain, out_weight):
+    rows, width = out_gate.shape
+    devices = lax.axis_size("seq")
+    taps = short_filter.shape[1]
+    table, inverse = transform_tables(rows)
+    order = jnp.bitwise_xor(lax.axis_index("seq"), jnp.array(OFFSETS, jnp.int32))
+    channel = lax.axis_index("ch").reshape(1)
+
+    rim = rim_rows(order, (out_gate, in_gate, values), taps - 1)
+    filter_blocks = swap_blocks(cut_filter(order, long_filter), FILTER_ORDER)
+    rims = lax.ppermute(rim, "seq", [(i, i + 1) for i in range(devices - 1)])
+    *mixed_slices, skip = mix_slices(order, in_gate, values, rims, short_filter, skip_gain)
+    mixed_blocks = swap_blocks(mixed_slices, SIGNAL_ORDER)
+    late = late_slices(order, out_gate, rims, short_filter)
+    weight_rows = weight_rows_of(order, channel, out_weight)
+    sent = (0, *(OFFSETS.index(offset) for offset in FILTER_ORDER))
+    filter_spectra = spectra_of(order, table, weight_rows, filter_blocks, sent, devices)
+    early, last = (tuple(OFFSETS.index(offset) for offset in group) for group in (EARLY, LATE))
+    early_spectra = spectra_of(order, table, weight_rows, mixed_blocks, early, devices)
+    long_blocks = conv_slices(order, table, inverse, filter_spectra, early_spectra, mixed_blocks, last, (late, weight_rows))
+    arrived = swap_blocks(long_blocks, OFFSETS[1:])
+
+    pieces = []
+    for chunk in range(devices // PER):
+        start = chunk * PER
+        mixed = gate_chunk(late, skip, arrived[start : start + PER], start)
+        across = lax.ppermute(mixed, "ch", [(i, i ^ 2) for i in range(4)])
+        joined = join([mixed, across])
+        pieces += [joined, lax.ppermute(joined, "ch", [(i, i ^ 1) for i in range(4)])]
+    total = project_slices(weight_rows, (0, 1, 2), pieces[:-2], None, F32)
+    return project_slices(weight_rows, (3,), pieces[-2:], total, BF16)
+
+
+def on_device_spans(out_gate, in_gate, values, short_filter, long_filter, skip_gain, out_weight):
     rows, width = out_gate.shape
     devices = lax.axis_size("seq")
     slices = width // LANES
@@ -292,7 +640,7 @@
 
     rim = jnp.stack([a[rows - (taps - 1) :] for a in (out_gate, in_gate, values)])
     rim = lax.ppermute(rim, "seq", [(i, i + 1) for i in range(devices - 1)])
-    rims = jnp.pad(rim.astype(F32), ((0, 0), (8 - (taps - 1), 0), (0, 0)))
+    rims = rim.astype(F32)
 
     filter_slices = long_filter.astype(BF16).reshape(rows, slices, LANES).transpose(1, 0, 2)
     filter_whole = send_spans(filter_slices)
@@ -312,6 +660,13 @@
 
 
 def solution(mesh):
+    devices = mesh.shape["seq"]
+
+    def on_device(*arrays):
+        width = arrays[0].shape[1]
+        sliced = devices == len(OFFSETS) and width == devices * LANES and mesh.shape["ch"] == len(PIECE_ORDER)
+        return (on_device_slices if sliced else on_device_spans)(*arrays)
+
     return jax.shard_map(
         on_device,
         mesh=mesh,

time: 138 us -> 87.9 us (0.64)
  Pallas kernels: 45.9 us -> 21.5 us
  waiting for transfers between devices: 27.4 us -> 8.54 us
  starting transfers between devices: 33.8 us -> 50.7 us
  blocking collectives: 14.8 us -> 0 us
  local copies, waits for them, and re-layouts: 12.8 us -> 6.06 us
    ppermute x7 -> x30, starting transfers between devices: 12 us -> 50.7 us  [the longest x21 32 us: swap_blocks(): lax.ppermute(blocks[place], 'seq', [(i, i ^ offset) for i in range(count)])]
    pallas_call x8 -> x18, Pallas kernels: 45.9 us -> 21.5 us  [the longest x1 5.91 us: conv_slices(): pl.pallas_call(functools.partial(conv_slices_kernel, places), in_specs=[p...]
    all_to_all x3 -> x0, starting transfers between devices: 21.9 us -> none  [exchange(): lax.all_to_all(blocks, 'seq', split_axis=0, concat_axis=0, tiled=True)]
    all_to_all x3 -> x0, waiting for transfers between devices: 21.1 us -> none  [exchange(): lax.all_to_all(blocks, 'seq', split_axis=0, concat_axis=0, tiled=True)]
    all_to_all x1 -> x0, blocking collectives: 14.8 us -> none  [exchange(): lax.all_to_all(blocks, 'seq', split_axis=0, concat_axis=0, tiled=True)]
    unnamed x15 -> x26, local copies, waits for them, and re-layouts: 10.1 us -> 6.06 us
    ppermute x7 -> x30, waiting for transfers between devices: 6.31 us -> 8.54 us  [the longest x21 7.46 us: swap_blocks(): lax.ppermute(blocks[place], 'seq', [(i, i ^ offset) for i in range(count)])]
    another operation x2 -> x0, local copies, waits for them, and re-layouts: 1.47 us -> none  [on_device(): jnp.stack([a[rows - (taps - 1):] for a in (out_gate, in_gate, values)])]
  transfers between devices with their start and end apart: 10 -> 30, of which waited for: 4 -> 5; matrix products, arithmetic and copies ran while one was open for 2% -> 0% of each run, Pallas kernels for 23% -> 15%
where the time goes in v2:
time: 87.9 us; the launch traced here: 87.7 us
  starting transfers between devices  50.7 us (58%)
  Pallas kernels  21.5 us (24%)
  waiting for transfers between devices  8.54 us (10%)
  local copies, waits for them, and re-layouts  6.06 us (7%)
    ppermute x21, starting transfers between devices, swap_blocks(): lax.ppermute(blocks[place], 'seq', [(i, i ^ offset) for i in range(count)])  32 us
    ppermute x4, starting transfers between devices, on_device_slices(): lax.ppermute(joined, 'ch', [(i, i ^ 1) for i in range(4)])  11.4 us
    ppermute x21, waiting for transfers between devices, swap_blocks(): lax.ppermute(blocks[place], 'seq', [(i, i ^ offset) for i in range(count)])  7.46 us
    unnamed x26, local copies, waits for them, and re-layouts  6.06 us
    pallas_call x1, Pallas kernels, conv_slices(): pl.pallas_call(functools.partial(conv_slices_kernel, places), in_specs=[p...  5.91 us
    pallas_call x2, Pallas kernels, project_slices(): pl.pallas_call(functools.partial(project_kernel_slices, chunks), in_specs...  4.53 us
    ppermute x4, starting transfers between devices, on_device_slices(): across = lax.ppermute(mixed, 'ch', [(i, i ^ 2) for i in range(4)])  4.2 us
    pallas_call x2, Pallas kernels, spectra_of(): pl.pallas_call(functools.partial(spectra_kernel, places), in_specs=[pl.Bl...  3.48 us
  transfers between devices with their start and end apart: 30, of which 5 were waited for; matrix products, arithmetic and copies ran while one was open for 0% of the time, Pallas kernels for 15%

profile of v2, /device:TPU:1, one launch (start us, length us, event | category | flops | bytes accessed | tf_op | source)
XLA Modules:
  0.0 87.7 jit_solution(16969068995230548198)
XLA Ops:
  0.0 0.7 broadcast_xor_fusion.order_ref
  0.7 1.4 %copy-done.6 = f32[384,1024]{1,0:T(8,128)S(1)} copy-done((f32[384,1024]{1,0:T(8,128)S(1)}, f32[384,1024]{1,0:T(8,128)}, u32[]{:S(2)}) %copy-start.6) | copy-done | bytes 1572888
  2.1 0.0 copy-start.12
  2.1 0.8 shard_map.104
  2.8 3.2 %collective-permute-start.1 = (bf16[384,128]{1,0:T(8,128)(2,1)S(1)}, bf16[384,128]{1,0:T(8,128)(2,1)S(1)}, u32[]{:S(2)}, u32[]{:S(2)}) collective-permute-start(bf16[384,128]{1,0:T(8,128)(2,1)S(1)} %get-tuple-element.32), channel_id=1, source_target_pairs={{0,16},{4,20},{8,24},{12,28},{16,0},{20,4},{24,8},{28,12},{1,17},{... | collective-permute-start | bytes 294920 | tf_op jit(solution)/shard_map/ppermute | solution.py:597
  6.1 1.2 %collective-permute-start.2 = (bf16[384,128]{1,0:T(8,128)(2,1)S(1)}, bf16[384,128]{1,0:T(8,128)(2,1)S(1)}, u32[]{:S(2)}, u32[]{:S(2)}) collective-permute-start(bf16[384,128]{1,0:T(8,128)(2,1)S(1)} %get-tuple-element.33), channel_id=1, source_target_pairs={{0,4},{4,0},{8,12},{12,8},{16,20},{20,16},{24,28},{28,24},{1,5},{5... | collective-permute-start | bytes 294920 | tf_op jit(solution)/shard_map/ppermute | solution.py:597
  7.3 0.0 collective-permute-start.3
  7.3 1.3 %collective-permute-start.4 = (bf16[384,128]{1,0:T(8,128)(2,1)S(1)}, bf16[384,128]{1,0:T(8,128)(2,1)S(1)}, u32[]{:S(2)}, u32[]{:S(2)}) collective-permute-start(bf16[384,128]{1,0:T(8,128)(2,1)S(1)} %get-tuple-element.35), channel_id=1, source_target_pairs={{0,8},{4,12},{8,0},{12,4},{16,24},{20,28},{24,16},{28,20},{1,9},{5... | collective-permute-start | bytes 294920 | tf_op jit(solution)/shard_map/ppermute | solution.py:597
  8.6 1.4 %shard_map.101 = bf16[6,1024]{1,0:T(8,128)(2,1)} custom-call(s32[8]{0:T(128)} %copy-done.8, bf16[384,1024]{1,0:T(8,128)(2,1)} %late_ref.1, bf16[384,1024]{1,0:T(8,128)(2,1)} %gate_ref.1, bf16[384,1024]{1,0:T(8,128)(2,1)} %value_ref.1), custom_call_target="tpu_custom_call" | custom-call | bytes 102400 | tf_op jit(solution)/shard_map/pallas_call | solution.py:335
  10.0 3.1 %collective-permute-start = (bf16[6,1024]{1,0:T(8,128)(2,1)}, bf16[6,1024]{1,0:T(8,128)(2,1)S(1)}, u32[]{:S(2)}, u32[]{:S(2)}) collective-permute-start(bf16[6,1024]{1,0:T(8,128)(2,1)} %shard_map.101), channel_id=1, source_target_pairs={{0,4},{4,8},{8,12},{12,16},{16,20},{20,24},{24,28},{1,5},{5,9},{9,... | collective-permute-start | bytes 36872 | tf_op jit(solution)/shard_map/ppermute | solution.py:611
  13.1 1.1 %collective-permute-done.rim_ref = bf16[6,1024]{1,0:T(8,128)(2,1)S(1)} collective-permute-done((bf16[6,1024]{1,0:T(8,128)(2,1)}, bf16[6,1024]{1,0:T(8,128)(2,1)S(1)}, u32[]{:S(2)}, u32[]{:S(2)}) %collective-permute-start) | collective-permute-done | bytes 12320 | tf_op jit(solution)/shard_map/ppermute | solution.py:611
  14.2 5.9 %collective-permute-start.5 = (bf16[384,128]{1,0:T(8,128)(2,1)S(1)}, bf16[384,128]{1,0:T(8,128)(2,1)S(1)}, u32[]{:S(2)}, u32[]{:S(2)}) collective-permute-start(bf16[384,128]{1,0:T(8,128)(2,1)S(1)} %get-tuple-element.36), channel_id=1, source_target_pairs={{0,24},{4,28},{8,16},{12,20},{16,8},{20,12},{24,0},{28,4},{1,25},{... | collective-permute-start | bytes 294920 | tf_op jit(solution)/shard_map/ppermute | solution.py:597
  20.1 0.6 copy-done.9
  20.7 2.3 %shard_map.103 = (bf16[384,128]{1,0:T(8,128)(2,1)S(1)}, bf16[384,128]{1,0:T(8,128)(2,1)}, bf16[384,128]{1,0:T(8,128)(2,1)}, bf16[384,128]{1,0:T(8,128)(2,1)S(1)}...) custom-call(s32[8]{0:T(128)S(1)} %copy-done.9, ...), custom_call_target="tpu_custom_call" | custom-call | flops 5505024 | bytes 3932160 | tf_op jit(solution)/shard_map/pallas_call | solution.py:365
  23.0 1.0 %collective-permute-start.7 = (bf16[384,128]{1,0:T(8,128)(2,1)S(1)}, bf16[384,128]{1,0:T(8,128)(2,1)S(1)}, u32[]{:S(2)}, u32[]{:S(2)}) collective-permute-start(bf16[384,128]{1,0:T(8,128)(2,1)S(1)} %get-tuple-element.38), channel_id=1, source_target_pairs={{0,28},{4,24},{8,20},{12,16},{16,12},{20,8},{24,4},{28,0},{1,29},{... | collective-permute-start | bytes 294920 | tf_op jit(solution)/shard_map/ppermute | solution.py:597
  24.0 0.0 collective-permute-done.3.refs_3_
  24.0 2.6 %collective-permute-start.8 = (bf16[384,128]{1,0:T(8,128)(2,1)}, bf16[384,128]{1,0:T(8,128)(2,1)S(1)}, u32[]{:S(2)}, u32[]{:S(2)}) collective-permute-start(bf16[384,128]{1,0:T(8,128)(2,1)} %get-tuple-element.40), channel_id=1, source_target_pairs={{0,16},{4,20},{8,24},{12,28},{16,0},{20,4},{24,8},{28,12},{1,17},{... | collective-permute-start | bytes 294920 | tf_op jit(solution)/shard_map/ppermute | solution.py:597
  26.6 0.0 collective-permute-done.4.refs_4_
  26.6 0.4 collective-permute-start.9
  27.0 3.4 %copy-done.1 = bf16[4096,1024]{1,0:T(8,128)(2,1)S(1)} copy-done((bf16[4096,1024]{1,0:T(8,128)(2,1)S(1)}, bf16[4096,1024]{1,0:T(8,128)(2,1)}, u32[]{:S(2)}) %copy-start.1) | copy-done | bytes 8388632
  30.3 0.6 copy-done.10
  31.0 1.5 %shard_map.100.weight_ref.refs_5_.rows_ref = bf16[8,4,128,1024]{3,2,1,0:T(8,128)(2,1)S(1)} custom-call(s32[8]{0:T(128)S(1)} %copy-done.10, s32[1]{0:T(128)} %bitcast.channel_ref, bf16[4096,1024]{1,0:T(8,128)(2,1)S(1)} %copy-done.1), custom_call_target="tpu_custom_call" | custom-call | bytes 16777216 | tf_op jit(solution)/shard_map/pallas_call | solution.py:535
  32.5 0.0 copy-start
  32.5 1.2 %shard_map.102.refs_4_.late_ref = f32[8,384,128]{2,1,0:T(8,128)S(1)} custom-call(s32[8]{0:T(128)S(1)} %copy-done.10, bf16[384,1024]{1,0:T(8,128)(2,1)S(1)} %copy-done.4, bf16[6,1024]{1,0:T(8,128)(2,1)S(1)} %collective-permute-done.rim_ref, f32[3,3,1024]{2,1,0:T(4,128)S(1)} %copy-done.7), custom_call_target="tpu_custom_call" | custom-call | flops 2359296 | bytes 2359296 | tf_op jit(solution)/shard_map/pallas_call | solution.py:385
  33.7 0.0 collective-permute-done.5.refs_5_
  33.7 1.0 %collective-permute-start.10 = (bf16[384,128]{1,0:T(8,128)(2,1)S(1)}, bf16[384,128]{1,0:T(8,128)(2,1)S(1)}, u32[]{:S(2)}, u32[]{:S(2)}) collective-permute-start(bf16[384,128]{1,0:T(8,128)(2,1)S(1)} %get-tuple-element.42), channel_id=1, source_target_pairs={{0,20},{4,16},{8,28},{12,24},{16,4},{20,0},{24,12},{28,8},{1,21},{... | collective-permute-start | bytes 294920 | tf_op jit(solution)/shard_map/ppermute | solution.py:597
  34.7 0.0 collective-permute-done.6.refs_6_
  34.7 0.4 collective-permute-start.11
  35.0 0.0 collective-permute-done.7.refs_7_
  35.0 3.1 %collective-permute-start.12 = (bf16[384,128]{1,0:T(8,128)(2,1)S(1)}, bf16[384,128]{1,0:T(8,128)(2,1)S(1)}, u32[]{:S(2)}, u32[]{:S(2)}) collective-permute-start(bf16[384,128]{1,0:T(8,128)(2,1)S(1)} %get-tuple-element.44), channel_id=1, source_target_pairs={{0,24},{4,28},{8,16},{12,20},{16,8},{20,12},{24,0},{28,4},{1,25},{... | collective-permute-start | bytes 294920 | tf_op jit(solution)/shard_map/ppermute | solution.py:597
  38.1 0.0 collective-permute-done.8.refs_1_
  38.2 0.1 collective-permute-start.13
  38.2 1.2 %collective-permute-start.14 = (bf16[384,128]{1,0:T(8,128)(2,1)S(1)}, bf16[384,128]{1,0:T(8,128)(2,1)S(1)}, u32[]{:S(2)}, u32[]{:S(2)}) collective-permute-start(bf16[384,128]{1,0:T(8,128)(2,1)S(1)} %get-tuple-element.46), channel_id=1, source_target_pairs={{0,28},{4,24},{8,20},{12,16},{16,12},{20,8},{24,4},{28,0},{1,29},{... | collective-permute-start | bytes 294920 | tf_op jit(solution)/shard_map/ppermute | solution.py:597
  39.4 2.1 %shard_map.105.filter_ref = f32[8,768,128]{2,1,0:T(8,128)S(1)} custom-call(s32[8]{0:T(128)S(1)} %copy-done.11, bf16[768,768]{1,0:T(8,128)(2,1)S(1)} %copy-done, bf16[8,4,128,1024]{3,2,1,0:T(8,128)(2,1)S(1)} %shard_map.100.weight_ref.refs_5_.rows_ref, bf16[384,128]{1,0:T(8,128)(2,1)S(1)} %get-tuple-element.31.refs_0_, ...), custom_call_target="tpu_custom_call" | custom-call | flops 1207959552 | bytes 3932160 | tf_op jit(solution)/shard_map/pallas_call | solution.py:414
  41.5 0.0 collective-permute-done.10.refs_3_
  41.5 0.0 copy-start.5
  41.5 1.4 %shard_map.106.early_ref = f32[8,768,128]{2,1,0:T(8,128)S(1)} custom-call(s32[8]{0:T(128)S(1)} %copy-done.11, bf16[768,768]{1,0:T(8,128)(2,1)S(1)} %copy-done, bf16[8,4,128,1024]{3,2,1,0:T(8,128)(2,1)S(1)} %shard_map.100.weight_ref.refs_5_.rows_ref, bf16[384,128]{1,0:T(8,128)(2,1)S(1)} %get-tuple-element.39.refs_0_, ...), custom_call_target="tpu_custom_call" | custom-call | flops 603979776 | bytes 1966080 | tf_op jit(solution)/shard_map/pallas_call | solution.py:414
  42.9 0.0 collective-permute-done.12.refs_1_
  42.9 2.6 %collective-permute-done.13.refs_2_ = bf16[384,128]{1,0:T(8,128)(2,1)S(1)} collective-permute-done((bf16[384,128]{1,0:T(8,128)(2,1)S(1)}, bf16[384,128]{1,0:T(8,128)(2,1)S(1)}, u32[]{:S(2)}, u32[]{:S(2)}) %collective-permute-start.13) | collective-permute-done | bytes 98336 | tf_op jit(solution)/shard_map/ppermute | solution.py:597
  45.6 0.6 collective-permute-done.14.refs_3_
  46.2 5.9 %shard_map.107 = (f32[8,768,128]{2,1,0:T(8,128)S(1)}, bf16[384,128]{1,0:T(8,128)(2,1)S(1)}, bf16[384,128]{1,0:T(8,128)(2,1)S(1)}, bf16[384,128]{1,0:T(8,128)(2,1...) custom-call(s32[8]{0:T(128)S(1)} %copy-done.11, ...), custom_call_target="tpu_custom_call", output_to_operand_aliasing={{0}: (4, {})} | custom-call | flops 2113929216 | bytes 16515072 | tf_op jit(solution)/shard_map/pallas_call | solution.py:483
  52.1 2.4 %collective-permute-start.19 = (bf16[384,128]{1,0:T(8,128)(2,1)S(1)}, bf16[384,128]{1,0:T(8,128)(2,1)S(1)}, u32[]{:S(2)}, u32[]{:S(2)}) collective-permute-start(bf16[384,128]{1,0:T(8,128)(2,1)S(1)} %get-tuple-element.50), channel_id=1, source_target_pairs={{0,16},{4,20},{8,24},{12,28},{16,0},{20,4},{24,8},{28,12},{1,17},{... | collective-permute-start | bytes 294920 | tf_op jit(solution)/shard_map/ppermute | solution.py:597
  54.5 0.6 collective-permute-start.22
  55.1 1.3 %collective-permute-start.23 = (bf16[384,128]{1,0:T(8,128)(2,1)S(1)}, bf16[384,128]{1,0:T(8,128)(2,1)S(1)}, u32[]{:S(2)}, u32[]{:S(2)}) collective-permute-start(bf16[384,128]{1,0:T(8,128)(2,1)S(1)} %get-tuple-element.52), channel_id=1, source_target_pairs={{0,8},{4,12},{8,0},{12,4},{16,24},{20,28},{24,16},{28,20},{1,9},{5... | collective-permute-start | bytes 294920 | tf_op jit(solution)/shard_map/ppermute | solution.py:597
  56.4 0.7 collective-permute-start.26
  57.1 2.5 %collective-permute-start.27 = (bf16[384,128]{1,0:T(8,128)(2,1)S(1)}, bf16[384,128]{1,0:T(8,128)(2,1)S(1)}, u32[]{:S(2)}, u32[]{:S(2)}) collective-permute-start(bf16[384,128]{1,0:T(8,128)(2,1)S(1)} %get-tuple-element.54), channel_id=1, source_target_pairs={{0,20},{4,16},{8,28},{12,24},{16,4},{20,0},{24,12},{28,8},{1,21},{... | collective-permute-start | bytes 294920 | tf_op jit(solution)/shard_map/ppermute | solution.py:597
  59.6 1.3 %collective-permute-start.15 = (bf16[384,128]{1,0:T(8,128)(2,1)S(1)}, bf16[384,128]{1,0:T(8,128)(2,1)S(1)}, u32[]{:S(2)}, u32[]{:S(2)}) collective-permute-start(bf16[384,128]{1,0:T(8,128)(2,1)S(1)} %get-tuple-element.47), channel_id=1, source_target_pairs={{0,24},{4,28},{8,16},{12,20},{16,8},{20,12},{24,0},{28,4},{1,25},{... | collective-permute-start | bytes 294920 | tf_op jit(solution)/shard_map/ppermute | solution.py:597
  60.9 2.0 %collective-permute-start.16 = (bf16[384,128]{1,0:T(8,128)(2,1)S(1)}, bf16[384,128]{1,0:T(8,128)(2,1)S(1)}, u32[]{:S(2)}, u32[]{:S(2)}) collective-permute-start(bf16[384,128]{1,0:T(8,128)(2,1)S(1)} %get-tuple-element.48), channel_id=1, source_target_pairs={{0,28},{4,24},{8,20},{12,16},{16,12},{20,8},{24,4},{28,0},{1,29},{... | collective-permute-start | bytes 294920 | tf_op jit(solution)/shard_map/ppermute | solution.py:597
  62.9 0.1 shard_map.110.refs_0_
  63.0 1.3 %collective-permute-start.20 = (bf16[384,256]{1,0:T(8,128)(2,1)S(1)}, bf16[384,256]{1,0:T(8,128)(2,1)S(1)}, u32[]{:S(2)}, u32[]{:S(2)}) collective-permute-start(bf16[384,256]{1,0:T(8,128)(2,1)S(1)} %shard_map.110.refs_0_), channel_id=1, source_target_pairs={{0,2},{1,3},{2,0},{3,1},{4,6},{5,7},{6,4},{7,5},{8,10},{9,11},{10,... | collective-permute-start | bytes 589832 | tf_op jit(solution)/shard_map/ppermute | solution.py:627
  64.3 0.1 shard_map.112.refs_0_
  64.4 0.3 collective-permute-start.24
  64.7 0.1 shard_map.114.refs_0_
  64.7 1.3 %collective-permute-start.28 = (bf16[384,256]{1,0:T(8,128)(2,1)S(1)}, bf16[384,256]{1,0:T(8,128)(2,1)S(1)}, u32[]{:S(2)}, u32[]{:S(2)}) collective-permute-start(bf16[384,256]{1,0:T(8,128)(2,1)S(1)} %shard_map.114.refs_0_), channel_id=1, source_target_pairs={{0,2},{1,3},{2,0},{3,1},{4,6},{5,7},{6,4},{7,5},{8,10},{9,11},{10,... | collective-permute-start | bytes 589832 | tf_op jit(solution)/shard_map/ppermute | solution.py:627
  66.0 0.7 collective-permute-done.15.refs_0_
  66.8 3.4 %collective-permute-done.16.refs_1_ = bf16[384,128]{1,0:T(8,128)(2,1)S(1)} collective-permute-done((bf16[384,128]{1,0:T(8,128)(2,1)S(1)}, bf16[384,128]{1,0:T(8,128)(2,1)S(1)}, u32[]{:S(2)}, u32[]{:S(2)}) %collective-permute-start.16) | collective-permute-done | bytes 98336 | tf_op jit(solution)/shard_map/ppermute | solution.py:597
  70.2 0.1 shard_map.108.refs_0_
  70.2 1.3 %collective-permute-start.17 = (bf16[384,256]{1,0:T(8,128)(2,1)S(1)}, bf16[384,256]{1,0:T(8,128)(2,1)S(1)}, u32[]{:S(2)}, u32[]{:S(2)}) collective-permute-start(bf16[384,256]{1,0:T(8,128)(2,1)S(1)} %shard_map.108.refs_0_), channel_id=1, source_target_pairs={{0,2},{1,3},{2,0},{3,1},{4,6},{5,7},{6,4},{7,5},{8,10},{9,11},{10,... | collective-permute-start | bytes 589832 | tf_op jit(solution)/shard_map/ppermute | solution.py:627
  71.6 4.4 %collective-permute-start.21 = (bf16[384,512]{1,0:T(8,128)(2,1)S(1)}, bf16[384,512]{1,0:T(8,128)(2,1)S(1)}, u32[]{:S(2)}, u32[]{:S(2)}) collective-permute-start(bf16[384,512]{1,0:T(8,128)(2,1)S(1)} %shard_map.111.refs_0_), channel_id=1, source_target_pairs={{0,1},{1,0},{2,3},{3,2},{4,5},{5,4},{6,7},{7,6},{8,9},{9,8},{10,11... | collective-permute-start | bytes 1179656 | tf_op jit(solution)/shard_map/ppermute | solution.py:629
  76.1 2.8 %collective-permute-start.25 = (bf16[384,512]{1,0:T(8,128)(2,1)S(1)}, bf16[384,512]{1,0:T(8,128)(2,1)S(1)}, u32[]{:S(2)}, u32[]{:S(2)}) collective-permute-start(bf16[384,512]{1,0:T(8,128)(2,1)S(1)} %shard_map.113.refs_2_), channel_id=1, source_target_pairs={{0,1},{1,0},{2,3},{3,2},{4,5},{5,4},{6,7},{7,6},{8,9},{9,8},{10,11... | collective-permute-start | bytes 1179656 | tf_op jit(solution)/shard_map/ppermute | solution.py:629
  78.9 2.1 %collective-permute-start.29 = (bf16[384,512]{1,0:T(8,128)(2,1)S(1)}, bf16[384,512]{1,0:T(8,128)(2,1)S(1)}, u32[]{:S(2)}, u32[]{:S(2)}) collective-permute-start(bf16[384,512]{1,0:T(8,128)(2,1)S(1)} %shard_map.115.refs_4_), channel_id=1, source_target_pairs={{0,1},{1,0},{2,3},{3,2},{4,5},{5,4},{6,7},{7,6},{8,9},{9,8},{10,11... | collective-permute-start | bytes 1179656 | tf_op jit(solution)/shard_map/ppermute | solution.py:629
  81.0 2.1 %collective-permute-start.18 = (bf16[384,512]{1,0:T(8,128)(2,1)S(1)}, bf16[384,512]{1,0:T(8,128)(2,1)S(1)}, u32[]{:S(2)}, u32[]{:S(2)}) collective-permute-start(bf16[384,512]{1,0:T(8,128)(2,1)S(1)} %shard_map.109.refs_0_), channel_id=1, source_target_pairs={{0,1},{1,0},{2,3},{3,2},{4,5},{5,4},{6,7},{7,6},{8,9},{9,8},{10,11... | collective-permute-start | bytes 1179656 | tf_op jit(solution)/shard_map/ppermute | solution.py:629
  83.1 2.6 %shard_map.116.refs_2_ = f32[384,1024]{1,0:T(8,128)S(1)} custom-call(bf16[8,4,128,1024]{3,2,1,0:T(8,128)(2,1)S(1)} %shard_map.100.weight_ref.refs_5_.rows_ref, bf16[384,512]{1,0:T(8,128)(2,1)S(1)} %shard_map.111.refs_0_, bf16[384,512]{1,0:T(8,128)(2,1)S(1)} %collective-permute-done.21.refs_1_, bf16[384,512]{1,0:T(8,128)(2,1)S(1)} %shard_map.113.refs_2_, ...), custom_call_target="tpu_custom_call" | custom-call | tf_op jit(solution)/shard_map/pallas_call | solution.py:582
  85.8 1.9 %shard_map.117 = bf16[384,1024]{1,0:T(8,128)(2,1)} custom-call(bf16[8,4,128,1024]{3,2,1,0:T(8,128)(2,1)S(1)} %shard_map.100.weight_ref.refs_5_.rows_ref, bf16[384,512]{1,0:T(8,128)(2,1)S(1)} %shard_map.109.refs_0_, bf16[384,512]{1,0:T(8,128)(2,1)S(1)} %collective-permute-done.18.refs_1_, f32[384,1024]{1,0:T(8,128)S(1)} %shard_map.116.refs_2_), custom_call_target="tpu_custom_call" | custom-call | tf_op jit(solution)/shard_map/pallas_call | solution.py:582
  (41 shorter events, 0.2 us)
Async XLA Ops:
  0.7 1.4 %copy-start.6 = (f32[384,1024]{1,0:T(8,128)S(1)}, f32[384,1024]{1,0:T(8,128)}, u32[]{:S(2)}) copy-start(f32[384,1024]{1,0:T(8,128)} %filter_ref.1) | copy-start | bytes 4718596
  2.1 6.5 %copy-start.8 = (s32[8]{0:T(128)}, s32[8]{0:T(128)S(1)}, u32[]{:S(2)}) copy-start(s32[8]{0:T(128)S(1)} %broadcast_xor_fusion.order_ref) | copy-start | bytes 100
  2.1 18.0 %copy-start.2 = (bf16[384,1024]{1,0:T(8,128)(2,1)S(1)}, bf16[384,1024]{1,0:T(8,128)(2,1)}, u32[]{:S(2)}) copy-start(bf16[384,1024]{1,0:T(8,128)(2,1)} %gate_ref.1) | copy-start | bytes 2359300
  2.1 18.0 %copy-start.3 = (bf16[384,1024]{1,0:T(8,128)(2,1)S(1)}, bf16[384,1024]{1,0:T(8,128)(2,1)}, u32[]{:S(2)}) copy-start(bf16[384,1024]{1,0:T(8,128)(2,1)} %value_ref.1) | copy-start | bytes 2359300
  2.1 18.0 %copy-start.7 = (f32[3,3,1024]{2,1,0:T(4,128)S(1)}, f32[3,3,1024]{2,1,0:T(4,128)}, u32[]{:S(2)}) copy-start(f32[3,3,1024]{2,1,0:T(4,128)} %taps_ref.3) | copy-start | bytes 110596
  2.1 18.0 %copy-start.12 = (f32[1024]{0:T(1024)S(1)}, f32[1024]{0:T(1024)}, u32[]{:S(2)}) copy-start(f32[1024]{0:T(1024)} %param.15) | copy-start | bytes 12292
  2.8 20.2 %collective-permute-start.1 = (bf16[384,128]{1,0:T(8,128)(2,1)S(1)}, bf16[384,128]{1,0:T(8,128)(2,1)S(1)}, u32[]{:S(2)}, u32[]{:S(2)}) collective-permute-start(bf16[384,128]{1,0:T(8,128)(2,1)S(1)} %get-tuple-element.32), channel_id=1, source_target_pairs={{0,16},{4,20},{8,24},{12,28},{16,0},{20,4},{24,8},{28,12},{1,17},{... | collective-permute-start | bytes 294920 | tf_op jit(solution)/shard_map/ppermute | solution.py:597
  6.1 17.0 %collective-permute-start.2 = (bf16[384,128]{1,0:T(8,128)(2,1)S(1)}, bf16[384,128]{1,0:T(8,128)(2,1)S(1)}, u32[]{:S(2)}, u32[]{:S(2)}) collective-permute-start(bf16[384,128]{1,0:T(8,128)(2,1)S(1)} %get-tuple-element.33), channel_id=1, source_target_pairs={{0,4},{4,0},{8,12},{12,8},{16,20},{20,16},{24,28},{28,24},{1,5},{5... | collective-permute-start | bytes 294920 | tf_op jit(solution)/shard_map/ppermute | solution.py:597
  7.3 16.8 %collective-permute-start.3 = (bf16[384,128]{1,0:T(8,128)(2,1)S(1)}, bf16[384,128]{1,0:T(8,128)(2,1)S(1)}, u32[]{:S(2)}, u32[]{:S(2)}) collective-permute-start(bf16[384,128]{1,0:T(8,128)(2,1)S(1)} %get-tuple-element.34), channel_id=1, source_target_pairs={{0,20},{4,16},{8,28},{12,24},{16,4},{20,0},{24,12},{28,8},{1,21},{... | collective-permute-start | bytes 294920 | tf_op jit(solution)/shard_map/ppermute | solution.py:597
  7.3 19.3 %collective-permute-start.4 = (bf16[384,128]{1,0:T(8,128)(2,1)S(1)}, bf16[384,128]{1,0:T(8,128)(2,1)S(1)}, u32[]{:S(2)}, u32[]{:S(2)}) collective-permute-start(bf16[384,128]{1,0:T(8,128)(2,1)S(1)} %get-tuple-element.35), channel_id=1, source_target_pairs={{0,8},{4,12},{8,0},{12,4},{16,24},{20,28},{24,16},{28,20},{1,9},{5... | collective-permute-start | bytes 294920 | tf_op jit(solution)/shard_map/ppermute | solution.py:597
  10.0 4.2 %collective-permute-start = (bf16[6,1024]{1,0:T(8,128)(2,1)}, bf16[6,1024]{1,0:T(8,128)(2,1)S(1)}, u32[]{:S(2)}, u32[]{:S(2)}) collective-permute-start(bf16[6,1024]{1,0:T(8,128)(2,1)} %shard_map.101), channel_id=1, source_target_pairs={{0,4},{4,8},{8,12},{12,16},{16,20},{20,24},{24,28},{1,5},{5,9},{9,... | collective-permute-start | bytes 36872 | tf_op jit(solution)/shard_map/ppermute | solution.py:611
  14.2 19.5 %collective-permute-start.5 = (bf16[384,128]{1,0:T(8,128)(2,1)S(1)}, bf16[384,128]{1,0:T(8,128)(2,1)S(1)}, u32[]{:S(2)}, u32[]{:S(2)}) collective-permute-start(bf16[384,128]{1,0:T(8,128)(2,1)S(1)} %get-tuple-element.36), channel_id=1, source_target_pairs={{0,24},{4,28},{8,16},{12,20},{16,8},{20,12},{24,0},{28,4},{1,25},{... | collective-permute-start | bytes 294920 | tf_op jit(solution)/shard_map/ppermute | solution.py:597
  20.1 0.6 copy-start.9
  23.0 11.6 %collective-permute-start.6 = (bf16[384,128]{1,0:T(8,128)(2,1)S(1)}, bf16[384,128]{1,0:T(8,128)(2,1)S(1)}, u32[]{:S(2)}, u32[]{:S(2)}) collective-permute-start(bf16[384,128]{1,0:T(8,128)(2,1)S(1)} %get-tuple-element.37), channel_id=1, source_target_pairs={{0,12},{4,8},{8,4},{12,0},{16,28},{20,24},{24,20},{28,16},{1,13},{... | collective-permute-start | bytes 294920 | tf_op jit(solution)/shard_map/ppermute | solution.py:597
  23.0 12.0 %collective-permute-start.7 = (bf16[384,128]{1,0:T(8,128)(2,1)S(1)}, bf16[384,128]{1,0:T(8,128)(2,1)S(1)}, u32[]{:S(2)}, u32[]{:S(2)}) collective-permute-start(bf16[384,128]{1,0:T(8,128)(2,1)S(1)} %get-tuple-element.38), channel_id=1, source_target_pairs={{0,28},{4,24},{8,20},{12,16},{16,12},{20,8},{24,4},{28,0},{1,29},{... | collective-permute-start | bytes 294920 | tf_op jit(solution)/shard_map/ppermute | solution.py:597
  24.0 14.1 %collective-permute-start.8 = (bf16[384,128]{1,0:T(8,128)(2,1)}, bf16[384,128]{1,0:T(8,128)(2,1)S(1)}, u32[]{:S(2)}, u32[]{:S(2)}) collective-permute-start(bf16[384,128]{1,0:T(8,128)(2,1)} %get-tuple-element.40), channel_id=1, source_target_pairs={{0,16},{4,20},{8,24},{12,28},{16,0},{20,4},{24,8},{28,12},{1,17},{... | collective-permute-start | bytes 294920 | tf_op jit(solution)/shard_map/ppermute | solution.py:597
  26.6 11.6 %collective-permute-start.9 = (bf16[384,128]{1,0:T(8,128)(2,1)}, bf16[384,128]{1,0:T(8,128)(2,1)S(1)}, u32[]{:S(2)}, u32[]{:S(2)}) collective-permute-start(bf16[384,128]{1,0:T(8,128)(2,1)} %get-tuple-element.41), channel_id=1, source_target_pairs={{0,4},{4,0},{8,12},{12,8},{16,20},{20,16},{24,28},{28,24},{1,5},{5... | collective-permute-start | bytes 294920 | tf_op jit(solution)/shard_map/ppermute | solution.py:597
  27.0 3.4 %copy-start.1 = (bf16[4096,1024]{1,0:T(8,128)(2,1)S(1)}, bf16[4096,1024]{1,0:T(8,128)(2,1)}, u32[]{:S(2)}) copy-start(bf16[4096,1024]{1,0:T(8,128)(2,1)} %weight_ref.1) | copy-start | bytes 25165828
  30.3 0.6 copy-start.10
  31.0 1.5 %copy-start.4 = (bf16[384,1024]{1,0:T(8,128)(2,1)S(1)}, bf16[384,1024]{1,0:T(8,128)(2,1)}, u32[]{:S(2)}) copy-start(bf16[384,1024]{1,0:T(8,128)(2,1)} %late_ref.1) | copy-start | bytes 2359300
  32.5 6.9 %copy-start = (bf16[768,768]{1,0:T(8,128)(2,1)S(1)}, bf16[768,768]{1,0:T(8,128)(2,1)}, u32[]{:S(2)}) copy-start(bf16[768,768]{1,0:T(8,128)(2,1)} %constant.16.clone.table_ref) | copy-start | bytes 3538948
  32.5 6.9 %copy-start.11 = (s32[8]{0:T(128)S(1)}, s32[8]{0:T(128)}, u32[]{:S(2)}) copy-start(s32[8]{0:T(128)} %copy-done.8) | copy-start | bytes 100
  33.7 7.8 %collective-permute-start.10 = (bf16[384,128]{1,0:T(8,128)(2,1)S(1)}, bf16[384,128]{1,0:T(8,128)(2,1)S(1)}, u32[]{:S(2)}, u32[]{:S(2)}) collective-permute-start(bf16[384,128]{1,0:T(8,128)(2,1)S(1)} %get-tuple-element.42), channel_id=1, source_target_pairs={{0,20},{4,16},{8,28},{12,24},{16,4},{20,0},{24,12},{28,8},{1,21},{... | collective-permute-start | bytes 294920 | tf_op jit(solution)/shard_map/ppermute | solution.py:597
  34.7 8.3 %collective-permute-start.11 = (bf16[384,128]{1,0:T(8,128)(2,1)S(1)}, bf16[384,128]{1,0:T(8,128)(2,1)S(1)}, u32[]{:S(2)}, u32[]{:S(2)}) collective-permute-start(bf16[384,128]{1,0:T(8,128)(2,1)S(1)} %get-tuple-element.43), channel_id=1, source_target_pairs={{0,8},{4,12},{8,0},{12,4},{16,24},{20,28},{24,16},{28,20},{1,9},{5... | collective-permute-start | bytes 294920 | tf_op jit(solution)/shard_map/ppermute | solution.py:597
  35.0 7.9 %collective-permute-start.12 = (bf16[384,128]{1,0:T(8,128)(2,1)S(1)}, bf16[384,128]{1,0:T(8,128)(2,1)S(1)}, u32[]{:S(2)}, u32[]{:S(2)}) collective-permute-start(bf16[384,128]{1,0:T(8,128)(2,1)S(1)} %get-tuple-element.44), channel_id=1, source_target_pairs={{0,24},{4,28},{8,16},{12,20},{16,8},{20,12},{24,0},{28,4},{1,25},{... | collective-permute-start | bytes 294920 | tf_op jit(solution)/shard_map/ppermute | solution.py:597
  38.2 7.4 %collective-permute-start.13 = (bf16[384,128]{1,0:T(8,128)(2,1)S(1)}, bf16[384,128]{1,0:T(8,128)(2,1)S(1)}, u32[]{:S(2)}, u32[]{:S(2)}) collective-permute-start(bf16[384,128]{1,0:T(8,128)(2,1)S(1)} %get-tuple-element.45), channel_id=1, source_target_pairs={{0,12},{4,8},{8,4},{12,0},{16,28},{20,24},{24,20},{28,16},{1,13},{... | collective-permute-start | bytes 294920 | tf_op jit(solution)/shard_map/ppermute | solution.py:597
  38.2 8.0 %collective-permute-start.14 = (bf16[384,128]{1,0:T(8,128)(2,1)S(1)}, bf16[384,128]{1,0:T(8,128)(2,1)S(1)}, u32[]{:S(2)}, u32[]{:S(2)}) collective-permute-start(bf16[384,128]{1,0:T(8,128)(2,1)S(1)} %get-tuple-element.46), channel_id=1, source_target_pairs={{0,28},{4,24},{8,20},{12,16},{16,12},{20,8},{24,4},{28,0},{1,29},{... | collective-permute-start | bytes 294920 | tf_op jit(solution)/shard_map/ppermute | solution.py:597
  41.5 4.7 %copy-start.5 = (bf16[384,2304]{1,0:T(8,128)(2,1)S(1)}, bf16[384,2304]{1,0:T(8,128)(2,1)}, u32[]{:S(2)}) copy-start(bf16[384,2304]{1,0:T(8,128)(2,1)} %constant.17.clone.inverse_ref) | copy-start | bytes 5308420
  52.1 7.5 %collective-permute-start.19 = (bf16[384,128]{1,0:T(8,128)(2,1)S(1)}, bf16[384,128]{1,0:T(8,128)(2,1)S(1)}, u32[]{:S(2)}, u32[]{:S(2)}) collective-permute-start(bf16[384,128]{1,0:T(8,128)(2,1)S(1)} %get-tuple-element.50), channel_id=1, source_target_pairs={{0,16},{4,20},{8,24},{12,28},{16,0},{20,4},{24,8},{28,12},{1,17},{... | collective-permute-start | bytes 294920 | tf_op jit(solution)/shard_map/ppermute | solution.py:597
  54.5 6.4 %collective-permute-start.22 = (bf16[384,128]{1,0:T(8,128)(2,1)S(1)}, bf16[384,128]{1,0:T(8,128)(2,1)S(1)}, u32[]{:S(2)}, u32[]{:S(2)}) collective-permute-start(bf16[384,128]{1,0:T(8,128)(2,1)S(1)} %get-tuple-element.51), channel_id=1, source_target_pairs={{0,4},{4,0},{8,12},{12,8},{16,20},{20,16},{24,28},{28,24},{1,5},{5... | collective-permute-start | bytes 294920 | tf_op jit(solution)/shard_map/ppermute | solution.py:597
  55.1 7.9 %collective-permute-start.23 = (bf16[384,128]{1,0:T(8,128)(2,1)S(1)}, bf16[384,128]{1,0:T(8,128)(2,1)S(1)}, u32[]{:S(2)}, u32[]{:S(2)}) collective-permute-start(bf16[384,128]{1,0:T(8,128)(2,1)S(1)} %get-tuple-element.52), channel_id=1, source_target_pairs={{0,8},{4,12},{8,0},{12,4},{16,24},{20,28},{24,16},{28,20},{1,9},{5... | collective-permute-start | bytes 294920 | tf_op jit(solution)/shard_map/ppermute | solution.py:597
  56.4 7.9 %collective-permute-start.26 = (bf16[384,128]{1,0:T(8,128)(2,1)S(1)}, bf16[384,128]{1,0:T(8,128)(2,1)S(1)}, u32[]{:S(2)}, u32[]{:S(2)}) collective-permute-start(bf16[384,128]{1,0:T(8,128)(2,1)S(1)} %get-tuple-element.53), channel_id=1, source_target_pairs={{0,12},{4,8},{8,4},{12,0},{16,28},{20,24},{24,20},{28,16},{1,13},{... | collective-permute-start | bytes 294920 | tf_op jit(solution)/shard_map/ppermute | solution.py:597
  57.1 7.5 %collective-permute-start.27 = (bf16[384,128]{1,0:T(8,128)(2,1)S(1)}, bf16[384,128]{1,0:T(8,128)(2,1)S(1)}, u32[]{:S(2)}, u32[]{:S(2)}) collective-permute-start(bf16[384,128]{1,0:T(8,128)(2,1)S(1)} %get-tuple-element.54), channel_id=1, source_target_pairs={{0,20},{4,16},{8,28},{12,24},{16,4},{20,0},{24,12},{28,8},{1,21},{... | collective-permute-start | bytes 294920 | tf_op jit(solution)/shard_map/ppermute | solution.py:597
  59.6 7.1 %collective-permute-start.15 = (bf16[384,128]{1,0:T(8,128)(2,1)S(1)}, bf16[384,128]{1,0:T(8,128)(2,1)S(1)}, u32[]{:S(2)}, u32[]{:S(2)}) collective-permute-start(bf16[384,128]{1,0:T(8,128)(2,1)S(1)} %get-tuple-element.47), channel_id=1, source_target_pairs={{0,24},{4,28},{8,16},{12,20},{16,8},{20,12},{24,0},{28,4},{1,25},{... | collective-permute-start | bytes 294920 | tf_op jit(solution)/shard_map/ppermute | solution.py:597
  60.9 9.3 %collective-permute-start.16 = (bf16[384,128]{1,0:T(8,128)(2,1)S(1)}, bf16[384,128]{1,0:T(8,128)(2,1)S(1)}, u32[]{:S(2)}, u32[]{:S(2)}) collective-permute-start(bf16[384,128]{1,0:T(8,128)(2,1)S(1)} %get-tuple-element.48), channel_id=1, source_target_pairs={{0,28},{4,24},{8,20},{12,16},{16,12},{20,8},{24,4},{28,0},{1,29},{... | collective-permute-start | bytes 294920 | tf_op jit(solution)/shard_map/ppermute | solution.py:597
  63.0 8.6 %collective-permute-start.20 = (bf16[384,256]{1,0:T(8,128)(2,1)S(1)}, bf16[384,256]{1,0:T(8,128)(2,1)S(1)}, u32[]{:S(2)}, u32[]{:S(2)}) collective-permute-start(bf16[384,256]{1,0:T(8,128)(2,1)S(1)} %shard_map.110.refs_0_), channel_id=1, source_target_pairs={{0,2},{1,3},{2,0},{3,1},{4,6},{5,7},{6,4},{7,5},{8,10},{9,11},{10,... | collective-permute-start | bytes 589832 | tf_op jit(solution)/shard_map/ppermute | solution.py:627
  64.4 11.7 %collective-permute-start.24 = (bf16[384,256]{1,0:T(8,128)(2,1)S(1)}, bf16[384,256]{1,0:T(8,128)(2,1)S(1)}, u32[]{:S(2)}, u32[]{:S(2)}) collective-permute-start(bf16[384,256]{1,0:T(8,128)(2,1)S(1)} %shard_map.112.refs_0_), channel_id=1, source_target_pairs={{0,2},{1,3},{2,0},{3,1},{4,6},{5,7},{6,4},{7,5},{8,10},{9,11},{10,... | collective-permute-start | bytes 589832 | tf_op jit(solution)/shard_map/ppermute | solution.py:627
  64.7 14.2 %collective-permute-start.28 = (bf16[384,256]{1,0:T(8,128)(2,1)S(1)}, bf16[384,256]{1,0:T(8,128)(2,1)S(1)}, u32[]{:S(2)}, u32[]{:S(2)}) collective-permute-start(bf16[384,256]{1,0:T(8,128)(2,1)S(1)} %shard_map.114.refs_0_), channel_id=1, source_target_pairs={{0,2},{1,3},{2,0},{3,1},{4,6},{5,7},{6,4},{7,5},{8,10},{9,11},{10,... | collective-permute-start | bytes 589832 | tf_op jit(solution)/shard_map/ppermute | solution.py:627
  70.2 10.7 %collective-permute-start.17 = (bf16[384,256]{1,0:T(8,128)(2,1)S(1)}, bf16[384,256]{1,0:T(8,128)(2,1)S(1)}, u32[]{:S(2)}, u32[]{:S(2)}) collective-permute-start(bf16[384,256]{1,0:T(8,128)(2,1)S(1)} %shard_map.108.refs_0_), channel_id=1, source_target_pairs={{0,2},{1,3},{2,0},{3,1},{4,6},{5,7},{6,4},{7,5},{8,10},{9,11},{10,... | collective-permute-start | bytes 589832 | tf_op jit(solution)/shard_map/ppermute | solution.py:627
  71.6 11.5 %collective-permute-start.21 = (bf16[384,512]{1,0:T(8,128)(2,1)S(1)}, bf16[384,512]{1,0:T(8,128)(2,1)S(1)}, u32[]{:S(2)}, u32[]{:S(2)}) collective-permute-start(bf16[384,512]{1,0:T(8,128)(2,1)S(1)} %shard_map.111.refs_0_), channel_id=1, source_target_pairs={{0,1},{1,0},{2,3},{3,2},{4,5},{5,4},{6,7},{7,6},{8,9},{9,8},{10,11... | collective-permute-start | bytes 1179656 | tf_op jit(solution)/shard_map/ppermute | solution.py:629
  76.1 7.0 %collective-permute-start.25 = (bf16[384,512]{1,0:T(8,128)(2,1)S(1)}, bf16[384,512]{1,0:T(8,128)(2,1)S(1)}, u32[]{:S(2)}, u32[]{:S(2)}) collective-permute-start(bf16[384,512]{1,0:T(8,128)(2,1)S(1)} %shard_map.113.refs_2_), channel_id=1, source_target_pairs={{0,1},{1,0},{2,3},{3,2},{4,5},{5,4},{6,7},{7,6},{8,9},{9,8},{10,11... | collective-permute-start | bytes 1179656 | tf_op jit(solution)/shard_map/ppermute | solution.py:629
  78.9 4.2 %collective-permute-start.29 = (bf16[384,512]{1,0:T(8,128)(2,1)S(1)}, bf16[384,512]{1,0:T(8,128)(2,1)S(1)}, u32[]{:S(2)}, u32[]{:S(2)}) collective-permute-start(bf16[384,512]{1,0:T(8,128)(2,1)S(1)} %shard_map.115.refs_4_), channel_id=1, source_target_pairs={{0,1},{1,0},{2,3},{3,2},{4,5},{5,4},{6,7},{7,6},{8,9},{9,8},{10,11... | collective-permute-start | bytes 1179656 | tf_op jit(solution)/shard_map/ppermute | solution.py:629
  81.0 4.7 %collective-permute-start.18 = (bf16[384,512]{1,0:T(8,128)(2,1)S(1)}, bf16[384,512]{1,0:T(8,128)(2,1)S(1)}, u32[]{:S(2)}, u32[]{:S(2)}) collective-permute-start(bf16[384,512]{1,0:T(8,128)(2,1)S(1)} %shard_map.109.refs_0_), channel_id=1, source_target_pairs={{0,1},{1,0},{2,3},{3,2},{4,5},{5,4},{6,7},{7,6},{8,9},{9,8},{10,11... | collective-permute-start | bytes 1179656 | tf_op jit(solution)/shard_map/ppermute | solution.py:629

commit v3 on v2

--- a/solution.py
+++ b/solution.py
@@ -11,6 +11,8 @@
 from jax.sharding import PartitionSpec as P
 
 LANES = 128
+TILE = 16
+CUT_VMEM = 56
 ROW_PARTS = 2
 BF16 = jnp.bfloat16
 F32 = jnp.float32
@@ -289,7 +291,12 @@
 EARLY = (0, 4, 1, 5)
 LATE = (2, 6, 3, 7)
 GROUP = 4
-PER = 2
+NEXT_OFFSETS = (1, 3, 7)
+KEEP = 2
+MIX_AFTER = 1
+CHUNKS = ((0, 2), (2, 4), (4, 6), (6, 8))
+PROJECTS = ((0, 1, 2), (3,))
+PROJECT_COSTS = (0, 0)
 PIECE_ORDER = (0, 2, 1, 3)
 
 
@@ -305,120 +312,184 @@
     return [pl.BlockSpec(memory_space=pltpu.VMEM)] * count
 
 
-def cut_kernel(order_ref, filter_ref, *out_refs):
+def cut_kernel(order_ref, filter_ref, *refs):
+    last_refs, (gate_top, value_top), out_refs = refs[:3], refs[3:5], refs[5:-1]
+    rows, width = filter_ref.shape
+    ends_ref = refs[-1]
+    ends = [ref[...].astype(F32)[-KEEP:] for ref in last_refs]
+    ends += [ref[...].astype(F32)[:KEEP] for ref in (gate_top, value_top)]
+    ends.append(jnp.zeros((TILE - 5 * KEEP, width), F32))
+    ends_ref[...] = jnp.concatenate(ends, axis=0).astype(BF16)
     for place, out_ref in enumerate(out_refs):
-        out_ref[...] = filter_ref[:, lanes_at(order_ref, place)].astype(BF16)
-
-
-def cut_filter(order, long_filter):
+        at = lanes_at(order_ref, place)
+        out_ref[:rows] = filter_ref[:, at].astype(BF16)
+        out_ref[rows : rows + TILE] = ends_ref[:, at]
+        if OFFSETS[place] in NEXT_OFFSETS:
+            for part in range(width // LANES):
+                out_ref[rows + (1 + part) * TILE : rows + (2 + part) * TILE] = ends_ref[:, part * LANES : (part + 1) * LANES]
+
+
+def cut_filter(order, long_filter, out_gate, in_gate, values):
     rows, width = long_filter.shape
     count = width // LANES
+    heights = [rows + TILE * (1 + count * (offset in NEXT_OFFSETS)) for offset in OFFSETS]
+    top = pl.BlockSpec((TILE, width), lambda i: (0, 0))
+    last = pl.BlockSpec((TILE, width), lambda i: (rows // TILE - 1, 0))
     return pl.pallas_call(
         cut_kernel,
-        in_specs=[pl.BlockSpec(memory_space=pltpu.SMEM)] + whole_specs(1),
+        grid=(1,),
+        in_specs=[pl.BlockSpec(memory_space=pltpu.SMEM), pl.BlockSpec((rows, width), lambda i: (0, 0))] + [last] * 3 + [top] * 2,
+        out_specs=[pl.BlockSpec((height, LANES), lambda i: (0, 0)) for height in heights],
+        out_shape=[jax.ShapeDtypeStruct((height, LANES), BF16) for height in heights],
+        scratch_shapes=[pltpu.VMEM((TILE, width), BF16)],
+        compiler_params=pltpu.CompilerParams(vmem_limit_bytes=CUT_VMEM << 20),
+        cost_estimate=cost(rows * width),
+    )(order, long_filter, out_gate, in_gate, values, in_gate, values)
+
+
+def mix_slices_kernel(order_ref, gate_ref, value_ref, taps_ref, after_ref, *rest):
+    del after_ref
+    out_refs, (pad_a, pad_b) = rest[:-2], rest[-2:]
+    keep = taps_ref.shape[1] - 1
+    for place, out_ref in enumerate(out_refs):
+        at = lanes_at(order_ref, place)
+        none = jnp.zeros((keep, LANES), F32)
+        first = short_conv(pad_a.at[place % 2], gate_ref[:, at].astype(F32), none, taps_ref[1, :, at])
+        second = short_conv(pad_b.at[place % 2], value_ref[:, at].astype(F32), none, taps_ref[2, :, at])
+        out_ref[...] = (first * second).astype(BF16)
+
+
+def mix_slices(order, in_gate, values, taps, after):
+    rows, width = in_gate.shape
+    count = width // LANES
+    return pl.pallas_call(
+        mix_slices_kernel,
+        in_specs=[pl.BlockSpec(memory_space=pltpu.SMEM)] + whole_specs(3) + [pl.BlockSpec(memory_space=pl.ANY)],
         out_specs=whole_specs(count),
         out_shape=[jax.ShapeDtypeStruct((rows, LANES), BF16)] * count,
-        compiler_params=pltpu.CompilerParams(vmem_limit_bytes=8 << 20),
-        cost_estimate=cost(rows * width),
-    )(order, long_filter)
-
-
-def rim_kernel(count, order_ref, *refs):
-    del order_ref
-    ends = [ref[...].astype(F32)[-count:] for ref in refs[:3]]
-    refs[-1][...] = jnp.concatenate(ends, axis=0).astype(BF16)
-
-
-def rim_rows(order, arrays, count):
-    rows, width = arrays[0].shape
-    last = pl.BlockSpec((16, width), lambda i: (rows // 16 - 1, 0))
-    return pl.pallas_call(
-        functools.partial(rim_kernel, count),
-        grid=(1,),
-        in_specs=[pl.BlockSpec(memory_space=pl.ANY)] + [last] * 3,
-        out_specs=pl.BlockSpec((3 * count, width), lambda i: (0, 0)),
-        out_shape=jax.ShapeDtypeStruct((3 * count, width), BF16),
-        compiler_params=pltpu.CompilerParams(vmem_limit_bytes=56 << 20),
-        cost_estimate=pl.CostEstimate(flops=0, bytes_accessed=100 * width, transcendentals=0),
-    )(order, *arrays)
-
-
-def rim_of(rim_ref, which, at):
-    count = rim_ref.shape[0] // 3
-    return rim_ref[:, at].astype(F32)[which * count : (which + 1) * count]
-
-
-def mix_slices_kernel(order_ref, gate_ref, value_ref, rim_ref, taps_ref, gain_ref, *rest):
-    out_refs, skip_ref, (pad_a, pad_b) = rest[:-3], rest[-3], rest[-2:]
-    for place, out_ref in enumerate(out_refs):
-        at = lanes_at(order_ref, place)
-        first = short_conv(pad_a.at[place % 2], gate_ref[:, at].astype(F32), rim_of(rim_ref, 1, at), taps_ref[1, :, at])
-        second = short_conv(pad_b.at[place % 2], value_ref[:, at].astype(F32), rim_of(rim_ref, 2, at), taps_ref[2, :, at])
-        mixed = first * second
-        out_ref[...] = mixed.astype(BF16)
-        skip_ref[place] = gain_ref[:, at] * mixed
-
-
-def mix_slices(order, in_gate, values, rims, taps, skip_gain):
-    rows, width = in_gate.shape
-    count = width // LANES
-    return pl.pallas_call(
-        mix_slices_kernel,
-        in_specs=[pl.BlockSpec(memory_space=pltpu.SMEM)] + whole_specs(5),
-        out_specs=whole_specs(count + 1),
-        out_shape=[jax.ShapeDtypeStruct((rows, LANES), BF16)] * count + [jax.ShapeDtypeStruct((count, rows, LANES), F32)],
         scratch_shapes=[pltpu.VMEM((2, rows + 8, LANES), F32)] * 2,
         compiler_params=pltpu.CompilerParams(vmem_limit_bytes=12 << 20),
-        cost_estimate=pl.CostEstimate(flops=14 * rows * width, bytes_accessed=10 * rows * width, transcendentals=0),
-    )(order, in_gate, values, rims, taps, skip_gain.reshape(1, width))
-
-
-def late_kernel(order_ref, late_ref, rim_ref, taps_ref, out_ref, pad):
-    for place in range(out_ref.shape[0]):
+        cost_estimate=cost(14 * rows * width, 1),
+    )(order, in_gate, values, taps, after)
+
+
+def side_slices_kernel(order_ref, late_ref, gate_ref, value_ref, *refs):
+    *before_refs, taps_ref, gain_ref, late_out, skip_out = refs[:-3]
+    pads = refs[-3:]
+    rows, keep = late_ref.shape[0], taps_ref.shape[1] - 1
+    own = order_ref[0]
+    for place in range(late_out.shape[0]):
         at = lanes_at(order_ref, place)
-        out_ref[place] = short_conv(pad.at[place % 2], late_ref[:, at].astype(F32), rim_of(rim_ref, 0, at), taps_ref[0, :, at])
-
-
-def late_slices(order, out_gate, rims, taps):
+        start = pl.multiple_of(rows + (1 + order_ref[place]) * TILE, TILE)
+        rim = jnp.zeros((TILE, LANES), F32)
+        for offset, ref in zip(NEXT_OFFSETS, before_refs, strict=True):
+            given = ref[pl.ds(start, TILE), :].astype(F32)
+            rim = jnp.where((own & offset) == (offset + 1) // 2, given, rim)
+        late, first, second = (
+            short_conv(
+                pad.at[place % 2],
+                ref[:, at].astype(F32),
+                rim[which * keep : (which + 1) * keep],
+                taps_ref[which, :, at],
+            )
+            for which, (pad, ref) in enumerate(zip(pads, (late_ref, gate_ref, value_ref), strict=True))
+        )
+        late_out[place] = late
+        skip_out[place] = gain_ref[:, at] * (first * second)
+
+
+def side_slices(order, out_gate, in_gate, values, filter_blocks, taps, skip_gain):
     rows, width = out_gate.shape
     count = width // LANES
-    return pl.pallas_call(
-        late_kernel,
-        in_specs=[pl.BlockSpec(memory_space=pltpu.SMEM)] + whole_specs(3),
-        out_specs=pl.BlockSpec(memory_space=pltpu.VMEM),
-        out_shape=jax.ShapeDtypeStruct((count, rows, LANES), F32),
-        scratch_shapes=[pltpu.VMEM((2, rows + 8, LANES), F32)],
-        compiler_params=pltpu.CompilerParams(vmem_limit_bytes=8 << 20),
-        cost_estimate=pl.CostEstimate(flops=6 * rows * width, bytes_accessed=6 * rows * width, transcendentals=0),
-    )(order, out_gate, rims, taps)
-
-
-def spectra_into(order_ref, places, table, signal_refs, out_ref):
-    columns = jnp.concatenate([ref[...] for ref in signal_refs], axis=1)
+    before = [filter_blocks[OFFSETS.index(offset)] for offset in NEXT_OFFSETS]
+    return pl.pallas_call(
+        side_slices_kernel,
+        in_specs=[pl.BlockSpec(memory_space=pltpu.SMEM)] + whole_specs(5 + len(before)),
+        out_specs=whole_specs(2),
+        out_shape=[jax.ShapeDtypeStruct((count, rows, LANES), F32)] * 2,
+        scratch_shapes=[pltpu.VMEM((2, rows + 8, LANES), F32)] * 3,
+        compiler_params=pltpu.CompilerParams(vmem_limit_bytes=16 << 20),
+        cost_estimate=cost(20 * rows * width, 1),
+    )(order, out_gate, in_gate, values, *before, taps, skip_gain.reshape(1, width))
+
+
+def spectra_into(order_ref, places, table, blocks, out_ref):
+    columns = jnp.concatenate(blocks, axis=1)
     spectra = jnp.dot(table, jnp.concatenate([columns, columns], axis=0), preferred_element_type=F32)
     for at, place in enumerate(places):
         out_ref[order_ref[place]] = spectra[:, at * LANES : (at + 1) * LANES]
 
 
-def spectra_kernel(places, order_ref, table_ref, weight_ref, *refs):
-    del weight_ref
-    signal_refs, out_ref = refs[:-1], refs[-1]
-    for base in range(0, len(signal_refs), GROUP):
-        end = base + GROUP
-        spectra_into(order_ref, places[base:end], table_ref[...], signal_refs[base:end], out_ref)
-
-
-def spectra_of(order, table, weight, blocks, places, count):
+def with_first(order_ref, places, signal_refs, first_ref):
+    blocks = []
+    for place, ref in zip(places, signal_refs, strict=True):
+        top = ref[:TILE].astype(F32)
+        row = lax.broadcasted_iota(jnp.int32, top.shape, 0)
+        top = jnp.where(row < KEEP, first_ref[order_ref[place]], top).astype(BF16)
+        blocks.append(jnp.concatenate([top, ref[TILE:]], axis=0))
+    return blocks
+
+
+def filter_kernel(places, order_ref, table_ref, taps_ref, after_ref, *refs):
+    del after_ref
+    *block_refs, out_ref, first_ref, ends_ref = refs
+    rows = table_ref.shape[0] // 2
+    for base in range(0, len(block_refs), GROUP):
+        blocks = [ref[:rows] for ref in block_refs[base : base + GROUP]]
+        spectra_into(order_ref, places[base : base + GROUP], table_ref[...], blocks, out_ref)
+    for place, ref in zip(places, block_refs, strict=True):
+        ends_ref[order_ref[place]] = ref[rows : rows + TILE].astype(F32)
+    count = taps_ref.shape[1]
+    at = lanes_at(order_ref, 0)
+    for block in range(len(block_refs)):
+        mixed = None
+        for which in range(2):
+            top = ends_ref[block, (3 + which) * KEEP : (4 + which) * KEEP]
+            end = jnp.zeros_like(top)
+            if block:
+                end = ends_ref[block - 1, (1 + which) * KEEP : (2 + which) * KEEP]
+            joined = jnp.concatenate([end, top], axis=0)
+            taps = taps_ref[1 + which, :, at]
+            total = taps[0:1] * joined[KEEP:]
+            for offset in range(1, count):
+                total = total + taps[offset : offset + 1] * joined[KEEP - offset : 2 * KEEP - offset]
+            mixed = total if mixed is None else mixed * total
+        first_ref[block] = jnp.concatenate([mixed, jnp.zeros((TILE - KEEP, LANES), F32)], axis=0)
+
+
+def filter_spectra_of(order, table, taps, blocks, places, after):
+    rows, lanes = table.shape[0] // 2, blocks[0].shape[1]
+    count = len(blocks)
+    return pl.pallas_call(
+        functools.partial(filter_kernel, places),
+        in_specs=[pl.BlockSpec(memory_space=pltpu.SMEM)] + whole_specs(2) + [pl.BlockSpec(memory_space=pl.ANY)] + whole_specs(count),
+        out_specs=whole_specs(2),
+        out_shape=[
+            jax.ShapeDtypeStruct((count, 2 * rows, lanes), F32),
+            jax.ShapeDtypeStruct((count, TILE, lanes), F32),
+        ],
+        scratch_shapes=[pltpu.VMEM((count, TILE, lanes), F32)],
+        compiler_params=pltpu.CompilerParams(vmem_limit_bytes=12 << 20),
+        cost_estimate=cost(8 * count * rows * rows * lanes, 1),
+    )(order, table, taps, after, *[blocks[place] for place in places])
+
+
+def early_kernel(places, order_ref, table_ref, first_ref, *refs):
+    blocks = with_first(order_ref, places, refs[:-1], first_ref)
+    spectra_into(order_ref, places, table_ref[...], blocks, refs[-1])
+
+
+def early_spectra_of(order, table, first, blocks, places):
     rows, lanes = blocks[0].shape
     given = len(places)
     return pl.pallas_call(
-        functools.partial(spectra_kernel, places),
-        in_specs=[pl.BlockSpec(memory_space=pltpu.SMEM)] + whole_specs(1) + [pl.BlockSpec(memory_space=pl.ANY)] + whole_specs(given),
+        functools.partial(early_kernel, places),
+        in_specs=[pl.BlockSpec(memory_space=pltpu.SMEM)] + whole_specs(2 + given),
         out_specs=pl.BlockSpec(memory_space=pltpu.VMEM),
-        out_shape=jax.ShapeDtypeStruct((count, 2 * rows, lanes), F32),
+        out_shape=jax.ShapeDtypeStruct((len(blocks), 2 * rows, lanes), F32),
         compiler_params=pltpu.CompilerParams(vmem_limit_bytes=12 << 20),
-        cost_estimate=pl.CostEstimate(flops=8 * given * rows * rows * lanes, bytes_accessed=10 * given * rows * lanes, transcendentals=0),
-    )(order, table, weight, *[blocks[place] for place in places])
+        cost_estimate=cost(8 * given * rows * rows * lanes, 1),
+    )(order, table, first, *[blocks[place] for place in places])
 
 
 def multiply_spectra(filter_ref, spectra_ref, high_ref, low_ref):
@@ -466,23 +537,24 @@
         out_ref[...] = result[:, at * LANES : (at + 1) * LANES]
 
 
-def conv_slices_kernel(places, order_ref, table_ref, inverse_ref, filter_ref, early_ref, *refs):
+def conv_slices_kernel(places, order_ref, table_ref, inverse_ref, filter_ref, early_ref, first_ref, *refs):
     del early_ref
     count = filter_ref.shape[0]
     signal_refs = refs[: len(places)]
     spectra_ref, *out_refs, high_ref, low_ref = refs[-count - 3 :]
-    spectra_into(order_ref, places, table_ref[...], signal_refs, spectra_ref)
+    blocks = with_first(order_ref, places, signal_refs, first_ref)
+    spectra_into(order_ref, places, table_ref[...], blocks, spectra_ref)
     multiply_spectra(filter_ref, spectra_ref, high_ref, low_ref)
     for base in range(0, count, GROUP):
         inverse_into(order_ref, base, inverse_ref[...], high_ref, low_ref, out_refs[base : base + GROUP])
 
 
-def conv_slices(order, table, inverse, filter_spectra, early_spectra, blocks, places, after):
+def conv_slices(order, table, inverse, filter_spectra, early_spectra, first, blocks, places, after):
     rows, lanes = blocks[0].shape
     count = filter_spectra.shape[0]
     _, *outs = pl.pallas_call(
         functools.partial(conv_slices_kernel, places),
-        in_specs=[pl.BlockSpec(memory_space=pltpu.SMEM)] + whole_specs(4 + len(places)) + [pl.BlockSpec(memory_space=pl.ANY)] * len(after),
+        in_specs=[pl.BlockSpec(memory_space=pltpu.SMEM)] + whole_specs(5 + len(places)) + [pl.BlockSpec(memory_space=pl.ANY)] * len(after),
         out_specs=whole_specs(1 + count),
         out_shape=[jax.ShapeDtypeStruct((count, 2 * rows, lanes), F32)]
         + [jax.ShapeDtypeStruct((rows, lanes), BF16)] * count,
@@ -490,7 +562,7 @@
         scratch_shapes=[pltpu.VMEM((count, 2 * rows, lanes), BF16)] * 2,
         compiler_params=pltpu.CompilerParams(vmem_limit_bytes=20 << 20),
         cost_estimate=cost(14 * count * rows * rows * lanes, 1),
-    )(order, table, inverse, filter_spectra, early_spectra, *[blocks[place] for place in places], *after)
+    )(order, table, inverse, filter_spectra, early_spectra, first, *[blocks[place] for place in places], *after)
     return outs
 
 
@@ -545,7 +617,7 @@
 
 def add_chunk(chunk, rows_ref, piece_refs, total):
     pieces = jnp.concatenate([ref[...] for ref in piece_refs], axis=1)
-    rows = [rows_ref[chunk * PER + at, offset] for offset in PIECE_ORDER for at in range(PER)]
+    rows = [rows_ref[place, offset] for offset in PIECE_ORDER for place in range(*CHUNKS[chunk])]
     product = jnp.dot(pieces, jnp.concatenate(rows, axis=0), preferred_element_type=F32)
     return product if total is None else total + product
 
@@ -575,8 +647,8 @@
     out_ref[...] = total.astype(out_ref.dtype)
 
 
-def project_slices(weight_rows, chunks, pieces, total, out_type):
-    rows, depth = pieces[0].shape
+def project_slices(weight_rows, chunks, pieces, total, out_type, scale):
+    rows = pieces[0].shape[0]
     width = weight_rows.shape[3]
     more = () if total is None else (total,)
     return pl.pallas_call(
@@ -585,7 +657,7 @@
         out_specs=pl.BlockSpec(memory_space=pltpu.VMEM),
         out_shape=jax.ShapeDtypeStruct((rows, width), out_type),
         compiler_params=pltpu.CompilerParams(vmem_limit_bytes=14 << 20),
-        cost_estimate=cost(0),
+        cost_estimate=cost(2 * rows * sum(piece.shape[1] for piece in pieces) * width, scale),
     )(weight_rows, *pieces, *more)
 
 
@@ -601,34 +673,34 @@
 def on_device_slices(out_gate, in_gate, values, short_filter, long_filter, skip_gain, out_weight):
     rows, width = out_gate.shape
     devices = lax.axis_size("seq")
-    taps = short_filter.shape[1]
     table, inverse = transform_tables(rows)
     order = jnp.bitwise_xor(lax.axis_index("seq"), jnp.array(OFFSETS, jnp.int32))
     channel = lax.axis_index("ch").reshape(1)
 
-    rim = rim_rows(order, (out_gate, in_gate, values), taps - 1)
-    filter_blocks = swap_blocks(cut_filter(order, long_filter), FILTER_ORDER)
-    rims = lax.ppermute(rim, "seq", [(i, i + 1) for i in range(devices - 1)])
-    *mixed_slices, skip = mix_slices(order, in_gate, values, rims, short_filter, skip_gain)
-    mixed_blocks = swap_blocks(mixed_slices, SIGNAL_ORDER)
-    late = late_slices(order, out_gate, rims, short_filter)
+    filter_blocks = swap_blocks(cut_filter(order, long_filter, out_gate, in_gate, values), FILTER_ORDER)
+    sent = (0, *(OFFSETS.index(offset) for offset in FILTER_ORDER))
+    mixed_blocks = swap_blocks(
+        mix_slices(order, in_gate, values, short_filter, filter_blocks[OFFSETS.index(MIX_AFTER)]), SIGNAL_ORDER
+    )
+    late, skip = side_slices(order, out_gate, in_gate, values, filter_blocks, short_filter, skip_gain)
     weight_rows = weight_rows_of(order, channel, out_weight)
-    sent = (0, *(OFFSETS.index(offset) for offset in FILTER_ORDER))
-    filter_spectra = spectra_of(order, table, weight_rows, filter_blocks, sent, devices)
+    filter_spectra, first = filter_spectra_of(order, table, short_filter, filter_blocks, sent, weight_rows)
     early, last = (tuple(OFFSETS.index(offset) for offset in group) for group in (EARLY, LATE))
-    early_spectra = spectra_of(order, table, weight_rows, mixed_blocks, early, devices)
-    long_blocks = conv_slices(order, table, inverse, filter_spectra, early_spectra, mixed_blocks, last, (late, weight_rows))
+    early_spectra = early_spectra_of(order, table, first, mixed_blocks, early)
+    long_blocks = conv_slices(order, table, inverse, filter_spectra, early_spectra, first, mixed_blocks, last, (late, weight_rows))
     arrived = swap_blocks(long_blocks, OFFSETS[1:])
 
     pieces = []
-    for chunk in range(devices // PER):
-        start = chunk * PER
-        mixed = gate_chunk(late, skip, arrived[start : start + PER], start)
+    for start, stop in CHUNKS:
+        mixed = gate_chunk(late, skip, arrived[start:stop], start)
         across = lax.ppermute(mixed, "ch", [(i, i ^ 2) for i in range(4)])
         joined = join([mixed, across])
-        pieces += [joined, lax.ppermute(joined, "ch", [(i, i ^ 1) for i in range(4)])]
-    total = project_slices(weight_rows, (0, 1, 2), pieces[:-2], None, F32)
-    return project_slices(weight_rows, (3,), pieces[-2:], total, BF16)
+        pieces.append((joined, lax.ppermute(joined, "ch", [(i, i ^ 1) for i in range(4)])))
+    total = None
+    for chunks, scale in zip(PROJECTS, PROJECT_COSTS, strict=True):
+        kind = BF16 if chunks == PROJECTS[-1] else F32
+        total = project_slices(weight_rows, chunks, [piece for chunk in chunks for piece in pieces[chunk]], total, kind, scale)
+    return total
 
 
 def on_device_spans(out_gate, in_gate, values, short_filter, long_filter, skip_gain, out_weight):
@@ -664,7 +736,8 @@
 
     def on_device(*arrays):
         width = arrays[0].shape[1]
-        sliced = devices == len(OFFSETS) and width == devices * LANES and mesh.shape["ch"] == len(PIECE_ORDER)
+        taps = arrays[3].shape[1]
+        sliced = taps == KEEP + 1 and devices == len(OFFSETS) and width == devices * LANES and mesh.shape["ch"] == len(PIECE_ORDER)
         return (on_device_slices if sliced else on_device_spans)(*arrays)
 
     return jax.shard_map(

time: 87.9 us -> 84.9 us (0.966)
  waiting for transfers between devices: 8.54 us -> 4.7 us
  local copies, waits for them, and re-layouts: 6.06 us -> 3.42 us
  Pallas kernels: 21.5 us -> 23 us
  starting transfers between devices: 50.7 us -> 52.2 us
    ppermute x21, starting transfers between devices: 32 us -> 36.4 us  [swap_blocks(): lax.ppermute(blocks[place], 'seq', [(i, i ^ offset) for i in range(count)])]
    ppermute x1 -> x0, starting transfers between devices: 3.1 us -> none  [on_device_slices(): rims = lax.ppermute(rim, 'seq', [(i, i + 1) for i in range(devices - 1)])]
    ppermute x21, waiting for transfers between devices: 7.46 us -> 4.68 us  [swap_blocks(): lax.ppermute(blocks[place], 'seq', [(i, i ^ offset) for i in range(count)])]
    unnamed x26 -> x20, local copies, waits for them, and re-layouts: 6.06 us -> 3.42 us
    pallas_call x5 -> x4, Pallas kernels: 6.8 us -> 8.63 us  [the longest x1 2.61 us: cut_filter(): pl.pallas_call(cut_kernel, grid=(1,), in_specs=[pl.BlockSpec(memory_space...]
    ppermute x1 -> x0, waiting for transfers between devices: 1.06 us -> none  [on_device_slices(): rims = lax.ppermute(rim, 'seq', [(i, i + 1) for i in range(devices - 1)])]
  transfers between devices with their start and end apart: 30 -> 29, of which waited for: 5 -> 3; matrix products, arithmetic and copies ran while one was open for 0% -> 0% of each run, Pallas kernels for 15% -> 15%
where the time goes in v3:
time: 84.9 us; the launch traced here: 84.8 us
  starting transfers between devices  52.2 us (61%)
  Pallas kernels  23 us (27%)
  waiting for transfers between devices  4.7 us (6%)
  local copies, waits for them, and re-layouts  3.42 us (4%)
  other arithmetic  1.24 us (1%)
    ppermute x21, starting transfers between devices, swap_blocks(): lax.ppermute(blocks[place], 'seq', [(i, i ^ offset) for i in range(count)])  36.4 us
    ppermute x4, starting transfers between devices, on_device_slices(): lax.ppermute(joined, 'ch', [(i, i ^ 1) for i in range(4)])  11.5 us
    pallas_call x1, Pallas kernels, conv_slices(): pl.pallas_call(functools.partial(conv_slices_kernel, places), in_specs=[p...  5.92 us
    ppermute x21, waiting for transfers between devices, swap_blocks(): lax.ppermute(blocks[place], 'seq', [(i, i ^ offset) for i in range(count)])  4.68 us
    pallas_call x2, Pallas kernels, project_slices(): pl.pallas_call(functools.partial(project_kernel_slices, chunks), in_specs...  4.53 us
    ppermute x4, starting transfers between devices, on_device_slices(): across = lax.ppermute(mixed, 'ch', [(i, i ^ 2) for i in range(4)])  4.22 us
    unnamed x20, local copies, waits for them, and re-layouts  3.42 us
    pallas_call x1, Pallas kernels, cut_filter(): pl.pallas_call(cut_kernel, grid=(1,), in_specs=[pl.BlockSpec(memory_space...  2.61 us
  transfers between devices with their start and end apart: 29, of which 3 were waited for; matrix products, arithmetic and copies ran while one was open for 0% of the time, Pallas kernels for 15%

profile of v3, /device:TPU:1, one launch (start us, length us, event | category | flops | bytes accessed | tf_op | source)
XLA Modules:
  0.0 84.8 jit_solution(5495513445792730744)
XLA Ops:
  0.0 1.2 %broadcast_xor_fusion.order_ref = s32[8]{0:T(128)} fusion(s32[8]{0:T(128)} %constant.15.clone, s32[]{:T(128)S(6)} %axis_index.23), kind=kLoop, calls=%fused_computation | loop fusion | flops 8 | bytes 68 | tf_op jit(solution)/shard_map/xor | solution.py:677
  1.2 2.6 %shard_map.101 = (bf16[400,128]{1,0:T(8,128)(2,1)}, bf16[400,128]{1,0:T(8,128)(2,1)}, bf16[528,128]{1,0:T(8,128)(2,1)}, bf16[400,128]{1,0:T(8,128)(2,1)}, bf16[5...) custom-call(s32[8]{0:T(128)} %broadcast_xor_fusion.order_ref, ...), custom_call_target="tpu_custom_call" | custom-call | tf_op jit(solution)/shard_map/pallas_call | solution.py:338
  3.9 2.0 %collective-permute-start = (bf16[528,128]{1,0:T(8,128)(2,1)}, bf16[528,128]{1,0:T(8,128)(2,1)S(1)}, u32[]{:S(2)}, u32[]{:S(2)}) collective-permute-start(bf16[528,128]{1,0:T(8,128)(2,1)} %get-tuple-element.33), channel_id=1, source_target_pairs={{0,4},{4,0},{8,12},{12,8},{16,20},{20,16},{24,28},{28,24},{1,5},{5... | collective-permute-start | bytes 405512 | tf_op jit(solution)/shard_map/ppermute | solution.py:669
  5.9 2.3 %collective-permute-start.3 = (bf16[400,128]{1,0:T(8,128)(2,1)}, bf16[400,128]{1,0:T(8,128)(2,1)S(1)}, u32[]{:S(2)}, u32[]{:S(2)}) collective-permute-start(bf16[400,128]{1,0:T(8,128)(2,1)} %get-tuple-element.39), channel_id=1, source_target_pairs={{0,16},{4,20},{8,24},{12,28},{16,0},{20,4},{24,8},{28,12},{1,17},{... | collective-permute-start | bytes 307208 | tf_op jit(solution)/shard_map/ppermute | solution.py:669
  8.2 0.0 collective-permute-start.4
  8.2 1.3 %collective-permute-start.5 = (bf16[400,128]{1,0:T(8,128)(2,1)}, bf16[400,128]{1,0:T(8,128)(2,1)S(1)}, u32[]{:S(2)}, u32[]{:S(2)}) collective-permute-start(bf16[400,128]{1,0:T(8,128)(2,1)} %get-tuple-element.41), channel_id=1, source_target_pairs={{0,8},{4,12},{8,0},{12,4},{16,24},{20,28},{24,16},{28,20},{1,9},{5... | collective-permute-start | bytes 307208 | tf_op jit(solution)/shard_map/ppermute | solution.py:669
  9.5 1.1 %collective-permute-start.1 = (bf16[528,128]{1,0:T(8,128)(2,1)}, bf16[528,128]{1,0:T(8,128)(2,1)S(1)}, u32[]{:S(2)}, u32[]{:S(2)}) collective-permute-start(bf16[528,128]{1,0:T(8,128)(2,1)} %get-tuple-element.34), channel_id=1, source_target_pairs={{0,12},{4,8},{8,4},{12,0},{16,28},{20,24},{24,20},{28,16},{1,13},{... | collective-permute-start | bytes 405512 | tf_op jit(solution)/shard_map/ppermute | solution.py:669
  10.6 0.0 collective-permute-done.3.refs_1_
  10.6 8.7 %collective-permute-start.2 = (bf16[528,128]{1,0:T(8,128)(2,1)}, bf16[528,128]{1,0:T(8,128)(2,1)S(1)}, u32[]{:S(2)}, u32[]{:S(2)}) collective-permute-start(bf16[528,128]{1,0:T(8,128)(2,1)} %get-tuple-element.35), channel_id=1, source_target_pairs={{0,28},{4,24},{8,20},{12,16},{16,12},{20,8},{24,4},{28,0},{1,29},{... | collective-permute-start | bytes 405512 | tf_op jit(solution)/shard_map/ppermute | solution.py:669
  19.4 0.0 collective-permute-done.refs_0_.refs_2_.after_ref
  19.4 0.0 collective-permute-start.6
  19.4 1.9 %shard_map.104 = (bf16[384,128]{1,0:T(8,128)(2,1)S(1)}, bf16[384,128]{1,0:T(8,128)(2,1)S(1)}, bf16[384,128]{1,0:T(8,128)(2,1)S(1)}, bf16[384,128]{1,0:T(8,128)(2...) custom-call(s32[8]{0:T(128)S(1)} %copy-done.8, ...), custom_call_target="tpu_custom_call" | custom-call | flops 5505024 | bytes 43008 | tf_op jit(solution)/shard_map/pallas_call | solution.py:365
  21.3 0.0 collective-permute-done.4.refs_3_
  21.3 0.1 collective-permute-start.7
  21.4 0.0 collective-permute-done.5.refs_4_
  21.4 1.3 %collective-permute-start.8 = (bf16[384,128]{1,0:T(8,128)(2,1)S(1)}, bf16[384,128]{1,0:T(8,128)(2,1)S(1)}, u32[]{:S(2)}, u32[]{:S(2)}) collective-permute-start(bf16[384,128]{1,0:T(8,128)(2,1)S(1)} %get-tuple-element.47), channel_id=1, source_target_pairs={{0,4},{4,0},{8,12},{12,8},{16,20},{20,16},{24,28},{28,24},{1,5},{5... | collective-permute-start | bytes 294920 | tf_op jit(solution)/shard_map/ppermute | solution.py:669
  22.7 3.4 %copy-done.3 = bf16[4096,1024]{1,0:T(8,128)(2,1)S(1)} copy-done((bf16[4096,1024]{1,0:T(8,128)(2,1)S(1)}, bf16[4096,1024]{1,0:T(8,128)(2,1)}, u32[]{:S(2)}) %copy-start.3) | copy-done | bytes 8388632
  26.1 1.7 %shard_map.100.after_ref.refs_5_.rows_ref = bf16[8,4,128,1024]{3,2,1,0:T(8,128)(2,1)S(1)} custom-call(s32[8]{0:T(128)S(1)} %copy-done.8, s32[1]{0:T(128)} %bitcast.channel_ref, bf16[4096,1024]{1,0:T(8,128)(2,1)S(1)} %copy-done.3), custom_call_target="tpu_custom_call" | custom-call | bytes 16777216 | tf_op jit(solution)/shard_map/pallas_call | solution.py:607
  27.8 0.0 collective-permute-done.6.refs_5_
  27.8 5.6 %collective-permute-start.9 = (bf16[384,128]{1,0:T(8,128)(2,1)S(1)}, bf16[384,128]{1,0:T(8,128)(2,1)S(1)}, u32[]{:S(2)}, u32[]{:S(2)}) collective-permute-start(bf16[384,128]{1,0:T(8,128)(2,1)S(1)} %get-tuple-element.48), channel_id=1, source_target_pairs={{0,20},{4,16},{8,28},{12,24},{16,4},{20,0},{24,12},{28,8},{1,21},{... | collective-permute-start | bytes 294920 | tf_op jit(solution)/shard_map/ppermute | solution.py:669
  33.3 0.0 collective-permute-done.2.refs_2_.refs_7_
  33.4 0.9 %collective-permute-start.11 = (bf16[384,128]{1,0:T(8,128)(2,1)S(1)}, bf16[384,128]{1,0:T(8,128)(2,1)S(1)}, u32[]{:S(2)}, u32[]{:S(2)}) collective-permute-start(bf16[384,128]{1,0:T(8,128)(2,1)S(1)} %get-tuple-element.50), channel_id=1, source_target_pairs={{0,24},{4,28},{8,16},{12,20},{16,8},{20,12},{24,0},{28,4},{1,25},{... | collective-permute-start | bytes 294920 | tf_op jit(solution)/shard_map/ppermute | solution.py:669
  34.2 1.2 %collective-permute-start.12 = (bf16[384,128]{1,0:T(8,128)(2,1)S(1)}, bf16[384,128]{1,0:T(8,128)(2,1)S(1)}, u32[]{:S(2)}, u32[]{:S(2)}) collective-permute-start(bf16[384,128]{1,0:T(8,128)(2,1)S(1)} %get-tuple-element.51), channel_id=1, source_target_pairs={{0,12},{4,8},{8,4},{12,0},{16,28},{20,24},{24,20},{28,16},{1,13},{... | collective-permute-start | bytes 294920 | tf_op jit(solution)/shard_map/ppermute | solution.py:669
  35.5 0.0 collective-permute-done.8.refs_2_
  35.5 2.6 %collective-permute-start.13 = (bf16[384,128]{1,0:T(8,128)(2,1)S(1)}, bf16[384,128]{1,0:T(8,128)(2,1)S(1)}, u32[]{:S(2)}, u32[]{:S(2)}) collective-permute-start(bf16[384,128]{1,0:T(8,128)(2,1)S(1)} %get-tuple-element.52), channel_id=1, source_target_pairs={{0,28},{4,24},{8,20},{12,16},{16,12},{20,8},{24,4},{28,0},{1,29},{... | collective-permute-start | bytes 294920 | tf_op jit(solution)/shard_map/ppermute | solution.py:669
  38.1 2.1 %shard_map.103 = (f32[8,768,128]{2,1,0:T(8,128)S(1)}, f32[8,16,128]{2,1,0:T(8,128)S(1)}) custom-call(s32[8]{0:T(128)S(1)} %copy-done.8, bf16[768,768]{1,0:T(8,128)(2,1)S(1)} %copy-done.2, f32[3,3,1024]{2,1,0:T(4,128)S(1)} %copy-done.6, bf16[8,4,128,1024]{3,2,1,0:T(8,128)(2,1)S(1)} %shard_map.100.after_ref.refs_5_.rows_ref, bf16[400,128]{1,0:T(8,128)(2,1)S(1)} %copy-done.7, ...), custom_call_target="tpu_custom_call" | custom-call | flops 1207959552 | bytes 9437184 | tf_op jit(solution)/shard_map/pallas_call | solution.py:463
  40.2 2.5 %shard_map.102 = (f32[8,384,128]{2,1,0:T(8,128)S(1)}, f32[8,384,128]{2,1,0:T(8,128)S(1)}) custom-call(s32[8]{0:T(128)S(1)} %copy-done.8, bf16[384,1024]{1,0:T(8,128)(2,1)S(1)} %copy-done.4, bf16[384,1024]{1,0:T(8,128)(2,1)S(1)} %copy-done, bf16[384,1024]{1,0:T(8,128)(2,1)S(1)} %copy-done.1, ...), custom_call_target="tpu_custom_call" | custom-call | flops 7864320 | bytes 61440 | tf_op jit(solution)/shard_map/pallas_call | solution.py:405
  42.8 0.0 copy-start.5
  42.8 1.4 %shard_map.105.early_ref = f32[8,768,128]{2,1,0:T(8,128)S(1)} custom-call(s32[8]{0:T(128)S(1)} %copy-done.8, bf16[768,768]{1,0:T(8,128)(2,1)S(1)} %copy-done.2, f32[8,16,128]{2,1,0:T(8,128)S(1)} %get-tuple-element.44.first_ref, bf16[384,128]{1,0:T(8,128)(2,1)S(1)} %get-tuple-element.45.refs_0_, bf16[384,128]{1,0:T(8,128)(2,1)S(1)} %collective-permute-done.7.refs_1_, ...), custom_call_target="tpu_custom_call" | custom-call | flops 603979776 | bytes 4718592 | tf_op jit(solution)/shard_map/pallas_call | solution.py:485
  44.2 0.6 collective-permute-done.12.refs_2_
  44.8 0.0 collective-permute-done.13.refs_3_
  44.8 5.9 %shard_map.106 = (f32[8,768,128]{2,1,0:T(8,128)S(1)}, bf16[384,128]{1,0:T(8,128)(2,1)S(1)}, bf16[384,128]{1,0:T(8,128)(2,1)S(1)}, bf16[384,128]{1,0:T(8,128)(2,1...) custom-call(s32[8]{0:T(128)S(1)} %copy-done.8, ...), custom_call_target="tpu_custom_call", output_to_operand_aliasing={{0}: (4, {})} | custom-call | flops 2113929216 | bytes 16515072 | tf_op jit(solution)/shard_map/pallas_call | solution.py:555
  50.7 1.9 %collective-permute-start.18 = (bf16[384,128]{1,0:T(8,128)(2,1)S(1)}, bf16[384,128]{1,0:T(8,128)(2,1)S(1)}, u32[]{:S(2)}, u32[]{:S(2)}) collective-permute-start(bf16[384,128]{1,0:T(8,128)(2,1)S(1)} %get-tuple-element.56), channel_id=1, source_target_pairs={{0,16},{4,20},{8,24},{12,28},{16,0},{20,4},{24,8},{28,12},{1,17},{... | collective-permute-start | bytes 294920 | tf_op jit(solution)/shard_map/ppermute | solution.py:669
  52.7 0.5 collective-permute-start.21
  53.2 1.1 %collective-permute-start.22 = (bf16[384,128]{1,0:T(8,128)(2,1)S(1)}, bf16[384,128]{1,0:T(8,128)(2,1)S(1)}, u32[]{:S(2)}, u32[]{:S(2)}) collective-permute-start(bf16[384,128]{1,0:T(8,128)(2,1)S(1)} %get-tuple-element.58), channel_id=1, source_target_pairs={{0,8},{4,12},{8,0},{12,4},{16,24},{20,28},{24,16},{28,20},{1,9},{5... | collective-permute-start | bytes 294920 | tf_op jit(solution)/shard_map/ppermute | solution.py:669
  54.3 1.2 %collective-permute-start.25 = (bf16[384,128]{1,0:T(8,128)(2,1)S(1)}, bf16[384,128]{1,0:T(8,128)(2,1)S(1)}, u32[]{:S(2)}, u32[]{:S(2)}) collective-permute-start(bf16[384,128]{1,0:T(8,128)(2,1)S(1)} %get-tuple-element.59), channel_id=1, source_target_pairs={{0,12},{4,8},{8,4},{12,0},{16,28},{20,24},{24,20},{28,16},{1,13},{... | collective-permute-start | bytes 294920 | tf_op jit(solution)/shard_map/ppermute | solution.py:669
  55.5 1.2 %collective-permute-start.26 = (bf16[384,128]{1,0:T(8,128)(2,1)S(1)}, bf16[384,128]{1,0:T(8,128)(2,1)S(1)}, u32[]{:S(2)}, u32[]{:S(2)}) collective-permute-start(bf16[384,128]{1,0:T(8,128)(2,1)S(1)} %get-tuple-element.60), channel_id=1, source_target_pairs={{0,20},{4,16},{8,28},{12,24},{16,4},{20,0},{24,12},{28,8},{1,21},{... | collective-permute-start | bytes 294920 | tf_op jit(solution)/shard_map/ppermute | solution.py:669
  56.7 2.4 %collective-permute-start.14 = (bf16[384,128]{1,0:T(8,128)(2,1)S(1)}, bf16[384,128]{1,0:T(8,128)(2,1)S(1)}, u32[]{:S(2)}, u32[]{:S(2)}) collective-permute-start(bf16[384,128]{1,0:T(8,128)(2,1)S(1)} %get-tuple-element.53), channel_id=1, source_target_pairs={{0,24},{4,28},{8,16},{12,20},{16,8},{20,12},{24,0},{28,4},{1,25},{... | collective-permute-start | bytes 294920 | tf_op jit(solution)/shard_map/ppermute | solution.py:669
  59.1 0.0 collective-permute-done.21.refs_0_
  59.1 0.9 %collective-permute-start.15 = (bf16[384,128]{1,0:T(8,128)(2,1)S(1)}, bf16[384,128]{1,0:T(8,128)(2,1)S(1)}, u32[]{:S(2)}, u32[]{:S(2)}) collective-permute-start(bf16[384,128]{1,0:T(8,128)(2,1)S(1)} %get-tuple-element.54), channel_id=1, source_target_pairs={{0,28},{4,24},{8,20},{12,16},{16,12},{20,8},{24,4},{28,0},{1,29},{... | collective-permute-start | bytes 294920 | tf_op jit(solution)/shard_map/ppermute | solution.py:669
  60.0 0.1 shard_map.109.refs_0_
  60.1 0.0 collective-permute-done.22.refs_1_
  60.1 1.3 %collective-permute-start.19 = (bf16[384,256]{1,0:T(8,128)(2,1)S(1)}, bf16[384,256]{1,0:T(8,128)(2,1)S(1)}, u32[]{:S(2)}, u32[]{:S(2)}) collective-permute-start(bf16[384,256]{1,0:T(8,128)(2,1)S(1)} %shard_map.109.refs_0_), channel_id=1, source_target_pairs={{0,2},{1,3},{2,0},{3,1},{4,6},{5,7},{6,4},{7,5},{8,10},{9,11},{10,... | collective-permute-start | bytes 589832 | tf_op jit(solution)/shard_map/ppermute | solution.py:696
  61.4 0.1 shard_map.111.refs_0_
  61.5 0.3 collective-permute-start.23
  61.8 0.1 shard_map.113.refs_0_
  61.8 1.3 %collective-permute-start.27 = (bf16[384,256]{1,0:T(8,128)(2,1)S(1)}, bf16[384,256]{1,0:T(8,128)(2,1)S(1)}, u32[]{:S(2)}, u32[]{:S(2)}) collective-permute-start(bf16[384,256]{1,0:T(8,128)(2,1)S(1)} %shard_map.113.refs_0_), channel_id=1, source_target_pairs={{0,2},{1,3},{2,0},{3,1},{4,6},{5,7},{6,4},{7,5},{8,10},{9,11},{10,... | collective-permute-start | bytes 589832 | tf_op jit(solution)/shard_map/ppermute | solution.py:696
  63.2 1.0 %collective-permute-done.14.refs_0_ = bf16[384,128]{1,0:T(8,128)(2,1)S(1)} collective-permute-done((bf16[384,128]{1,0:T(8,128)(2,1)S(1)}, bf16[384,128]{1,0:T(8,128)(2,1)S(1)}, u32[]{:S(2)}, u32[]{:S(2)}) %collective-permute-start.14) | collective-permute-done | bytes 98336 | tf_op jit(solution)/shard_map/ppermute | solution.py:669
  64.2 3.0 %collective-permute-done.15.refs_1_ = bf16[384,128]{1,0:T(8,128)(2,1)S(1)} collective-permute-done((bf16[384,128]{1,0:T(8,128)(2,1)S(1)}, bf16[384,128]{1,0:T(8,128)(2,1)S(1)}, u32[]{:S(2)}, u32[]{:S(2)}) %collective-permute-start.15) | collective-permute-done | bytes 98336 | tf_op jit(solution)/shard_map/ppermute | solution.py:669
  67.2 0.1 shard_map.107.refs_0_
  67.3 1.3 %collective-permute-start.16 = (bf16[384,256]{1,0:T(8,128)(2,1)S(1)}, bf16[384,256]{1,0:T(8,128)(2,1)S(1)}, u32[]{:S(2)}, u32[]{:S(2)}) collective-permute-start(bf16[384,256]{1,0:T(8,128)(2,1)S(1)} %shard_map.107.refs_0_), channel_id=1, source_target_pairs={{0,2},{1,3},{2,0},{3,1},{4,6},{5,7},{6,4},{7,5},{8,10},{9,11},{10,... | collective-permute-start | bytes 589832 | tf_op jit(solution)/shard_map/ppermute | solution.py:696
  68.6 0.0 collective-permute-done.19.refs_1_
  68.6 4.8 %collective-permute-start.20 = (bf16[384,512]{1,0:T(8,128)(2,1)S(1)}, bf16[384,512]{1,0:T(8,128)(2,1)S(1)}, u32[]{:S(2)}, u32[]{:S(2)}) collective-permute-start(bf16[384,512]{1,0:T(8,128)(2,1)S(1)} %shard_map.110.refs_0_), channel_id=1, source_target_pairs={{0,1},{1,0},{2,3},{3,2},{4,5},{5,4},{6,7},{7,6},{8,9},{9,8},{10,11... | collective-permute-start | bytes 1179656 | tf_op jit(solution)/shard_map/ppermute | solution.py:698
  73.4 0.0 collective-permute-done.23.refs_1_
  73.4 2.5 %collective-permute-start.24 = (bf16[384,512]{1,0:T(8,128)(2,1)S(1)}, bf16[384,512]{1,0:T(8,128)(2,1)S(1)}, u32[]{:S(2)}, u32[]{:S(2)}) collective-permute-start(bf16[384,512]{1,0:T(8,128)(2,1)S(1)} %shard_map.112.refs_2_), channel_id=1, source_target_pairs={{0,1},{1,0},{2,3},{3,2},{4,5},{5,4},{6,7},{7,6},{8,9},{9,8},{10,11... | collective-permute-start | bytes 1179656 | tf_op jit(solution)/shard_map/ppermute | solution.py:698
  76.0 0.0 collective-permute-done.27.refs_1_
  76.0 2.1 %collective-permute-start.28 = (bf16[384,512]{1,0:T(8,128)(2,1)S(1)}, bf16[384,512]{1,0:T(8,128)(2,1)S(1)}, u32[]{:S(2)}, u32[]{:S(2)}) collective-permute-start(bf16[384,512]{1,0:T(8,128)(2,1)S(1)} %shard_map.114.refs_4_), channel_id=1, source_target_pairs={{0,1},{1,0},{2,3},{3,2},{4,5},{5,4},{6,7},{7,6},{8,9},{9,8},{10,11... | collective-permute-start | bytes 1179656 | tf_op jit(solution)/shard_map/ppermute | solution.py:698
  78.1 0.1 shard_map.108.refs_0_
  78.1 2.1 %collective-permute-start.17 = (bf16[384,512]{1,0:T(8,128)(2,1)S(1)}, bf16[384,512]{1,0:T(8,128)(2,1)S(1)}, u32[]{:S(2)}, u32[]{:S(2)}) collective-permute-start(bf16[384,512]{1,0:T(8,128)(2,1)S(1)} %shard_map.108.refs_0_), channel_id=1, source_target_pairs={{0,1},{1,0},{2,3},{3,2},{4,5},{5,4},{6,7},{7,6},{8,9},{9,8},{10,11... | collective-permute-start | bytes 1179656 | tf_op jit(solution)/shard_map/ppermute | solution.py:698
  80.2 0.0 collective-permute-done.24.refs_3_
  80.2 0.0 collective-permute-done.28.refs_5_
  80.2 2.6 %shard_map.115.refs_2_ = f32[384,1024]{1,0:T(8,128)S(1)} custom-call(bf16[8,4,128,1024]{3,2,1,0:T(8,128)(2,1)S(1)} %shard_map.100.after_ref.refs_5_.rows_ref, bf16[384,512]{1,0:T(8,128)(2,1)S(1)} %shard_map.110.refs_0_, bf16[384,512]{1,0:T(8,128)(2,1)S(1)} %collective-permute-done.20.refs_1_, bf16[384,512]{1,0:T(8,128)(2,1)S(1)} %shard_map.112.refs_2_, ...), custom_call_target="tpu_custom_call" | custom-call | tf_op jit(solution)/shard_map/pallas_call | solution.py:654
  82.9 0.0 collective-permute-done.17.refs_1_
  82.9 1.9 %shard_map.116 = bf16[384,1024]{1,0:T(8,128)(2,1)} custom-call(bf16[8,4,128,1024]{3,2,1,0:T(8,128)(2,1)S(1)} %shard_map.100.after_ref.refs_5_.rows_ref, bf16[384,512]{1,0:T(8,128)(2,1)S(1)} %shard_map.108.refs_0_, bf16[384,512]{1,0:T(8,128)(2,1)S(1)} %collective-permute-done.17.refs_1_, f32[384,1024]{1,0:T(8,128)S(1)} %shard_map.115.refs_2_), custom_call_target="tpu_custom_call" | custom-call | tf_op jit(solution)/shard_map/pallas_call | solution.py:654
  (32 shorter events, 0.1 us)
Async XLA Ops:
  1.2 18.2 %copy-start = (bf16[384,1024]{1,0:T(8,128)(2,1)S(1)}, bf16[384,1024]{1,0:T(8,128)(2,1)}, u32[]{:S(2)}) copy-start(bf16[384,1024]{1,0:T(8,128)(2,1)} %gate_ref.3) | copy-start | bytes 2359300
  1.2 18.2 %copy-start.1 = (bf16[384,1024]{1,0:T(8,128)(2,1)S(1)}, bf16[384,1024]{1,0:T(8,128)(2,1)}, u32[]{:S(2)}) copy-start(bf16[384,1024]{1,0:T(8,128)(2,1)} %value_ref.3) | copy-start | bytes 2359300
  1.2 18.2 %copy-start.6 = (f32[3,3,1024]{2,1,0:T(4,128)S(1)}, f32[3,3,1024]{2,1,0:T(4,128)}, u32[]{:S(2)}) copy-start(f32[3,3,1024]{2,1,0:T(4,128)} %taps_ref.3) | copy-start | bytes 110596
  1.2 18.2 %copy-start.8 = (s32[8]{0:T(128)S(1)}, s32[8]{0:T(128)}, u32[]{:S(2)}) copy-start(s32[8]{0:T(128)} %broadcast_xor_fusion.order_ref) | copy-start | bytes 100
  3.9 15.5 %collective-permute-start = (bf16[528,128]{1,0:T(8,128)(2,1)}, bf16[528,128]{1,0:T(8,128)(2,1)S(1)}, u32[]{:S(2)}, u32[]{:S(2)}) collective-permute-start(bf16[528,128]{1,0:T(8,128)(2,1)} %get-tuple-element.33), channel_id=1, source_target_pairs={{0,4},{4,0},{8,12},{12,8},{16,20},{20,16},{24,28},{28,24},{1,5},{5... | collective-permute-start | bytes 405512 | tf_op jit(solution)/shard_map/ppermute | solution.py:669
  5.9 4.7 %collective-permute-start.3 = (bf16[400,128]{1,0:T(8,128)(2,1)}, bf16[400,128]{1,0:T(8,128)(2,1)S(1)}, u32[]{:S(2)}, u32[]{:S(2)}) collective-permute-start(bf16[400,128]{1,0:T(8,128)(2,1)} %get-tuple-element.39), channel_id=1, source_target_pairs={{0,16},{4,20},{8,24},{12,28},{16,0},{20,4},{24,8},{28,12},{1,17},{... | collective-permute-start | bytes 307208 | tf_op jit(solution)/shard_map/ppermute | solution.py:669
  8.2 13.1 %collective-permute-start.4 = (bf16[400,128]{1,0:T(8,128)(2,1)}, bf16[400,128]{1,0:T(8,128)(2,1)S(1)}, u32[]{:S(2)}, u32[]{:S(2)}) collective-permute-start(bf16[400,128]{1,0:T(8,128)(2,1)} %get-tuple-element.40), channel_id=1, source_target_pairs={{0,20},{4,16},{8,28},{12,24},{16,4},{20,0},{24,12},{28,8},{1,21},{... | collective-permute-start | bytes 307208 | tf_op jit(solution)/shard_map/ppermute | solution.py:669
  8.2 13.2 %collective-permute-start.5 = (bf16[400,128]{1,0:T(8,128)(2,1)}, bf16[400,128]{1,0:T(8,128)(2,1)S(1)}, u32[]{:S(2)}, u32[]{:S(2)}) collective-permute-start(bf16[400,128]{1,0:T(8,128)(2,1)} %get-tuple-element.41), channel_id=1, source_target_pairs={{0,8},{4,12},{8,0},{12,4},{16,24},{20,28},{24,16},{28,20},{1,9},{5... | collective-permute-start | bytes 307208 | tf_op jit(solution)/shard_map/ppermute | solution.py:669
  9.5 23.8 %collective-permute-start.1 = (bf16[528,128]{1,0:T(8,128)(2,1)}, bf16[528,128]{1,0:T(8,128)(2,1)S(1)}, u32[]{:S(2)}, u32[]{:S(2)}) collective-permute-start(bf16[528,128]{1,0:T(8,128)(2,1)} %get-tuple-element.34), channel_id=1, source_target_pairs={{0,12},{4,8},{8,4},{12,0},{16,28},{20,24},{24,20},{28,16},{1,13},{... | collective-permute-start | bytes 405512 | tf_op jit(solution)/shard_map/ppermute | solution.py:669
  10.6 22.7 %collective-permute-start.2 = (bf16[528,128]{1,0:T(8,128)(2,1)}, bf16[528,128]{1,0:T(8,128)(2,1)S(1)}, u32[]{:S(2)}, u32[]{:S(2)}) collective-permute-start(bf16[528,128]{1,0:T(8,128)(2,1)} %get-tuple-element.35), channel_id=1, source_target_pairs={{0,28},{4,24},{8,20},{12,16},{16,12},{20,8},{24,4},{28,0},{1,29},{... | collective-permute-start | bytes 405512 | tf_op jit(solution)/shard_map/ppermute | solution.py:669
  19.4 8.4 %collective-permute-start.6 = (bf16[400,128]{1,0:T(8,128)(2,1)}, bf16[400,128]{1,0:T(8,128)(2,1)S(1)}, u32[]{:S(2)}, u32[]{:S(2)}) collective-permute-start(bf16[400,128]{1,0:T(8,128)(2,1)} %get-tuple-element.42), channel_id=1, source_target_pairs={{0,24},{4,28},{8,16},{12,20},{16,8},{20,12},{24,0},{28,4},{1,25},{... | collective-permute-start | bytes 307208 | tf_op jit(solution)/shard_map/ppermute | solution.py:669
  21.3 12.9 %collective-permute-start.7 = (bf16[384,128]{1,0:T(8,128)(2,1)S(1)}, bf16[384,128]{1,0:T(8,128)(2,1)S(1)}, u32[]{:S(2)}, u32[]{:S(2)}) collective-permute-start(bf16[384,128]{1,0:T(8,128)(2,1)S(1)} %get-tuple-element.46), channel_id=1, source_target_pairs={{0,16},{4,20},{8,24},{12,28},{16,0},{20,4},{24,8},{28,12},{1,17},{... | collective-permute-start | bytes 294920 | tf_op jit(solution)/shard_map/ppermute | solution.py:669
  21.4 14.1 %collective-permute-start.8 = (bf16[384,128]{1,0:T(8,128)(2,1)S(1)}, bf16[384,128]{1,0:T(8,128)(2,1)S(1)}, u32[]{:S(2)}, u32[]{:S(2)}) collective-permute-start(bf16[384,128]{1,0:T(8,128)(2,1)S(1)} %get-tuple-element.47), channel_id=1, source_target_pairs={{0,4},{4,0},{8,12},{12,8},{16,20},{20,16},{24,28},{28,24},{1,5},{5... | collective-permute-start | bytes 294920 | tf_op jit(solution)/shard_map/ppermute | solution.py:669
  22.7 3.4 %copy-start.3 = (bf16[4096,1024]{1,0:T(8,128)(2,1)S(1)}, bf16[4096,1024]{1,0:T(8,128)(2,1)}, u32[]{:S(2)}) copy-start(bf16[4096,1024]{1,0:T(8,128)(2,1)} %weight_ref.1) | copy-start | bytes 25165828
  26.0 12.0 %copy-start.2 = (bf16[768,768]{1,0:T(8,128)(2,1)S(1)}, bf16[768,768]{1,0:T(8,128)(2,1)}, u32[]{:S(2)}) copy-start(bf16[768,768]{1,0:T(8,128)(2,1)} %constant.16.clone.table_ref) | copy-start | bytes 3538948
  26.0 12.0 %copy-start.7 = (bf16[400,128]{1,0:T(8,128)(2,1)S(1)}, bf16[400,128]{1,0:T(8,128)(2,1)}, u32[]{:S(2)}) copy-start(bf16[400,128]{1,0:T(8,128)(2,1)} %get-tuple-element.38.refs_0_) | copy-start | bytes 307204
  27.8 15.0 %collective-permute-start.9 = (bf16[384,128]{1,0:T(8,128)(2,1)S(1)}, bf16[384,128]{1,0:T(8,128)(2,1)S(1)}, u32[]{:S(2)}, u32[]{:S(2)}) collective-permute-start(bf16[384,128]{1,0:T(8,128)(2,1)S(1)} %get-tuple-element.48), channel_id=1, source_target_pairs={{0,20},{4,16},{8,28},{12,24},{16,4},{20,0},{24,12},{28,8},{1,21},{... | collective-permute-start | bytes 294920 | tf_op jit(solution)/shard_map/ppermute | solution.py:669
  33.3 10.8 %collective-permute-start.10 = (bf16[384,128]{1,0:T(8,128)(2,1)S(1)}, bf16[384,128]{1,0:T(8,128)(2,1)S(1)}, u32[]{:S(2)}, u32[]{:S(2)}) collective-permute-start(bf16[384,128]{1,0:T(8,128)(2,1)S(1)} %get-tuple-element.49), channel_id=1, source_target_pairs={{0,8},{4,12},{8,0},{12,4},{16,24},{20,28},{24,16},{28,20},{1,9},{5... | collective-permute-start | bytes 294920 | tf_op jit(solution)/shard_map/ppermute | solution.py:669
  33.4 10.8 %collective-permute-start.11 = (bf16[384,128]{1,0:T(8,128)(2,1)S(1)}, bf16[384,128]{1,0:T(8,128)(2,1)S(1)}, u32[]{:S(2)}, u32[]{:S(2)}) collective-permute-start(bf16[384,128]{1,0:T(8,128)(2,1)S(1)} %get-tuple-element.50), channel_id=1, source_target_pairs={{0,24},{4,28},{8,16},{12,20},{16,8},{20,12},{24,0},{28,4},{1,25},{... | collective-permute-start | bytes 294920 | tf_op jit(solution)/shard_map/ppermute | solution.py:669
  34.2 10.6 %collective-permute-start.12 = (bf16[384,128]{1,0:T(8,128)(2,1)S(1)}, bf16[384,128]{1,0:T(8,128)(2,1)S(1)}, u32[]{:S(2)}, u32[]{:S(2)}) collective-permute-start(bf16[384,128]{1,0:T(8,128)(2,1)S(1)} %get-tuple-element.51), channel_id=1, source_target_pairs={{0,12},{4,8},{8,4},{12,0},{16,28},{20,24},{24,20},{28,16},{1,13},{... | collective-permute-start | bytes 294920 | tf_op jit(solution)/shard_map/ppermute | solution.py:669
  35.5 9.3 %collective-permute-start.13 = (bf16[384,128]{1,0:T(8,128)(2,1)S(1)}, bf16[384,128]{1,0:T(8,128)(2,1)S(1)}, u32[]{:S(2)}, u32[]{:S(2)}) collective-permute-start(bf16[384,128]{1,0:T(8,128)(2,1)S(1)} %get-tuple-element.52), channel_id=1, source_target_pairs={{0,28},{4,24},{8,20},{12,16},{16,12},{20,8},{24,4},{28,0},{1,29},{... | collective-permute-start | bytes 294920 | tf_op jit(solution)/shard_map/ppermute | solution.py:669
  38.1 2.1 %copy-start.4 = (bf16[384,1024]{1,0:T(8,128)(2,1)S(1)}, bf16[384,1024]{1,0:T(8,128)(2,1)}, u32[]{:S(2)}) copy-start(bf16[384,1024]{1,0:T(8,128)(2,1)} %late_ref.1) | copy-start | bytes 2359300
  38.1 2.1 %copy-start.9 = (f32[1024]{0:T(1024)S(1)}, f32[1024]{0:T(1024)}, u32[]{:S(2)}) copy-start(f32[1024]{0:T(1024)} %param.15) | copy-start | bytes 12292
  42.8 2.0 %copy-start.5 = (bf16[384,2304]{1,0:T(8,128)(2,1)S(1)}, bf16[384,2304]{1,0:T(8,128)(2,1)}, u32[]{:S(2)}) copy-start(bf16[384,2304]{1,0:T(8,128)(2,1)} %constant.17.clone.inverse_ref) | copy-start | bytes 5308420
  50.7 6.0 %collective-permute-start.18 = (bf16[384,128]{1,0:T(8,128)(2,1)S(1)}, bf16[384,128]{1,0:T(8,128)(2,1)S(1)}, u32[]{:S(2)}, u32[]{:S(2)}) collective-permute-start(bf16[384,128]{1,0:T(8,128)(2,1)S(1)} %get-tuple-element.56), channel_id=1, source_target_pairs={{0,16},{4,20},{8,24},{12,28},{16,0},{20,4},{24,8},{28,12},{1,17},{... | collective-permute-start | bytes 294920 | tf_op jit(solution)/shard_map/ppermute | solution.py:669
  52.7 6.4 %collective-permute-start.21 = (bf16[384,128]{1,0:T(8,128)(2,1)S(1)}, bf16[384,128]{1,0:T(8,128)(2,1)S(1)}, u32[]{:S(2)}, u32[]{:S(2)}) collective-permute-start(bf16[384,128]{1,0:T(8,128)(2,1)S(1)} %get-tuple-element.57), channel_id=1, source_target_pairs={{0,4},{4,0},{8,12},{12,8},{16,20},{20,16},{24,28},{28,24},{1,5},{5... | collective-permute-start | bytes 294920 | tf_op jit(solution)/shard_map/ppermute | solution.py:669
  53.2 6.9 %collective-permute-start.22 = (bf16[384,128]{1,0:T(8,128)(2,1)S(1)}, bf16[384,128]{1,0:T(8,128)(2,1)S(1)}, u32[]{:S(2)}, u32[]{:S(2)}) collective-permute-start(bf16[384,128]{1,0:T(8,128)(2,1)S(1)} %get-tuple-element.58), channel_id=1, source_target_pairs={{0,8},{4,12},{8,0},{12,4},{16,24},{20,28},{24,16},{28,20},{1,9},{5... | collective-permute-start | bytes 294920 | tf_op jit(solution)/shard_map/ppermute | solution.py:669
  54.3 7.2 %collective-permute-start.25 = (bf16[384,128]{1,0:T(8,128)(2,1)S(1)}, bf16[384,128]{1,0:T(8,128)(2,1)S(1)}, u32[]{:S(2)}, u32[]{:S(2)}) collective-permute-start(bf16[384,128]{1,0:T(8,128)(2,1)S(1)} %get-tuple-element.59), channel_id=1, source_target_pairs={{0,12},{4,8},{8,4},{12,0},{16,28},{20,24},{24,20},{28,16},{1,13},{... | collective-permute-start | bytes 294920 | tf_op jit(solution)/shard_map/ppermute | solution.py:669
  55.5 6.3 %collective-permute-start.26 = (bf16[384,128]{1,0:T(8,128)(2,1)S(1)}, bf16[384,128]{1,0:T(8,128)(2,1)S(1)}, u32[]{:S(2)}, u32[]{:S(2)}) collective-permute-start(bf16[384,128]{1,0:T(8,128)(2,1)S(1)} %get-tuple-element.60), channel_id=1, source_target_pairs={{0,20},{4,16},{8,28},{12,24},{16,4},{20,0},{24,12},{28,8},{1,21},{... | collective-permute-start | bytes 294920 | tf_op jit(solution)/shard_map/ppermute | solution.py:669
  56.7 7.5 %collective-permute-start.14 = (bf16[384,128]{1,0:T(8,128)(2,1)S(1)}, bf16[384,128]{1,0:T(8,128)(2,1)S(1)}, u32[]{:S(2)}, u32[]{:S(2)}) collective-permute-start(bf16[384,128]{1,0:T(8,128)(2,1)S(1)} %get-tuple-element.53), channel_id=1, source_target_pairs={{0,24},{4,28},{8,16},{12,20},{16,8},{20,12},{24,0},{28,4},{1,25},{... | collective-permute-start | bytes 294920 | tf_op jit(solution)/shard_map/ppermute | solution.py:669
  59.1 8.1 %collective-permute-start.15 = (bf16[384,128]{1,0:T(8,128)(2,1)S(1)}, bf16[384,128]{1,0:T(8,128)(2,1)S(1)}, u32[]{:S(2)}, u32[]{:S(2)}) collective-permute-start(bf16[384,128]{1,0:T(8,128)(2,1)S(1)} %get-tuple-element.54), channel_id=1, source_target_pairs={{0,28},{4,24},{8,20},{12,16},{16,12},{20,8},{24,4},{28,0},{1,29},{... | collective-permute-start | bytes 294920 | tf_op jit(solution)/shard_map/ppermute | solution.py:669
  60.1 8.5 %collective-permute-start.19 = (bf16[384,256]{1,0:T(8,128)(2,1)S(1)}, bf16[384,256]{1,0:T(8,128)(2,1)S(1)}, u32[]{:S(2)}, u32[]{:S(2)}) collective-permute-start(bf16[384,256]{1,0:T(8,128)(2,1)S(1)} %shard_map.109.refs_0_), channel_id=1, source_target_pairs={{0,2},{1,3},{2,0},{3,1},{4,6},{5,7},{6,4},{7,5},{8,10},{9,11},{10,... | collective-permute-start | bytes 589832 | tf_op jit(solution)/shard_map/ppermute | solution.py:696
  61.5 11.9 %collective-permute-start.23 = (bf16[384,256]{1,0:T(8,128)(2,1)S(1)}, bf16[384,256]{1,0:T(8,128)(2,1)S(1)}, u32[]{:S(2)}, u32[]{:S(2)}) collective-permute-start(bf16[384,256]{1,0:T(8,128)(2,1)S(1)} %shard_map.111.refs_0_), channel_id=1, source_target_pairs={{0,2},{1,3},{2,0},{3,1},{4,6},{5,7},{6,4},{7,5},{8,10},{9,11},{10,... | collective-permute-start | bytes 589832 | tf_op jit(solution)/shard_map/ppermute | solution.py:696
  61.8 14.1 %collective-permute-start.27 = (bf16[384,256]{1,0:T(8,128)(2,1)S(1)}, bf16[384,256]{1,0:T(8,128)(2,1)S(1)}, u32[]{:S(2)}, u32[]{:S(2)}) collective-permute-start(bf16[384,256]{1,0:T(8,128)(2,1)S(1)} %shard_map.113.refs_0_), channel_id=1, source_target_pairs={{0,2},{1,3},{2,0},{3,1},{4,6},{5,7},{6,4},{7,5},{8,10},{9,11},{10,... | collective-permute-start | bytes 589832 | tf_op jit(solution)/shard_map/ppermute | solution.py:696
  67.3 10.8 %collective-permute-start.16 = (bf16[384,256]{1,0:T(8,128)(2,1)S(1)}, bf16[384,256]{1,0:T(8,128)(2,1)S(1)}, u32[]{:S(2)}, u32[]{:S(2)}) collective-permute-start(bf16[384,256]{1,0:T(8,128)(2,1)S(1)} %shard_map.107.refs_0_), channel_id=1, source_target_pairs={{0,2},{1,3},{2,0},{3,1},{4,6},{5,7},{6,4},{7,5},{8,10},{9,11},{10,... | collective-permute-start | bytes 589832 | tf_op jit(solution)/shard_map/ppermute | solution.py:696
  68.6 11.6 %collective-permute-start.20 = (bf16[384,512]{1,0:T(8,128)(2,1)S(1)}, bf16[384,512]{1,0:T(8,128)(2,1)S(1)}, u32[]{:S(2)}, u32[]{:S(2)}) collective-permute-start(bf16[384,512]{1,0:T(8,128)(2,1)S(1)} %shard_map.110.refs_0_), channel_id=1, source_target_pairs={{0,1},{1,0},{2,3},{3,2},{4,5},{5,4},{6,7},{7,6},{8,9},{9,8},{10,11... | collective-permute-start | bytes 1179656 | tf_op jit(solution)/shard_map/ppermute | solution.py:698
  73.4 6.8 %collective-permute-start.24 = (bf16[384,512]{1,0:T(8,128)(2,1)S(1)}, bf16[384,512]{1,0:T(8,128)(2,1)S(1)}, u32[]{:S(2)}, u32[]{:S(2)}) collective-permute-start(bf16[384,512]{1,0:T(8,128)(2,1)S(1)} %shard_map.112.refs_2_), channel_id=1, source_target_pairs={{0,1},{1,0},{2,3},{3,2},{4,5},{5,4},{6,7},{7,6},{8,9},{9,8},{10,11... | collective-permute-start | bytes 1179656 | tf_op jit(solution)/shard_map/ppermute | solution.py:698
  76.0 4.2 %collective-permute-start.28 = (bf16[384,512]{1,0:T(8,128)(2,1)S(1)}, bf16[384,512]{1,0:T(8,128)(2,1)S(1)}, u32[]{:S(2)}, u32[]{:S(2)}) collective-permute-start(bf16[384,512]{1,0:T(8,128)(2,1)S(1)} %shard_map.114.refs_4_), channel_id=1, source_target_pairs={{0,1},{1,0},{2,3},{3,2},{4,5},{5,4},{6,7},{7,6},{8,9},{9,8},{10,11... | collective-permute-start | bytes 1179656 | tf_op jit(solution)/shard_map/ppermute | solution.py:698
  78.1 4.7 %collective-permute-start.17 = (bf16[384,512]{1,0:T(8,128)(2,1)S(1)}, bf16[384,512]{1,0:T(8,128)(2,1)S(1)}, u32[]{:S(2)}, u32[]{:S(2)}) collective-permute-start(bf16[384,512]{1,0:T(8,128)(2,1)S(1)} %shard_map.108.refs_0_), channel_id=1, source_target_pairs={{0,1},{1,0},{2,3},{3,2},{4,5},{5,4},{6,7},{7,6},{8,9},{9,8},{10,11... | collective-permute-start | bytes 1179656 | tf_op jit(solution)/shard_map/ppermute | solution.py:698

commit v4 on v3

--- a/solution.py
+++ b/solution.py
@@ -288,6 +288,7 @@
 OFFSETS = (0, 4, 1, 2, 3, 5, 6, 7)
 FILTER_ORDER = (4, 1, 5, 2, 6, 3, 7)
 SIGNAL_ORDER = (4, 1, 5, 2, 6, 3, 7)
+RESULT_ORDER = (4, 1, 2, 3, 5, 6, 7)
 EARLY = (0, 4, 1, 5)
 LATE = (2, 6, 3, 7)
 GROUP = 4
@@ -312,7 +313,8 @@
     return [pl.BlockSpec(memory_space=pltpu.VMEM)] * count
 
 
-def cut_kernel(order_ref, filter_ref, *refs):
+def cut_kernel(filter_ref, *refs):
+    own = lax.axis_index("seq")
     last_refs, (gate_top, value_top), out_refs = refs[:3], refs[3:5], refs[5:-1]
     rows, width = filter_ref.shape
     ends_ref = refs[-1]
@@ -321,7 +323,7 @@
     ends.append(jnp.zeros((TILE - 5 * KEEP, width), F32))
     ends_ref[...] = jnp.concatenate(ends, axis=0).astype(BF16)
     for place, out_ref in enumerate(out_refs):
-        at = lanes_at(order_ref, place)
+        at = pl.ds(pl.multiple_of((own ^ OFFSETS[place]) * LANES, LANES), LANES)
         out_ref[:rows] = filter_ref[:, at].astype(BF16)
         out_ref[rows : rows + TILE] = ends_ref[:, at]
         if OFFSETS[place] in NEXT_OFFSETS:
@@ -329,7 +331,7 @@
                 out_ref[rows + (1 + part) * TILE : rows + (2 + part) * TILE] = ends_ref[:, part * LANES : (part + 1) * LANES]
 
 
-def cut_filter(order, long_filter, out_gate, in_gate, values):
+def cut_filter(long_filter, out_gate, in_gate, values):
     rows, width = long_filter.shape
     count = width // LANES
     heights = [rows + TILE * (1 + count * (offset in NEXT_OFFSETS)) for offset in OFFSETS]
@@ -338,13 +340,13 @@
     return pl.pallas_call(
         cut_kernel,
         grid=(1,),
-        in_specs=[pl.BlockSpec(memory_space=pltpu.SMEM), pl.BlockSpec((rows, width), lambda i: (0, 0))] + [last] * 3 + [top] * 2,
+        in_specs=[pl.BlockSpec((rows, width), lambda i: (0, 0))] + [last] * 3 + [top] * 2,
         out_specs=[pl.BlockSpec((height, LANES), lambda i: (0, 0)) for height in heights],
         out_shape=[jax.ShapeDtypeStruct((height, LANES), BF16) for height in heights],
         scratch_shapes=[pltpu.VMEM((TILE, width), BF16)],
         compiler_params=pltpu.CompilerParams(vmem_limit_bytes=CUT_VMEM << 20),
         cost_estimate=cost(rows * width),
-    )(order, long_filter, out_gate, in_gate, values, in_gate, values)
+    )(long_filter, out_gate, in_gate, values, in_gate, values)
 
 
 def mix_slices_kernel(order_ref, gate_ref, value_ref, taps_ref, after_ref, *rest):
@@ -677,7 +679,7 @@
     order = jnp.bitwise_xor(lax.axis_index("seq"), jnp.array(OFFSETS, jnp.int32))
     channel = lax.axis_index("ch").reshape(1)
 
-    filter_blocks = swap_blocks(cut_filter(order, long_filter, out_gate, in_gate, values), FILTER_ORDER)
+    filter_blocks = swap_blocks(cut_filter(long_filter, out_gate, in_gate, values), FILTER_ORDER)
     sent = (0, *(OFFSETS.index(offset) for offset in FILTER_ORDER))
     mixed_blocks = swap_blocks(
         mix_slices(order, in_gate, values, short_filter, filter_blocks[OFFSETS.index(MIX_AFTER)]), SIGNAL_ORDER
@@ -688,7 +690,7 @@
     early, last = (tuple(OFFSETS.index(offset) for offset in group) for group in (EARLY, LATE))
     early_spectra = early_spectra_of(order, table, first, mixed_blocks, early)
     long_blocks = conv_slices(order, table, inverse, filter_spectra, early_spectra, first, mixed_blocks, last, (late, weight_rows))
-    arrived = swap_blocks(long_blocks, OFFSETS[1:])
+    arrived = swap_blocks(long_blocks, RESULT_ORDER)
 
     pieces = []
     for start, stop in CHUNKS:

time: 84.9 us -> 82.9 us (0.976)
  other arithmetic: 1.24 us -> 0.01 us
  waiting for transfers between devices: 4.7 us -> 3.68 us
    xor x1, other arithmetic: 1.24 us -> 0.01 us  [on_device_slices(): jnp.bitwise_xor(lax.axis_index('seq'), jnp.array(OFFSETS, jnp.int32))]
    ppermute x4, starting transfers between devices: 11.5 us -> 12.6 us  [on_device_slices(): lax.ppermute(joined, 'ch', [(i, i ^ 1) for i in range(4)])]
    ppermute x21, waiting for transfers between devices: 4.68 us -> 3.66 us  [swap_blocks(): lax.ppermute(blocks[place], 'seq', [(i, i ^ offset) for i in range(count)])]
    ppermute x21, starting transfers between devices: 36.4 us -> 35.6 us  [swap_blocks(): lax.ppermute(blocks[place], 'seq', [(i, i ^ offset) for i in range(count)])]
  transfers between devices with their start and end apart: 29 -> 29, of which waited for: 3 -> 4; matrix products, arithmetic and copies ran while one was open for 0% -> 0% of each run, Pallas kernels for 15% -> 15%
where the time goes in v4:
time: 82.9 us; the launch traced here: 82.8 us
  starting transfers between devices  52.4 us (63%)
  Pallas kernels  23 us (28%)
  waiting for transfers between devices  3.68 us (4%)
  local copies, waits for them, and re-layouts  3.42 us (4%)
    ppermute x21, starting transfers between devices, swap_blocks(): lax.ppermute(blocks[place], 'seq', [(i, i ^ offset) for i in range(count)])  35.6 us
    ppermute x4, starting transfers between devices, on_device_slices(): lax.ppermute(joined, 'ch', [(i, i ^ 1) for i in range(4)])  12.6 us
    pallas_call x1, Pallas kernels, conv_slices(): pl.pallas_call(functools.partial(conv_slices_kernel, places), in_specs=[p...  5.92 us
    pallas_call x2, Pallas kernels, project_slices(): pl.pallas_call(functools.partial(project_kernel_slices, chunks), in_specs...  4.53 us
    ppermute x4, starting transfers between devices, on_device_slices(): across = lax.ppermute(mixed, 'ch', [(i, i ^ 2) for i in range(4)])  4.2 us
    ppermute x21, waiting for transfers between devices, swap_blocks(): lax.ppermute(blocks[place], 'seq', [(i, i ^ offset) for i in range(count)])  3.66 us
    unnamed x20, local copies, waits for them, and re-layouts  3.42 us
    pallas_call x1, Pallas kernels, cut_filter(): pl.pallas_call(cut_kernel, grid=(1,), in_specs=[pl.BlockSpec((rows, width...  2.61 us
  transfers between devices with their start and end apart: 29, of which 4 were waited for; matrix products, arithmetic and copies ran while one was open for 0% of the time, Pallas kernels for 15%

profile of v4, /device:TPU:1, one launch (start us, length us, event | category | flops | bytes accessed | tf_op | source)
XLA Modules:
  0.0 82.8 jit_solution(2017195876314126288)
XLA Ops:
  0.0 2.6 %shard_map.101 = (bf16[400,128]{1,0:T(8,128)(2,1)}, bf16[400,128]{1,0:T(8,128)(2,1)}, bf16[528,128]{1,0:T(8,128)(2,1)}, bf16[400,128]{1,0:T(8,128)(2,1)}, bf16[5...) custom-call(f32[384,1024]{1,0:T(8,128)} %filter_ref.1, ...), custom_call_target="tpu_custom_call" | custom-call | tf_op jit(solution)/shard_map/pallas_call | solution.py:340
  2.6 2.0 %collective-permute-start = (bf16[528,128]{1,0:T(8,128)(2,1)}, bf16[528,128]{1,0:T(8,128)(2,1)S(1)}, u32[]{:S(2)}, u32[]{:S(2)}) collective-permute-start(bf16[528,128]{1,0:T(8,128)(2,1)} %get-tuple-element.33), channel_id=1, source_target_pairs={{0,4},{4,0},{8,12},{12,8},{16,20},{20,16},{24,28},{28,24},{1,5},{5... | collective-permute-start | bytes 405512 | tf_op jit(solution)/shard_map/ppermute | solution.py:671
  4.7 2.3 %collective-permute-start.3 = (bf16[400,128]{1,0:T(8,128)(2,1)}, bf16[400,128]{1,0:T(8,128)(2,1)S(1)}, u32[]{:S(2)}, u32[]{:S(2)}) collective-permute-start(bf16[400,128]{1,0:T(8,128)(2,1)} %get-tuple-element.39), channel_id=1, source_target_pairs={{0,16},{4,20},{8,24},{12,28},{16,0},{20,4},{24,8},{28,12},{1,17},{... | collective-permute-start | bytes 307208 | tf_op jit(solution)/shard_map/ppermute | solution.py:671
  7.0 0.0 collective-permute-start.4
  7.0 1.3 %collective-permute-start.5 = (bf16[400,128]{1,0:T(8,128)(2,1)}, bf16[400,128]{1,0:T(8,128)(2,1)S(1)}, u32[]{:S(2)}, u32[]{:S(2)}) collective-permute-start(bf16[400,128]{1,0:T(8,128)(2,1)} %get-tuple-element.41), channel_id=1, source_target_pairs={{0,8},{4,12},{8,0},{12,4},{16,24},{20,28},{24,16},{28,20},{1,9},{5... | collective-permute-start | bytes 307208 | tf_op jit(solution)/shard_map/ppermute | solution.py:671
  8.3 2.2 %collective-permute-start.6 = (bf16[400,128]{1,0:T(8,128)(2,1)}, bf16[400,128]{1,0:T(8,128)(2,1)S(1)}, u32[]{:S(2)}, u32[]{:S(2)}) collective-permute-start(bf16[400,128]{1,0:T(8,128)(2,1)} %get-tuple-element.42), channel_id=1, source_target_pairs={{0,24},{4,28},{8,16},{12,20},{16,8},{20,12},{24,0},{28,4},{1,25},{... | collective-permute-start | bytes 307208 | tf_op jit(solution)/shard_map/ppermute | solution.py:671
  10.5 5.9 %collective-permute-start.1 = (bf16[528,128]{1,0:T(8,128)(2,1)}, bf16[528,128]{1,0:T(8,128)(2,1)S(1)}, u32[]{:S(2)}, u32[]{:S(2)}) collective-permute-start(bf16[528,128]{1,0:T(8,128)(2,1)} %get-tuple-element.34), channel_id=1, source_target_pairs={{0,12},{4,8},{8,4},{12,0},{16,28},{20,24},{24,20},{28,16},{1,13},{... | collective-permute-start | bytes 405512 | tf_op jit(solution)/shard_map/ppermute | solution.py:671
  16.4 0.0 collective-permute-done.refs_0_.refs_2_.after_ref
  16.4 2.9 %collective-permute-start.2 = (bf16[528,128]{1,0:T(8,128)(2,1)}, bf16[528,128]{1,0:T(8,128)(2,1)S(1)}, u32[]{:S(2)}, u32[]{:S(2)}) collective-permute-start(bf16[528,128]{1,0:T(8,128)(2,1)} %get-tuple-element.35), channel_id=1, source_target_pairs={{0,28},{4,24},{8,20},{12,16},{16,12},{20,8},{24,4},{28,0},{1,29},{... | collective-permute-start | bytes 405512 | tf_op jit(solution)/shard_map/ppermute | solution.py:671
  19.3 1.9 %shard_map.104 = (bf16[384,128]{1,0:T(8,128)(2,1)S(1)}, bf16[384,128]{1,0:T(8,128)(2,1)S(1)}, bf16[384,128]{1,0:T(8,128)(2,1)S(1)}, bf16[384,128]{1,0:T(8,128)(2...) custom-call(s32[8]{0:T(128)S(1)} %broadcast_xor_fusion.order_ref, ...), custom_call_target="tpu_custom_call" | custom-call | flops 5505024 | bytes 43008 | tf_op jit(solution)/shard_map/pallas_call | solution.py:367
  21.2 0.4 collective-permute-start.7
  21.6 1.2 %collective-permute-start.8 = (bf16[384,128]{1,0:T(8,128)(2,1)S(1)}, bf16[384,128]{1,0:T(8,128)(2,1)S(1)}, u32[]{:S(2)}, u32[]{:S(2)}) collective-permute-start(bf16[384,128]{1,0:T(8,128)(2,1)S(1)} %get-tuple-element.47), channel_id=1, source_target_pairs={{0,4},{4,0},{8,12},{12,8},{16,20},{20,16},{24,28},{28,24},{1,5},{5... | collective-permute-start | bytes 294920 | tf_op jit(solution)/shard_map/ppermute | solution.py:671
  22.7 3.4 %copy-done.3 = bf16[4096,1024]{1,0:T(8,128)(2,1)S(1)} copy-done((bf16[4096,1024]{1,0:T(8,128)(2,1)S(1)}, bf16[4096,1024]{1,0:T(8,128)(2,1)}, u32[]{:S(2)}) %copy-start.3) | copy-done | bytes 8388632
  26.1 1.7 %shard_map.100.after_ref.refs_5_.rows_ref = bf16[8,4,128,1024]{3,2,1,0:T(8,128)(2,1)S(1)} custom-call(s32[8]{0:T(128)S(1)} %broadcast_xor_fusion.order_ref, s32[1]{0:T(128)} %bitcast.channel_ref, bf16[4096,1024]{1,0:T(8,128)(2,1)S(1)} %copy-done.3), custom_call_target="tpu_custom_call" | custom-call | bytes 16777216 | tf_op jit(solution)/shard_map/pallas_call | solution.py:609
  27.8 0.0 collective-permute-done.6.refs_5_
  27.9 2.1 %collective-permute-start.9 = (bf16[384,128]{1,0:T(8,128)(2,1)S(1)}, bf16[384,128]{1,0:T(8,128)(2,1)S(1)}, u32[]{:S(2)}, u32[]{:S(2)}) collective-permute-start(bf16[384,128]{1,0:T(8,128)(2,1)S(1)} %get-tuple-element.48), channel_id=1, source_target_pairs={{0,20},{4,16},{8,28},{12,24},{16,4},{20,0},{24,12},{28,8},{1,21},{... | collective-permute-start | bytes 294920 | tf_op jit(solution)/shard_map/ppermute | solution.py:671
  30.0 1.5 %collective-permute-start.10 = (bf16[384,128]{1,0:T(8,128)(2,1)S(1)}, bf16[384,128]{1,0:T(8,128)(2,1)S(1)}, u32[]{:S(2)}, u32[]{:S(2)}) collective-permute-start(bf16[384,128]{1,0:T(8,128)(2,1)S(1)} %get-tuple-element.49), channel_id=1, source_target_pairs={{0,8},{4,12},{8,0},{12,4},{16,24},{20,28},{24,16},{28,20},{1,9},{5... | collective-permute-start | bytes 294920 | tf_op jit(solution)/shard_map/ppermute | solution.py:671
  31.4 0.0 collective-permute-done.2.refs_2_.refs_7_
  31.4 0.0 collective-permute-start.11
  31.5 0.0 collective-permute-done.7.refs_1_
  31.5 1.5 %collective-permute-start.12 = (bf16[384,128]{1,0:T(8,128)(2,1)S(1)}, bf16[384,128]{1,0:T(8,128)(2,1)S(1)}, u32[]{:S(2)}, u32[]{:S(2)}) collective-permute-start(bf16[384,128]{1,0:T(8,128)(2,1)S(1)} %get-tuple-element.51), channel_id=1, source_target_pairs={{0,12},{4,8},{8,4},{12,0},{16,28},{20,24},{24,20},{28,16},{1,13},{... | collective-permute-start | bytes 294920 | tf_op jit(solution)/shard_map/ppermute | solution.py:671
  33.0 0.0 collective-permute-done.8.refs_2_
  33.0 1.8 %collective-permute-start.13 = (bf16[384,128]{1,0:T(8,128)(2,1)S(1)}, bf16[384,128]{1,0:T(8,128)(2,1)S(1)}, u32[]{:S(2)}, u32[]{:S(2)}) collective-permute-start(bf16[384,128]{1,0:T(8,128)(2,1)S(1)} %get-tuple-element.52), channel_id=1, source_target_pairs={{0,28},{4,24},{8,20},{12,16},{16,12},{20,8},{24,4},{28,0},{1,29},{... | collective-permute-start | bytes 294920 | tf_op jit(solution)/shard_map/ppermute | solution.py:671
  34.8 2.1 %shard_map.103 = (f32[8,768,128]{2,1,0:T(8,128)S(1)}, f32[8,16,128]{2,1,0:T(8,128)S(1)}) custom-call(s32[8]{0:T(128)S(1)} %broadcast_xor_fusion.order_ref, bf16[768,768]{1,0:T(8,128)(2,1)S(1)} %copy-done.2, f32[3,3,1024]{2,1,0:T(4,128)S(1)} %copy-done.6, bf16[8,4,128,1024]{3,2,1,0:T(8,128)(2,1)S(1)} %shard_map.100.after_ref.refs_5_.rows_ref, ...), custom_call_target="tpu_custom_call" | custom-call | flops 1207959552 | bytes 9437184 | tf_op jit(solution)/shard_map/pallas_call | solution.py:465
  36.9 2.5 %shard_map.102 = (f32[8,384,128]{2,1,0:T(8,128)S(1)}, f32[8,384,128]{2,1,0:T(8,128)S(1)}) custom-call(s32[8]{0:T(128)S(1)} %broadcast_xor_fusion.order_ref, bf16[384,1024]{1,0:T(8,128)(2,1)S(1)} %copy-done.4, bf16[384,1024]{1,0:T(8,128)(2,1)S(1)} %copy-done, bf16[384,1024]{1,0:T(8,128)(2,1)S(1)} %copy-done.1, ...), custom_call_target="tpu_custom_call" | custom-call | flops 7864320 | bytes 61440 | tf_op jit(solution)/shard_map/pallas_call | solution.py:407
  39.5 0.0 copy-start.5
  39.5 1.4 %shard_map.105.early_ref = f32[8,768,128]{2,1,0:T(8,128)S(1)} custom-call(s32[8]{0:T(128)S(1)} %broadcast_xor_fusion.order_ref, bf16[768,768]{1,0:T(8,128)(2,1)S(1)} %copy-done.2, f32[8,16,128]{2,1,0:T(8,128)S(1)} %get-tuple-element.44.first_ref, bf16[384,128]{1,0:T(8,128)(2,1)S(1)} %get-tuple-element.45.refs_0_, ...), custom_call_target="tpu_custom_call" | custom-call | flops 603979776 | bytes 4718592 | tf_op jit(solution)/shard_map/pallas_call | solution.py:487
  40.9 0.0 collective-permute-done.10.refs_0_
  40.9 0.0 collective-permute-done.11.refs_1_
  40.9 0.7 collective-permute-done.13.refs_3_
  41.6 5.9 %shard_map.106 = (f32[8,768,128]{2,1,0:T(8,128)S(1)}, bf16[384,128]{1,0:T(8,128)(2,1)S(1)}, bf16[384,128]{1,0:T(8,128)(2,1)S(1)}, bf16[384,128]{1,0:T(8,128)(2,1...) custom-call(s32[8]{0:T(128)S(1)} %broadcast_xor_fusion.order_ref, ...), custom_call_target="tpu_custom_call", output_to_operand_aliasing={{0}: (4, {})} | custom-call | flops 2113929216 | bytes 16515072 | tf_op jit(solution)/shard_map/pallas_call | solution.py:557
  47.5 2.1 %collective-permute-start.18 = (bf16[384,128]{1,0:T(8,128)(2,1)S(1)}, bf16[384,128]{1,0:T(8,128)(2,1)S(1)}, u32[]{:S(2)}, u32[]{:S(2)}) collective-permute-start(bf16[384,128]{1,0:T(8,128)(2,1)S(1)} %get-tuple-element.56), channel_id=1, source_target_pairs={{0,16},{4,20},{8,24},{12,28},{16,0},{20,4},{24,8},{28,12},{1,17},{... | collective-permute-start | bytes 294920 | tf_op jit(solution)/shard_map/ppermute | solution.py:671
  49.6 2.7 %collective-permute-start.21 = (bf16[384,128]{1,0:T(8,128)(2,1)S(1)}, bf16[384,128]{1,0:T(8,128)(2,1)S(1)}, u32[]{:S(2)}, u32[]{:S(2)}) collective-permute-start(bf16[384,128]{1,0:T(8,128)(2,1)S(1)} %get-tuple-element.57), channel_id=1, source_target_pairs={{0,4},{4,0},{8,12},{12,8},{16,20},{20,16},{24,28},{28,24},{1,5},{5... | collective-permute-start | bytes 294920 | tf_op jit(solution)/shard_map/ppermute | solution.py:671
  52.3 0.0 collective-permute-start.22
  52.3 1.2 %collective-permute-start.25 = (bf16[384,128]{1,0:T(8,128)(2,1)S(1)}, bf16[384,128]{1,0:T(8,128)(2,1)S(1)}, u32[]{:S(2)}, u32[]{:S(2)}) collective-permute-start(bf16[384,128]{1,0:T(8,128)(2,1)S(1)} %get-tuple-element.59), channel_id=1, source_target_pairs={{0,12},{4,8},{8,4},{12,0},{16,28},{20,24},{24,20},{28,16},{1,13},{... | collective-permute-start | bytes 294920 | tf_op jit(solution)/shard_map/ppermute | solution.py:671
  53.5 1.3 %collective-permute-start.26 = (bf16[384,128]{1,0:T(8,128)(2,1)S(1)}, bf16[384,128]{1,0:T(8,128)(2,1)S(1)}, u32[]{:S(2)}, u32[]{:S(2)}) collective-permute-start(bf16[384,128]{1,0:T(8,128)(2,1)S(1)} %get-tuple-element.60), channel_id=1, source_target_pairs={{0,20},{4,16},{8,28},{12,24},{16,4},{20,0},{24,12},{28,8},{1,21},{... | collective-permute-start | bytes 294920 | tf_op jit(solution)/shard_map/ppermute | solution.py:671
  54.8 2.0 %collective-permute-start.14 = (bf16[384,128]{1,0:T(8,128)(2,1)S(1)}, bf16[384,128]{1,0:T(8,128)(2,1)S(1)}, u32[]{:S(2)}, u32[]{:S(2)}) collective-permute-start(bf16[384,128]{1,0:T(8,128)(2,1)S(1)} %get-tuple-element.53), channel_id=1, source_target_pairs={{0,24},{4,28},{8,16},{12,20},{16,8},{20,12},{24,0},{28,4},{1,25},{... | collective-permute-start | bytes 294920 | tf_op jit(solution)/shard_map/ppermute | solution.py:671
  56.8 1.2 %collective-permute-start.15 = (bf16[384,128]{1,0:T(8,128)(2,1)S(1)}, bf16[384,128]{1,0:T(8,128)(2,1)S(1)}, u32[]{:S(2)}, u32[]{:S(2)}) collective-permute-start(bf16[384,128]{1,0:T(8,128)(2,1)S(1)} %get-tuple-element.54), channel_id=1, source_target_pairs={{0,28},{4,24},{8,20},{12,16},{16,12},{20,8},{24,4},{28,0},{1,29},{... | collective-permute-start | bytes 294920 | tf_op jit(solution)/shard_map/ppermute | solution.py:671
  58.0 0.1 shard_map.109.refs_0_
  58.0 0.0 collective-permute-done.22.refs_1_
  58.1 1.3 %collective-permute-start.19 = (bf16[384,256]{1,0:T(8,128)(2,1)S(1)}, bf16[384,256]{1,0:T(8,128)(2,1)S(1)}, u32[]{:S(2)}, u32[]{:S(2)}) collective-permute-start(bf16[384,256]{1,0:T(8,128)(2,1)S(1)} %shard_map.109.refs_0_), channel_id=1, source_target_pairs={{0,2},{1,3},{2,0},{3,1},{4,6},{5,7},{6,4},{7,5},{8,10},{9,11},{10,... | collective-permute-start | bytes 589832 | tf_op jit(solution)/shard_map/ppermute | solution.py:698
  59.4 0.1 shard_map.111.refs_0_
  59.4 0.0 collective-permute-done.25.refs_0_
  59.4 0.3 collective-permute-start.23
  59.7 0.1 collective-permute-done.26.refs_1_
  59.8 0.1 shard_map.113.refs_0_
  59.9 1.3 %collective-permute-start.27 = (bf16[384,256]{1,0:T(8,128)(2,1)S(1)}, bf16[384,256]{1,0:T(8,128)(2,1)S(1)}, u32[]{:S(2)}, u32[]{:S(2)}) collective-permute-start(bf16[384,256]{1,0:T(8,128)(2,1)S(1)} %shard_map.113.refs_0_), channel_id=1, source_target_pairs={{0,2},{1,3},{2,0},{3,1},{4,6},{5,7},{6,4},{7,5},{8,10},{9,11},{10,... | collective-permute-start | bytes 589832 | tf_op jit(solution)/shard_map/ppermute | solution.py:698
  61.2 1.1 %collective-permute-done.14.refs_0_ = bf16[384,128]{1,0:T(8,128)(2,1)S(1)} collective-permute-done((bf16[384,128]{1,0:T(8,128)(2,1)S(1)}, bf16[384,128]{1,0:T(8,128)(2,1)S(1)}, u32[]{:S(2)}, u32[]{:S(2)}) %collective-permute-start.14) | collective-permute-done | bytes 98336 | tf_op jit(solution)/shard_map/ppermute | solution.py:671
  62.3 1.7 %collective-permute-done.15.refs_1_ = bf16[384,128]{1,0:T(8,128)(2,1)S(1)} collective-permute-done((bf16[384,128]{1,0:T(8,128)(2,1)S(1)}, bf16[384,128]{1,0:T(8,128)(2,1)S(1)}, u32[]{:S(2)}, u32[]{:S(2)}) %collective-permute-start.15) | collective-permute-done | bytes 98336 | tf_op jit(solution)/shard_map/ppermute | solution.py:671
  64.1 0.1 shard_map.107.refs_0_
  64.1 1.3 %collective-permute-start.16 = (bf16[384,256]{1,0:T(8,128)(2,1)S(1)}, bf16[384,256]{1,0:T(8,128)(2,1)S(1)}, u32[]{:S(2)}, u32[]{:S(2)}) collective-permute-start(bf16[384,256]{1,0:T(8,128)(2,1)S(1)} %shard_map.107.refs_0_), channel_id=1, source_target_pairs={{0,2},{1,3},{2,0},{3,1},{4,6},{5,7},{6,4},{7,5},{8,10},{9,11},{10,... | collective-permute-start | bytes 589832 | tf_op jit(solution)/shard_map/ppermute | solution.py:698
  65.4 0.0 collective-permute-done.19.refs_1_
  65.5 5.7 %collective-permute-start.20 = (bf16[384,512]{1,0:T(8,128)(2,1)S(1)}, bf16[384,512]{1,0:T(8,128)(2,1)S(1)}, u32[]{:S(2)}, u32[]{:S(2)}) collective-permute-start(bf16[384,512]{1,0:T(8,128)(2,1)S(1)} %shard_map.110.refs_0_), channel_id=1, source_target_pairs={{0,1},{1,0},{2,3},{3,2},{4,5},{5,4},{6,7},{7,6},{8,9},{9,8},{10,11... | collective-permute-start | bytes 1179656 | tf_op jit(solution)/shard_map/ppermute | solution.py:700
  71.2 0.0 collective-permute-done.23.refs_1_
  71.2 2.7 %collective-permute-start.24 = (bf16[384,512]{1,0:T(8,128)(2,1)S(1)}, bf16[384,512]{1,0:T(8,128)(2,1)S(1)}, u32[]{:S(2)}, u32[]{:S(2)}) collective-permute-start(bf16[384,512]{1,0:T(8,128)(2,1)S(1)} %shard_map.112.refs_2_), channel_id=1, source_target_pairs={{0,1},{1,0},{2,3},{3,2},{4,5},{5,4},{6,7},{7,6},{8,9},{9,8},{10,11... | collective-permute-start | bytes 1179656 | tf_op jit(solution)/shard_map/ppermute | solution.py:700
  74.0 0.0 collective-permute-done.27.refs_1_
  74.0 2.1 %collective-permute-start.28 = (bf16[384,512]{1,0:T(8,128)(2,1)S(1)}, bf16[384,512]{1,0:T(8,128)(2,1)S(1)}, u32[]{:S(2)}, u32[]{:S(2)}) collective-permute-start(bf16[384,512]{1,0:T(8,128)(2,1)S(1)} %shard_map.114.refs_4_), channel_id=1, source_target_pairs={{0,1},{1,0},{2,3},{3,2},{4,5},{5,4},{6,7},{7,6},{8,9},{9,8},{10,11... | collective-permute-start | bytes 1179656 | tf_op jit(solution)/shard_map/ppermute | solution.py:700
  76.1 0.0 collective-permute-done.16.refs_1_
  76.1 0.1 shard_map.108.refs_0_
  76.1 2.1 %collective-permute-start.17 = (bf16[384,512]{1,0:T(8,128)(2,1)S(1)}, bf16[384,512]{1,0:T(8,128)(2,1)S(1)}, u32[]{:S(2)}, u32[]{:S(2)}) collective-permute-start(bf16[384,512]{1,0:T(8,128)(2,1)S(1)} %shard_map.108.refs_0_), channel_id=1, source_target_pairs={{0,1},{1,0},{2,3},{3,2},{4,5},{5,4},{6,7},{7,6},{8,9},{9,8},{10,11... | collective-permute-start | bytes 1179656 | tf_op jit(solution)/shard_map/ppermute | solution.py:700
  78.2 0.0 collective-permute-done.20.refs_1_
  78.2 0.0 collective-permute-done.24.refs_3_
  78.2 2.6 %shard_map.115.refs_2_ = f32[384,1024]{1,0:T(8,128)S(1)} custom-call(bf16[8,4,128,1024]{3,2,1,0:T(8,128)(2,1)S(1)} %shard_map.100.after_ref.refs_5_.rows_ref, bf16[384,512]{1,0:T(8,128)(2,1)S(1)} %shard_map.110.refs_0_, bf16[384,512]{1,0:T(8,128)(2,1)S(1)} %collective-permute-done.20.refs_1_, bf16[384,512]{1,0:T(8,128)(2,1)S(1)} %shard_map.112.refs_2_, ...), custom_call_target="tpu_custom_call" | custom-call | tf_op jit(solution)/shard_map/pallas_call | solution.py:656
  80.9 1.9 %shard_map.116 = bf16[384,1024]{1,0:T(8,128)(2,1)} custom-call(bf16[8,4,128,1024]{3,2,1,0:T(8,128)(2,1)S(1)} %shard_map.100.after_ref.refs_5_.rows_ref, bf16[384,512]{1,0:T(8,128)(2,1)S(1)} %shard_map.108.refs_0_, bf16[384,512]{1,0:T(8,128)(2,1)S(1)} %collective-permute-done.17.refs_1_, f32[384,1024]{1,0:T(8,128)S(1)} %shard_map.115.refs_2_), custom_call_target="tpu_custom_call" | custom-call | tf_op jit(solution)/shard_map/pallas_call | solution.py:656
  (32 shorter events, 0.1 us)
Async XLA Ops:
  0.0 19.3 %copy-start.9 = (s32[8]{0:T(128)S(1)}, s32[8]{0:T(128)}, u32[]{:S(2)}) copy-start(s32[8]{0:T(128)} %constant.15.clone) | copy-start | bytes 100
  0.0 19.3 %copy-start.1 = (bf16[384,1024]{1,0:T(8,128)(2,1)S(1)}, bf16[384,1024]{1,0:T(8,128)(2,1)}, u32[]{:S(2)}) copy-start(bf16[384,1024]{1,0:T(8,128)(2,1)} %value_ref.3) | copy-start | bytes 2359300
  0.0 19.3 %copy-start = (bf16[384,1024]{1,0:T(8,128)(2,1)S(1)}, bf16[384,1024]{1,0:T(8,128)(2,1)}, u32[]{:S(2)}) copy-start(bf16[384,1024]{1,0:T(8,128)(2,1)} %gate_ref.3) | copy-start | bytes 2359300
  0.0 19.3 %copy-start.6 = (f32[3,3,1024]{2,1,0:T(4,128)S(1)}, f32[3,3,1024]{2,1,0:T(4,128)}, u32[]{:S(2)}) copy-start(f32[3,3,1024]{2,1,0:T(4,128)} %taps_ref.3) | copy-start | bytes 110596
  2.6 13.7 %collective-permute-start = (bf16[528,128]{1,0:T(8,128)(2,1)}, bf16[528,128]{1,0:T(8,128)(2,1)S(1)}, u32[]{:S(2)}, u32[]{:S(2)}) collective-permute-start(bf16[528,128]{1,0:T(8,128)(2,1)} %get-tuple-element.33), channel_id=1, source_target_pairs={{0,4},{4,0},{8,12},{12,8},{16,20},{20,16},{24,28},{28,24},{1,5},{5... | collective-permute-start | bytes 405512 | tf_op jit(solution)/shard_map/ppermute | solution.py:671
  4.7 5.8 %collective-permute-start.3 = (bf16[400,128]{1,0:T(8,128)(2,1)}, bf16[400,128]{1,0:T(8,128)(2,1)S(1)}, u32[]{:S(2)}, u32[]{:S(2)}) collective-permute-start(bf16[400,128]{1,0:T(8,128)(2,1)} %get-tuple-element.39), channel_id=1, source_target_pairs={{0,16},{4,20},{8,24},{12,28},{16,0},{20,4},{24,8},{28,12},{1,17},{... | collective-permute-start | bytes 307208 | tf_op jit(solution)/shard_map/ppermute | solution.py:671
  7.0 14.2 %collective-permute-start.4 = (bf16[400,128]{1,0:T(8,128)(2,1)}, bf16[400,128]{1,0:T(8,128)(2,1)S(1)}, u32[]{:S(2)}, u32[]{:S(2)}) collective-permute-start(bf16[400,128]{1,0:T(8,128)(2,1)} %get-tuple-element.40), channel_id=1, source_target_pairs={{0,20},{4,16},{8,28},{12,24},{16,4},{20,0},{24,12},{28,8},{1,21},{... | collective-permute-start | bytes 307208 | tf_op jit(solution)/shard_map/ppermute | solution.py:671
  7.0 14.6 %collective-permute-start.5 = (bf16[400,128]{1,0:T(8,128)(2,1)}, bf16[400,128]{1,0:T(8,128)(2,1)S(1)}, u32[]{:S(2)}, u32[]{:S(2)}) collective-permute-start(bf16[400,128]{1,0:T(8,128)(2,1)} %get-tuple-element.41), channel_id=1, source_target_pairs={{0,8},{4,12},{8,0},{12,4},{16,24},{20,28},{24,16},{28,20},{1,9},{5... | collective-permute-start | bytes 307208 | tf_op jit(solution)/shard_map/ppermute | solution.py:671
  8.3 19.5 %collective-permute-start.6 = (bf16[400,128]{1,0:T(8,128)(2,1)}, bf16[400,128]{1,0:T(8,128)(2,1)S(1)}, u32[]{:S(2)}, u32[]{:S(2)}) collective-permute-start(bf16[400,128]{1,0:T(8,128)(2,1)} %get-tuple-element.42), channel_id=1, source_target_pairs={{0,24},{4,28},{8,16},{12,20},{16,8},{20,12},{24,0},{28,4},{1,25},{... | collective-permute-start | bytes 307208 | tf_op jit(solution)/shard_map/ppermute | solution.py:671
  10.5 19.5 %collective-permute-start.1 = (bf16[528,128]{1,0:T(8,128)(2,1)}, bf16[528,128]{1,0:T(8,128)(2,1)S(1)}, u32[]{:S(2)}, u32[]{:S(2)}) collective-permute-start(bf16[528,128]{1,0:T(8,128)(2,1)} %get-tuple-element.34), channel_id=1, source_target_pairs={{0,12},{4,8},{8,4},{12,0},{16,28},{20,24},{24,20},{28,16},{1,13},{... | collective-permute-start | bytes 405512 | tf_op jit(solution)/shard_map/ppermute | solution.py:671
  16.4 15.1 %collective-permute-start.2 = (bf16[528,128]{1,0:T(8,128)(2,1)}, bf16[528,128]{1,0:T(8,128)(2,1)S(1)}, u32[]{:S(2)}, u32[]{:S(2)}) collective-permute-start(bf16[528,128]{1,0:T(8,128)(2,1)} %get-tuple-element.35), channel_id=1, source_target_pairs={{0,28},{4,24},{8,20},{12,16},{16,12},{20,8},{24,4},{28,0},{1,29},{... | collective-permute-start | bytes 405512 | tf_op jit(solution)/shard_map/ppermute | solution.py:671
  21.2 10.3 %collective-permute-start.7 = (bf16[384,128]{1,0:T(8,128)(2,1)S(1)}, bf16[384,128]{1,0:T(8,128)(2,1)S(1)}, u32[]{:S(2)}, u32[]{:S(2)}) collective-permute-start(bf16[384,128]{1,0:T(8,128)(2,1)S(1)} %get-tuple-element.46), channel_id=1, source_target_pairs={{0,16},{4,20},{8,24},{12,28},{16,0},{20,4},{24,8},{28,12},{1,17},{... | collective-permute-start | bytes 294920 | tf_op jit(solution)/shard_map/ppermute | solution.py:671
  21.6 11.4 %collective-permute-start.8 = (bf16[384,128]{1,0:T(8,128)(2,1)S(1)}, bf16[384,128]{1,0:T(8,128)(2,1)S(1)}, u32[]{:S(2)}, u32[]{:S(2)}) collective-permute-start(bf16[384,128]{1,0:T(8,128)(2,1)S(1)} %get-tuple-element.47), channel_id=1, source_target_pairs={{0,4},{4,0},{8,12},{12,8},{16,20},{20,16},{24,28},{28,24},{1,5},{5... | collective-permute-start | bytes 294920 | tf_op jit(solution)/shard_map/ppermute | solution.py:671
  22.7 3.4 %copy-start.3 = (bf16[4096,1024]{1,0:T(8,128)(2,1)S(1)}, bf16[4096,1024]{1,0:T(8,128)(2,1)}, u32[]{:S(2)}) copy-start(bf16[4096,1024]{1,0:T(8,128)(2,1)} %weight_ref.1) | copy-start | bytes 25165828
  26.1 8.7 %copy-start.2 = (bf16[768,768]{1,0:T(8,128)(2,1)S(1)}, bf16[768,768]{1,0:T(8,128)(2,1)}, u32[]{:S(2)}) copy-start(bf16[768,768]{1,0:T(8,128)(2,1)} %constant.16.clone.table_ref) | copy-start | bytes 3538948
  26.1 8.7 %copy-start.7 = (bf16[400,128]{1,0:T(8,128)(2,1)S(1)}, bf16[400,128]{1,0:T(8,128)(2,1)}, u32[]{:S(2)}) copy-start(bf16[400,128]{1,0:T(8,128)(2,1)} %get-tuple-element.38.refs_0_) | copy-start | bytes 307204
  27.9 11.6 %collective-permute-start.9 = (bf16[384,128]{1,0:T(8,128)(2,1)S(1)}, bf16[384,128]{1,0:T(8,128)(2,1)S(1)}, u32[]{:S(2)}, u32[]{:S(2)}) collective-permute-start(bf16[384,128]{1,0:T(8,128)(2,1)S(1)} %get-tuple-element.48), channel_id=1, source_target_pairs={{0,20},{4,16},{8,28},{12,24},{16,4},{20,0},{24,12},{28,8},{1,21},{... | collective-permute-start | bytes 294920 | tf_op jit(solution)/shard_map/ppermute | solution.py:671
  30.0 10.9 %collective-permute-start.10 = (bf16[384,128]{1,0:T(8,128)(2,1)S(1)}, bf16[384,128]{1,0:T(8,128)(2,1)S(1)}, u32[]{:S(2)}, u32[]{:S(2)}) collective-permute-start(bf16[384,128]{1,0:T(8,128)(2,1)S(1)} %get-tuple-element.49), channel_id=1, source_target_pairs={{0,8},{4,12},{8,0},{12,4},{16,24},{20,28},{24,16},{28,20},{1,9},{5... | collective-permute-start | bytes 294920 | tf_op jit(solution)/shard_map/ppermute | solution.py:671
  31.4 9.5 %collective-permute-start.11 = (bf16[384,128]{1,0:T(8,128)(2,1)S(1)}, bf16[384,128]{1,0:T(8,128)(2,1)S(1)}, u32[]{:S(2)}, u32[]{:S(2)}) collective-permute-start(bf16[384,128]{1,0:T(8,128)(2,1)S(1)} %get-tuple-element.50), channel_id=1, source_target_pairs={{0,24},{4,28},{8,16},{12,20},{16,8},{20,12},{24,0},{28,4},{1,25},{... | collective-permute-start | bytes 294920 | tf_op jit(solution)/shard_map/ppermute | solution.py:671
  31.5 9.4 %collective-permute-start.12 = (bf16[384,128]{1,0:T(8,128)(2,1)S(1)}, bf16[384,128]{1,0:T(8,128)(2,1)S(1)}, u32[]{:S(2)}, u32[]{:S(2)}) collective-permute-start(bf16[384,128]{1,0:T(8,128)(2,1)S(1)} %get-tuple-element.51), channel_id=1, source_target_pairs={{0,12},{4,8},{8,4},{12,0},{16,28},{20,24},{24,20},{28,16},{1,13},{... | collective-permute-start | bytes 294920 | tf_op jit(solution)/shard_map/ppermute | solution.py:671
  33.0 8.6 %collective-permute-start.13 = (bf16[384,128]{1,0:T(8,128)(2,1)S(1)}, bf16[384,128]{1,0:T(8,128)(2,1)S(1)}, u32[]{:S(2)}, u32[]{:S(2)}) collective-permute-start(bf16[384,128]{1,0:T(8,128)(2,1)S(1)} %get-tuple-element.52), channel_id=1, source_target_pairs={{0,28},{4,24},{8,20},{12,16},{16,12},{20,8},{24,4},{28,0},{1,29},{... | collective-permute-start | bytes 294920 | tf_op jit(solution)/shard_map/ppermute | solution.py:671
  34.8 2.1 %copy-start.4 = (bf16[384,1024]{1,0:T(8,128)(2,1)S(1)}, bf16[384,1024]{1,0:T(8,128)(2,1)}, u32[]{:S(2)}) copy-start(bf16[384,1024]{1,0:T(8,128)(2,1)} %late_ref.1) | copy-start | bytes 2359300
  34.8 2.1 %copy-start.8 = (f32[1024]{0:T(1024)S(1)}, f32[1024]{0:T(1024)}, u32[]{:S(2)}) copy-start(f32[1024]{0:T(1024)} %param.15) | copy-start | bytes 12292
  39.5 2.1 %copy-start.5 = (bf16[384,2304]{1,0:T(8,128)(2,1)S(1)}, bf16[384,2304]{1,0:T(8,128)(2,1)}, u32[]{:S(2)}) copy-start(bf16[384,2304]{1,0:T(8,128)(2,1)} %constant.17.clone.inverse_ref) | copy-start | bytes 5308420
  47.5 7.3 %collective-permute-start.18 = (bf16[384,128]{1,0:T(8,128)(2,1)S(1)}, bf16[384,128]{1,0:T(8,128)(2,1)S(1)}, u32[]{:S(2)}, u32[]{:S(2)}) collective-permute-start(bf16[384,128]{1,0:T(8,128)(2,1)S(1)} %get-tuple-element.56), channel_id=1, source_target_pairs={{0,16},{4,20},{8,24},{12,28},{16,0},{20,4},{24,8},{28,12},{1,17},{... | collective-permute-start | bytes 294920 | tf_op jit(solution)/shard_map/ppermute | solution.py:671
  49.6 7.2 %collective-permute-start.21 = (bf16[384,128]{1,0:T(8,128)(2,1)S(1)}, bf16[384,128]{1,0:T(8,128)(2,1)S(1)}, u32[]{:S(2)}, u32[]{:S(2)}) collective-permute-start(bf16[384,128]{1,0:T(8,128)(2,1)S(1)} %get-tuple-element.57), channel_id=1, source_target_pairs={{0,4},{4,0},{8,12},{12,8},{16,20},{20,16},{24,28},{28,24},{1,5},{5... | collective-permute-start | bytes 294920 | tf_op jit(solution)/shard_map/ppermute | solution.py:671
  52.3 5.7 %collective-permute-start.22 = (bf16[384,128]{1,0:T(8,128)(2,1)S(1)}, bf16[384,128]{1,0:T(8,128)(2,1)S(1)}, u32[]{:S(2)}, u32[]{:S(2)}) collective-permute-start(bf16[384,128]{1,0:T(8,128)(2,1)S(1)} %get-tuple-element.58), channel_id=1, source_target_pairs={{0,8},{4,12},{8,0},{12,4},{16,24},{20,28},{24,16},{28,20},{1,9},{5... | collective-permute-start | bytes 294920 | tf_op jit(solution)/shard_map/ppermute | solution.py:671
  52.3 7.1 %collective-permute-start.25 = (bf16[384,128]{1,0:T(8,128)(2,1)S(1)}, bf16[384,128]{1,0:T(8,128)(2,1)S(1)}, u32[]{:S(2)}, u32[]{:S(2)}) collective-permute-start(bf16[384,128]{1,0:T(8,128)(2,1)S(1)} %get-tuple-element.59), channel_id=1, source_target_pairs={{0,12},{4,8},{8,4},{12,0},{16,28},{20,24},{24,20},{28,16},{1,13},{... | collective-permute-start | bytes 294920 | tf_op jit(solution)/shard_map/ppermute | solution.py:671
  53.5 6.3 %collective-permute-start.26 = (bf16[384,128]{1,0:T(8,128)(2,1)S(1)}, bf16[384,128]{1,0:T(8,128)(2,1)S(1)}, u32[]{:S(2)}, u32[]{:S(2)}) collective-permute-start(bf16[384,128]{1,0:T(8,128)(2,1)S(1)} %get-tuple-element.60), channel_id=1, source_target_pairs={{0,20},{4,16},{8,28},{12,24},{16,4},{20,0},{24,12},{28,8},{1,21},{... | collective-permute-start | bytes 294920 | tf_op jit(solution)/shard_map/ppermute | solution.py:671
  54.8 7.5 %collective-permute-start.14 = (bf16[384,128]{1,0:T(8,128)(2,1)S(1)}, bf16[384,128]{1,0:T(8,128)(2,1)S(1)}, u32[]{:S(2)}, u32[]{:S(2)}) collective-permute-start(bf16[384,128]{1,0:T(8,128)(2,1)S(1)} %get-tuple-element.53), channel_id=1, source_target_pairs={{0,24},{4,28},{8,16},{12,20},{16,8},{20,12},{24,0},{28,4},{1,25},{... | collective-permute-start | bytes 294920 | tf_op jit(solution)/shard_map/ppermute | solution.py:671
  56.8 7.3 %collective-permute-start.15 = (bf16[384,128]{1,0:T(8,128)(2,1)S(1)}, bf16[384,128]{1,0:T(8,128)(2,1)S(1)}, u32[]{:S(2)}, u32[]{:S(2)}) collective-permute-start(bf16[384,128]{1,0:T(8,128)(2,1)S(1)} %get-tuple-element.54), channel_id=1, source_target_pairs={{0,28},{4,24},{8,20},{12,16},{16,12},{20,8},{24,4},{28,0},{1,29},{... | collective-permute-start | bytes 294920 | tf_op jit(solution)/shard_map/ppermute | solution.py:671
  58.1 7.4 %collective-permute-start.19 = (bf16[384,256]{1,0:T(8,128)(2,1)S(1)}, bf16[384,256]{1,0:T(8,128)(2,1)S(1)}, u32[]{:S(2)}, u32[]{:S(2)}) collective-permute-start(bf16[384,256]{1,0:T(8,128)(2,1)S(1)} %shard_map.109.refs_0_), channel_id=1, source_target_pairs={{0,2},{1,3},{2,0},{3,1},{4,6},{5,7},{6,4},{7,5},{8,10},{9,11},{10,... | collective-permute-start | bytes 589832 | tf_op jit(solution)/shard_map/ppermute | solution.py:698
  59.4 11.8 %collective-permute-start.23 = (bf16[384,256]{1,0:T(8,128)(2,1)S(1)}, bf16[384,256]{1,0:T(8,128)(2,1)S(1)}, u32[]{:S(2)}, u32[]{:S(2)}) collective-permute-start(bf16[384,256]{1,0:T(8,128)(2,1)S(1)} %shard_map.111.refs_0_), channel_id=1, source_target_pairs={{0,2},{1,3},{2,0},{3,1},{4,6},{5,7},{6,4},{7,5},{8,10},{9,11},{10,... | collective-permute-start | bytes 589832 | tf_op jit(solution)/shard_map/ppermute | solution.py:698
  59.9 14.0 %collective-permute-start.27 = (bf16[384,256]{1,0:T(8,128)(2,1)S(1)}, bf16[384,256]{1,0:T(8,128)(2,1)S(1)}, u32[]{:S(2)}, u32[]{:S(2)}) collective-permute-start(bf16[384,256]{1,0:T(8,128)(2,1)S(1)} %shard_map.113.refs_0_), channel_id=1, source_target_pairs={{0,2},{1,3},{2,0},{3,1},{4,6},{5,7},{6,4},{7,5},{8,10},{9,11},{10,... | collective-permute-start | bytes 589832 | tf_op jit(solution)/shard_map/ppermute | solution.py:698
  64.1 11.9 %collective-permute-start.16 = (bf16[384,256]{1,0:T(8,128)(2,1)S(1)}, bf16[384,256]{1,0:T(8,128)(2,1)S(1)}, u32[]{:S(2)}, u32[]{:S(2)}) collective-permute-start(bf16[384,256]{1,0:T(8,128)(2,1)S(1)} %shard_map.107.refs_0_), channel_id=1, source_target_pairs={{0,2},{1,3},{2,0},{3,1},{4,6},{5,7},{6,4},{7,5},{8,10},{9,11},{10,... | collective-permute-start | bytes 589832 | tf_op jit(solution)/shard_map/ppermute | solution.py:698
  65.5 12.7 %collective-permute-start.20 = (bf16[384,512]{1,0:T(8,128)(2,1)S(1)}, bf16[384,512]{1,0:T(8,128)(2,1)S(1)}, u32[]{:S(2)}, u32[]{:S(2)}) collective-permute-start(bf16[384,512]{1,0:T(8,128)(2,1)S(1)} %shard_map.110.refs_0_), channel_id=1, source_target_pairs={{0,1},{1,0},{2,3},{3,2},{4,5},{5,4},{6,7},{7,6},{8,9},{9,8},{10,11... | collective-permute-start | bytes 1179656 | tf_op jit(solution)/shard_map/ppermute | solution.py:700
  71.2 7.0 %collective-permute-start.24 = (bf16[384,512]{1,0:T(8,128)(2,1)S(1)}, bf16[384,512]{1,0:T(8,128)(2,1)S(1)}, u32[]{:S(2)}, u32[]{:S(2)}) collective-permute-start(bf16[384,512]{1,0:T(8,128)(2,1)S(1)} %shard_map.112.refs_2_), channel_id=1, source_target_pairs={{0,1},{1,0},{2,3},{3,2},{4,5},{5,4},{6,7},{7,6},{8,9},{9,8},{10,11... | collective-permute-start | bytes 1179656 | tf_op jit(solution)/shard_map/ppermute | solution.py:700
  74.0 4.2 %collective-permute-start.28 = (bf16[384,512]{1,0:T(8,128)(2,1)S(1)}, bf16[384,512]{1,0:T(8,128)(2,1)S(1)}, u32[]{:S(2)}, u32[]{:S(2)}) collective-permute-start(bf16[384,512]{1,0:T(8,128)(2,1)S(1)} %shard_map.114.refs_4_), channel_id=1, source_target_pairs={{0,1},{1,0},{2,3},{3,2},{4,5},{5,4},{6,7},{7,6},{8,9},{9,8},{10,11... | collective-permute-start | bytes 1179656 | tf_op jit(solution)/shard_map/ppermute | solution.py:700
  76.1 4.7 %collective-permute-start.17 = (bf16[384,512]{1,0:T(8,128)(2,1)S(1)}, bf16[384,512]{1,0:T(8,128)(2,1)S(1)}, u32[]{:S(2)}, u32[]{:S(2)}) collective-permute-start(bf16[384,512]{1,0:T(8,128)(2,1)S(1)} %shard_map.108.refs_0_), channel_id=1, source_target_pairs={{0,1},{1,0},{2,3},{3,2},{4,5},{5,4},{6,7},{7,6},{8,9},{9,8},{10,11... | collective-permute-start | bytes 1179656 | tf_op jit(solution)/shard_map/ppermute | solution.py:700

commit v5 on v4

--- a/solution.py
+++ b/solution.py
@@ -321,20 +321,21 @@
     ends = [ref[...].astype(F32)[-KEEP:] for ref in last_refs]
     ends += [ref[...].astype(F32)[:KEEP] for ref in (gate_top, value_top)]
     ends.append(jnp.zeros((TILE - 5 * KEEP, width), F32))
-    ends_ref[...] = jnp.concatenate(ends, axis=0).astype(BF16)
+    ends_ref[...] = jnp.concatenate(ends, axis=0)
     for place, out_ref in enumerate(out_refs):
         at = pl.ds(pl.multiple_of((own ^ OFFSETS[place]) * LANES, LANES), LANES)
         out_ref[:rows] = filter_ref[:, at].astype(BF16)
-        out_ref[rows : rows + TILE] = ends_ref[:, at]
+        out_ref[rows : rows + TILE] = ends_ref[:, at].astype(BF16)
         if OFFSETS[place] in NEXT_OFFSETS:
-            for part in range(width // LANES):
-                out_ref[rows + (1 + part) * TILE : rows + (2 + part) * TILE] = ends_ref[:, part * LANES : (part + 1) * LANES]
+            for part in range(width // (2 * LANES)):
+                pair = [ends_ref[: TILE // 2, q * LANES : (q + 1) * LANES] for q in (2 * part, 2 * part + 1)]
+                out_ref[rows + (1 + part) * TILE : rows + (2 + part) * TILE] = jnp.concatenate(pair, axis=0).astype(BF16)
 
 
 def cut_filter(long_filter, out_gate, in_gate, values):
     rows, width = long_filter.shape
     count = width // LANES
-    heights = [rows + TILE * (1 + count * (offset in NEXT_OFFSETS)) for offset in OFFSETS]
+    heights = [rows + TILE * (1 + count // 2 * (offset in NEXT_OFFSETS)) for offset in OFFSETS]
     top = pl.BlockSpec((TILE, width), lambda i: (0, 0))
     last = pl.BlockSpec((TILE, width), lambda i: (rows // TILE - 1, 0))
     return pl.pallas_call(
@@ -343,7 +344,7 @@
         in_specs=[pl.BlockSpec((rows, width), lambda i: (0, 0))] + [last] * 3 + [top] * 2,
         out_specs=[pl.BlockSpec((height, LANES), lambda i: (0, 0)) for height in heights],
         out_shape=[jax.ShapeDtypeStruct((height, LANES), BF16) for height in heights],
-        scratch_shapes=[pltpu.VMEM((TILE, width), BF16)],
+        scratch_shapes=[pltpu.VMEM((TILE, width), F32)],
         compiler_params=pltpu.CompilerParams(vmem_limit_bytes=CUT_VMEM << 20),
         cost_estimate=cost(rows * width),
     )(long_filter, out_gate, in_gate, values, in_gate, values)
@@ -382,10 +383,11 @@
     own = order_ref[0]
     for place in range(late_out.shape[0]):
         at = lanes_at(order_ref, place)
-        start = pl.multiple_of(rows + (1 + order_ref[place]) * TILE, TILE)
-        rim = jnp.zeros((TILE, LANES), F32)
+        start = pl.multiple_of(rows + (1 + order_ref[place] // 2) * TILE, TILE)
+        rim = jnp.zeros((TILE // 2, LANES), F32)
         for offset, ref in zip(NEXT_OFFSETS, before_refs, strict=True):
             given = ref[pl.ds(start, TILE), :].astype(F32)
+            given = jnp.where(order_ref[place] % 2 == 1, given[TILE // 2 :], given[: TILE // 2])
             rim = jnp.where((own & offset) == (offset + 1) // 2, given, rim)
         late, first, second = (
             short_conv(

time: 82.9 us -> 82.1 us (level)
    ppermute x4, starting transfers between devices: 12.6 us -> 13.5 us  [on_device_slices(): lax.ppermute(joined, 'ch', [(i, i ^ 1) for i in range(4)])]
  transfers between devices with their start and end apart: 29 -> 29, of which waited for: 4 -> 2; matrix products, arithmetic and copies ran while one was open for 0% -> 0% of each run, Pallas kernels for 15% -> 15%
where the time goes in v5:
time: 82.1 us; the launch traced here: 82 us
  starting transfers between devices  52.1 us (63%)
  Pallas kernels  23 us (28%)
  local copies, waits for them, and re-layouts  3.42 us (4%)
  waiting for transfers between devices  3.19 us (4%)
    ppermute x21, starting transfers between devices, swap_blocks(): lax.ppermute(blocks[place], 'seq', [(i, i ^ offset) for i in range(count)])  34.8 us
    ppermute x4, starting transfers between devices, on_device_slices(): lax.ppermute(joined, 'ch', [(i, i ^ 1) for i in range(4)])  13.5 us
    pallas_call x1, Pallas kernels, conv_slices(): pl.pallas_call(functools.partial(conv_slices_kernel, places), in_specs=[p...  5.92 us
    pallas_call x2, Pallas kernels, project_slices(): pl.pallas_call(functools.partial(project_kernel_slices, chunks), in_specs...  4.53 us
    ppermute x4, starting transfers between devices, on_device_slices(): across = lax.ppermute(mixed, 'ch', [(i, i ^ 2) for i in range(4)])  3.86 us
    unnamed x20, local copies, waits for them, and re-layouts  3.42 us
    ppermute x21, waiting for transfers between devices, swap_blocks(): lax.ppermute(blocks[place], 'seq', [(i, i ^ offset) for i in range(count)])  3.17 us
    pallas_call x1, Pallas kernels, cut_filter(): pl.pallas_call(cut_kernel, grid=(1,), in_specs=[pl.BlockSpec((rows, width...  2.6 us
  transfers between devices with their start and end apart: 29, of which 2 were waited for; matrix products, arithmetic and copies ran while one was open for 0% of the time, Pallas kernels for 15%

profile of v5, /device:TPU:1, one launch (start us, length us, event | category | flops | bytes accessed | tf_op | source)
XLA Modules:
  0.0 82.0 jit_solution(4550296390070622786)
XLA Ops:
  0.0 2.6 %shard_map.101 = (bf16[400,128]{1,0:T(8,128)(2,1)}, bf16[400,128]{1,0:T(8,128)(2,1)}, bf16[464,128]{1,0:T(8,128)(2,1)}, bf16[400,128]{1,0:T(8,128)(2,1)}, bf16[4...) custom-call(f32[384,1024]{1,0:T(8,128)} %filter_ref.1, ...), custom_call_target="tpu_custom_call" | custom-call | tf_op jit(solution)/shard_map/pallas_call | solution.py:341
  2.6 2.0 %collective-permute-start = (bf16[464,128]{1,0:T(8,128)(2,1)}, bf16[464,128]{1,0:T(8,128)(2,1)S(1)}, u32[]{:S(2)}, u32[]{:S(2)}) collective-permute-start(bf16[464,128]{1,0:T(8,128)(2,1)} %get-tuple-element.33), channel_id=1, source_target_pairs={{0,4},{4,0},{8,12},{12,8},{16,20},{20,16},{24,28},{28,24},{1,5},{5... | collective-permute-start | bytes 356360 | tf_op jit(solution)/shard_map/ppermute | solution.py:673
  4.7 2.3 %collective-permute-start.3 = (bf16[400,128]{1,0:T(8,128)(2,1)}, bf16[400,128]{1,0:T(8,128)(2,1)S(1)}, u32[]{:S(2)}, u32[]{:S(2)}) collective-permute-start(bf16[400,128]{1,0:T(8,128)(2,1)} %get-tuple-element.39), channel_id=1, source_target_pairs={{0,16},{4,20},{8,24},{12,28},{16,0},{20,4},{24,8},{28,12},{1,17},{... | collective-permute-start | bytes 307208 | tf_op jit(solution)/shard_map/ppermute | solution.py:673
  7.0 0.0 collective-permute-start.4
  7.0 1.3 %collective-permute-start.5 = (bf16[400,128]{1,0:T(8,128)(2,1)}, bf16[400,128]{1,0:T(8,128)(2,1)S(1)}, u32[]{:S(2)}, u32[]{:S(2)}) collective-permute-start(bf16[400,128]{1,0:T(8,128)(2,1)} %get-tuple-element.41), channel_id=1, source_target_pairs={{0,8},{4,12},{8,0},{12,4},{16,24},{20,28},{24,16},{28,20},{1,9},{5... | collective-permute-start | bytes 307208 | tf_op jit(solution)/shard_map/ppermute | solution.py:673
  8.3 2.2 %collective-permute-start.6 = (bf16[400,128]{1,0:T(8,128)(2,1)}, bf16[400,128]{1,0:T(8,128)(2,1)S(1)}, u32[]{:S(2)}, u32[]{:S(2)}) collective-permute-start(bf16[400,128]{1,0:T(8,128)(2,1)} %get-tuple-element.42), channel_id=1, source_target_pairs={{0,24},{4,28},{8,16},{12,20},{16,8},{20,12},{24,0},{28,4},{1,25},{... | collective-permute-start | bytes 307208 | tf_op jit(solution)/shard_map/ppermute | solution.py:673
  10.5 0.0 collective-permute-done.3.refs_1_
  10.5 5.9 %collective-permute-start.1 = (bf16[464,128]{1,0:T(8,128)(2,1)}, bf16[464,128]{1,0:T(8,128)(2,1)S(1)}, u32[]{:S(2)}, u32[]{:S(2)}) collective-permute-start(bf16[464,128]{1,0:T(8,128)(2,1)} %get-tuple-element.34), channel_id=1, source_target_pairs={{0,12},{4,8},{8,4},{12,0},{16,28},{20,24},{24,20},{28,16},{1,13},{... | collective-permute-start | bytes 356360 | tf_op jit(solution)/shard_map/ppermute | solution.py:673
  16.3 0.0 collective-permute-done.refs_0_.refs_2_.after_ref
  16.3 2.9 %collective-permute-start.2 = (bf16[464,128]{1,0:T(8,128)(2,1)}, bf16[464,128]{1,0:T(8,128)(2,1)S(1)}, u32[]{:S(2)}, u32[]{:S(2)}) collective-permute-start(bf16[464,128]{1,0:T(8,128)(2,1)} %get-tuple-element.35), channel_id=1, source_target_pairs={{0,28},{4,24},{8,20},{12,16},{16,12},{20,8},{24,4},{28,0},{1,29},{... | collective-permute-start | bytes 356360 | tf_op jit(solution)/shard_map/ppermute | solution.py:673
  19.3 1.9 %shard_map.104 = (bf16[384,128]{1,0:T(8,128)(2,1)S(1)}, bf16[384,128]{1,0:T(8,128)(2,1)S(1)}, bf16[384,128]{1,0:T(8,128)(2,1)S(1)}, bf16[384,128]{1,0:T(8,128)(2...) custom-call(s32[8]{0:T(128)S(1)} %broadcast_xor_fusion.order_ref, ...), custom_call_target="tpu_custom_call" | custom-call | flops 5505024 | bytes 43008 | tf_op jit(solution)/shard_map/pallas_call | solution.py:368
  21.2 0.0 collective-permute-done.4.refs_3_
  21.2 0.4 collective-permute-start.7
  21.6 0.0 collective-permute-done.5.refs_4_
  21.6 1.2 %collective-permute-start.8 = (bf16[384,128]{1,0:T(8,128)(2,1)S(1)}, bf16[384,128]{1,0:T(8,128)(2,1)S(1)}, u32[]{:S(2)}, u32[]{:S(2)}) collective-permute-start(bf16[384,128]{1,0:T(8,128)(2,1)S(1)} %get-tuple-element.47), channel_id=1, source_target_pairs={{0,4},{4,0},{8,12},{12,8},{16,20},{20,16},{24,28},{28,24},{1,5},{5... | collective-permute-start | bytes 294920 | tf_op jit(solution)/shard_map/ppermute | solution.py:673
  22.7 3.4 %copy-done.3 = bf16[4096,1024]{1,0:T(8,128)(2,1)S(1)} copy-done((bf16[4096,1024]{1,0:T(8,128)(2,1)S(1)}, bf16[4096,1024]{1,0:T(8,128)(2,1)}, u32[]{:S(2)}) %copy-start.3) | copy-done | bytes 8388632
  26.1 1.7 %shard_map.100.after_ref.refs_5_.rows_ref = bf16[8,4,128,1024]{3,2,1,0:T(8,128)(2,1)S(1)} custom-call(s32[8]{0:T(128)S(1)} %broadcast_xor_fusion.order_ref, s32[1]{0:T(128)} %bitcast.channel_ref, bf16[4096,1024]{1,0:T(8,128)(2,1)S(1)} %copy-done.3), custom_call_target="tpu_custom_call" | custom-call | bytes 16777216 | tf_op jit(solution)/shard_map/pallas_call | solution.py:611
  27.8 0.0 collective-permute-done.6.refs_5_
  27.8 2.1 %collective-permute-start.9 = (bf16[384,128]{1,0:T(8,128)(2,1)S(1)}, bf16[384,128]{1,0:T(8,128)(2,1)S(1)}, u32[]{:S(2)}, u32[]{:S(2)}) collective-permute-start(bf16[384,128]{1,0:T(8,128)(2,1)S(1)} %get-tuple-element.48), channel_id=1, source_target_pairs={{0,20},{4,16},{8,28},{12,24},{16,4},{20,0},{24,12},{28,8},{1,21},{... | collective-permute-start | bytes 294920 | tf_op jit(solution)/shard_map/ppermute | solution.py:673
  30.0 0.0 collective-permute-done.1.refs_1_.refs_6_
  30.0 1.5 %collective-permute-start.10 = (bf16[384,128]{1,0:T(8,128)(2,1)S(1)}, bf16[384,128]{1,0:T(8,128)(2,1)S(1)}, u32[]{:S(2)}, u32[]{:S(2)}) collective-permute-start(bf16[384,128]{1,0:T(8,128)(2,1)S(1)} %get-tuple-element.49), channel_id=1, source_target_pairs={{0,8},{4,12},{8,0},{12,4},{16,24},{20,28},{24,16},{28,20},{1,9},{5... | collective-permute-start | bytes 294920 | tf_op jit(solution)/shard_map/ppermute | solution.py:673
  31.4 0.0 collective-permute-done.2.refs_2_.refs_7_
  31.4 0.0 collective-permute-start.11
  31.5 0.0 collective-permute-done.7.refs_1_
  31.5 1.3 %collective-permute-start.12 = (bf16[384,128]{1,0:T(8,128)(2,1)S(1)}, bf16[384,128]{1,0:T(8,128)(2,1)S(1)}, u32[]{:S(2)}, u32[]{:S(2)}) collective-permute-start(bf16[384,128]{1,0:T(8,128)(2,1)S(1)} %get-tuple-element.51), channel_id=1, source_target_pairs={{0,12},{4,8},{8,4},{12,0},{16,28},{20,24},{24,20},{28,16},{1,13},{... | collective-permute-start | bytes 294920 | tf_op jit(solution)/shard_map/ppermute | solution.py:673
  32.8 0.0 collective-permute-done.8.refs_2_
  32.8 2.0 %collective-permute-start.13 = (bf16[384,128]{1,0:T(8,128)(2,1)S(1)}, bf16[384,128]{1,0:T(8,128)(2,1)S(1)}, u32[]{:S(2)}, u32[]{:S(2)}) collective-permute-start(bf16[384,128]{1,0:T(8,128)(2,1)S(1)} %get-tuple-element.52), channel_id=1, source_target_pairs={{0,28},{4,24},{8,20},{12,16},{16,12},{20,8},{24,4},{28,0},{1,29},{... | collective-permute-start | bytes 294920 | tf_op jit(solution)/shard_map/ppermute | solution.py:673
  34.8 2.1 %shard_map.103 = (f32[8,768,128]{2,1,0:T(8,128)S(1)}, f32[8,16,128]{2,1,0:T(8,128)S(1)}) custom-call(s32[8]{0:T(128)S(1)} %broadcast_xor_fusion.order_ref, bf16[768,768]{1,0:T(8,128)(2,1)S(1)} %copy-done.2, f32[3,3,1024]{2,1,0:T(4,128)S(1)} %copy-done.6, bf16[8,4,128,1024]{3,2,1,0:T(8,128)(2,1)S(1)} %shard_map.100.after_ref.refs_5_.rows_ref, ...), custom_call_target="tpu_custom_call" | custom-call | flops 1207959552 | bytes 9437184 | tf_op jit(solution)/shard_map/pallas_call | solution.py:467
  36.9 2.5 %shard_map.102 = (f32[8,384,128]{2,1,0:T(8,128)S(1)}, f32[8,384,128]{2,1,0:T(8,128)S(1)}) custom-call(s32[8]{0:T(128)S(1)} %broadcast_xor_fusion.order_ref, bf16[384,1024]{1,0:T(8,128)(2,1)S(1)} %copy-done.4, bf16[384,1024]{1,0:T(8,128)(2,1)S(1)} %copy-done, bf16[384,1024]{1,0:T(8,128)(2,1)S(1)} %copy-done.1, ...), custom_call_target="tpu_custom_call" | custom-call | flops 7864320 | bytes 61440 | tf_op jit(solution)/shard_map/pallas_call | solution.py:409
  39.5 0.0 copy-start.5
  39.5 1.4 %shard_map.105.early_ref = f32[8,768,128]{2,1,0:T(8,128)S(1)} custom-call(s32[8]{0:T(128)S(1)} %broadcast_xor_fusion.order_ref, bf16[768,768]{1,0:T(8,128)(2,1)S(1)} %copy-done.2, f32[8,16,128]{2,1,0:T(8,128)S(1)} %get-tuple-element.44.first_ref, bf16[384,128]{1,0:T(8,128)(2,1)S(1)} %get-tuple-element.45.refs_0_, ...), custom_call_target="tpu_custom_call" | custom-call | flops 603979776 | bytes 4718592 | tf_op jit(solution)/shard_map/pallas_call | solution.py:489
  40.9 0.0 collective-permute-done.11.refs_1_
  40.9 0.7 collective-permute-done.13.refs_3_
  41.6 5.9 %shard_map.106 = (f32[8,768,128]{2,1,0:T(8,128)S(1)}, bf16[384,128]{1,0:T(8,128)(2,1)S(1)}, bf16[384,128]{1,0:T(8,128)(2,1)S(1)}, bf16[384,128]{1,0:T(8,128)(2,1...) custom-call(s32[8]{0:T(128)S(1)} %broadcast_xor_fusion.order_ref, ...), custom_call_target="tpu_custom_call", output_to_operand_aliasing={{0}: (4, {})} | custom-call | flops 2113929216 | bytes 16515072 | tf_op jit(solution)/shard_map/pallas_call | solution.py:559
  47.5 1.8 %collective-permute-start.18 = (bf16[384,128]{1,0:T(8,128)(2,1)S(1)}, bf16[384,128]{1,0:T(8,128)(2,1)S(1)}, u32[]{:S(2)}, u32[]{:S(2)}) collective-permute-start(bf16[384,128]{1,0:T(8,128)(2,1)S(1)} %get-tuple-element.56), channel_id=1, source_target_pairs={{0,16},{4,20},{8,24},{12,28},{16,0},{20,4},{24,8},{28,12},{1,17},{... | collective-permute-start | bytes 294920 | tf_op jit(solution)/shard_map/ppermute | solution.py:673
  49.3 1.3 %collective-permute-start.21 = (bf16[384,128]{1,0:T(8,128)(2,1)S(1)}, bf16[384,128]{1,0:T(8,128)(2,1)S(1)}, u32[]{:S(2)}, u32[]{:S(2)}) collective-permute-start(bf16[384,128]{1,0:T(8,128)(2,1)S(1)} %get-tuple-element.57), channel_id=1, source_target_pairs={{0,4},{4,0},{8,12},{12,8},{16,20},{20,16},{24,28},{28,24},{1,5},{5... | collective-permute-start | bytes 294920 | tf_op jit(solution)/shard_map/ppermute | solution.py:673
  50.6 0.0 collective-permute-start.22
  50.6 1.4 %collective-permute-start.25 = (bf16[384,128]{1,0:T(8,128)(2,1)S(1)}, bf16[384,128]{1,0:T(8,128)(2,1)S(1)}, u32[]{:S(2)}, u32[]{:S(2)}) collective-permute-start(bf16[384,128]{1,0:T(8,128)(2,1)S(1)} %get-tuple-element.59), channel_id=1, source_target_pairs={{0,12},{4,8},{8,4},{12,0},{16,28},{20,24},{24,20},{28,16},{1,13},{... | collective-permute-start | bytes 294920 | tf_op jit(solution)/shard_map/ppermute | solution.py:673
  51.9 1.5 %collective-permute-start.26 = (bf16[384,128]{1,0:T(8,128)(2,1)S(1)}, bf16[384,128]{1,0:T(8,128)(2,1)S(1)}, u32[]{:S(2)}, u32[]{:S(2)}) collective-permute-start(bf16[384,128]{1,0:T(8,128)(2,1)S(1)} %get-tuple-element.60), channel_id=1, source_target_pairs={{0,20},{4,16},{8,28},{12,24},{16,4},{20,0},{24,12},{28,8},{1,21},{... | collective-permute-start | bytes 294920 | tf_op jit(solution)/shard_map/ppermute | solution.py:673
  53.4 0.0 collective-permute-done.18.refs_1_
  53.4 1.6 %collective-permute-start.14 = (bf16[384,128]{1,0:T(8,128)(2,1)S(1)}, bf16[384,128]{1,0:T(8,128)(2,1)S(1)}, u32[]{:S(2)}, u32[]{:S(2)}) collective-permute-start(bf16[384,128]{1,0:T(8,128)(2,1)S(1)} %get-tuple-element.53), channel_id=1, source_target_pairs={{0,24},{4,28},{8,16},{12,20},{16,8},{20,12},{24,0},{28,4},{1,25},{... | collective-permute-start | bytes 294920 | tf_op jit(solution)/shard_map/ppermute | solution.py:673
  55.0 2.2 %collective-permute-start.15 = (bf16[384,128]{1,0:T(8,128)(2,1)S(1)}, bf16[384,128]{1,0:T(8,128)(2,1)S(1)}, u32[]{:S(2)}, u32[]{:S(2)}) collective-permute-start(bf16[384,128]{1,0:T(8,128)(2,1)S(1)} %get-tuple-element.54), channel_id=1, source_target_pairs={{0,28},{4,24},{8,20},{12,16},{16,12},{20,8},{24,4},{28,0},{1,29},{... | collective-permute-start | bytes 294920 | tf_op jit(solution)/shard_map/ppermute | solution.py:673
  57.2 0.1 shard_map.109.refs_0_
  57.3 0.0 collective-permute-done.22.refs_1_
  57.3 1.3 %collective-permute-start.19 = (bf16[384,256]{1,0:T(8,128)(2,1)S(1)}, bf16[384,256]{1,0:T(8,128)(2,1)S(1)}, u32[]{:S(2)}, u32[]{:S(2)}) collective-permute-start(bf16[384,256]{1,0:T(8,128)(2,1)S(1)} %shard_map.109.refs_0_), channel_id=1, source_target_pairs={{0,2},{1,3},{2,0},{3,1},{4,6},{5,7},{6,4},{7,5},{8,10},{9,11},{10,... | collective-permute-start | bytes 589832 | tf_op jit(solution)/shard_map/ppermute | solution.py:700
  58.6 0.1 shard_map.111.refs_0_
  58.7 0.3 collective-permute-start.23
  59.0 2.4 %collective-permute-done.26.refs_1_ = bf16[384,128]{1,0:T(8,128)(2,1)S(1)} collective-permute-done((bf16[384,128]{1,0:T(8,128)(2,1)S(1)}, bf16[384,128]{1,0:T(8,128)(2,1)S(1)}, u32[]{:S(2)}, u32[]{:S(2)}) %collective-permute-start.26) | collective-permute-done | bytes 98336 | tf_op jit(solution)/shard_map/ppermute | solution.py:673
  61.4 0.1 shard_map.113.refs_0_
  61.5 1.3 %collective-permute-start.27 = (bf16[384,256]{1,0:T(8,128)(2,1)S(1)}, bf16[384,256]{1,0:T(8,128)(2,1)S(1)}, u32[]{:S(2)}, u32[]{:S(2)}) collective-permute-start(bf16[384,256]{1,0:T(8,128)(2,1)S(1)} %shard_map.113.refs_0_), channel_id=1, source_target_pairs={{0,2},{1,3},{2,0},{3,1},{4,6},{5,7},{6,4},{7,5},{8,10},{9,11},{10,... | collective-permute-start | bytes 589832 | tf_op jit(solution)/shard_map/ppermute | solution.py:700
  62.8 0.1 shard_map.107.refs_0_
  62.8 1.0 %collective-permute-start.16 = (bf16[384,256]{1,0:T(8,128)(2,1)S(1)}, bf16[384,256]{1,0:T(8,128)(2,1)S(1)}, u32[]{:S(2)}, u32[]{:S(2)}) collective-permute-start(bf16[384,256]{1,0:T(8,128)(2,1)S(1)} %shard_map.107.refs_0_), channel_id=1, source_target_pairs={{0,2},{1,3},{2,0},{3,1},{4,6},{5,7},{6,4},{7,5},{8,10},{9,11},{10,... | collective-permute-start | bytes 589832 | tf_op jit(solution)/shard_map/ppermute | solution.py:700
  63.8 7.2 %collective-permute-start.20 = (bf16[384,512]{1,0:T(8,128)(2,1)S(1)}, bf16[384,512]{1,0:T(8,128)(2,1)S(1)}, u32[]{:S(2)}, u32[]{:S(2)}) collective-permute-start(bf16[384,512]{1,0:T(8,128)(2,1)S(1)} %shard_map.110.refs_0_), channel_id=1, source_target_pairs={{0,1},{1,0},{2,3},{3,2},{4,5},{5,4},{6,7},{7,6},{8,9},{9,8},{10,11... | collective-permute-start | bytes 1179656 | tf_op jit(solution)/shard_map/ppermute | solution.py:702
  71.1 2.1 %collective-permute-start.24 = (bf16[384,512]{1,0:T(8,128)(2,1)S(1)}, bf16[384,512]{1,0:T(8,128)(2,1)S(1)}, u32[]{:S(2)}, u32[]{:S(2)}) collective-permute-start(bf16[384,512]{1,0:T(8,128)(2,1)S(1)} %shard_map.112.refs_2_), channel_id=1, source_target_pairs={{0,1},{1,0},{2,3},{3,2},{4,5},{5,4},{6,7},{7,6},{8,9},{9,8},{10,11... | collective-permute-start | bytes 1179656 | tf_op jit(solution)/shard_map/ppermute | solution.py:702
  73.2 0.0 collective-permute-done.27.refs_1_
  73.2 2.1 %collective-permute-start.28 = (bf16[384,512]{1,0:T(8,128)(2,1)S(1)}, bf16[384,512]{1,0:T(8,128)(2,1)S(1)}, u32[]{:S(2)}, u32[]{:S(2)}) collective-permute-start(bf16[384,512]{1,0:T(8,128)(2,1)S(1)} %shard_map.114.refs_4_), channel_id=1, source_target_pairs={{0,1},{1,0},{2,3},{3,2},{4,5},{5,4},{6,7},{7,6},{8,9},{9,8},{10,11... | collective-permute-start | bytes 1179656 | tf_op jit(solution)/shard_map/ppermute | solution.py:702
  75.3 0.0 collective-permute-done.16.refs_1_
  75.3 2.1 %collective-permute-start.17 = (bf16[384,512]{1,0:T(8,128)(2,1)S(1)}, bf16[384,512]{1,0:T(8,128)(2,1)S(1)}, u32[]{:S(2)}, u32[]{:S(2)}) collective-permute-start(bf16[384,512]{1,0:T(8,128)(2,1)S(1)} %shard_map.108.refs_0_), channel_id=1, source_target_pairs={{0,1},{1,0},{2,3},{3,2},{4,5},{5,4},{6,7},{7,6},{8,9},{9,8},{10,11... | collective-permute-start | bytes 1179656 | tf_op jit(solution)/shard_map/ppermute | solution.py:702
  77.4 0.0 collective-permute-done.20.refs_1_
  77.4 0.0 collective-permute-done.24.refs_3_
  77.4 0.0 collective-permute-done.28.refs_5_
  77.4 2.6 %shard_map.115.refs_2_ = f32[384,1024]{1,0:T(8,128)S(1)} custom-call(bf16[8,4,128,1024]{3,2,1,0:T(8,128)(2,1)S(1)} %shard_map.100.after_ref.refs_5_.rows_ref, bf16[384,512]{1,0:T(8,128)(2,1)S(1)} %shard_map.110.refs_0_, bf16[384,512]{1,0:T(8,128)(2,1)S(1)} %collective-permute-done.20.refs_1_, bf16[384,512]{1,0:T(8,128)(2,1)S(1)} %shard_map.112.refs_2_, ...), custom_call_target="tpu_custom_call" | custom-call | tf_op jit(solution)/shard_map/pallas_call | solution.py:658
  80.1 0.0 collective-permute-done.17.refs_1_
  80.1 1.9 %shard_map.116 = bf16[384,1024]{1,0:T(8,128)(2,1)} custom-call(bf16[8,4,128,1024]{3,2,1,0:T(8,128)(2,1)S(1)} %shard_map.100.after_ref.refs_5_.rows_ref, bf16[384,512]{1,0:T(8,128)(2,1)S(1)} %shard_map.108.refs_0_, bf16[384,512]{1,0:T(8,128)(2,1)S(1)} %collective-permute-done.17.refs_1_, f32[384,1024]{1,0:T(8,128)S(1)} %shard_map.115.refs_2_), custom_call_target="tpu_custom_call" | custom-call | tf_op jit(solution)/shard_map/pallas_call | solution.py:658
  (32 shorter events, 0.2 us)
Async XLA Ops:
  0.0 19.3 %copy-start.9 = (s32[8]{0:T(128)S(1)}, s32[8]{0:T(128)}, u32[]{:S(2)}) copy-start(s32[8]{0:T(128)} %constant.15.clone) | copy-start | bytes 100
  0.0 19.3 %copy-start.1 = (bf16[384,1024]{1,0:T(8,128)(2,1)S(1)}, bf16[384,1024]{1,0:T(8,128)(2,1)}, u32[]{:S(2)}) copy-start(bf16[384,1024]{1,0:T(8,128)(2,1)} %value_ref.3) | copy-start | bytes 2359300
  0.0 19.3 %copy-start = (bf16[384,1024]{1,0:T(8,128)(2,1)S(1)}, bf16[384,1024]{1,0:T(8,128)(2,1)}, u32[]{:S(2)}) copy-start(bf16[384,1024]{1,0:T(8,128)(2,1)} %gate_ref.3) | copy-start | bytes 2359300
  0.0 19.3 %copy-start.6 = (f32[3,3,1024]{2,1,0:T(4,128)S(1)}, f32[3,3,1024]{2,1,0:T(4,128)}, u32[]{:S(2)}) copy-start(f32[3,3,1024]{2,1,0:T(4,128)} %taps_ref.3) | copy-start | bytes 110596
  2.6 13.7 %collective-permute-start = (bf16[464,128]{1,0:T(8,128)(2,1)}, bf16[464,128]{1,0:T(8,128)(2,1)S(1)}, u32[]{:S(2)}, u32[]{:S(2)}) collective-permute-start(bf16[464,128]{1,0:T(8,128)(2,1)} %get-tuple-element.33), channel_id=1, source_target_pairs={{0,4},{4,0},{8,12},{12,8},{16,20},{20,16},{24,28},{28,24},{1,5},{5... | collective-permute-start | bytes 356360 | tf_op jit(solution)/shard_map/ppermute | solution.py:673
  4.7 5.8 %collective-permute-start.3 = (bf16[400,128]{1,0:T(8,128)(2,1)}, bf16[400,128]{1,0:T(8,128)(2,1)S(1)}, u32[]{:S(2)}, u32[]{:S(2)}) collective-permute-start(bf16[400,128]{1,0:T(8,128)(2,1)} %get-tuple-element.39), channel_id=1, source_target_pairs={{0,16},{4,20},{8,24},{12,28},{16,0},{20,4},{24,8},{28,12},{1,17},{... | collective-permute-start | bytes 307208 | tf_op jit(solution)/shard_map/ppermute | solution.py:673
  7.0 14.2 %collective-permute-start.4 = (bf16[400,128]{1,0:T(8,128)(2,1)}, bf16[400,128]{1,0:T(8,128)(2,1)S(1)}, u32[]{:S(2)}, u32[]{:S(2)}) collective-permute-start(bf16[400,128]{1,0:T(8,128)(2,1)} %get-tuple-element.40), channel_id=1, source_target_pairs={{0,20},{4,16},{8,28},{12,24},{16,4},{20,0},{24,12},{28,8},{1,21},{... | collective-permute-start | bytes 307208 | tf_op jit(solution)/shard_map/ppermute | solution.py:673
  7.0 14.6 %collective-permute-start.5 = (bf16[400,128]{1,0:T(8,128)(2,1)}, bf16[400,128]{1,0:T(8,128)(2,1)S(1)}, u32[]{:S(2)}, u32[]{:S(2)}) collective-permute-start(bf16[400,128]{1,0:T(8,128)(2,1)} %get-tuple-element.41), channel_id=1, source_target_pairs={{0,8},{4,12},{8,0},{12,4},{16,24},{20,28},{24,16},{28,20},{1,9},{5... | collective-permute-start | bytes 307208 | tf_op jit(solution)/shard_map/ppermute | solution.py:673
  8.3 19.5 %collective-permute-start.6 = (bf16[400,128]{1,0:T(8,128)(2,1)}, bf16[400,128]{1,0:T(8,128)(2,1)S(1)}, u32[]{:S(2)}, u32[]{:S(2)}) collective-permute-start(bf16[400,128]{1,0:T(8,128)(2,1)} %get-tuple-element.42), channel_id=1, source_target_pairs={{0,24},{4,28},{8,16},{12,20},{16,8},{20,12},{24,0},{28,4},{1,25},{... | collective-permute-start | bytes 307208 | tf_op jit(solution)/shard_map/ppermute | solution.py:673
  10.5 19.5 %collective-permute-start.1 = (bf16[464,128]{1,0:T(8,128)(2,1)}, bf16[464,128]{1,0:T(8,128)(2,1)S(1)}, u32[]{:S(2)}, u32[]{:S(2)}) collective-permute-start(bf16[464,128]{1,0:T(8,128)(2,1)} %get-tuple-element.34), channel_id=1, source_target_pairs={{0,12},{4,8},{8,4},{12,0},{16,28},{20,24},{24,20},{28,16},{1,13},{... | collective-permute-start | bytes 356360 | tf_op jit(solution)/shard_map/ppermute | solution.py:673
  16.3 15.1 %collective-permute-start.2 = (bf16[464,128]{1,0:T(8,128)(2,1)}, bf16[464,128]{1,0:T(8,128)(2,1)S(1)}, u32[]{:S(2)}, u32[]{:S(2)}) collective-permute-start(bf16[464,128]{1,0:T(8,128)(2,1)} %get-tuple-element.35), channel_id=1, source_target_pairs={{0,28},{4,24},{8,20},{12,16},{16,12},{20,8},{24,4},{28,0},{1,29},{... | collective-permute-start | bytes 356360 | tf_op jit(solution)/shard_map/ppermute | solution.py:673
  21.2 10.3 %collective-permute-start.7 = (bf16[384,128]{1,0:T(8,128)(2,1)S(1)}, bf16[384,128]{1,0:T(8,128)(2,1)S(1)}, u32[]{:S(2)}, u32[]{:S(2)}) collective-permute-start(bf16[384,128]{1,0:T(8,128)(2,1)S(1)} %get-tuple-element.46), channel_id=1, source_target_pairs={{0,16},{4,20},{8,24},{12,28},{16,0},{20,4},{24,8},{28,12},{1,17},{... | collective-permute-start | bytes 294920 | tf_op jit(solution)/shard_map/ppermute | solution.py:673
  21.6 11.2 %collective-permute-start.8 = (bf16[384,128]{1,0:T(8,128)(2,1)S(1)}, bf16[384,128]{1,0:T(8,128)(2,1)S(1)}, u32[]{:S(2)}, u32[]{:S(2)}) collective-permute-start(bf16[384,128]{1,0:T(8,128)(2,1)S(1)} %get-tuple-element.47), channel_id=1, source_target_pairs={{0,4},{4,0},{8,12},{12,8},{16,20},{20,16},{24,28},{28,24},{1,5},{5... | collective-permute-start | bytes 294920 | tf_op jit(solution)/shard_map/ppermute | solution.py:673
  22.7 3.4 %copy-start.3 = (bf16[4096,1024]{1,0:T(8,128)(2,1)S(1)}, bf16[4096,1024]{1,0:T(8,128)(2,1)}, u32[]{:S(2)}) copy-start(bf16[4096,1024]{1,0:T(8,128)(2,1)} %weight_ref.1) | copy-start | bytes 25165828
  26.1 8.7 %copy-start.2 = (bf16[768,768]{1,0:T(8,128)(2,1)S(1)}, bf16[768,768]{1,0:T(8,128)(2,1)}, u32[]{:S(2)}) copy-start(bf16[768,768]{1,0:T(8,128)(2,1)} %constant.16.clone.table_ref) | copy-start | bytes 3538948
  26.1 8.7 %copy-start.7 = (bf16[400,128]{1,0:T(8,128)(2,1)S(1)}, bf16[400,128]{1,0:T(8,128)(2,1)}, u32[]{:S(2)}) copy-start(bf16[400,128]{1,0:T(8,128)(2,1)} %get-tuple-element.38.refs_0_) | copy-start | bytes 307204
  27.8 11.6 %collective-permute-start.9 = (bf16[384,128]{1,0:T(8,128)(2,1)S(1)}, bf16[384,128]{1,0:T(8,128)(2,1)S(1)}, u32[]{:S(2)}, u32[]{:S(2)}) collective-permute-start(bf16[384,128]{1,0:T(8,128)(2,1)S(1)} %get-tuple-element.48), channel_id=1, source_target_pairs={{0,20},{4,16},{8,28},{12,24},{16,4},{20,0},{24,12},{28,8},{1,21},{... | collective-permute-start | bytes 294920 | tf_op jit(solution)/shard_map/ppermute | solution.py:673
  30.0 10.9 %collective-permute-start.10 = (bf16[384,128]{1,0:T(8,128)(2,1)S(1)}, bf16[384,128]{1,0:T(8,128)(2,1)S(1)}, u32[]{:S(2)}, u32[]{:S(2)}) collective-permute-start(bf16[384,128]{1,0:T(8,128)(2,1)S(1)} %get-tuple-element.49), channel_id=1, source_target_pairs={{0,8},{4,12},{8,0},{12,4},{16,24},{20,28},{24,16},{28,20},{1,9},{5... | collective-permute-start | bytes 294920 | tf_op jit(solution)/shard_map/ppermute | solution.py:673
  31.4 9.5 %collective-permute-start.11 = (bf16[384,128]{1,0:T(8,128)(2,1)S(1)}, bf16[384,128]{1,0:T(8,128)(2,1)S(1)}, u32[]{:S(2)}, u32[]{:S(2)}) collective-permute-start(bf16[384,128]{1,0:T(8,128)(2,1)S(1)} %get-tuple-element.50), channel_id=1, source_target_pairs={{0,24},{4,28},{8,16},{12,20},{16,8},{20,12},{24,0},{28,4},{1,25},{... | collective-permute-start | bytes 294920 | tf_op jit(solution)/shard_map/ppermute | solution.py:673
  31.5 9.4 %collective-permute-start.12 = (bf16[384,128]{1,0:T(8,128)(2,1)S(1)}, bf16[384,128]{1,0:T(8,128)(2,1)S(1)}, u32[]{:S(2)}, u32[]{:S(2)}) collective-permute-start(bf16[384,128]{1,0:T(8,128)(2,1)S(1)} %get-tuple-element.51), channel_id=1, source_target_pairs={{0,12},{4,8},{8,4},{12,0},{16,28},{20,24},{24,20},{28,16},{1,13},{... | collective-permute-start | bytes 294920 | tf_op jit(solution)/shard_map/ppermute | solution.py:673
  32.8 8.8 %collective-permute-start.13 = (bf16[384,128]{1,0:T(8,128)(2,1)S(1)}, bf16[384,128]{1,0:T(8,128)(2,1)S(1)}, u32[]{:S(2)}, u32[]{:S(2)}) collective-permute-start(bf16[384,128]{1,0:T(8,128)(2,1)S(1)} %get-tuple-element.52), channel_id=1, source_target_pairs={{0,28},{4,24},{8,20},{12,16},{16,12},{20,8},{24,4},{28,0},{1,29},{... | collective-permute-start | bytes 294920 | tf_op jit(solution)/shard_map/ppermute | solution.py:673
  34.8 2.1 %copy-start.4 = (bf16[384,1024]{1,0:T(8,128)(2,1)S(1)}, bf16[384,1024]{1,0:T(8,128)(2,1)}, u32[]{:S(2)}) copy-start(bf16[384,1024]{1,0:T(8,128)(2,1)} %late_ref.1) | copy-start | bytes 2359300
  34.8 2.1 %copy-start.8 = (f32[1024]{0:T(1024)S(1)}, f32[1024]{0:T(1024)}, u32[]{:S(2)}) copy-start(f32[1024]{0:T(1024)} %param.15) | copy-start | bytes 12292
  39.5 2.1 %copy-start.5 = (bf16[384,2304]{1,0:T(8,128)(2,1)S(1)}, bf16[384,2304]{1,0:T(8,128)(2,1)}, u32[]{:S(2)}) copy-start(bf16[384,2304]{1,0:T(8,128)(2,1)} %constant.17.clone.inverse_ref) | copy-start | bytes 5308420
  47.5 5.9 %collective-permute-start.18 = (bf16[384,128]{1,0:T(8,128)(2,1)S(1)}, bf16[384,128]{1,0:T(8,128)(2,1)S(1)}, u32[]{:S(2)}, u32[]{:S(2)}) collective-permute-start(bf16[384,128]{1,0:T(8,128)(2,1)S(1)} %get-tuple-element.56), channel_id=1, source_target_pairs={{0,16},{4,20},{8,24},{12,28},{16,0},{20,4},{24,8},{28,12},{1,17},{... | collective-permute-start | bytes 294920 | tf_op jit(solution)/shard_map/ppermute | solution.py:673
  49.3 5.8 %collective-permute-start.21 = (bf16[384,128]{1,0:T(8,128)(2,1)S(1)}, bf16[384,128]{1,0:T(8,128)(2,1)S(1)}, u32[]{:S(2)}, u32[]{:S(2)}) collective-permute-start(bf16[384,128]{1,0:T(8,128)(2,1)S(1)} %get-tuple-element.57), channel_id=1, source_target_pairs={{0,4},{4,0},{8,12},{12,8},{16,20},{20,16},{24,28},{28,24},{1,5},{5... | collective-permute-start | bytes 294920 | tf_op jit(solution)/shard_map/ppermute | solution.py:673
  50.6 6.7 %collective-permute-start.22 = (bf16[384,128]{1,0:T(8,128)(2,1)S(1)}, bf16[384,128]{1,0:T(8,128)(2,1)S(1)}, u32[]{:S(2)}, u32[]{:S(2)}) collective-permute-start(bf16[384,128]{1,0:T(8,128)(2,1)S(1)} %get-tuple-element.58), channel_id=1, source_target_pairs={{0,8},{4,12},{8,0},{12,4},{16,24},{20,28},{24,16},{28,20},{1,9},{5... | collective-permute-start | bytes 294920 | tf_op jit(solution)/shard_map/ppermute | solution.py:673
  50.6 8.1 %collective-permute-start.25 = (bf16[384,128]{1,0:T(8,128)(2,1)S(1)}, bf16[384,128]{1,0:T(8,128)(2,1)S(1)}, u32[]{:S(2)}, u32[]{:S(2)}) collective-permute-start(bf16[384,128]{1,0:T(8,128)(2,1)S(1)} %get-tuple-element.59), channel_id=1, source_target_pairs={{0,12},{4,8},{8,4},{12,0},{16,28},{20,24},{24,20},{28,16},{1,13},{... | collective-permute-start | bytes 294920 | tf_op jit(solution)/shard_map/ppermute | solution.py:673
  51.9 9.4 %collective-permute-start.26 = (bf16[384,128]{1,0:T(8,128)(2,1)S(1)}, bf16[384,128]{1,0:T(8,128)(2,1)S(1)}, u32[]{:S(2)}, u32[]{:S(2)}) collective-permute-start(bf16[384,128]{1,0:T(8,128)(2,1)S(1)} %get-tuple-element.60), channel_id=1, source_target_pairs={{0,20},{4,16},{8,28},{12,24},{16,4},{20,0},{24,12},{28,8},{1,21},{... | collective-permute-start | bytes 294920 | tf_op jit(solution)/shard_map/ppermute | solution.py:673
  53.4 9.3 %collective-permute-start.14 = (bf16[384,128]{1,0:T(8,128)(2,1)S(1)}, bf16[384,128]{1,0:T(8,128)(2,1)S(1)}, u32[]{:S(2)}, u32[]{:S(2)}) collective-permute-start(bf16[384,128]{1,0:T(8,128)(2,1)S(1)} %get-tuple-element.53), channel_id=1, source_target_pairs={{0,24},{4,28},{8,16},{12,20},{16,8},{20,12},{24,0},{28,4},{1,25},{... | collective-permute-start | bytes 294920 | tf_op jit(solution)/shard_map/ppermute | solution.py:673
  55.0 7.7 %collective-permute-start.15 = (bf16[384,128]{1,0:T(8,128)(2,1)S(1)}, bf16[384,128]{1,0:T(8,128)(2,1)S(1)}, u32[]{:S(2)}, u32[]{:S(2)}) collective-permute-start(bf16[384,128]{1,0:T(8,128)(2,1)S(1)} %get-tuple-element.54), channel_id=1, source_target_pairs={{0,28},{4,24},{8,20},{12,16},{16,12},{20,8},{24,4},{28,0},{1,29},{... | collective-permute-start | bytes 294920 | tf_op jit(solution)/shard_map/ppermute | solution.py:673
  57.3 6.5 %collective-permute-start.19 = (bf16[384,256]{1,0:T(8,128)(2,1)S(1)}, bf16[384,256]{1,0:T(8,128)(2,1)S(1)}, u32[]{:S(2)}, u32[]{:S(2)}) collective-permute-start(bf16[384,256]{1,0:T(8,128)(2,1)S(1)} %shard_map.109.refs_0_), channel_id=1, source_target_pairs={{0,2},{1,3},{2,0},{3,1},{4,6},{5,7},{6,4},{7,5},{8,10},{9,11},{10,... | collective-permute-start | bytes 589832 | tf_op jit(solution)/shard_map/ppermute | solution.py:700
  58.7 12.4 %collective-permute-start.23 = (bf16[384,256]{1,0:T(8,128)(2,1)S(1)}, bf16[384,256]{1,0:T(8,128)(2,1)S(1)}, u32[]{:S(2)}, u32[]{:S(2)}) collective-permute-start(bf16[384,256]{1,0:T(8,128)(2,1)S(1)} %shard_map.111.refs_0_), channel_id=1, source_target_pairs={{0,2},{1,3},{2,0},{3,1},{4,6},{5,7},{6,4},{7,5},{8,10},{9,11},{10,... | collective-permute-start | bytes 589832 | tf_op jit(solution)/shard_map/ppermute | solution.py:700
  61.5 11.7 %collective-permute-start.27 = (bf16[384,256]{1,0:T(8,128)(2,1)S(1)}, bf16[384,256]{1,0:T(8,128)(2,1)S(1)}, u32[]{:S(2)}, u32[]{:S(2)}) collective-permute-start(bf16[384,256]{1,0:T(8,128)(2,1)S(1)} %shard_map.113.refs_0_), channel_id=1, source_target_pairs={{0,2},{1,3},{2,0},{3,1},{4,6},{5,7},{6,4},{7,5},{8,10},{9,11},{10,... | collective-permute-start | bytes 589832 | tf_op jit(solution)/shard_map/ppermute | solution.py:700
  62.8 12.5 %collective-permute-start.16 = (bf16[384,256]{1,0:T(8,128)(2,1)S(1)}, bf16[384,256]{1,0:T(8,128)(2,1)S(1)}, u32[]{:S(2)}, u32[]{:S(2)}) collective-permute-start(bf16[384,256]{1,0:T(8,128)(2,1)S(1)} %shard_map.107.refs_0_), channel_id=1, source_target_pairs={{0,2},{1,3},{2,0},{3,1},{4,6},{5,7},{6,4},{7,5},{8,10},{9,11},{10,... | collective-permute-start | bytes 589832 | tf_op jit(solution)/shard_map/ppermute | solution.py:700
  63.8 13.6 %collective-permute-start.20 = (bf16[384,512]{1,0:T(8,128)(2,1)S(1)}, bf16[384,512]{1,0:T(8,128)(2,1)S(1)}, u32[]{:S(2)}, u32[]{:S(2)}) collective-permute-start(bf16[384,512]{1,0:T(8,128)(2,1)S(1)} %shard_map.110.refs_0_), channel_id=1, source_target_pairs={{0,1},{1,0},{2,3},{3,2},{4,5},{5,4},{6,7},{7,6},{8,9},{9,8},{10,11... | collective-permute-start | bytes 1179656 | tf_op jit(solution)/shard_map/ppermute | solution.py:702
  71.1 6.3 %collective-permute-start.24 = (bf16[384,512]{1,0:T(8,128)(2,1)S(1)}, bf16[384,512]{1,0:T(8,128)(2,1)S(1)}, u32[]{:S(2)}, u32[]{:S(2)}) collective-permute-start(bf16[384,512]{1,0:T(8,128)(2,1)S(1)} %shard_map.112.refs_2_), channel_id=1, source_target_pairs={{0,1},{1,0},{2,3},{3,2},{4,5},{5,4},{6,7},{7,6},{8,9},{9,8},{10,11... | collective-permute-start | bytes 1179656 | tf_op jit(solution)/shard_map/ppermute | solution.py:702
  73.2 4.2 %collective-permute-start.28 = (bf16[384,512]{1,0:T(8,128)(2,1)S(1)}, bf16[384,512]{1,0:T(8,128)(2,1)S(1)}, u32[]{:S(2)}, u32[]{:S(2)}) collective-permute-start(bf16[384,512]{1,0:T(8,128)(2,1)S(1)} %shard_map.114.refs_4_), channel_id=1, source_target_pairs={{0,1},{1,0},{2,3},{3,2},{4,5},{5,4},{6,7},{7,6},{8,9},{9,8},{10,11... | collective-permute-start | bytes 1179656 | tf_op jit(solution)/shard_map/ppermute | solution.py:702
  75.3 4.7 %collective-permute-start.17 = (bf16[384,512]{1,0:T(8,128)(2,1)S(1)}, bf16[384,512]{1,0:T(8,128)(2,1)S(1)}, u32[]{:S(2)}, u32[]{:S(2)}) collective-permute-start(bf16[384,512]{1,0:T(8,128)(2,1)S(1)} %shard_map.108.refs_0_), channel_id=1, source_target_pairs={{0,1},{1,0},{2,3},{3,2},{4,5},{5,4},{6,7},{7,6},{8,9},{9,8},{10,11... | collective-permute-start | bytes 1179656 | tf_op jit(solution)/shard_map/ppermute | solution.py:702

commit v6 on v5

--- a/solution.py
+++ b/solution.py
@@ -285,10 +285,10 @@
     return arrived.reshape(count, cut, rows, lanes // cut).transpose(0, 2, 1, 3).reshape(count, rows, lanes)
 
 
-OFFSETS = (0, 4, 1, 2, 3, 5, 6, 7)
-FILTER_ORDER = (4, 1, 5, 2, 6, 3, 7)
+OFFSETS = (0, 4, 1, 2, 3, 6, 5, 7)
+FILTER_ORDER = (4, 1, 6, 2, 5, 3, 7)
 SIGNAL_ORDER = (4, 1, 5, 2, 6, 3, 7)
-RESULT_ORDER = (4, 1, 2, 3, 5, 6, 7)
+RESULT_ORDER = (4, 1, 2, 3, 6, 5, 7)
 EARLY = (0, 4, 1, 5)
 LATE = (2, 6, 3, 7)
 GROUP = 4

time: 82.1 us -> 81.7 us (level)
  starting transfers between devices: 52.1 us -> 48.5 us
  waiting for transfers between devices: 3.19 us -> 6.41 us
    ppermute x21, waiting for transfers between devices: 3.17 us -> 6.39 us  [swap_blocks(): lax.ppermute(blocks[place], 'seq', [(i, i ^ offset) for i in range(count)])]
    ppermute x4, starting transfers between devices: 13.5 us -> 10.3 us  [on_device_slices(): lax.ppermute(joined, 'ch', [(i, i ^ 1) for i in range(4)])]
  transfers between devices with their start and end apart: 29 -> 29, of which waited for: 2 -> 3; matrix products, arithmetic and copies ran while one was open for 0% -> 0% of each run, Pallas kernels for 15% -> 15%
where the time goes in v6:
time: 81.7 us; the launch traced here: 81.6 us
  starting transfers between devices  48.5 us (59%)
  Pallas kernels  23 us (28%)
  waiting for transfers between devices  6.41 us (8%)
  local copies, waits for them, and re-layouts  3.42 us (4%)
    ppermute x21, starting transfers between devices, swap_blocks(): lax.ppermute(blocks[place], 'seq', [(i, i ^ offset) for i in range(count)])  34 us
    ppermute x4, starting transfers between devices, on_device_slices(): lax.ppermute(joined, 'ch', [(i, i ^ 1) for i in range(4)])  10.3 us
    ppermute x21, waiting for transfers between devices, swap_blocks(): lax.ppermute(blocks[place], 'seq', [(i, i ^ offset) for i in range(count)])  6.39 us
    pallas_call x1, Pallas kernels, conv_slices(): pl.pallas_call(functools.partial(conv_slices_kernel, places), in_specs=[p...  5.92 us
    pallas_call x2, Pallas kernels, project_slices(): pl.pallas_call(functools.partial(project_kernel_slices, chunks), in_specs...  4.53 us
    ppermute x4, starting transfers between devices, on_device_slices(): across = lax.ppermute(mixed, 'ch', [(i, i ^ 2) for i in range(4)])  4.2 us
    unnamed x20, local copies, waits for them, and re-layouts  3.42 us
    pallas_call x1, Pallas kernels, cut_filter(): pl.pallas_call(cut_kernel, grid=(1,), in_specs=[pl.BlockSpec((rows, width...  2.6 us
  transfers between devices with their start and end apart: 29, of which 3 were waited for; matrix products, arithmetic and copies ran while one was open for 0% of the time, Pallas kernels for 15%

profile of v6, /device:TPU:1, one launch (start us, length us, event | category | flops | bytes accessed | tf_op | source)
XLA Modules:
  0.0 81.6 jit_solution(18094169869448438529)
XLA Ops:
  0.0 2.6 %shard_map.101 = (bf16[400,128]{1,0:T(8,128)(2,1)}, bf16[400,128]{1,0:T(8,128)(2,1)}, bf16[464,128]{1,0:T(8,128)(2,1)}, bf16[400,128]{1,0:T(8,128)(2,1)}, bf16[4...) custom-call(f32[384,1024]{1,0:T(8,128)} %filter_ref.1, ...), custom_call_target="tpu_custom_call" | custom-call | tf_op jit(solution)/shard_map/pallas_call | solution.py:341
  2.6 2.0 %collective-permute-start = (bf16[464,128]{1,0:T(8,128)(2,1)}, bf16[464,128]{1,0:T(8,128)(2,1)S(1)}, u32[]{:S(2)}, u32[]{:S(2)}) collective-permute-start(bf16[464,128]{1,0:T(8,128)(2,1)} %get-tuple-element.33), channel_id=1, source_target_pairs={{0,4},{4,0},{8,12},{12,8},{16,20},{20,16},{24,28},{28,24},{1,5},{5... | collective-permute-start | bytes 356360 | tf_op jit(solution)/shard_map/ppermute | solution.py:673
  4.7 2.3 %collective-permute-start.3 = (bf16[400,128]{1,0:T(8,128)(2,1)}, bf16[400,128]{1,0:T(8,128)(2,1)S(1)}, u32[]{:S(2)}, u32[]{:S(2)}) collective-permute-start(bf16[400,128]{1,0:T(8,128)(2,1)} %get-tuple-element.39), channel_id=1, source_target_pairs={{0,16},{4,20},{8,24},{12,28},{16,0},{20,4},{24,8},{28,12},{1,17},{... | collective-permute-start | bytes 307208 | tf_op jit(solution)/shard_map/ppermute | solution.py:673
  7.0 1.1 %collective-permute-start.4 = (bf16[400,128]{1,0:T(8,128)(2,1)}, bf16[400,128]{1,0:T(8,128)(2,1)S(1)}, u32[]{:S(2)}, u32[]{:S(2)}) collective-permute-start(bf16[400,128]{1,0:T(8,128)(2,1)} %get-tuple-element.40), channel_id=1, source_target_pairs={{0,24},{4,28},{8,16},{12,20},{16,8},{20,12},{24,0},{28,4},{1,25},{... | collective-permute-start | bytes 307208 | tf_op jit(solution)/shard_map/ppermute | solution.py:673
  8.0 0.2 collective-permute-start.5
  8.3 2.2 %collective-permute-start.6 = (bf16[400,128]{1,0:T(8,128)(2,1)}, bf16[400,128]{1,0:T(8,128)(2,1)S(1)}, u32[]{:S(2)}, u32[]{:S(2)}) collective-permute-start(bf16[400,128]{1,0:T(8,128)(2,1)} %get-tuple-element.42), channel_id=1, source_target_pairs={{0,20},{4,16},{8,28},{12,24},{16,4},{20,0},{24,12},{28,8},{1,21},{... | collective-permute-start | bytes 307208 | tf_op jit(solution)/shard_map/ppermute | solution.py:673
  10.5 0.0 collective-permute-done.3.refs_1_
  10.5 5.8 %collective-permute-start.1 = (bf16[464,128]{1,0:T(8,128)(2,1)}, bf16[464,128]{1,0:T(8,128)(2,1)S(1)}, u32[]{:S(2)}, u32[]{:S(2)}) collective-permute-start(bf16[464,128]{1,0:T(8,128)(2,1)} %get-tuple-element.34), channel_id=1, source_target_pairs={{0,12},{4,8},{8,4},{12,0},{16,28},{20,24},{24,20},{28,16},{1,13},{... | collective-permute-start | bytes 356360 | tf_op jit(solution)/shard_map/ppermute | solution.py:673
  16.3 0.0 collective-permute-done.refs_0_.refs_2_.after_ref
  16.3 3.0 %collective-permute-start.2 = (bf16[464,128]{1,0:T(8,128)(2,1)}, bf16[464,128]{1,0:T(8,128)(2,1)S(1)}, u32[]{:S(2)}, u32[]{:S(2)}) collective-permute-start(bf16[464,128]{1,0:T(8,128)(2,1)} %get-tuple-element.35), channel_id=1, source_target_pairs={{0,28},{4,24},{8,20},{12,16},{16,12},{20,8},{24,4},{28,0},{1,29},{... | collective-permute-start | bytes 356360 | tf_op jit(solution)/shard_map/ppermute | solution.py:673
  19.3 1.9 %shard_map.104 = (bf16[384,128]{1,0:T(8,128)(2,1)S(1)}, bf16[384,128]{1,0:T(8,128)(2,1)S(1)}, bf16[384,128]{1,0:T(8,128)(2,1)S(1)}, bf16[384,128]{1,0:T(8,128)(2...) custom-call(s32[8]{0:T(128)S(1)} %broadcast_xor_fusion.order_ref, ...), custom_call_target="tpu_custom_call" | custom-call | flops 5505024 | bytes 43008 | tf_op jit(solution)/shard_map/pallas_call | solution.py:368
  21.1 0.0 collective-permute-done.4.refs_3_
  21.1 0.5 collective-permute-start.7
  21.7 1.1 %collective-permute-start.8 = (bf16[384,128]{1,0:T(8,128)(2,1)S(1)}, bf16[384,128]{1,0:T(8,128)(2,1)S(1)}, u32[]{:S(2)}, u32[]{:S(2)}) collective-permute-start(bf16[384,128]{1,0:T(8,128)(2,1)S(1)} %get-tuple-element.47), channel_id=1, source_target_pairs={{0,4},{4,0},{8,12},{12,8},{16,20},{20,16},{24,28},{28,24},{1,5},{5... | collective-permute-start | bytes 294920 | tf_op jit(solution)/shard_map/ppermute | solution.py:673
  22.7 3.4 %copy-done.3 = bf16[4096,1024]{1,0:T(8,128)(2,1)S(1)} copy-done((bf16[4096,1024]{1,0:T(8,128)(2,1)S(1)}, bf16[4096,1024]{1,0:T(8,128)(2,1)}, u32[]{:S(2)}) %copy-start.3) | copy-done | bytes 8388632
  26.1 1.7 %shard_map.100.after_ref.refs_5_.rows_ref = bf16[8,4,128,1024]{3,2,1,0:T(8,128)(2,1)S(1)} custom-call(s32[8]{0:T(128)S(1)} %broadcast_xor_fusion.order_ref, s32[1]{0:T(128)} %bitcast.channel_ref, bf16[4096,1024]{1,0:T(8,128)(2,1)S(1)} %copy-done.3), custom_call_target="tpu_custom_call" | custom-call | bytes 16777216 | tf_op jit(solution)/shard_map/pallas_call | solution.py:611
  27.8 0.0 collective-permute-done.6.refs_5_
  27.8 2.1 %collective-permute-start.9 = (bf16[384,128]{1,0:T(8,128)(2,1)S(1)}, bf16[384,128]{1,0:T(8,128)(2,1)S(1)}, u32[]{:S(2)}, u32[]{:S(2)}) collective-permute-start(bf16[384,128]{1,0:T(8,128)(2,1)S(1)} %get-tuple-element.48), channel_id=1, source_target_pairs={{0,20},{4,16},{8,28},{12,24},{16,4},{20,0},{24,12},{28,8},{1,21},{... | collective-permute-start | bytes 294920 | tf_op jit(solution)/shard_map/ppermute | solution.py:673
  29.9 0.0 collective-permute-done.1.refs_1_.refs_6_
  29.9 1.5 %collective-permute-start.10 = (bf16[384,128]{1,0:T(8,128)(2,1)S(1)}, bf16[384,128]{1,0:T(8,128)(2,1)S(1)}, u32[]{:S(2)}, u32[]{:S(2)}) collective-permute-start(bf16[384,128]{1,0:T(8,128)(2,1)S(1)} %get-tuple-element.49), channel_id=1, source_target_pairs={{0,8},{4,12},{8,0},{12,4},{16,24},{20,28},{24,16},{28,20},{1,9},{5... | collective-permute-start | bytes 294920 | tf_op jit(solution)/shard_map/ppermute | solution.py:673
  31.4 0.0 collective-permute-done.2.refs_2_.refs_7_
  31.4 0.1 collective-permute-start.11
  31.6 0.0 collective-permute-done.7.refs_1_
  31.6 0.8 %collective-permute-start.12 = (bf16[384,128]{1,0:T(8,128)(2,1)S(1)}, bf16[384,128]{1,0:T(8,128)(2,1)S(1)}, u32[]{:S(2)}, u32[]{:S(2)}) collective-permute-start(bf16[384,128]{1,0:T(8,128)(2,1)S(1)} %get-tuple-element.51), channel_id=1, source_target_pairs={{0,12},{4,8},{8,4},{12,0},{16,28},{20,24},{24,20},{28,16},{1,13},{... | collective-permute-start | bytes 294920 | tf_op jit(solution)/shard_map/ppermute | solution.py:673
  32.4 2.4 %collective-permute-start.13 = (bf16[384,128]{1,0:T(8,128)(2,1)S(1)}, bf16[384,128]{1,0:T(8,128)(2,1)S(1)}, u32[]{:S(2)}, u32[]{:S(2)}) collective-permute-start(bf16[384,128]{1,0:T(8,128)(2,1)S(1)} %get-tuple-element.52), channel_id=1, source_target_pairs={{0,28},{4,24},{8,20},{12,16},{16,12},{20,8},{24,4},{28,0},{1,29},{... | collective-permute-start | bytes 294920 | tf_op jit(solution)/shard_map/ppermute | solution.py:673
  34.8 2.1 %shard_map.103 = (f32[8,768,128]{2,1,0:T(8,128)S(1)}, f32[8,16,128]{2,1,0:T(8,128)S(1)}) custom-call(s32[8]{0:T(128)S(1)} %broadcast_xor_fusion.order_ref, bf16[768,768]{1,0:T(8,128)(2,1)S(1)} %copy-done.2, f32[3,3,1024]{2,1,0:T(4,128)S(1)} %copy-done.6, bf16[8,4,128,1024]{3,2,1,0:T(8,128)(2,1)S(1)} %shard_map.100.after_ref.refs_5_.rows_ref, ...), custom_call_target="tpu_custom_call" | custom-call | flops 1207959552 | bytes 9437184 | tf_op jit(solution)/shard_map/pallas_call | solution.py:467
  36.9 2.5 %shard_map.102 = (f32[8,384,128]{2,1,0:T(8,128)S(1)}, f32[8,384,128]{2,1,0:T(8,128)S(1)}) custom-call(s32[8]{0:T(128)S(1)} %broadcast_xor_fusion.order_ref, bf16[384,1024]{1,0:T(8,128)(2,1)S(1)} %copy-done.4, bf16[384,1024]{1,0:T(8,128)(2,1)S(1)} %copy-done, bf16[384,1024]{1,0:T(8,128)(2,1)S(1)} %copy-done.1, ...), custom_call_target="tpu_custom_call" | custom-call | flops 7864320 | bytes 61440 | tf_op jit(solution)/shard_map/pallas_call | solution.py:409
  39.4 0.0 copy-start.5
  39.5 1.4 %shard_map.105.early_ref = f32[8,768,128]{2,1,0:T(8,128)S(1)} custom-call(s32[8]{0:T(128)S(1)} %broadcast_xor_fusion.order_ref, bf16[768,768]{1,0:T(8,128)(2,1)S(1)} %copy-done.2, f32[8,16,128]{2,1,0:T(8,128)S(1)} %get-tuple-element.44.first_ref, bf16[384,128]{1,0:T(8,128)(2,1)S(1)} %get-tuple-element.45.refs_0_, ...), custom_call_target="tpu_custom_call" | custom-call | flops 603979776 | bytes 4718592 | tf_op jit(solution)/shard_map/pallas_call | solution.py:489
  40.9 0.0 collective-permute-done.11.refs_1_
  40.9 0.0 collective-permute-done.12.refs_2_
  40.9 0.6 collective-permute-done.13.refs_3_
  41.5 5.9 %shard_map.106 = (f32[8,768,128]{2,1,0:T(8,128)S(1)}, bf16[384,128]{1,0:T(8,128)(2,1)S(1)}, bf16[384,128]{1,0:T(8,128)(2,1)S(1)}, bf16[384,128]{1,0:T(8,128)(2,1...) custom-call(s32[8]{0:T(128)S(1)} %broadcast_xor_fusion.order_ref, ...), custom_call_target="tpu_custom_call", output_to_operand_aliasing={{0}: (4, {})} | custom-call | flops 2113929216 | bytes 16515072 | tf_op jit(solution)/shard_map/pallas_call | solution.py:559
  47.4 1.8 %collective-permute-start.18 = (bf16[384,128]{1,0:T(8,128)(2,1)S(1)}, bf16[384,128]{1,0:T(8,128)(2,1)S(1)}, u32[]{:S(2)}, u32[]{:S(2)}) collective-permute-start(bf16[384,128]{1,0:T(8,128)(2,1)S(1)} %get-tuple-element.56), channel_id=1, source_target_pairs={{0,16},{4,20},{8,24},{12,28},{16,0},{20,4},{24,8},{28,12},{1,17},{... | collective-permute-start | bytes 294920 | tf_op jit(solution)/shard_map/ppermute | solution.py:673
  49.2 1.3 %collective-permute-start.21 = (bf16[384,128]{1,0:T(8,128)(2,1)S(1)}, bf16[384,128]{1,0:T(8,128)(2,1)S(1)}, u32[]{:S(2)}, u32[]{:S(2)}) collective-permute-start(bf16[384,128]{1,0:T(8,128)(2,1)S(1)} %get-tuple-element.57), channel_id=1, source_target_pairs={{0,4},{4,0},{8,12},{12,8},{16,20},{20,16},{24,28},{28,24},{1,5},{5... | collective-permute-start | bytes 294920 | tf_op jit(solution)/shard_map/ppermute | solution.py:673
  50.5 1.3 %collective-permute-start.25 = (bf16[384,128]{1,0:T(8,128)(2,1)S(1)}, bf16[384,128]{1,0:T(8,128)(2,1)S(1)}, u32[]{:S(2)}, u32[]{:S(2)}) collective-permute-start(bf16[384,128]{1,0:T(8,128)(2,1)S(1)} %get-tuple-element.59), channel_id=1, source_target_pairs={{0,12},{4,8},{8,4},{12,0},{16,28},{20,24},{24,20},{28,16},{1,13},{... | collective-permute-start | bytes 294920 | tf_op jit(solution)/shard_map/ppermute | solution.py:673
  51.9 1.8 %collective-permute-start.26 = (bf16[384,128]{1,0:T(8,128)(2,1)S(1)}, bf16[384,128]{1,0:T(8,128)(2,1)S(1)}, u32[]{:S(2)}, u32[]{:S(2)}) collective-permute-start(bf16[384,128]{1,0:T(8,128)(2,1)S(1)} %get-tuple-element.60), channel_id=1, source_target_pairs={{0,24},{4,28},{8,16},{12,20},{16,8},{20,12},{24,0},{28,4},{1,25},{... | collective-permute-start | bytes 294920 | tf_op jit(solution)/shard_map/ppermute | solution.py:673
  53.7 1.0 %collective-permute-start.14 = (bf16[384,128]{1,0:T(8,128)(2,1)S(1)}, bf16[384,128]{1,0:T(8,128)(2,1)S(1)}, u32[]{:S(2)}, u32[]{:S(2)}) collective-permute-start(bf16[384,128]{1,0:T(8,128)(2,1)S(1)} %get-tuple-element.53), channel_id=1, source_target_pairs={{0,20},{4,16},{8,28},{12,24},{16,4},{20,0},{24,12},{28,8},{1,21},{... | collective-permute-start | bytes 294920 | tf_op jit(solution)/shard_map/ppermute | solution.py:673
  54.6 0.0 collective-permute-done.21.refs_0_
  54.6 1.7 %collective-permute-start.15 = (bf16[384,128]{1,0:T(8,128)(2,1)S(1)}, bf16[384,128]{1,0:T(8,128)(2,1)S(1)}, u32[]{:S(2)}, u32[]{:S(2)}) collective-permute-start(bf16[384,128]{1,0:T(8,128)(2,1)S(1)} %get-tuple-element.54), channel_id=1, source_target_pairs={{0,28},{4,24},{8,20},{12,16},{16,12},{20,8},{24,4},{28,0},{1,29},{... | collective-permute-start | bytes 294920 | tf_op jit(solution)/shard_map/ppermute | solution.py:673
  56.3 0.1 shard_map.109.refs_0_
  56.3 0.0 collective-permute-done.22.refs_1_
  56.4 1.3 %collective-permute-start.19 = (bf16[384,256]{1,0:T(8,128)(2,1)S(1)}, bf16[384,256]{1,0:T(8,128)(2,1)S(1)}, u32[]{:S(2)}, u32[]{:S(2)}) collective-permute-start(bf16[384,256]{1,0:T(8,128)(2,1)S(1)} %shard_map.109.refs_0_), channel_id=1, source_target_pairs={{0,2},{1,3},{2,0},{3,1},{4,6},{5,7},{6,4},{7,5},{8,10},{9,11},{10,... | collective-permute-start | bytes 589832 | tf_op jit(solution)/shard_map/ppermute | solution.py:700
  57.7 0.1 shard_map.111.refs_0_
  57.7 0.0 collective-permute-done.25.refs_0_
  57.7 0.3 collective-permute-start.23
  58.0 0.2 collective-permute-done.26.refs_1_
  58.2 0.1 shard_map.113.refs_0_
  58.3 1.3 %collective-permute-start.27 = (bf16[384,256]{1,0:T(8,128)(2,1)S(1)}, bf16[384,256]{1,0:T(8,128)(2,1)S(1)}, u32[]{:S(2)}, u32[]{:S(2)}) collective-permute-start(bf16[384,256]{1,0:T(8,128)(2,1)S(1)} %shard_map.113.refs_0_), channel_id=1, source_target_pairs={{0,2},{1,3},{2,0},{3,1},{4,6},{5,7},{6,4},{7,5},{8,10},{9,11},{10,... | collective-permute-start | bytes 589832 | tf_op jit(solution)/shard_map/ppermute | solution.py:700
  59.6 5.6 %collective-permute-done.14.refs_0_ = bf16[384,128]{1,0:T(8,128)(2,1)S(1)} collective-permute-done((bf16[384,128]{1,0:T(8,128)(2,1)S(1)}, bf16[384,128]{1,0:T(8,128)(2,1)S(1)}, u32[]{:S(2)}, u32[]{:S(2)}) %collective-permute-start.14) | collective-permute-done | bytes 98336 | tf_op jit(solution)/shard_map/ppermute | solution.py:673
  65.2 0.0 collective-permute-done.15.refs_1_
  65.2 0.1 shard_map.107.refs_0_
  65.2 1.3 %collective-permute-start.16 = (bf16[384,256]{1,0:T(8,128)(2,1)S(1)}, bf16[384,256]{1,0:T(8,128)(2,1)S(1)}, u32[]{:S(2)}, u32[]{:S(2)}) collective-permute-start(bf16[384,256]{1,0:T(8,128)(2,1)S(1)} %shard_map.107.refs_0_), channel_id=1, source_target_pairs={{0,2},{1,3},{2,0},{3,1},{4,6},{5,7},{6,4},{7,5},{8,10},{9,11},{10,... | collective-permute-start | bytes 589832 | tf_op jit(solution)/shard_map/ppermute | solution.py:700
  66.5 0.0 collective-permute-done.19.refs_1_
  66.6 4.6 %collective-permute-start.20 = (bf16[384,512]{1,0:T(8,128)(2,1)S(1)}, bf16[384,512]{1,0:T(8,128)(2,1)S(1)}, u32[]{:S(2)}, u32[]{:S(2)}) collective-permute-start(bf16[384,512]{1,0:T(8,128)(2,1)S(1)} %shard_map.110.refs_0_), channel_id=1, source_target_pairs={{0,1},{1,0},{2,3},{3,2},{4,5},{5,4},{6,7},{7,6},{8,9},{9,8},{10,11... | collective-permute-start | bytes 1179656 | tf_op jit(solution)/shard_map/ppermute | solution.py:702
  71.2 1.6 %collective-permute-start.24 = (bf16[384,512]{1,0:T(8,128)(2,1)S(1)}, bf16[384,512]{1,0:T(8,128)(2,1)S(1)}, u32[]{:S(2)}, u32[]{:S(2)}) collective-permute-start(bf16[384,512]{1,0:T(8,128)(2,1)S(1)} %shard_map.112.refs_2_), channel_id=1, source_target_pairs={{0,1},{1,0},{2,3},{3,2},{4,5},{5,4},{6,7},{7,6},{8,9},{9,8},{10,11... | collective-permute-start | bytes 1179656 | tf_op jit(solution)/shard_map/ppermute | solution.py:702
  72.8 2.1 %collective-permute-start.28 = (bf16[384,512]{1,0:T(8,128)(2,1)S(1)}, bf16[384,512]{1,0:T(8,128)(2,1)S(1)}, u32[]{:S(2)}, u32[]{:S(2)}) collective-permute-start(bf16[384,512]{1,0:T(8,128)(2,1)S(1)} %shard_map.114.refs_4_), channel_id=1, source_target_pairs={{0,1},{1,0},{2,3},{3,2},{4,5},{5,4},{6,7},{7,6},{8,9},{9,8},{10,11... | collective-permute-start | bytes 1179656 | tf_op jit(solution)/shard_map/ppermute | solution.py:702
  74.9 0.0 collective-permute-done.16.refs_1_
  74.9 2.1 %collective-permute-start.17 = (bf16[384,512]{1,0:T(8,128)(2,1)S(1)}, bf16[384,512]{1,0:T(8,128)(2,1)S(1)}, u32[]{:S(2)}, u32[]{:S(2)}) collective-permute-start(bf16[384,512]{1,0:T(8,128)(2,1)S(1)} %shard_map.108.refs_0_), channel_id=1, source_target_pairs={{0,1},{1,0},{2,3},{3,2},{4,5},{5,4},{6,7},{7,6},{8,9},{9,8},{10,11... | collective-permute-start | bytes 1179656 | tf_op jit(solution)/shard_map/ppermute | solution.py:702
  77.0 0.0 collective-permute-done.20.refs_1_
  77.0 0.0 collective-permute-done.24.refs_3_
  77.0 2.6 %shard_map.115.refs_2_ = f32[384,1024]{1,0:T(8,128)S(1)} custom-call(bf16[8,4,128,1024]{3,2,1,0:T(8,128)(2,1)S(1)} %shard_map.100.after_ref.refs_5_.rows_ref, bf16[384,512]{1,0:T(8,128)(2,1)S(1)} %shard_map.110.refs_0_, bf16[384,512]{1,0:T(8,128)(2,1)S(1)} %collective-permute-done.20.refs_1_, bf16[384,512]{1,0:T(8,128)(2,1)S(1)} %shard_map.112.refs_2_, ...), custom_call_target="tpu_custom_call" | custom-call | tf_op jit(solution)/shard_map/pallas_call | solution.py:658
  79.7 0.0 collective-permute-done.17.refs_1_
  79.7 1.9 %shard_map.116 = bf16[384,1024]{1,0:T(8,128)(2,1)} custom-call(bf16[8,4,128,1024]{3,2,1,0:T(8,128)(2,1)S(1)} %shard_map.100.after_ref.refs_5_.rows_ref, bf16[384,512]{1,0:T(8,128)(2,1)S(1)} %shard_map.108.refs_0_, bf16[384,512]{1,0:T(8,128)(2,1)S(1)} %collective-permute-done.17.refs_1_, f32[384,1024]{1,0:T(8,128)S(1)} %shard_map.115.refs_2_), custom_call_target="tpu_custom_call" | custom-call | tf_op jit(solution)/shard_map/pallas_call | solution.py:658
  (32 shorter events, 0.2 us)
Async XLA Ops:
  0.0 19.2 %copy-start.9 = (s32[8]{0:T(128)S(1)}, s32[8]{0:T(128)}, u32[]{:S(2)}) copy-start(s32[8]{0:T(128)} %constant.15.clone) | copy-start | bytes 100
  0.0 19.3 %copy-start.1 = (bf16[384,1024]{1,0:T(8,128)(2,1)S(1)}, bf16[384,1024]{1,0:T(8,128)(2,1)}, u32[]{:S(2)}) copy-start(bf16[384,1024]{1,0:T(8,128)(2,1)} %value_ref.3) | copy-start | bytes 2359300
  0.0 19.3 %copy-start = (bf16[384,1024]{1,0:T(8,128)(2,1)S(1)}, bf16[384,1024]{1,0:T(8,128)(2,1)}, u32[]{:S(2)}) copy-start(bf16[384,1024]{1,0:T(8,128)(2,1)} %gate_ref.3) | copy-start | bytes 2359300
  0.0 19.3 %copy-start.6 = (f32[3,3,1024]{2,1,0:T(4,128)S(1)}, f32[3,3,1024]{2,1,0:T(4,128)}, u32[]{:S(2)}) copy-start(f32[3,3,1024]{2,1,0:T(4,128)} %taps_ref.3) | copy-start | bytes 110596
  2.6 13.6 %collective-permute-start = (bf16[464,128]{1,0:T(8,128)(2,1)}, bf16[464,128]{1,0:T(8,128)(2,1)S(1)}, u32[]{:S(2)}, u32[]{:S(2)}) collective-permute-start(bf16[464,128]{1,0:T(8,128)(2,1)} %get-tuple-element.33), channel_id=1, source_target_pairs={{0,4},{4,0},{8,12},{12,8},{16,20},{20,16},{24,28},{28,24},{1,5},{5... | collective-permute-start | bytes 356360 | tf_op jit(solution)/shard_map/ppermute | solution.py:673
  4.7 5.8 %collective-permute-start.3 = (bf16[400,128]{1,0:T(8,128)(2,1)}, bf16[400,128]{1,0:T(8,128)(2,1)S(1)}, u32[]{:S(2)}, u32[]{:S(2)}) collective-permute-start(bf16[400,128]{1,0:T(8,128)(2,1)} %get-tuple-element.39), channel_id=1, source_target_pairs={{0,16},{4,20},{8,24},{12,28},{16,0},{20,4},{24,8},{28,12},{1,17},{... | collective-permute-start | bytes 307208 | tf_op jit(solution)/shard_map/ppermute | solution.py:673
  7.0 14.2 %collective-permute-start.4 = (bf16[400,128]{1,0:T(8,128)(2,1)}, bf16[400,128]{1,0:T(8,128)(2,1)S(1)}, u32[]{:S(2)}, u32[]{:S(2)}) collective-permute-start(bf16[400,128]{1,0:T(8,128)(2,1)} %get-tuple-element.40), channel_id=1, source_target_pairs={{0,24},{4,28},{8,16},{12,20},{16,8},{20,12},{24,0},{28,4},{1,25},{... | collective-permute-start | bytes 307208 | tf_op jit(solution)/shard_map/ppermute | solution.py:673
  8.0 13.6 %collective-permute-start.5 = (bf16[400,128]{1,0:T(8,128)(2,1)}, bf16[400,128]{1,0:T(8,128)(2,1)S(1)}, u32[]{:S(2)}, u32[]{:S(2)}) collective-permute-start(bf16[400,128]{1,0:T(8,128)(2,1)} %get-tuple-element.41), channel_id=1, source_target_pairs={{0,8},{4,12},{8,0},{12,4},{16,24},{20,28},{24,16},{28,20},{1,9},{5... | collective-permute-start | bytes 307208 | tf_op jit(solution)/shard_map/ppermute | solution.py:673
  8.3 19.6 %collective-permute-start.6 = (bf16[400,128]{1,0:T(8,128)(2,1)}, bf16[400,128]{1,0:T(8,128)(2,1)S(1)}, u32[]{:S(2)}, u32[]{:S(2)}) collective-permute-start(bf16[400,128]{1,0:T(8,128)(2,1)} %get-tuple-element.42), channel_id=1, source_target_pairs={{0,20},{4,16},{8,28},{12,24},{16,4},{20,0},{24,12},{28,8},{1,21},{... | collective-permute-start | bytes 307208 | tf_op jit(solution)/shard_map/ppermute | solution.py:673
  10.5 19.4 %collective-permute-start.1 = (bf16[464,128]{1,0:T(8,128)(2,1)}, bf16[464,128]{1,0:T(8,128)(2,1)S(1)}, u32[]{:S(2)}, u32[]{:S(2)}) collective-permute-start(bf16[464,128]{1,0:T(8,128)(2,1)} %get-tuple-element.34), channel_id=1, source_target_pairs={{0,12},{4,8},{8,4},{12,0},{16,28},{20,24},{24,20},{28,16},{1,13},{... | collective-permute-start | bytes 356360 | tf_op jit(solution)/shard_map/ppermute | solution.py:673
  16.3 15.2 %collective-permute-start.2 = (bf16[464,128]{1,0:T(8,128)(2,1)}, bf16[464,128]{1,0:T(8,128)(2,1)S(1)}, u32[]{:S(2)}, u32[]{:S(2)}) collective-permute-start(bf16[464,128]{1,0:T(8,128)(2,1)} %get-tuple-element.35), channel_id=1, source_target_pairs={{0,28},{4,24},{8,20},{12,16},{16,12},{20,8},{24,4},{28,0},{1,29},{... | collective-permute-start | bytes 356360 | tf_op jit(solution)/shard_map/ppermute | solution.py:673
  21.1 10.4 %collective-permute-start.7 = (bf16[384,128]{1,0:T(8,128)(2,1)S(1)}, bf16[384,128]{1,0:T(8,128)(2,1)S(1)}, u32[]{:S(2)}, u32[]{:S(2)}) collective-permute-start(bf16[384,128]{1,0:T(8,128)(2,1)S(1)} %get-tuple-element.46), channel_id=1, source_target_pairs={{0,16},{4,20},{8,24},{12,28},{16,0},{20,4},{24,8},{28,12},{1,17},{... | collective-permute-start | bytes 294920 | tf_op jit(solution)/shard_map/ppermute | solution.py:673
  21.7 10.7 %collective-permute-start.8 = (bf16[384,128]{1,0:T(8,128)(2,1)S(1)}, bf16[384,128]{1,0:T(8,128)(2,1)S(1)}, u32[]{:S(2)}, u32[]{:S(2)}) collective-permute-start(bf16[384,128]{1,0:T(8,128)(2,1)S(1)} %get-tuple-element.47), channel_id=1, source_target_pairs={{0,4},{4,0},{8,12},{12,8},{16,20},{20,16},{24,28},{28,24},{1,5},{5... | collective-permute-start | bytes 294920 | tf_op jit(solution)/shard_map/ppermute | solution.py:673
  22.7 3.4 %copy-start.3 = (bf16[4096,1024]{1,0:T(8,128)(2,1)S(1)}, bf16[4096,1024]{1,0:T(8,128)(2,1)}, u32[]{:S(2)}) copy-start(bf16[4096,1024]{1,0:T(8,128)(2,1)} %weight_ref.1) | copy-start | bytes 25165828
  26.1 8.7 %copy-start.2 = (bf16[768,768]{1,0:T(8,128)(2,1)S(1)}, bf16[768,768]{1,0:T(8,128)(2,1)}, u32[]{:S(2)}) copy-start(bf16[768,768]{1,0:T(8,128)(2,1)} %constant.16.clone.table_ref) | copy-start | bytes 3538948
  26.1 8.7 %copy-start.7 = (bf16[400,128]{1,0:T(8,128)(2,1)S(1)}, bf16[400,128]{1,0:T(8,128)(2,1)}, u32[]{:S(2)}) copy-start(bf16[400,128]{1,0:T(8,128)(2,1)} %get-tuple-element.38.refs_0_) | copy-start | bytes 307204
  27.8 11.6 %collective-permute-start.9 = (bf16[384,128]{1,0:T(8,128)(2,1)S(1)}, bf16[384,128]{1,0:T(8,128)(2,1)S(1)}, u32[]{:S(2)}, u32[]{:S(2)}) collective-permute-start(bf16[384,128]{1,0:T(8,128)(2,1)S(1)} %get-tuple-element.48), channel_id=1, source_target_pairs={{0,20},{4,16},{8,28},{12,24},{16,4},{20,0},{24,12},{28,8},{1,21},{... | collective-permute-start | bytes 294920 | tf_op jit(solution)/shard_map/ppermute | solution.py:673
  29.9 10.9 %collective-permute-start.10 = (bf16[384,128]{1,0:T(8,128)(2,1)S(1)}, bf16[384,128]{1,0:T(8,128)(2,1)S(1)}, u32[]{:S(2)}, u32[]{:S(2)}) collective-permute-start(bf16[384,128]{1,0:T(8,128)(2,1)S(1)} %get-tuple-element.49), channel_id=1, source_target_pairs={{0,8},{4,12},{8,0},{12,4},{16,24},{20,28},{24,16},{28,20},{1,9},{5... | collective-permute-start | bytes 294920 | tf_op jit(solution)/shard_map/ppermute | solution.py:673
  31.4 9.4 %collective-permute-start.11 = (bf16[384,128]{1,0:T(8,128)(2,1)S(1)}, bf16[384,128]{1,0:T(8,128)(2,1)S(1)}, u32[]{:S(2)}, u32[]{:S(2)}) collective-permute-start(bf16[384,128]{1,0:T(8,128)(2,1)S(1)} %get-tuple-element.50), channel_id=1, source_target_pairs={{0,24},{4,28},{8,16},{12,20},{16,8},{20,12},{24,0},{28,4},{1,25},{... | collective-permute-start | bytes 294920 | tf_op jit(solution)/shard_map/ppermute | solution.py:673
  31.6 9.3 %collective-permute-start.12 = (bf16[384,128]{1,0:T(8,128)(2,1)S(1)}, bf16[384,128]{1,0:T(8,128)(2,1)S(1)}, u32[]{:S(2)}, u32[]{:S(2)}) collective-permute-start(bf16[384,128]{1,0:T(8,128)(2,1)S(1)} %get-tuple-element.51), channel_id=1, source_target_pairs={{0,12},{4,8},{8,4},{12,0},{16,28},{20,24},{24,20},{28,16},{1,13},{... | collective-permute-start | bytes 294920 | tf_op jit(solution)/shard_map/ppermute | solution.py:673
  32.4 9.1 %collective-permute-start.13 = (bf16[384,128]{1,0:T(8,128)(2,1)S(1)}, bf16[384,128]{1,0:T(8,128)(2,1)S(1)}, u32[]{:S(2)}, u32[]{:S(2)}) collective-permute-start(bf16[384,128]{1,0:T(8,128)(2,1)S(1)} %get-tuple-element.52), channel_id=1, source_target_pairs={{0,28},{4,24},{8,20},{12,16},{16,12},{20,8},{24,4},{28,0},{1,29},{... | collective-permute-start | bytes 294920 | tf_op jit(solution)/shard_map/ppermute | solution.py:673
  34.8 2.1 %copy-start.4 = (bf16[384,1024]{1,0:T(8,128)(2,1)S(1)}, bf16[384,1024]{1,0:T(8,128)(2,1)}, u32[]{:S(2)}) copy-start(bf16[384,1024]{1,0:T(8,128)(2,1)} %late_ref.1) | copy-start | bytes 2359300
  34.8 2.1 %copy-start.8 = (f32[1024]{0:T(1024)S(1)}, f32[1024]{0:T(1024)}, u32[]{:S(2)}) copy-start(f32[1024]{0:T(1024)} %param.15) | copy-start | bytes 12292
  39.4 2.0 %copy-start.5 = (bf16[384,2304]{1,0:T(8,128)(2,1)S(1)}, bf16[384,2304]{1,0:T(8,128)(2,1)}, u32[]{:S(2)}) copy-start(bf16[384,2304]{1,0:T(8,128)(2,1)} %constant.17.clone.inverse_ref) | copy-start | bytes 5308420
  47.4 6.2 %collective-permute-start.18 = (bf16[384,128]{1,0:T(8,128)(2,1)S(1)}, bf16[384,128]{1,0:T(8,128)(2,1)S(1)}, u32[]{:S(2)}, u32[]{:S(2)}) collective-permute-start(bf16[384,128]{1,0:T(8,128)(2,1)S(1)} %get-tuple-element.56), channel_id=1, source_target_pairs={{0,16},{4,20},{8,24},{12,28},{16,0},{20,4},{24,8},{28,12},{1,17},{... | collective-permute-start | bytes 294920 | tf_op jit(solution)/shard_map/ppermute | solution.py:673
  49.2 5.4 %collective-permute-start.21 = (bf16[384,128]{1,0:T(8,128)(2,1)S(1)}, bf16[384,128]{1,0:T(8,128)(2,1)S(1)}, u32[]{:S(2)}, u32[]{:S(2)}) collective-permute-start(bf16[384,128]{1,0:T(8,128)(2,1)S(1)} %get-tuple-element.57), channel_id=1, source_target_pairs={{0,4},{4,0},{8,12},{12,8},{16,20},{20,16},{24,28},{28,24},{1,5},{5... | collective-permute-start | bytes 294920 | tf_op jit(solution)/shard_map/ppermute | solution.py:673
  50.5 5.8 %collective-permute-start.22 = (bf16[384,128]{1,0:T(8,128)(2,1)S(1)}, bf16[384,128]{1,0:T(8,128)(2,1)S(1)}, u32[]{:S(2)}, u32[]{:S(2)}) collective-permute-start(bf16[384,128]{1,0:T(8,128)(2,1)S(1)} %get-tuple-element.58), channel_id=1, source_target_pairs={{0,8},{4,12},{8,0},{12,4},{16,24},{20,28},{24,16},{28,20},{1,9},{5... | collective-permute-start | bytes 294920 | tf_op jit(solution)/shard_map/ppermute | solution.py:673
  50.5 7.2 %collective-permute-start.25 = (bf16[384,128]{1,0:T(8,128)(2,1)S(1)}, bf16[384,128]{1,0:T(8,128)(2,1)S(1)}, u32[]{:S(2)}, u32[]{:S(2)}) collective-permute-start(bf16[384,128]{1,0:T(8,128)(2,1)S(1)} %get-tuple-element.59), channel_id=1, source_target_pairs={{0,12},{4,8},{8,4},{12,0},{16,28},{20,24},{24,20},{28,16},{1,13},{... | collective-permute-start | bytes 294920 | tf_op jit(solution)/shard_map/ppermute | solution.py:673
  51.9 6.4 %collective-permute-start.26 = (bf16[384,128]{1,0:T(8,128)(2,1)S(1)}, bf16[384,128]{1,0:T(8,128)(2,1)S(1)}, u32[]{:S(2)}, u32[]{:S(2)}) collective-permute-start(bf16[384,128]{1,0:T(8,128)(2,1)S(1)} %get-tuple-element.60), channel_id=1, source_target_pairs={{0,24},{4,28},{8,16},{12,20},{16,8},{20,12},{24,0},{28,4},{1,25},{... | collective-permute-start | bytes 294920 | tf_op jit(solution)/shard_map/ppermute | solution.py:673
  53.7 11.5 %collective-permute-start.14 = (bf16[384,128]{1,0:T(8,128)(2,1)S(1)}, bf16[384,128]{1,0:T(8,128)(2,1)S(1)}, u32[]{:S(2)}, u32[]{:S(2)}) collective-permute-start(bf16[384,128]{1,0:T(8,128)(2,1)S(1)} %get-tuple-element.53), channel_id=1, source_target_pairs={{0,20},{4,16},{8,28},{12,24},{16,4},{20,0},{24,12},{28,8},{1,21},{... | collective-permute-start | bytes 294920 | tf_op jit(solution)/shard_map/ppermute | solution.py:673
  54.6 10.5 %collective-permute-start.15 = (bf16[384,128]{1,0:T(8,128)(2,1)S(1)}, bf16[384,128]{1,0:T(8,128)(2,1)S(1)}, u32[]{:S(2)}, u32[]{:S(2)}) collective-permute-start(bf16[384,128]{1,0:T(8,128)(2,1)S(1)} %get-tuple-element.54), channel_id=1, source_target_pairs={{0,28},{4,24},{8,20},{12,16},{16,12},{20,8},{24,4},{28,0},{1,29},{... | collective-permute-start | bytes 294920 | tf_op jit(solution)/shard_map/ppermute | solution.py:673
  56.4 10.2 %collective-permute-start.19 = (bf16[384,256]{1,0:T(8,128)(2,1)S(1)}, bf16[384,256]{1,0:T(8,128)(2,1)S(1)}, u32[]{:S(2)}, u32[]{:S(2)}) collective-permute-start(bf16[384,256]{1,0:T(8,128)(2,1)S(1)} %shard_map.109.refs_0_), channel_id=1, source_target_pairs={{0,2},{1,3},{2,0},{3,1},{4,6},{5,7},{6,4},{7,5},{8,10},{9,11},{10,... | collective-permute-start | bytes 589832 | tf_op jit(solution)/shard_map/ppermute | solution.py:700
  57.7 13.4 %collective-permute-start.23 = (bf16[384,256]{1,0:T(8,128)(2,1)S(1)}, bf16[384,256]{1,0:T(8,128)(2,1)S(1)}, u32[]{:S(2)}, u32[]{:S(2)}) collective-permute-start(bf16[384,256]{1,0:T(8,128)(2,1)S(1)} %shard_map.111.refs_0_), channel_id=1, source_target_pairs={{0,2},{1,3},{2,0},{3,1},{4,6},{5,7},{6,4},{7,5},{8,10},{9,11},{10,... | collective-permute-start | bytes 589832 | tf_op jit(solution)/shard_map/ppermute | solution.py:700
  58.3 14.5 %collective-permute-start.27 = (bf16[384,256]{1,0:T(8,128)(2,1)S(1)}, bf16[384,256]{1,0:T(8,128)(2,1)S(1)}, u32[]{:S(2)}, u32[]{:S(2)}) collective-permute-start(bf16[384,256]{1,0:T(8,128)(2,1)S(1)} %shard_map.113.refs_0_), channel_id=1, source_target_pairs={{0,2},{1,3},{2,0},{3,1},{4,6},{5,7},{6,4},{7,5},{8,10},{9,11},{10,... | collective-permute-start | bytes 589832 | tf_op jit(solution)/shard_map/ppermute | solution.py:700
  65.2 9.7 %collective-permute-start.16 = (bf16[384,256]{1,0:T(8,128)(2,1)S(1)}, bf16[384,256]{1,0:T(8,128)(2,1)S(1)}, u32[]{:S(2)}, u32[]{:S(2)}) collective-permute-start(bf16[384,256]{1,0:T(8,128)(2,1)S(1)} %shard_map.107.refs_0_), channel_id=1, source_target_pairs={{0,2},{1,3},{2,0},{3,1},{4,6},{5,7},{6,4},{7,5},{8,10},{9,11},{10,... | collective-permute-start | bytes 589832 | tf_op jit(solution)/shard_map/ppermute | solution.py:700
  66.6 10.4 %collective-permute-start.20 = (bf16[384,512]{1,0:T(8,128)(2,1)S(1)}, bf16[384,512]{1,0:T(8,128)(2,1)S(1)}, u32[]{:S(2)}, u32[]{:S(2)}) collective-permute-start(bf16[384,512]{1,0:T(8,128)(2,1)S(1)} %shard_map.110.refs_0_), channel_id=1, source_target_pairs={{0,1},{1,0},{2,3},{3,2},{4,5},{5,4},{6,7},{7,6},{8,9},{9,8},{10,11... | collective-permute-start | bytes 1179656 | tf_op jit(solution)/shard_map/ppermute | solution.py:702
  71.2 5.8 %collective-permute-start.24 = (bf16[384,512]{1,0:T(8,128)(2,1)S(1)}, bf16[384,512]{1,0:T(8,128)(2,1)S(1)}, u32[]{:S(2)}, u32[]{:S(2)}) collective-permute-start(bf16[384,512]{1,0:T(8,128)(2,1)S(1)} %shard_map.112.refs_2_), channel_id=1, source_target_pairs={{0,1},{1,0},{2,3},{3,2},{4,5},{5,4},{6,7},{7,6},{8,9},{9,8},{10,11... | collective-permute-start | bytes 1179656 | tf_op jit(solution)/shard_map/ppermute | solution.py:702
  72.8 4.2 %collective-permute-start.28 = (bf16[384,512]{1,0:T(8,128)(2,1)S(1)}, bf16[384,512]{1,0:T(8,128)(2,1)S(1)}, u32[]{:S(2)}, u32[]{:S(2)}) collective-permute-start(bf16[384,512]{1,0:T(8,128)(2,1)S(1)} %shard_map.114.refs_4_), channel_id=1, source_target_pairs={{0,1},{1,0},{2,3},{3,2},{4,5},{5,4},{6,7},{7,6},{8,9},{9,8},{10,11... | collective-permute-start | bytes 1179656 | tf_op jit(solution)/shard_map/ppermute | solution.py:702
  74.9 4.7 %collective-permute-start.17 = (bf16[384,512]{1,0:T(8,128)(2,1)S(1)}, bf16[384,512]{1,0:T(8,128)(2,1)S(1)}, u32[]{:S(2)}, u32[]{:S(2)}) collective-permute-start(bf16[384,512]{1,0:T(8,128)(2,1)S(1)} %shard_map.108.refs_0_), channel_id=1, source_target_pairs={{0,1},{1,0},{2,3},{3,2},{4,5},{5,4},{6,7},{7,6},{8,9},{9,8},{10,11... | collective-permute-start | bytes 1179656 | tf_op jit(solution)/shard_map/ppermute | solution.py:702

commit v7 on v6

--- a/solution.py
+++ b/solution.py
@@ -549,8 +549,7 @@
     blocks = with_first(order_ref, places, signal_refs, first_ref)
     spectra_into(order_ref, places, table_ref[...], blocks, spectra_ref)
     multiply_spectra(filter_ref, spectra_ref, high_ref, low_ref)
-    for base in range(0, count, GROUP):
-        inverse_into(order_ref, base, inverse_ref[...], high_ref, low_ref, out_refs[base : base + GROUP])
+    inverse_into(order_ref, 0, inverse_ref[...], high_ref, low_ref, out_refs)
 
 
 def conv_slices(order, table, inverse, filter_spectra, early_spectra, first, blocks, places, after):

time: 81.7 us -> 81.7 us (level)
  no operation moved by 1% of the time
where the time goes in v7:
time: 81.7 us; the launch traced here: 81.6 us
  starting transfers between devices  48.5 us (59%)
  Pallas kernels  23 us (28%)
  waiting for transfers between devices  6.41 us (8%)
  local copies, waits for them, and re-layouts  3.42 us (4%)
    ppermute x21, starting transfers between devices, swap_blocks(): lax.ppermute(blocks[place], 'seq', [(i, i ^ offset) for i in range(count)])  34 us
    ppermute x4, starting transfers between devices, on_device_slices(): lax.ppermute(joined, 'ch', [(i, i ^ 1) for i in range(4)])  10.3 us
    ppermute x21, waiting for transfers between devices, swap_blocks(): lax.ppermute(blocks[place], 'seq', [(i, i ^ offset) for i in range(count)])  6.39 us
    pallas_call x1, Pallas kernels, conv_slices(): pl.pallas_call(functools.partial(conv_slices_kernel, places), in_specs=[p...  5.92 us
    pallas_call x2, Pallas kernels, project_slices(): pl.pallas_call(functools.partial(project_kernel_slices, chunks), in_specs...  4.53 us
    ppermute x4, starting transfers between devices, on_device_slices(): across = lax.ppermute(mixed, 'ch', [(i, i ^ 2) for i in range(4)])  4.2 us
    unnamed x20, local copies, waits for them, and re-layouts  3.42 us
    pallas_call x1, Pallas kernels, cut_filter(): pl.pallas_call(cut_kernel, grid=(1,), in_specs=[pl.BlockSpec((rows, width...  2.6 us
  transfers between devices with their start and end apart: 29, of which 3 were waited for; matrix products, arithmetic and copies ran while one was open for 0% of the time, Pallas kernels for 15%

profile of v7, /device:TPU:1, one launch (start us, length us, event | category | flops | bytes accessed | tf_op | source)
XLA Modules:
  0.0 81.6 jit_solution(4198714697329440667)
XLA Ops:
  0.0 2.6 %shard_map.101 = (bf16[400,128]{1,0:T(8,128)(2,1)}, bf16[400,128]{1,0:T(8,128)(2,1)}, bf16[464,128]{1,0:T(8,128)(2,1)}, bf16[400,128]{1,0:T(8,128)(2,1)}, bf16[4...) custom-call(f32[384,1024]{1,0:T(8,128)} %filter_ref.1, ...), custom_call_target="tpu_custom_call" | custom-call | tf_op jit(solution)/shard_map/pallas_call | solution.py:341
  2.6 2.0 %collective-permute-start = (bf16[464,128]{1,0:T(8,128)(2,1)}, bf16[464,128]{1,0:T(8,128)(2,1)S(1)}, u32[]{:S(2)}, u32[]{:S(2)}) collective-permute-start(bf16[464,128]{1,0:T(8,128)(2,1)} %get-tuple-element.33), channel_id=1, source_target_pairs={{0,4},{4,0},{8,12},{12,8},{16,20},{20,16},{24,28},{28,24},{1,5},{5... | collective-permute-start | bytes 356360 | tf_op jit(solution)/shard_map/ppermute | solution.py:672
  4.7 2.3 %collective-permute-start.3 = (bf16[400,128]{1,0:T(8,128)(2,1)}, bf16[400,128]{1,0:T(8,128)(2,1)S(1)}, u32[]{:S(2)}, u32[]{:S(2)}) collective-permute-start(bf16[400,128]{1,0:T(8,128)(2,1)} %get-tuple-element.39), channel_id=1, source_target_pairs={{0,16},{4,20},{8,24},{12,28},{16,0},{20,4},{24,8},{28,12},{1,17},{... | collective-permute-start | bytes 307208 | tf_op jit(solution)/shard_map/ppermute | solution.py:672
  7.0 1.1 %collective-permute-start.4 = (bf16[400,128]{1,0:T(8,128)(2,1)}, bf16[400,128]{1,0:T(8,128)(2,1)S(1)}, u32[]{:S(2)}, u32[]{:S(2)}) collective-permute-start(bf16[400,128]{1,0:T(8,128)(2,1)} %get-tuple-element.40), channel_id=1, source_target_pairs={{0,24},{4,28},{8,16},{12,20},{16,8},{20,12},{24,0},{28,4},{1,25},{... | collective-permute-start | bytes 307208 | tf_op jit(solution)/shard_map/ppermute | solution.py:672
  8.0 0.2 collective-permute-start.5
  8.3 2.2 %collective-permute-start.6 = (bf16[400,128]{1,0:T(8,128)(2,1)}, bf16[400,128]{1,0:T(8,128)(2,1)S(1)}, u32[]{:S(2)}, u32[]{:S(2)}) collective-permute-start(bf16[400,128]{1,0:T(8,128)(2,1)} %get-tuple-element.42), channel_id=1, source_target_pairs={{0,20},{4,16},{8,28},{12,24},{16,4},{20,0},{24,12},{28,8},{1,21},{... | collective-permute-start | bytes 307208 | tf_op jit(solution)/shard_map/ppermute | solution.py:672
  10.5 0.0 collective-permute-done.3.refs_1_
  10.5 5.8 %collective-permute-start.1 = (bf16[464,128]{1,0:T(8,128)(2,1)}, bf16[464,128]{1,0:T(8,128)(2,1)S(1)}, u32[]{:S(2)}, u32[]{:S(2)}) collective-permute-start(bf16[464,128]{1,0:T(8,128)(2,1)} %get-tuple-element.34), channel_id=1, source_target_pairs={{0,12},{4,8},{8,4},{12,0},{16,28},{20,24},{24,20},{28,16},{1,13},{... | collective-permute-start | bytes 356360 | tf_op jit(solution)/shard_map/ppermute | solution.py:672
  16.3 0.0 collective-permute-done.refs_0_.refs_2_.after_ref
  16.3 3.0 %collective-permute-start.2 = (bf16[464,128]{1,0:T(8,128)(2,1)}, bf16[464,128]{1,0:T(8,128)(2,1)S(1)}, u32[]{:S(2)}, u32[]{:S(2)}) collective-permute-start(bf16[464,128]{1,0:T(8,128)(2,1)} %get-tuple-element.35), channel_id=1, source_target_pairs={{0,28},{4,24},{8,20},{12,16},{16,12},{20,8},{24,4},{28,0},{1,29},{... | collective-permute-start | bytes 356360 | tf_op jit(solution)/shard_map/ppermute | solution.py:672
  19.3 1.9 %shard_map.104 = (bf16[384,128]{1,0:T(8,128)(2,1)S(1)}, bf16[384,128]{1,0:T(8,128)(2,1)S(1)}, bf16[384,128]{1,0:T(8,128)(2,1)S(1)}, bf16[384,128]{1,0:T(8,128)(2...) custom-call(s32[8]{0:T(128)S(1)} %broadcast_xor_fusion.order_ref, ...), custom_call_target="tpu_custom_call" | custom-call | flops 5505024 | bytes 43008 | tf_op jit(solution)/shard_map/pallas_call | solution.py:368
  21.1 0.0 collective-permute-done.4.refs_3_
  21.1 0.5 collective-permute-start.7
  21.7 1.1 %collective-permute-start.8 = (bf16[384,128]{1,0:T(8,128)(2,1)S(1)}, bf16[384,128]{1,0:T(8,128)(2,1)S(1)}, u32[]{:S(2)}, u32[]{:S(2)}) collective-permute-start(bf16[384,128]{1,0:T(8,128)(2,1)S(1)} %get-tuple-element.47), channel_id=1, source_target_pairs={{0,4},{4,0},{8,12},{12,8},{16,20},{20,16},{24,28},{28,24},{1,5},{5... | collective-permute-start | bytes 294920 | tf_op jit(solution)/shard_map/ppermute | solution.py:672
  22.7 3.4 %copy-done.3 = bf16[4096,1024]{1,0:T(8,128)(2,1)S(1)} copy-done((bf16[4096,1024]{1,0:T(8,128)(2,1)S(1)}, bf16[4096,1024]{1,0:T(8,128)(2,1)}, u32[]{:S(2)}) %copy-start.3) | copy-done | bytes 8388632
  26.1 1.7 %shard_map.100.after_ref.refs_5_.rows_ref = bf16[8,4,128,1024]{3,2,1,0:T(8,128)(2,1)S(1)} custom-call(s32[8]{0:T(128)S(1)} %broadcast_xor_fusion.order_ref, s32[1]{0:T(128)} %bitcast.channel_ref, bf16[4096,1024]{1,0:T(8,128)(2,1)S(1)} %copy-done.3), custom_call_target="tpu_custom_call" | custom-call | bytes 16777216 | tf_op jit(solution)/shard_map/pallas_call | solution.py:610
  27.8 0.0 collective-permute-done.6.refs_5_
  27.8 2.1 %collective-permute-start.9 = (bf16[384,128]{1,0:T(8,128)(2,1)S(1)}, bf16[384,128]{1,0:T(8,128)(2,1)S(1)}, u32[]{:S(2)}, u32[]{:S(2)}) collective-permute-start(bf16[384,128]{1,0:T(8,128)(2,1)S(1)} %get-tuple-element.48), channel_id=1, source_target_pairs={{0,20},{4,16},{8,28},{12,24},{16,4},{20,0},{24,12},{28,8},{1,21},{... | collective-permute-start | bytes 294920 | tf_op jit(solution)/shard_map/ppermute | solution.py:672
  29.9 0.0 collective-permute-done.1.refs_1_.refs_6_
  29.9 1.5 %collective-permute-start.10 = (bf16[384,128]{1,0:T(8,128)(2,1)S(1)}, bf16[384,128]{1,0:T(8,128)(2,1)S(1)}, u32[]{:S(2)}, u32[]{:S(2)}) collective-permute-start(bf16[384,128]{1,0:T(8,128)(2,1)S(1)} %get-tuple-element.49), channel_id=1, source_target_pairs={{0,8},{4,12},{8,0},{12,4},{16,24},{20,28},{24,16},{28,20},{1,9},{5... | collective-permute-start | bytes 294920 | tf_op jit(solution)/shard_map/ppermute | solution.py:672
  31.4 0.0 collective-permute-done.2.refs_2_.refs_7_
  31.4 0.1 collective-permute-start.11
  31.6 0.0 collective-permute-done.7.refs_1_
  31.6 0.8 %collective-permute-start.12 = (bf16[384,128]{1,0:T(8,128)(2,1)S(1)}, bf16[384,128]{1,0:T(8,128)(2,1)S(1)}, u32[]{:S(2)}, u32[]{:S(2)}) collective-permute-start(bf16[384,128]{1,0:T(8,128)(2,1)S(1)} %get-tuple-element.51), channel_id=1, source_target_pairs={{0,12},{4,8},{8,4},{12,0},{16,28},{20,24},{24,20},{28,16},{1,13},{... | collective-permute-start | bytes 294920 | tf_op jit(solution)/shard_map/ppermute | solution.py:672
  32.4 2.4 %collective-permute-start.13 = (bf16[384,128]{1,0:T(8,128)(2,1)S(1)}, bf16[384,128]{1,0:T(8,128)(2,1)S(1)}, u32[]{:S(2)}, u32[]{:S(2)}) collective-permute-start(bf16[384,128]{1,0:T(8,128)(2,1)S(1)} %get-tuple-element.52), channel_id=1, source_target_pairs={{0,28},{4,24},{8,20},{12,16},{16,12},{20,8},{24,4},{28,0},{1,29},{... | collective-permute-start | bytes 294920 | tf_op jit(solution)/shard_map/ppermute | solution.py:672
  34.8 2.1 %shard_map.103 = (f32[8,768,128]{2,1,0:T(8,128)S(1)}, f32[8,16,128]{2,1,0:T(8,128)S(1)}) custom-call(s32[8]{0:T(128)S(1)} %broadcast_xor_fusion.order_ref, bf16[768,768]{1,0:T(8,128)(2,1)S(1)} %copy-done.2, f32[3,3,1024]{2,1,0:T(4,128)S(1)} %copy-done.6, bf16[8,4,128,1024]{3,2,1,0:T(8,128)(2,1)S(1)} %shard_map.100.after_ref.refs_5_.rows_ref, ...), custom_call_target="tpu_custom_call" | custom-call | flops 1207959552 | bytes 9437184 | tf_op jit(solution)/shard_map/pallas_call | solution.py:467
  36.9 2.5 %shard_map.102 = (f32[8,384,128]{2,1,0:T(8,128)S(1)}, f32[8,384,128]{2,1,0:T(8,128)S(1)}) custom-call(s32[8]{0:T(128)S(1)} %broadcast_xor_fusion.order_ref, bf16[384,1024]{1,0:T(8,128)(2,1)S(1)} %copy-done.4, bf16[384,1024]{1,0:T(8,128)(2,1)S(1)} %copy-done, bf16[384,1024]{1,0:T(8,128)(2,1)S(1)} %copy-done.1, ...), custom_call_target="tpu_custom_call" | custom-call | flops 7864320 | bytes 61440 | tf_op jit(solution)/shard_map/pallas_call | solution.py:409
  39.4 0.0 copy-start.5
  39.5 1.4 %shard_map.105.early_ref = f32[8,768,128]{2,1,0:T(8,128)S(1)} custom-call(s32[8]{0:T(128)S(1)} %broadcast_xor_fusion.order_ref, bf16[768,768]{1,0:T(8,128)(2,1)S(1)} %copy-done.2, f32[8,16,128]{2,1,0:T(8,128)S(1)} %get-tuple-element.44.first_ref, bf16[384,128]{1,0:T(8,128)(2,1)S(1)} %get-tuple-element.45.refs_0_, ...), custom_call_target="tpu_custom_call" | custom-call | flops 603979776 | bytes 4718592 | tf_op jit(solution)/shard_map/pallas_call | solution.py:489
  40.9 0.0 collective-permute-done.11.refs_1_
  40.9 0.6 collective-permute-done.13.refs_3_
  41.5 5.9 %shard_map.106 = (f32[8,768,128]{2,1,0:T(8,128)S(1)}, bf16[384,128]{1,0:T(8,128)(2,1)S(1)}, bf16[384,128]{1,0:T(8,128)(2,1)S(1)}, bf16[384,128]{1,0:T(8,128)(2,1...) custom-call(s32[8]{0:T(128)S(1)} %broadcast_xor_fusion.order_ref, ...), custom_call_target="tpu_custom_call", output_to_operand_aliasing={{0}: (4, {})} | custom-call | flops 2113929216 | bytes 16515072 | tf_op jit(solution)/shard_map/pallas_call | solution.py:558
  47.4 1.8 %collective-permute-start.18 = (bf16[384,128]{1,0:T(8,128)(2,1)S(1)}, bf16[384,128]{1,0:T(8,128)(2,1)S(1)}, u32[]{:S(2)}, u32[]{:S(2)}) collective-permute-start(bf16[384,128]{1,0:T(8,128)(2,1)S(1)} %get-tuple-element.56), channel_id=1, source_target_pairs={{0,16},{4,20},{8,24},{12,28},{16,0},{20,4},{24,8},{28,12},{1,17},{... | collective-permute-start | bytes 294920 | tf_op jit(solution)/shard_map/ppermute | solution.py:672
  49.2 1.3 %collective-permute-start.21 = (bf16[384,128]{1,0:T(8,128)(2,1)S(1)}, bf16[384,128]{1,0:T(8,128)(2,1)S(1)}, u32[]{:S(2)}, u32[]{:S(2)}) collective-permute-start(bf16[384,128]{1,0:T(8,128)(2,1)S(1)} %get-tuple-element.57), channel_id=1, source_target_pairs={{0,4},{4,0},{8,12},{12,8},{16,20},{20,16},{24,28},{28,24},{1,5},{5... | collective-permute-start | bytes 294920 | tf_op jit(solution)/shard_map/ppermute | solution.py:672
  50.5 1.3 %collective-permute-start.25 = (bf16[384,128]{1,0:T(8,128)(2,1)S(1)}, bf16[384,128]{1,0:T(8,128)(2,1)S(1)}, u32[]{:S(2)}, u32[]{:S(2)}) collective-permute-start(bf16[384,128]{1,0:T(8,128)(2,1)S(1)} %get-tuple-element.59), channel_id=1, source_target_pairs={{0,12},{4,8},{8,4},{12,0},{16,28},{20,24},{24,20},{28,16},{1,13},{... | collective-permute-start | bytes 294920 | tf_op jit(solution)/shard_map/ppermute | solution.py:672
  51.9 1.8 %collective-permute-start.26 = (bf16[384,128]{1,0:T(8,128)(2,1)S(1)}, bf16[384,128]{1,0:T(8,128)(2,1)S(1)}, u32[]{:S(2)}, u32[]{:S(2)}) collective-permute-start(bf16[384,128]{1,0:T(8,128)(2,1)S(1)} %get-tuple-element.60), channel_id=1, source_target_pairs={{0,24},{4,28},{8,16},{12,20},{16,8},{20,12},{24,0},{28,4},{1,25},{... | collective-permute-start | bytes 294920 | tf_op jit(solution)/shard_map/ppermute | solution.py:672
  53.7 0.0 collective-permute-done.18.refs_1_
  53.7 1.0 %collective-permute-start.14 = (bf16[384,128]{1,0:T(8,128)(2,1)S(1)}, bf16[384,128]{1,0:T(8,128)(2,1)S(1)}, u32[]{:S(2)}, u32[]{:S(2)}) collective-permute-start(bf16[384,128]{1,0:T(8,128)(2,1)S(1)} %get-tuple-element.53), channel_id=1, source_target_pairs={{0,20},{4,16},{8,28},{12,24},{16,4},{20,0},{24,12},{28,8},{1,21},{... | collective-permute-start | bytes 294920 | tf_op jit(solution)/shard_map/ppermute | solution.py:672
  54.6 0.0 collective-permute-done.21.refs_0_
  54.6 1.7 %collective-permute-start.15 = (bf16[384,128]{1,0:T(8,128)(2,1)S(1)}, bf16[384,128]{1,0:T(8,128)(2,1)S(1)}, u32[]{:S(2)}, u32[]{:S(2)}) collective-permute-start(bf16[384,128]{1,0:T(8,128)(2,1)S(1)} %get-tuple-element.54), channel_id=1, source_target_pairs={{0,28},{4,24},{8,20},{12,16},{16,12},{20,8},{24,4},{28,0},{1,29},{... | collective-permute-start | bytes 294920 | tf_op jit(solution)/shard_map/ppermute | solution.py:672
  56.3 0.1 shard_map.109.refs_0_
  56.3 0.0 collective-permute-done.22.refs_1_
  56.4 1.3 %collective-permute-start.19 = (bf16[384,256]{1,0:T(8,128)(2,1)S(1)}, bf16[384,256]{1,0:T(8,128)(2,1)S(1)}, u32[]{:S(2)}, u32[]{:S(2)}) collective-permute-start(bf16[384,256]{1,0:T(8,128)(2,1)S(1)} %shard_map.109.refs_0_), channel_id=1, source_target_pairs={{0,2},{1,3},{2,0},{3,1},{4,6},{5,7},{6,4},{7,5},{8,10},{9,11},{10,... | collective-permute-start | bytes 589832 | tf_op jit(solution)/shard_map/ppermute | solution.py:699
  57.7 0.1 shard_map.111.refs_0_
  57.7 0.3 collective-permute-start.23
  58.0 0.2 collective-permute-done.26.refs_1_
  58.2 0.1 shard_map.113.refs_0_
  58.3 1.3 %collective-permute-start.27 = (bf16[384,256]{1,0:T(8,128)(2,1)S(1)}, bf16[384,256]{1,0:T(8,128)(2,1)S(1)}, u32[]{:S(2)}, u32[]{:S(2)}) collective-permute-start(bf16[384,256]{1,0:T(8,128)(2,1)S(1)} %shard_map.113.refs_0_), channel_id=1, source_target_pairs={{0,2},{1,3},{2,0},{3,1},{4,6},{5,7},{6,4},{7,5},{8,10},{9,11},{10,... | collective-permute-start | bytes 589832 | tf_op jit(solution)/shard_map/ppermute | solution.py:699
  59.6 5.6 %collective-permute-done.14.refs_0_ = bf16[384,128]{1,0:T(8,128)(2,1)S(1)} collective-permute-done((bf16[384,128]{1,0:T(8,128)(2,1)S(1)}, bf16[384,128]{1,0:T(8,128)(2,1)S(1)}, u32[]{:S(2)}, u32[]{:S(2)}) %collective-permute-start.14) | collective-permute-done | bytes 98336 | tf_op jit(solution)/shard_map/ppermute | solution.py:672
  65.2 0.1 shard_map.107.refs_0_
  65.2 1.3 %collective-permute-start.16 = (bf16[384,256]{1,0:T(8,128)(2,1)S(1)}, bf16[384,256]{1,0:T(8,128)(2,1)S(1)}, u32[]{:S(2)}, u32[]{:S(2)}) collective-permute-start(bf16[384,256]{1,0:T(8,128)(2,1)S(1)} %shard_map.107.refs_0_), channel_id=1, source_target_pairs={{0,2},{1,3},{2,0},{3,1},{4,6},{5,7},{6,4},{7,5},{8,10},{9,11},{10,... | collective-permute-start | bytes 589832 | tf_op jit(solution)/shard_map/ppermute | solution.py:699
  66.5 0.0 collective-permute-done.19.refs_1_
  66.6 4.6 %collective-permute-start.20 = (bf16[384,512]{1,0:T(8,128)(2,1)S(1)}, bf16[384,512]{1,0:T(8,128)(2,1)S(1)}, u32[]{:S(2)}, u32[]{:S(2)}) collective-permute-start(bf16[384,512]{1,0:T(8,128)(2,1)S(1)} %shard_map.110.refs_0_), channel_id=1, source_target_pairs={{0,1},{1,0},{2,3},{3,2},{4,5},{5,4},{6,7},{7,6},{8,9},{9,8},{10,11... | collective-permute-start | bytes 1179656 | tf_op jit(solution)/shard_map/ppermute | solution.py:701
  71.2 1.6 %collective-permute-start.24 = (bf16[384,512]{1,0:T(8,128)(2,1)S(1)}, bf16[384,512]{1,0:T(8,128)(2,1)S(1)}, u32[]{:S(2)}, u32[]{:S(2)}) collective-permute-start(bf16[384,512]{1,0:T(8,128)(2,1)S(1)} %shard_map.112.refs_2_), channel_id=1, source_target_pairs={{0,1},{1,0},{2,3},{3,2},{4,5},{5,4},{6,7},{7,6},{8,9},{9,8},{10,11... | collective-permute-start | bytes 1179656 | tf_op jit(solution)/shard_map/ppermute | solution.py:701
  72.8 0.0 collective-permute-done.27.refs_1_
  72.8 2.1 %collective-permute-start.28 = (bf16[384,512]{1,0:T(8,128)(2,1)S(1)}, bf16[384,512]{1,0:T(8,128)(2,1)S(1)}, u32[]{:S(2)}, u32[]{:S(2)}) collective-permute-start(bf16[384,512]{1,0:T(8,128)(2,1)S(1)} %shard_map.114.refs_4_), channel_id=1, source_target_pairs={{0,1},{1,0},{2,3},{3,2},{4,5},{5,4},{6,7},{7,6},{8,9},{9,8},{10,11... | collective-permute-start | bytes 1179656 | tf_op jit(solution)/shard_map/ppermute | solution.py:701
  74.9 0.0 collective-permute-done.16.refs_1_
  74.9 2.1 %collective-permute-start.17 = (bf16[384,512]{1,0:T(8,128)(2,1)S(1)}, bf16[384,512]{1,0:T(8,128)(2,1)S(1)}, u32[]{:S(2)}, u32[]{:S(2)}) collective-permute-start(bf16[384,512]{1,0:T(8,128)(2,1)S(1)} %shard_map.108.refs_0_), channel_id=1, source_target_pairs={{0,1},{1,0},{2,3},{3,2},{4,5},{5,4},{6,7},{7,6},{8,9},{9,8},{10,11... | collective-permute-start | bytes 1179656 | tf_op jit(solution)/shard_map/ppermute | solution.py:701
  77.0 0.0 collective-permute-done.20.refs_1_
  77.0 0.0 collective-permute-done.24.refs_3_
  77.0 0.0 collective-permute-done.28.refs_5_
  77.0 2.6 %shard_map.115.refs_2_ = f32[384,1024]{1,0:T(8,128)S(1)} custom-call(bf16[8,4,128,1024]{3,2,1,0:T(8,128)(2,1)S(1)} %shard_map.100.after_ref.refs_5_.rows_ref, bf16[384,512]{1,0:T(8,128)(2,1)S(1)} %shard_map.110.refs_0_, bf16[384,512]{1,0:T(8,128)(2,1)S(1)} %collective-permute-done.20.refs_1_, bf16[384,512]{1,0:T(8,128)(2,1)S(1)} %shard_map.112.refs_2_, ...), custom_call_target="tpu_custom_call" | custom-call | tf_op jit(solution)/shard_map/pallas_call | solution.py:657
  79.7 0.0 collective-permute-done.17.refs_1_
  79.7 1.9 %shard_map.116 = bf16[384,1024]{1,0:T(8,128)(2,1)} custom-call(bf16[8,4,128,1024]{3,2,1,0:T(8,128)(2,1)S(1)} %shard_map.100.after_ref.refs_5_.rows_ref, bf16[384,512]{1,0:T(8,128)(2,1)S(1)} %shard_map.108.refs_0_, bf16[384,512]{1,0:T(8,128)(2,1)S(1)} %collective-permute-done.17.refs_1_, f32[384,1024]{1,0:T(8,128)S(1)} %shard_map.115.refs_2_), custom_call_target="tpu_custom_call" | custom-call | tf_op jit(solution)/shard_map/pallas_call | solution.py:657
  (32 shorter events, 0.2 us)
Async XLA Ops:
  0.0 19.2 %copy-start.9 = (s32[8]{0:T(128)S(1)}, s32[8]{0:T(128)}, u32[]{:S(2)}) copy-start(s32[8]{0:T(128)} %constant.15.clone) | copy-start | bytes 100
  0.0 19.3 %copy-start.1 = (bf16[384,1024]{1,0:T(8,128)(2,1)S(1)}, bf16[384,1024]{1,0:T(8,128)(2,1)}, u32[]{:S(2)}) copy-start(bf16[384,1024]{1,0:T(8,128)(2,1)} %value_ref.3) | copy-start | bytes 2359300
  0.0 19.3 %copy-start = (bf16[384,1024]{1,0:T(8,128)(2,1)S(1)}, bf16[384,1024]{1,0:T(8,128)(2,1)}, u32[]{:S(2)}) copy-start(bf16[384,1024]{1,0:T(8,128)(2,1)} %gate_ref.3) | copy-start | bytes 2359300
  0.0 19.3 %copy-start.6 = (f32[3,3,1024]{2,1,0:T(4,128)S(1)}, f32[3,3,1024]{2,1,0:T(4,128)}, u32[]{:S(2)}) copy-start(f32[3,3,1024]{2,1,0:T(4,128)} %taps_ref.3) | copy-start | bytes 110596
  2.6 13.6 %collective-permute-start = (bf16[464,128]{1,0:T(8,128)(2,1)}, bf16[464,128]{1,0:T(8,128)(2,1)S(1)}, u32[]{:S(2)}, u32[]{:S(2)}) collective-permute-start(bf16[464,128]{1,0:T(8,128)(2,1)} %get-tuple-element.33), channel_id=1, source_target_pairs={{0,4},{4,0},{8,12},{12,8},{16,20},{20,16},{24,28},{28,24},{1,5},{5... | collective-permute-start | bytes 356360 | tf_op jit(solution)/shard_map/ppermute | solution.py:672
  4.7 5.8 %collective-permute-start.3 = (bf16[400,128]{1,0:T(8,128)(2,1)}, bf16[400,128]{1,0:T(8,128)(2,1)S(1)}, u32[]{:S(2)}, u32[]{:S(2)}) collective-permute-start(bf16[400,128]{1,0:T(8,128)(2,1)} %get-tuple-element.39), channel_id=1, source_target_pairs={{0,16},{4,20},{8,24},{12,28},{16,0},{20,4},{24,8},{28,12},{1,17},{... | collective-permute-start | bytes 307208 | tf_op jit(solution)/shard_map/ppermute | solution.py:672
  7.0 14.2 %collective-permute-start.4 = (bf16[400,128]{1,0:T(8,128)(2,1)}, bf16[400,128]{1,0:T(8,128)(2,1)S(1)}, u32[]{:S(2)}, u32[]{:S(2)}) collective-permute-start(bf16[400,128]{1,0:T(8,128)(2,1)} %get-tuple-element.40), channel_id=1, source_target_pairs={{0,24},{4,28},{8,16},{12,20},{16,8},{20,12},{24,0},{28,4},{1,25},{... | collective-permute-start | bytes 307208 | tf_op jit(solution)/shard_map/ppermute | solution.py:672
  8.0 13.6 %collective-permute-start.5 = (bf16[400,128]{1,0:T(8,128)(2,1)}, bf16[400,128]{1,0:T(8,128)(2,1)S(1)}, u32[]{:S(2)}, u32[]{:S(2)}) collective-permute-start(bf16[400,128]{1,0:T(8,128)(2,1)} %get-tuple-element.41), channel_id=1, source_target_pairs={{0,8},{4,12},{8,0},{12,4},{16,24},{20,28},{24,16},{28,20},{1,9},{5... | collective-permute-start | bytes 307208 | tf_op jit(solution)/shard_map/ppermute | solution.py:672
  8.3 19.6 %collective-permute-start.6 = (bf16[400,128]{1,0:T(8,128)(2,1)}, bf16[400,128]{1,0:T(8,128)(2,1)S(1)}, u32[]{:S(2)}, u32[]{:S(2)}) collective-permute-start(bf16[400,128]{1,0:T(8,128)(2,1)} %get-tuple-element.42), channel_id=1, source_target_pairs={{0,20},{4,16},{8,28},{12,24},{16,4},{20,0},{24,12},{28,8},{1,21},{... | collective-permute-start | bytes 307208 | tf_op jit(solution)/shard_map/ppermute | solution.py:672
  10.5 19.4 %collective-permute-start.1 = (bf16[464,128]{1,0:T(8,128)(2,1)}, bf16[464,128]{1,0:T(8,128)(2,1)S(1)}, u32[]{:S(2)}, u32[]{:S(2)}) collective-permute-start(bf16[464,128]{1,0:T(8,128)(2,1)} %get-tuple-element.34), channel_id=1, source_target_pairs={{0,12},{4,8},{8,4},{12,0},{16,28},{20,24},{24,20},{28,16},{1,13},{... | collective-permute-start | bytes 356360 | tf_op jit(solution)/shard_map/ppermute | solution.py:672
  16.3 15.2 %collective-permute-start.2 = (bf16[464,128]{1,0:T(8,128)(2,1)}, bf16[464,128]{1,0:T(8,128)(2,1)S(1)}, u32[]{:S(2)}, u32[]{:S(2)}) collective-permute-start(bf16[464,128]{1,0:T(8,128)(2,1)} %get-tuple-element.35), channel_id=1, source_target_pairs={{0,28},{4,24},{8,20},{12,16},{16,12},{20,8},{24,4},{28,0},{1,29},{... | collective-permute-start | bytes 356360 | tf_op jit(solution)/shard_map/ppermute | solution.py:672
  21.1 10.4 %collective-permute-start.7 = (bf16[384,128]{1,0:T(8,128)(2,1)S(1)}, bf16[384,128]{1,0:T(8,128)(2,1)S(1)}, u32[]{:S(2)}, u32[]{:S(2)}) collective-permute-start(bf16[384,128]{1,0:T(8,128)(2,1)S(1)} %get-tuple-element.46), channel_id=1, source_target_pairs={{0,16},{4,20},{8,24},{12,28},{16,0},{20,4},{24,8},{28,12},{1,17},{... | collective-permute-start | bytes 294920 | tf_op jit(solution)/shard_map/ppermute | solution.py:672
  21.7 10.7 %collective-permute-start.8 = (bf16[384,128]{1,0:T(8,128)(2,1)S(1)}, bf16[384,128]{1,0:T(8,128)(2,1)S(1)}, u32[]{:S(2)}, u32[]{:S(2)}) collective-permute-start(bf16[384,128]{1,0:T(8,128)(2,1)S(1)} %get-tuple-element.47), channel_id=1, source_target_pairs={{0,4},{4,0},{8,12},{12,8},{16,20},{20,16},{24,28},{28,24},{1,5},{5... | collective-permute-start | bytes 294920 | tf_op jit(solution)/shard_map/ppermute | solution.py:672
  22.7 3.4 %copy-start.3 = (bf16[4096,1024]{1,0:T(8,128)(2,1)S(1)}, bf16[4096,1024]{1,0:T(8,128)(2,1)}, u32[]{:S(2)}) copy-start(bf16[4096,1024]{1,0:T(8,128)(2,1)} %weight_ref.1) | copy-start | bytes 25165828
  26.1 8.7 %copy-start.2 = (bf16[768,768]{1,0:T(8,128)(2,1)S(1)}, bf16[768,768]{1,0:T(8,128)(2,1)}, u32[]{:S(2)}) copy-start(bf16[768,768]{1,0:T(8,128)(2,1)} %constant.16.clone.table_ref) | copy-start | bytes 3538948
  26.1 8.7 %copy-start.7 = (bf16[400,128]{1,0:T(8,128)(2,1)S(1)}, bf16[400,128]{1,0:T(8,128)(2,1)}, u32[]{:S(2)}) copy-start(bf16[400,128]{1,0:T(8,128)(2,1)} %get-tuple-element.38.refs_0_) | copy-start | bytes 307204
  27.8 11.6 %collective-permute-start.9 = (bf16[384,128]{1,0:T(8,128)(2,1)S(1)}, bf16[384,128]{1,0:T(8,128)(2,1)S(1)}, u32[]{:S(2)}, u32[]{:S(2)}) collective-permute-start(bf16[384,128]{1,0:T(8,128)(2,1)S(1)} %get-tuple-element.48), channel_id=1, source_target_pairs={{0,20},{4,16},{8,28},{12,24},{16,4},{20,0},{24,12},{28,8},{1,21},{... | collective-permute-start | bytes 294920 | tf_op jit(solution)/shard_map/ppermute | solution.py:672
  29.9 10.9 %collective-permute-start.10 = (bf16[384,128]{1,0:T(8,128)(2,1)S(1)}, bf16[384,128]{1,0:T(8,128)(2,1)S(1)}, u32[]{:S(2)}, u32[]{:S(2)}) collective-permute-start(bf16[384,128]{1,0:T(8,128)(2,1)S(1)} %get-tuple-element.49), channel_id=1, source_target_pairs={{0,8},{4,12},{8,0},{12,4},{16,24},{20,28},{24,16},{28,20},{1,9},{5... | collective-permute-start | bytes 294920 | tf_op jit(solution)/shard_map/ppermute | solution.py:672
  31.4 9.4 %collective-permute-start.11 = (bf16[384,128]{1,0:T(8,128)(2,1)S(1)}, bf16[384,128]{1,0:T(8,128)(2,1)S(1)}, u32[]{:S(2)}, u32[]{:S(2)}) collective-permute-start(bf16[384,128]{1,0:T(8,128)(2,1)S(1)} %get-tuple-element.50), channel_id=1, source_target_pairs={{0,24},{4,28},{8,16},{12,20},{16,8},{20,12},{24,0},{28,4},{1,25},{... | collective-permute-start | bytes 294920 | tf_op jit(solution)/shard_map/ppermute | solution.py:672
  31.6 9.3 %collective-permute-start.12 = (bf16[384,128]{1,0:T(8,128)(2,1)S(1)}, bf16[384,128]{1,0:T(8,128)(2,1)S(1)}, u32[]{:S(2)}, u32[]{:S(2)}) collective-permute-start(bf16[384,128]{1,0:T(8,128)(2,1)S(1)} %get-tuple-element.51), channel_id=1, source_target_pairs={{0,12},{4,8},{8,4},{12,0},{16,28},{20,24},{24,20},{28,16},{1,13},{... | collective-permute-start | bytes 294920 | tf_op jit(solution)/shard_map/ppermute | solution.py:672
  32.4 9.1 %collective-permute-start.13 = (bf16[384,128]{1,0:T(8,128)(2,1)S(1)}, bf16[384,128]{1,0:T(8,128)(2,1)S(1)}, u32[]{:S(2)}, u32[]{:S(2)}) collective-permute-start(bf16[384,128]{1,0:T(8,128)(2,1)S(1)} %get-tuple-element.52), channel_id=1, source_target_pairs={{0,28},{4,24},{8,20},{12,16},{16,12},{20,8},{24,4},{28,0},{1,29},{... | collective-permute-start | bytes 294920 | tf_op jit(solution)/shard_map/ppermute | solution.py:672
  34.8 2.1 %copy-start.4 = (bf16[384,1024]{1,0:T(8,128)(2,1)S(1)}, bf16[384,1024]{1,0:T(8,128)(2,1)}, u32[]{:S(2)}) copy-start(bf16[384,1024]{1,0:T(8,128)(2,1)} %late_ref.1) | copy-start | bytes 2359300
  34.8 2.1 %copy-start.8 = (f32[1024]{0:T(1024)S(1)}, f32[1024]{0:T(1024)}, u32[]{:S(2)}) copy-start(f32[1024]{0:T(1024)} %param.15) | copy-start | bytes 12292
  39.4 2.0 %copy-start.5 = (bf16[384,2304]{1,0:T(8,128)(2,1)S(1)}, bf16[384,2304]{1,0:T(8,128)(2,1)}, u32[]{:S(2)}) copy-start(bf16[384,2304]{1,0:T(8,128)(2,1)} %constant.17.clone.inverse_ref) | copy-start | bytes 5308420
  47.4 6.2 %collective-permute-start.18 = (bf16[384,128]{1,0:T(8,128)(2,1)S(1)}, bf16[384,128]{1,0:T(8,128)(2,1)S(1)}, u32[]{:S(2)}, u32[]{:S(2)}) collective-permute-start(bf16[384,128]{1,0:T(8,128)(2,1)S(1)} %get-tuple-element.56), channel_id=1, source_target_pairs={{0,16},{4,20},{8,24},{12,28},{16,0},{20,4},{24,8},{28,12},{1,17},{... | collective-permute-start | bytes 294920 | tf_op jit(solution)/shard_map/ppermute | solution.py:672
  49.2 5.4 %collective-permute-start.21 = (bf16[384,128]{1,0:T(8,128)(2,1)S(1)}, bf16[384,128]{1,0:T(8,128)(2,1)S(1)}, u32[]{:S(2)}, u32[]{:S(2)}) collective-permute-start(bf16[384,128]{1,0:T(8,128)(2,1)S(1)} %get-tuple-element.57), channel_id=1, source_target_pairs={{0,4},{4,0},{8,12},{12,8},{16,20},{20,16},{24,28},{28,24},{1,5},{5... | collective-permute-start | bytes 294920 | tf_op jit(solution)/shard_map/ppermute | solution.py:672
  50.5 5.8 %collective-permute-start.22 = (bf16[384,128]{1,0:T(8,128)(2,1)S(1)}, bf16[384,128]{1,0:T(8,128)(2,1)S(1)}, u32[]{:S(2)}, u32[]{:S(2)}) collective-permute-start(bf16[384,128]{1,0:T(8,128)(2,1)S(1)} %get-tuple-element.58), channel_id=1, source_target_pairs={{0,8},{4,12},{8,0},{12,4},{16,24},{20,28},{24,16},{28,20},{1,9},{5... | collective-permute-start | bytes 294920 | tf_op jit(solution)/shard_map/ppermute | solution.py:672
  50.5 7.2 %collective-permute-start.25 = (bf16[384,128]{1,0:T(8,128)(2,1)S(1)}, bf16[384,128]{1,0:T(8,128)(2,1)S(1)}, u32[]{:S(2)}, u32[]{:S(2)}) collective-permute-start(bf16[384,128]{1,0:T(8,128)(2,1)S(1)} %get-tuple-element.59), channel_id=1, source_target_pairs={{0,12},{4,8},{8,4},{12,0},{16,28},{20,24},{24,20},{28,16},{1,13},{... | collective-permute-start | bytes 294920 | tf_op jit(solution)/shard_map/ppermute | solution.py:672
  51.9 6.4 %collective-permute-start.26 = (bf16[384,128]{1,0:T(8,128)(2,1)S(1)}, bf16[384,128]{1,0:T(8,128)(2,1)S(1)}, u32[]{:S(2)}, u32[]{:S(2)}) collective-permute-start(bf16[384,128]{1,0:T(8,128)(2,1)S(1)} %get-tuple-element.60), channel_id=1, source_target_pairs={{0,24},{4,28},{8,16},{12,20},{16,8},{20,12},{24,0},{28,4},{1,25},{... | collective-permute-start | bytes 294920 | tf_op jit(solution)/shard_map/ppermute | solution.py:672
  53.7 11.5 %collective-permute-start.14 = (bf16[384,128]{1,0:T(8,128)(2,1)S(1)}, bf16[384,128]{1,0:T(8,128)(2,1)S(1)}, u32[]{:S(2)}, u32[]{:S(2)}) collective-permute-start(bf16[384,128]{1,0:T(8,128)(2,1)S(1)} %get-tuple-element.53), channel_id=1, source_target_pairs={{0,20},{4,16},{8,28},{12,24},{16,4},{20,0},{24,12},{28,8},{1,21},{... | collective-permute-start | bytes 294920 | tf_op jit(solution)/shard_map/ppermute | solution.py:672
  54.6 10.5 %collective-permute-start.15 = (bf16[384,128]{1,0:T(8,128)(2,1)S(1)}, bf16[384,128]{1,0:T(8,128)(2,1)S(1)}, u32[]{:S(2)}, u32[]{:S(2)}) collective-permute-start(bf16[384,128]{1,0:T(8,128)(2,1)S(1)} %get-tuple-element.54), channel_id=1, source_target_pairs={{0,28},{4,24},{8,20},{12,16},{16,12},{20,8},{24,4},{28,0},{1,29},{... | collective-permute-start | bytes 294920 | tf_op jit(solution)/shard_map/ppermute | solution.py:672
  56.4 10.2 %collective-permute-start.19 = (bf16[384,256]{1,0:T(8,128)(2,1)S(1)}, bf16[384,256]{1,0:T(8,128)(2,1)S(1)}, u32[]{:S(2)}, u32[]{:S(2)}) collective-permute-start(bf16[384,256]{1,0:T(8,128)(2,1)S(1)} %shard_map.109.refs_0_), channel_id=1, source_target_pairs={{0,2},{1,3},{2,0},{3,1},{4,6},{5,7},{6,4},{7,5},{8,10},{9,11},{10,... | collective-permute-start | bytes 589832 | tf_op jit(solution)/shard_map/ppermute | solution.py:699
  57.7 13.4 %collective-permute-start.23 = (bf16[384,256]{1,0:T(8,128)(2,1)S(1)}, bf16[384,256]{1,0:T(8,128)(2,1)S(1)}, u32[]{:S(2)}, u32[]{:S(2)}) collective-permute-start(bf16[384,256]{1,0:T(8,128)(2,1)S(1)} %shard_map.111.refs_0_), channel_id=1, source_target_pairs={{0,2},{1,3},{2,0},{3,1},{4,6},{5,7},{6,4},{7,5},{8,10},{9,11},{10,... | collective-permute-start | bytes 589832 | tf_op jit(solution)/shard_map/ppermute | solution.py:699
  58.3 14.5 %collective-permute-start.27 = (bf16[384,256]{1,0:T(8,128)(2,1)S(1)}, bf16[384,256]{1,0:T(8,128)(2,1)S(1)}, u32[]{:S(2)}, u32[]{:S(2)}) collective-permute-start(bf16[384,256]{1,0:T(8,128)(2,1)S(1)} %shard_map.113.refs_0_), channel_id=1, source_target_pairs={{0,2},{1,3},{2,0},{3,1},{4,6},{5,7},{6,4},{7,5},{8,10},{9,11},{10,... | collective-permute-start | bytes 589832 | tf_op jit(solution)/shard_map/ppermute | solution.py:699
  65.2 9.7 %collective-permute-start.16 = (bf16[384,256]{1,0:T(8,128)(2,1)S(1)}, bf16[384,256]{1,0:T(8,128)(2,1)S(1)}, u32[]{:S(2)}, u32[]{:S(2)}) collective-permute-start(bf16[384,256]{1,0:T(8,128)(2,1)S(1)} %shard_map.107.refs_0_), channel_id=1, source_target_pairs={{0,2},{1,3},{2,0},{3,1},{4,6},{5,7},{6,4},{7,5},{8,10},{9,11},{10,... | collective-permute-start | bytes 589832 | tf_op jit(solution)/shard_map/ppermute | solution.py:699
  66.6 10.4 %collective-permute-start.20 = (bf16[384,512]{1,0:T(8,128)(2,1)S(1)}, bf16[384,512]{1,0:T(8,128)(2,1)S(1)}, u32[]{:S(2)}, u32[]{:S(2)}) collective-permute-start(bf16[384,512]{1,0:T(8,128)(2,1)S(1)} %shard_map.110.refs_0_), channel_id=1, source_target_pairs={{0,1},{1,0},{2,3},{3,2},{4,5},{5,4},{6,7},{7,6},{8,9},{9,8},{10,11... | collective-permute-start | bytes 1179656 | tf_op jit(solution)/shard_map/ppermute | solution.py:701
  71.2 5.8 %collective-permute-start.24 = (bf16[384,512]{1,0:T(8,128)(2,1)S(1)}, bf16[384,512]{1,0:T(8,128)(2,1)S(1)}, u32[]{:S(2)}, u32[]{:S(2)}) collective-permute-start(bf16[384,512]{1,0:T(8,128)(2,1)S(1)} %shard_map.112.refs_2_), channel_id=1, source_target_pairs={{0,1},{1,0},{2,3},{3,2},{4,5},{5,4},{6,7},{7,6},{8,9},{9,8},{10,11... | collective-permute-start | bytes 1179656 | tf_op jit(solution)/shard_map/ppermute | solution.py:701
  72.8 4.2 %collective-permute-start.28 = (bf16[384,512]{1,0:T(8,128)(2,1)S(1)}, bf16[384,512]{1,0:T(8,128)(2,1)S(1)}, u32[]{:S(2)}, u32[]{:S(2)}) collective-permute-start(bf16[384,512]{1,0:T(8,128)(2,1)S(1)} %shard_map.114.refs_4_), channel_id=1, source_target_pairs={{0,1},{1,0},{2,3},{3,2},{4,5},{5,4},{6,7},{7,6},{8,9},{9,8},{10,11... | collective-permute-start | bytes 1179656 | tf_op jit(solution)/shard_map/ppermute | solution.py:701
  74.9 4.7 %collective-permute-start.17 = (bf16[384,512]{1,0:T(8,128)(2,1)S(1)}, bf16[384,512]{1,0:T(8,128)(2,1)S(1)}, u32[]{:S(2)}, u32[]{:S(2)}) collective-permute-start(bf16[384,512]{1,0:T(8,128)(2,1)S(1)} %shard_map.108.refs_0_), channel_id=1, source_target_pairs={{0,1},{1,0},{2,3},{3,2},{4,5},{5,4},{6,7},{7,6},{8,9},{9,8},{10,11... | collective-permute-start | bytes 1179656 | tf_op jit(solution)/shard_map/ppermute | solution.py:701
